TPU v7x, 512 devices: a whole 4x8x8 slice. The times are simulated.
512 devices in a mesh: tok: 32 (over y_lo, z), mdl: 16 (over y_hi, x, core).
Axes of the slice: x: 4, y: 8 (y_hi: 2, y_lo: 4; y = y_hi * 4 + y_lo), z: 8, core: 2. Of those that a mesh axis runs over, the one named last changes fastest.
Arguments:
- activations: bfloat16 [6144, 8192], P('tok'), may hold values from -6 to 6
- rotation: float32 [8192, 8192], P('tok', 'mdl'), may hold values from -6 to 6
- value_weight: bfloat16 [8192, 1024], P('mdl'), may hold values from -0.0625 to 0.0625
- token_code: int32 [6144], P('tok'), may hold values from 1 to 8
- channel_code: int32 [1024], replicated, may hold values from 1 to 8
Outputs:
- new_rows: float32 [256, 8192], P('tok', 'mdl')
- recon_error: float32 [6144, 1024], P('tok')
All inputs are finite; a program needn't handle non-finite values.
Results may differ from a plain program's by a relative error of at most 0.004.
Values may be sent and summed in bfloat16 or wider, within the bound.
No kernel may reach another device: no remote copies, remote signals or barrier semaphores. Data moves between devices by JAX's collectives and lax.ppermute only.
A program may use at most 64 MiB of HBM per device.

v0:
```python
import math

import jax
import jax.numpy as jnp
from jax import lax
from jax.sharding import PartitionSpec as P

WIN = 8


STEP_GAIN = 0.4


def cayley_terms(mats, stack_a, stack_g):
    row_total = stack_a.shape[0]
    stacked = jnp.concatenate([stack_a, stack_g], 0)
    products = lax.psum(
        jnp.einsum("rd,kd->rk", mats, stacked, preferred_element_type=jnp.float32), "mdl"
    )
    return (
        products[:, :row_total].astype(jnp.bfloat16),
        products[:, row_total:].astype(jnp.bfloat16),
    )


def partial_rows(left_a, left_g, stack_a, stack_g):
    return jnp.dot(left_a, stack_g, preferred_element_type=jnp.float32) - jnp.dot(
        left_g, stack_a, preferred_element_type=jnp.float32
    )


def local(activations, rotation, value_weight, token_code, channel_code):
    n_tok = lax.axis_size("tok")
    tok_pos = lax.axis_index("tok")
    mdl_pos = lax.axis_index("mdl")
    block_rows = rotation.shape[0]
    narrow = rotation.shape[1]
    model_width = activations.shape[1]
    channels = value_weight.shape[1]
    chan_share = channels // n_tok
    tok_rows = activations.shape[0]
    width_root = math.sqrt(model_width)
    rot_b = rotation.astype(jnp.bfloat16)
    own_cols = lax.dynamic_slice_in_dim(value_weight, tok_pos * chan_share, chan_share, 1)
    weight_rows = lax.all_gather(own_cols.T, "mdl", axis=1, tiled=True)
    rot_panel = lax.all_gather(rot_b, "tok", axis=0, tiled=True)
    rotated = jnp.dot(activations, rot_panel, preferred_element_type=jnp.float32)
    turned = jnp.dot(weight_rows, rot_panel, preferred_element_type=jnp.float32)
    window = rot_panel.reshape(n_tok, block_rows, narrow)[:, :WIN].reshape(n_tok * WIN, narrow)
    rotated = rotated / width_root
    turned = turned / width_root
    act_clip = token_code.astype(jnp.float32)[:, None] * 0.5
    act_tanh = jnp.tanh(rotated / act_clip)
    quant_act = (act_clip * act_tanh).astype(jnp.bfloat16)
    own_codes = lax.dynamic_slice_in_dim(channel_code, tok_pos * chan_share, chan_share, 0)
    weight_clip = own_codes.astype(jnp.float32)[:, None] / (4.0 * width_root)
    weight_tanh = jnp.tanh(turned / weight_clip)
    quant_weight = (weight_clip * weight_tanh).astype(jnp.bfloat16)
    weight_full = lax.all_gather(quant_weight, "tok", axis=0, tiled=True)
    own_feats = lax.dynamic_slice_in_dim(activations, mdl_pos * narrow, narrow, 1)
    partial_err = jnp.einsum(
        "td,cd->tc", quant_act, weight_full, preferred_element_type=jnp.float32
    ) - jnp.dot(own_feats, value_weight, preferred_element_type=jnp.float32)
    recon_error = lax.psum(partial_err, "mdl")
    error_bf = recon_error.astype(jnp.bfloat16)
    grad_act = (
        jnp.dot(error_bf, weight_full, preferred_element_type=jnp.float32)
        * (1.0 - act_tanh * act_tanh)
    ).astype(jnp.bfloat16)
    grad_quant = lax.psum_scatter(
        jnp.einsum("tc,td->cd", error_bf, quant_act, preferred_element_type=jnp.float32),
        "tok",
        scatter_dimension=0,
        tiled=True,
    )
    grad_turned = (grad_quant * (1.0 - weight_tanh * weight_tanh)).astype(jnp.bfloat16)
    stack_a = jnp.concatenate([rotated.astype(jnp.bfloat16), turned.astype(jnp.bfloat16)], 0)
    stack_g = jnp.concatenate([grad_act, grad_turned], 0)
    step_size = STEP_GAIN / math.sqrt(tok_rows * n_tok * channels)
    own_rows = rotation[:WIN]
    left_a, left_g = cayley_terms(window, stack_a, stack_g)
    first_sum = lax.psum(partial_rows(left_a, left_g, stack_a, stack_g), "tok")
    all_rows = lax.all_gather(own_rows, "tok", axis=0, tiled=True)
    updated = all_rows - step_size * first_sum
    second_in = (all_rows + updated).astype(jnp.bfloat16)
    next_a, next_g = cayley_terms(second_in, stack_a, stack_g)
    last_sum = lax.psum_scatter(
        partial_rows(next_a, next_g, stack_a, stack_g), "tok", scatter_dimension=0, tiled=True
    )
    new_rows = own_rows - 0.5 * step_size * last_sum
    return (new_rows, recon_error)


def solution(mesh):
    in_specs = (P("tok", None), P("tok", "mdl"), P("mdl", None), P("tok"), P())
    out_specs = (P("tok", "mdl"), P("tok", None))
    return jax.shard_map(local, mesh=mesh, in_specs=in_specs, out_specs=out_specs, check_vma=False)
```

profile of v0, /device:TPU:4, one launch (start us, length us, event | category | flops | bytes accessed | tf_op | source)
XLA Modules:
  0.0 1352.6 jit_solution(14827833877006518270)
XLA Ops:
  7.2 0.0 copy-start
  7.2 0.0 all-gather.3.cloned.1.call-start
  7.2 1.9 convert_element_type.37
  9.2 0.0 all-gather.3.cloned.1.call-update
  9.2 0.0 all-gather.5.cloned.1.call-start
  9.2 0.8 convert_multiply_fusion.1
  10.0 1.0 dynamic-slice_bitcast_fusion
  11.0 43.7 %all_gather.14 = bf16[32,8192]{0,1:T(8,128)(2,1)} all-gather(bf16[32,512]{0,1:T(8,128)(2,1)S(1)} %dynamic-slice_bitcast_fusion), channel_id=1, replica_groups=mesh['tok'=32,'mdl'=16] {'mdl'}, dimensions={1}, use_global_device_ids=true | all-gather | bytes 557056 | tf_op jit(solution)/shard_map/all_gather | solution.py:45
  54.7 130.8 %all-gather.3.cloned.1.call-done = bf16[8192,512]{1,0:T(8,128)(2,1)} async-done(((bf16[256,512]{1,0:T(8,128)(2,1)}), bf16[8192,512]{1,0:T(8,128)(2,1)}) %all-gather.3.cloned.1.call-update) | async-done | bytes 8388624 | tf_op jit(solution)/shard_map/all_gather | solution.py:46
  185.5 6.2 multiply_convert_fusion.2
  191.7 0.0 copy-done.8
  191.7 0.0 all-gather.5.cloned.1.call-update
  191.7 0.0 all-reduce.5.cloned.1.call-start
  191.8 0.0 copy-done.9
  191.8 5.9 fusion.25
  197.8 148.9 %all-gather.5.cloned.1.call-done = bf16[1024,512]{1,0:T(8,128)(2,1)} async-done(((bf16[32,512]{1,0:T(8,128)(2,1)}), bf16[1024,512]{1,0:T(8,128)(2,1)}) %all-gather.5.cloned.1.call-update) | async-done | bytes 1048592 | tf_op jit(solution)/shard_map/all_gather | solution.py:59
  346.7 2.0 fusion.23
  348.7 1.3 convolution_subtract_fusion
  349.9 0.0 all-reduce.5.cloned.1.call-update
  350.0 0.0 reduce-scatter.3.cloned.1.call-start
  350.0 170.1 %all-reduce.5.cloned.1.call-done = f32[192,1024]{1,0:T(8,128)} async-done(((f32[192,1024]{1,0:T(8,128)}), f32[192,1024]{1,0:T(8,128)}) %all-reduce.5.cloned.1.call-update) | async-done | bytes 786448 | tf_op jit(solution)/shard_map/psum | solution.py:64
  520.2 3.2 fusion.5
  523.3 0.0 reduce-scatter.3.cloned.1.call-update
  523.3 0.0 all-reduce.7.cloned.1.call-start
  523.4 1.9 fusion
  525.3 0.0 copy-start.2
  525.3 0.0 slice-start
  525.3 173.0 %reduce-scatter.3.cloned.1.call-done = f32[32,512]{1,0:T(8,128)} async-done(((f32[1024,512]{1,0:T(8,128)}), f32[32,512]{1,0:T(8,128)}) %reduce-scatter.3.cloned.1.call-update) | async-done | bytes 65552 | tf_op jit(solution)/shard_map/reduce_scatter | solution.py:70
  698.4 1.0 fusion.24
  699.4 0.6 copy-done.4
  700.0 0.0 copy-done.6
  700.0 2.0 convolution_bitcast_fusion
  702.0 76.4 %all-reduce.8 = bf16[256,448]{0,1:T(8,128)(2,1)S(1)} all-reduce(f32[256,448]{0,1:T(8,128)} %convolution_bitcast_fusion), channel_id=1, replica_groups=mesh['tok'=32,'mdl'=16] {'mdl'}, use_global_device_ids=true, to_apply=%region_2.0 | all-reduce | flops 114688 | bytes 688128 | tf_op jit(solution)/shard_map/psum | solution.py:17
  778.5 1.2 fusion.10
  779.7 2.0 convolution_subtract_fusion.2
  781.7 0.0 all-reduce.7.cloned.1.call-update
  781.7 0.0 reduce-scatter.5.cloned.1.call-start
  781.8 0.0 slice-done
  781.8 82.3 %all_gather.12 = f32[256,512]{1,0:T(8,128)} all-gather(f32[8,512]{1,0:T(8,128)S(1)} %slice-done), channel_id=1, replica_groups=mesh['tok'=32,'mdl'=16] {'tok'}, dimensions={0}, use_global_device_ids=true | all-gather | bytes 540672 | tf_op jit(solution)/shard_map/all_gather | solution.py:83
  864.1 229.1 %all-reduce.7.cloned.1.call-done = f32[256,512]{1,0:T(8,128)} async-done(((f32[256,512]{1,0:T(8,128)}), f32[256,512]{1,0:T(8,128)}) %all-reduce.7.cloned.1.call-update) | async-done | bytes 524304 | tf_op jit(solution)/shard_map/psum | solution.py:82
  1093.2 2.4 fusion.2
  1095.6 76.2 %all-reduce.9 = bf16[256,448]{0,1:T(8,128)(2,1)S(1)} all-reduce(f32[256,448]{0,1:T(8,128)} %fusion.2), channel_id=1, replica_groups=mesh['tok'=32,'mdl'=16] {'mdl'}, use_global_device_ids=true, to_apply=%region_4.0 | all-reduce | flops 114688 | bytes 688128 | tf_op jit(solution)/shard_map/psum | solution.py:17
  1171.8 1.2 fusion.9
  1173.0 2.0 convolution_subtract_fusion.1
  1175.0 0.0 reduce-scatter.5.cloned.1.call-update
  1175.0 167.4 %reduce-scatter.5.cloned.1.call-done = f32[8,512]{1,0:T(8,128)} async-done(((f32[256,512]{1,0:T(8,128)}), f32[8,512]{1,0:T(8,128)}) %reduce-scatter.5.cloned.1.call-update) | async-done | bytes 16400 | tf_op jit(solution)/shard_map/reduce_scatter | solution.py:87
  1342.4 1.3 multiply_subtract_fusion
  1343.7 2.1 copy.13
  (15 shorter events, 0.0 us)
Async XLA Ops:
  7.2 184.7 %copy-start = (bf16[192,8192]{1,0:T(8,128)(2,1)S(1)}, bf16[192,8192]{1,0:T(8,128)(2,1)}, u32[]{:S(2)}) copy-start(bf16[192,8192]{1,0:T(8,128)(2,1)} %param.5) | copy-start | bytes 9437188
  7.2 178.3 %all-gather.3.cloned.1.call-start = ((), (), s32[]{:S(2)}) async-start(), calls=%async_computation.2 | async-start | bytes 8650752 | tf_op jit(solution)/shard_map/all_gather | solution.py:46
  9.2 337.5 %all-gather.5.cloned.1.call-start = ((), (), s32[]{:S(2)}) async-start(), calls=%async_computation.3 | async-start | bytes 1081344 | tf_op jit(solution)/shard_map/all_gather | solution.py:59
  10.0 181.7 %copy-start.8 = (f32[32]{0:T(128)}, f32[32]{0:T(128)S(1)}, u32[]{:S(2)}) copy-start(f32[32]{0:T(128)S(1)} %convert_multiply_fusion.1) | copy-start | bytes 388
  54.7 137.1 %copy-start.9 = (s32[192]{0:T(256)S(1)}, s32[192]{0:T(256)}, u32[]{:S(2)}) copy-start(s32[192]{0:T(256)} %param.8) | copy-start | bytes 2308
  191.7 328.4 %all-reduce.5.cloned.1.call-start = ((), (), s32[]{:S(2)}) async-start(), calls=%async_computation.4 | async-start | bytes 1572864 | tf_op jit(solution)/shard_map/psum | solution.py:64
  197.8 501.6 %copy-start.3 = (bf16[192,512]{1,0:T(8,128)(2,1)}, bf16[192,512]{1,0:T(8,128)(2,1)S(1)}, u32[]{:S(2)}) copy-start(bf16[192,512]{1,0:T(8,128)(2,1)S(1)} %get-tuple-element.6) | copy-start | bytes 589828
  346.7 2.0 copy-start.1
  350.0 348.4 %reduce-scatter.3.cloned.1.call-start = ((), (), s32[]{:S(2)}) async-start(), calls=%async_computation.5 | async-start | bytes 2162688 | tf_op jit(solution)/shard_map/reduce_scatter | solution.py:70
  523.3 569.9 %all-reduce.7.cloned.1.call-start = ((), (), s32[]{:S(2)}) async-start(), calls=%async_computation.6 | async-start | bytes 1048576 | tf_op jit(solution)/shard_map/psum | solution.py:82
  525.3 174.1 %copy-start.2 = (bf16[192,512]{1,0:T(8,128)(2,1)}, bf16[192,512]{1,0:T(8,128)(2,1)S(1)}, u32[]{:S(2)}) copy-start(bf16[192,512]{1,0:T(8,128)(2,1)S(1)} %fusion) | copy-start | bytes 589828
  525.3 256.4 %slice-start = ((f32[256,512]{1,0:T(8,128)}), f32[8,512]{1,0:T(8,128)S(1)}, s32[]{:S(2)}) async-start(f32[256,512]{1,0:T(8,128)} %param.6), calls=%async_computation.8 | async-start | bytes 32768 | tf_op jit(solution)/shard_map/slice | solution.py:80
  699.4 0.6 copy-start.4
  699.4 0.6 copy-start.6
  702.0 391.2 %copy-start.5 = (bf16[32,512]{1,0:T(8,128)(2,1)S(1)}, bf16[32,512]{1,0:T(8,128)(2,1)}, u32[]{:S(2)}) copy-start(bf16[32,512]{1,0:T(8,128)(2,1)} %copy-done.4) | copy-start | bytes 98308
  702.0 391.2 %copy-start.7 = (bf16[32,512]{1,0:T(8,128)(2,1)S(1)}, bf16[32,512]{1,0:T(8,128)(2,1)}, u32[]{:S(2)}) copy-start(bf16[32,512]{1,0:T(8,128)(2,1)} %copy-done.6) | copy-start | bytes 98308
  781.7 560.7 %reduce-scatter.5.cloned.1.call-start = ((), (), s32[]{:S(2)}) async-start(), calls=%async_computation.7 | async-start | bytes 540672 | tf_op jit(solution)/shard_map/reduce_scatter | solution.py:87
Sparse Core Ops, SparseCore 0:
  10.7 174.7 all-gather.2
  191.9 154.7 all-gather.4
  350.2 169.9 all-reduce.4
  523.5 174.8 reduce-scatter.2
  781.8 311.3 all-reduce.6
  1175.1 167.2 reduce-scatter.4
where the time goes:
time: 1350 us
  waiting for transfers between devices  1020 us (76%)
  blocking collectives  279 us (21%)
  matrix products  31.2 us (2%)
  between operations  14.3 us (1%)
    psum x1, waiting for transfers between devices, local(): first_sum = lax.psum(partial_rows(left_a, left_g, stack_a, stack_g), 'tok')  229 us
    reduce_scatter x1, waiting for transfers between devices, local(): lax.psum_scatter(jnp.einsum('tc,td->cd', error_bf, quant_act, preferred_e...  173 us
    psum x1, waiting for transfers between devices, local(): recon_error = lax.psum(partial_err, 'mdl')  170 us
    reduce_scatter x1, waiting for transfers between devices, local(): lax.psum_scatter(partial_rows(next_a, next_g, stack_a, stack_g), 'tok', s...  167 us
    psum x2, blocking collectives, cayley_terms(): lax.psum(jnp.einsum('rd,kd->rk', mats, stacked, preferred_element_type=jn...  153 us
    all_gather x1, waiting for transfers between devices, local(): weight_full = lax.all_gather(quant_weight, 'tok', axis=0, tiled=True)  149 us
    all_gather x1, waiting for transfers between devices, local(): rot_panel = lax.all_gather(rot_b, 'tok', axis=0, tiled=True)  131 us
    all_gather x1, blocking collectives, local(): all_rows = lax.all_gather(own_rows, 'tok', axis=0, tiled=True)  82.3 us
  transfers between devices with their start and end apart: 6, of which 6 were waited for; matrix products, arithmetic and copies ran while one was open for 1% of the time, Pallas kernels for 0%

commit v1 on v0

v1 whole, which is shorter than its diff:
```python
import math

import jax
import jax.numpy as jnp
from jax import lax
from jax.sharding import PartitionSpec as P

WIN = 8


STEP_GAIN = 0.4


def gather_blocks(own, axis):
    parts = lax.axis_size(axis)
    return lax.all_to_all(jnp.broadcast_to(own[None], (parts,) + own.shape), axis, 0, 0)


def sum_blocks(blocks, axis):
    return jnp.sum(lax.all_to_all(blocks, axis, 0, 0).astype(jnp.float32), 0)


def cayley_lefts(mats, stack_a, stack_g):
    rows = mats.shape[0]
    row_total = stack_a.shape[0]
    parts = lax.axis_size("mdl")
    stacked = jnp.concatenate([stack_a, stack_g], 0)
    products = jnp.einsum("rd,kd->rk", mats, stacked, preferred_element_type=jnp.float32)
    products = products.astype(jnp.bfloat16).reshape(parts, rows // parts, 2 * row_total)
    own_sum = sum_blocks(products, "mdl").astype(jnp.bfloat16)
    lefts = gather_blocks(own_sum, "mdl").reshape(rows, 2 * row_total)
    return lefts[:, :row_total], lefts[:, row_total:]


def cayley_own(mats, stack_a, stack_g):
    left_a, left_g = cayley_lefts(mats, stack_a, stack_g)
    partial = jnp.dot(left_a, stack_g, preferred_element_type=jnp.float32) - jnp.dot(
        left_g, stack_a, preferred_element_type=jnp.float32
    )
    parts = lax.axis_size("tok")
    return sum_blocks(partial.reshape(parts, -1, partial.shape[1]), "tok")


def local(activations, rotation, value_weight, token_code, channel_code):
    n_tok = lax.axis_size("tok")
    n_mdl = lax.axis_size("mdl")
    tok_pos = lax.axis_index("tok")
    mdl_pos = lax.axis_index("mdl")
    block_rows = rotation.shape[0]
    narrow = rotation.shape[1]
    model_width = activations.shape[1]
    channels = value_weight.shape[1]
    chan_share = channels // n_tok
    tok_rows = activations.shape[0]
    width_root = math.sqrt(model_width)
    rot_b = rotation.astype(jnp.bfloat16)
    rot_panel = lax.all_gather(rot_b, "tok", axis=0, tiled=True)
    own_cols = lax.dynamic_slice_in_dim(value_weight, tok_pos * chan_share, chan_share, 1)
    weight_rows = gather_blocks(own_cols.T, "mdl").transpose(1, 0, 2).reshape(chan_share, model_width)
    own_feats = lax.dynamic_slice_in_dim(activations, mdl_pos * narrow, narrow, 1)
    plain = jnp.dot(own_feats, value_weight, preferred_element_type=jnp.float32)

    turned = jnp.dot(weight_rows, rot_panel, preferred_element_type=jnp.float32) / width_root
    own_codes = lax.dynamic_slice_in_dim(channel_code, tok_pos * chan_share, chan_share, 0)
    weight_clip = own_codes.astype(jnp.float32)[:, None] / (4.0 * width_root)
    weight_tanh = jnp.tanh(turned / weight_clip)
    quant_weight = (weight_clip * weight_tanh).astype(jnp.bfloat16)
    weight_full = gather_blocks(quant_weight, "tok").reshape(channels, narrow)

    rotated = jnp.dot(activations, rot_panel, preferred_element_type=jnp.float32) / width_root
    act_clip = token_code.astype(jnp.float32)[:, None] * 0.5
    act_tanh = jnp.tanh(rotated / act_clip)
    quant_act = (act_clip * act_tanh).astype(jnp.bfloat16)
    window = rot_panel.reshape(n_tok, block_rows, narrow)[:, :WIN].reshape(n_tok * WIN, narrow)

    partial_err = (
        jnp.einsum("td,cd->tc", quant_act, weight_full, preferred_element_type=jnp.float32) - plain
    )
    lanes = channels * 2 // n_mdl
    halves = partial_err.reshape(2, tok_rows // 2, n_mdl // 2, lanes).transpose(0, 2, 1, 3)
    own_err = sum_blocks(halves.reshape(n_mdl, tok_rows // 2, lanes), "mdl")
    recon_error = gather_blocks(own_err, "mdl").reshape(2, n_mdl // 2, tok_rows // 2, lanes)
    recon_error = recon_error.transpose(0, 2, 1, 3).reshape(tok_rows, channels)
    error_bf = recon_error.astype(jnp.bfloat16)
    grad_quant = sum_blocks(
        jnp.einsum("tc,td->cd", error_bf, quant_act, preferred_element_type=jnp.float32)
        .astype(jnp.bfloat16)
        .reshape(n_tok, chan_share, narrow),
        "tok",
    )
    grad_act = (
        jnp.dot(error_bf, weight_full, preferred_element_type=jnp.float32)
        * (1.0 - act_tanh * act_tanh)
    ).astype(jnp.bfloat16)
    grad_turned = (grad_quant * (1.0 - weight_tanh * weight_tanh)).astype(jnp.bfloat16)
    stack_a = jnp.concatenate([rotated.astype(jnp.bfloat16), turned.astype(jnp.bfloat16)], 0)
    stack_g = jnp.concatenate([grad_act, grad_turned], 0)
    step_size = STEP_GAIN / math.sqrt(tok_rows * n_tok * channels)
    own_rows = rotation[:WIN]
    moved = own_rows - step_size * cayley_own(window, stack_a, stack_g)
    second_in = gather_blocks((own_rows + moved).astype(jnp.bfloat16), "tok")
    second_in = second_in.reshape(n_tok * WIN, narrow)
    new_rows = own_rows - 0.5 * step_size * cayley_own(second_in, stack_a, stack_g)
    return (new_rows, recon_error)


def solution(mesh):
    in_specs = (P("tok", None), P("tok", "mdl"), P("mdl", None), P("tok"), P())
    out_specs = (P("tok", "mdl"), P("tok", None))
    return jax.shard_map(local, mesh=mesh, in_specs=in_specs, out_specs=out_specs, check_vma=False)
```

time: 1350 us -> 483 us (0.36)
  the two profiles are of different devices: /device:TPU:4 before, /device:TPU:64 now
where the time goes in v1:
time: 483 us; the launch traced here: 481 us
  waiting for transfers between devices  210 us (43%)
  blocking collectives  185 us (38%)
  matrix products  27.4 us (6%)
  starting transfers between devices  22.1 us (5%)
  between operations  14.3 us (3%)
  other arithmetic  11.8 us (2%)
  local copies, waits for them, and re-layouts  11.1 us (2%)
    all_gather x1, waiting for transfers between devices, local(): rot_panel = lax.all_gather(rot_b, 'tok', axis=0, tiled=True)  157 us
    all_to_all x5, blocking collectives, sum_blocks(): return jnp.sum(lax.all_to_all(blocks, axis, 0, 0).astype(jnp.float32), 0)  110 us
    all_to_all x4, blocking collectives, gather_blocks(): lax.all_to_all(jnp.broadcast_to(own[None], (parts,) + own.shape), axis, 0...  74.6 us
    all_to_all x2, waiting for transfers between devices, gather_blocks(): lax.all_to_all(jnp.broadcast_to(own[None], (parts,) + own.shape), axis, 0...  27.6 us
    all_to_all x1, waiting for transfers between devices, sum_blocks(): return jnp.sum(lax.all_to_all(blocks, axis, 0, 0).astype(jnp.float32), 0)  25.1 us
    all_to_all x2, starting transfers between devices, gather_blocks(): lax.all_to_all(jnp.broadcast_to(own[None], (parts,) + own.shape), axis, 0...  14.2 us
  transfers between devices with their start and end apart: 4, of which 4 were waited for; matrix products, arithmetic and copies ran while one was open for 3% of the time, Pallas kernels for 0%

profile of v1, /device:TPU:64, one launch (start us, length us, event | category | flops | bytes accessed | tf_op | source)
XLA Modules:
  0.0 481.1 jit_solution(5757672321225676747)
XLA Ops:
  7.2 2.0 convert_element_type.57
  9.2 1.0 dynamic-slice_bitcast_fusion
  10.3 0.9 broadcast_in_dim.12
  11.2 9.7 %all-to-all-start = ((bf16[16,32,512]{2,1,0:T(8,128)(2,1)}), bf16[16,32,512]{2,1,0:T(8,128)(2,1)}, u32[]{:S(2)}, u32[]{:S(2)}) async-start(bf16[16,32,512]{2,1,0:T(8,128)(2,1)} %broadcast_in_dim.12), calls=%async_computation | async-start | bytes 1048576 | tf_op jit(solution)/shard_map/all_to_all | solution.py:16
  20.9 0.8 convert_multiply_fusion.1
  21.7 16.0 %all-to-all-done = bf16[16,32,512]{2,1,0:T(8,128)(2,1)} async-done(((bf16[16,32,512]{2,1,0:T(8,128)(2,1)}), bf16[16,32,512]{2,1,0:T(8,128)(2,1)}, u32[]{:S(2)}, u32[]{:S(2)}) %all-to-all-start) | async-done | bytes 524320 | tf_op jit(solution)/shard_map/all_to_all | solution.py:16
  37.6 1.9 copy.25
  39.5 157.0 %all-gather.2.cloned.1.call-done = bf16[8192,512]{1,0:T(8,128)(2,1)} async-done(((bf16[256,512]{1,0:T(8,128)(2,1)}), bf16[8192,512]{1,0:T(8,128)(2,1)}) %all-gather.2.cloned.1.call-update) | async-done | bytes 8388624 | tf_op jit(solution)/shard_map/all_gather | solution.py:57
  196.6 5.7 %multiply_convert_fusion.2 = (bf16[32,512]{1,0:T(8,128)(2,1)S(1)}, f32[32,512]{1,0:T(8,128)}) fusion(f32[32]{0:T(128)S(1)} %convert_multiply_fusion.1, bf16[32,8192]{1,0:T(8,128)(2,1)} %bitcast.54, bf16[8192,512]{1,0:T(8,128)(2,1)} %all-gather.2.cloned.1.call-done), kind=kOutput, calls=%fused_computation.35 | convolution fusion | flops 268500992 | bytes 9011328 | tf_op jit(solution)/shard_map/dot_general | solution.py:63
  202.3 1.1 broadcast_in_dim.13
  203.4 4.5 all-to-all-start.1
  207.9 5.9 %fusion.26 = (bf16[192,512]{1,0:T(8,128)(2,1)S(1)}, f32[192,512]{1,0:T(8,128)}) fusion(bf16[192,8192]{1,0:T(8,128)(2,1)S(1)} %copy-done, bf16[8192,512]{1,0:T(8,128)(2,1)} %all-gather.2.cloned.1.call-done), kind=kOutput, calls=%fused_computation.51 | convolution fusion | flops 1610809344 | bytes 12124160 | tf_op jit(solution)/shard_map/dot_general | solution.py:70
  213.8 11.6 %all-to-all-done.1 = bf16[32,32,512]{2,1,0:T(8,128)(2,1)} async-done(((bf16[32,32,512]{2,1,0:T(8,128)(2,1)}), bf16[32,32,512]{2,1,0:T(8,128)(2,1)}, u32[]{:S(2)}, u32[]{:S(2)}) %all-to-all-start.1) | async-done | bytes 1048608 | tf_op jit(solution)/shard_map/all_to_all | solution.py:16
  225.4 1.9 fusion.24
  227.2 1.6 fusion
  229.2 26.7 %all_to_all.60 = f32[16,96,128]{2,1,0:T(8,128)} all-to-all(f32[16,96,128]{2,1,0:T(8,128)S(1)} %bitcast.56), channel_id=1, replica_groups=mesh['tok'=32,'mdl'=16] {'mdl'}, dimensions={0} | all-to-all | bytes 1572864 | tf_op jit(solution)/shard_map/all_to_all | solution.py:20
  255.9 1.2 reduce_sum.60
  257.1 28.6 %all_to_all.61 = f32[16,96,128]{2,1,0:T(8,128)S(1)} all-to-all(f32[16,96,128]{2,1,0:T(8,128)S(1)} %broadcast_in_dim.14), channel_id=1, replica_groups=mesh['tok'=32,'mdl'=16] {'mdl'}, dimensions={0} | all-to-all | bytes 1572864 | tf_op jit(solution)/shard_map/all_to_all | solution.py:16
  285.8 0.9 copy-done.1
  286.6 0.5 copy.22
  287.2 0.9 copy-done.3
  288.1 2.5 convolution_convert_fusion
  290.6 7.9 %all-to-all-start.4 = ((bf16[32,32,512]{2,1,0:T(8,128)(2,1)}), bf16[32,32,512]{2,1,0:T(8,128)(2,1)}, u32[]{:S(2)}, u32[]{:S(2)}) async-start(bf16[32,32,512]{2,1,0:T(8,128)(2,1)} %bitcast.58), calls=%async_computation.4 | async-start | bytes 2097152 | tf_op jit(solution)/shard_map/all_to_all | solution.py:20
  298.5 1.2 convert_element_type.64
  299.9 1.7 fusion.3
  301.6 25.1 %all-to-all-done.4 = bf16[32,32,512]{2,1,0:T(8,128)(2,1)} async-done(((bf16[32,32,512]{2,1,0:T(8,128)(2,1)}), bf16[32,32,512]{2,1,0:T(8,128)(2,1)}, u32[]{:S(2)}, u32[]{:S(2)}) %all-to-all-start.4) | async-done | bytes 1048608 | tf_op jit(solution)/shard_map/all_to_all | solution.py:20
  326.7 1.4 convert_reduce_fusion
  328.1 1.0 fusion.25
  329.1 0.6 copy-done.5
  329.8 2.0 fusion.4
  331.7 1.8 copy.23
  333.5 15.6 %all_to_all.62 = bf16[16,16,448]{2,1,0:T(8,128)(2,1)S(1)} all-to-all(bf16[16,16,448]{2,1,0:T(8,128)(2,1)} %bitcast.59), channel_id=1, replica_groups=mesh['tok'=32,'mdl'=16] {'mdl'}, dimensions={0} | all-to-all | bytes 458752 | tf_op jit(solution)/shard_map/all_to_all | solution.py:20
  349.2 14.7 %all_to_all.63 = bf16[16,16,448]{2,1,0:T(8,128)(2,1)S(1)} all-to-all(bf16[16,16,448]{2,1,0:T(8,128)(2,1)S(1)} %broadcast_in_dim.15), channel_id=1, replica_groups=mesh['tok'=32,'mdl'=16] {'mdl'}, dimensions={0} | all-to-all | bytes 458752 | tf_op jit(solution)/shard_map/all_to_all | solution.py:16
  363.8 1.2 fusion.11
  365.0 1.2 fusion.2
  366.3 26.6 %all_to_all.64 = f32[32,8,512]{2,1,0:T(8,128)} all-to-all(f32[32,8,512]{2,1,0:T(8,128)S(1)} %fusion.2), channel_id=1, replica_groups=mesh['tok'=32,'mdl'=16] {'tok'}, dimensions={0} | all-to-all | bytes 1048576 | tf_op jit(solution)/shard_map/all_to_all | solution.py:20
  392.9 1.1 reduce_sum.63
  394.0 0.7 fusion.16
  394.7 16.6 %all_to_all.65 = bf16[32,8,512]{2,1,0:T(8,128)(2,1)S(1)} all-to-all(bf16[32,8,512]{2,1,0:T(8,128)(2,1)S(1)} %broadcast_in_dim.16), channel_id=1, replica_groups=mesh['tok'=32,'mdl'=16] {'tok'}, dimensions={0} | all-to-all | bytes 524288 | tf_op jit(solution)/shard_map/all_to_all | solution.py:16
  411.4 1.4 convolution_convert_fusion.1
  412.7 0.8 copy.24
  413.6 15.6 %all_to_all.66 = bf16[16,16,448]{2,1,0:T(8,128)(2,1)S(1)} all-to-all(bf16[16,16,448]{2,1,0:T(8,128)(2,1)} %bitcast.60), channel_id=1, replica_groups=mesh['tok'=32,'mdl'=16] {'mdl'}, dimensions={0} | all-to-all | bytes 458752 | tf_op jit(solution)/shard_map/all_to_all | solution.py:20
  429.2 14.7 %all_to_all.67 = bf16[16,16,448]{2,1,0:T(8,128)(2,1)S(1)} all-to-all(bf16[16,16,448]{2,1,0:T(8,128)(2,1)S(1)} %broadcast_in_dim.17), channel_id=1, replica_groups=mesh['tok'=32,'mdl'=16] {'mdl'}, dimensions={0} | all-to-all | bytes 458752 | tf_op jit(solution)/shard_map/all_to_all | solution.py:16
  443.9 1.1 fusion.10
  445.1 1.2 fusion.1
  446.3 25.6 %all_to_all.68 = f32[32,8,512]{2,1,0:T(8,128)} all-to-all(f32[32,8,512]{2,1,0:T(8,128)S(1)} %fusion.1), channel_id=1, replica_groups=mesh['tok'=32,'mdl'=16] {'tok'}, dimensions={0} | all-to-all | bytes 1048576 | tf_op jit(solution)/shard_map/all_to_all | solution.py:20
  471.9 1.1 reduce_sum.65
  473.0 1.3 multiply_subtract_fusion
  (31 shorter events, 1.0 us)
Async XLA Ops:
  7.2 200.7 %copy-start = (bf16[192,8192]{1,0:T(8,128)(2,1)S(1)}, bf16[192,8192]{1,0:T(8,128)(2,1)}, u32[]{:S(2)}) copy-start(bf16[192,8192]{1,0:T(8,128)(2,1)} %param.5) | copy-start | bytes 9437188
  7.2 189.4 %all-gather.2.cloned.1.call-start = ((), (), s32[]{:S(2)}) async-start(), calls=%async_computation.12 | async-start | bytes 8650752 | tf_op jit(solution)/shard_map/all_gather | solution.py:57
  11.2 26.5 %all-to-all-start = ((bf16[16,32,512]{2,1,0:T(8,128)(2,1)}), bf16[16,32,512]{2,1,0:T(8,128)(2,1)}, u32[]{:S(2)}, u32[]{:S(2)}) async-start(bf16[16,32,512]{2,1,0:T(8,128)(2,1)} %broadcast_in_dim.12), calls=%async_computation | async-start | bytes 1048576 | tf_op jit(solution)/shard_map/all_to_all | solution.py:16
  196.6 11.3 %copy-start.9 = (s32[192]{0:T(256)S(1)}, s32[192]{0:T(256)}, u32[]{:S(2)}) copy-start(s32[192]{0:T(256)} %param.8) | copy-start | bytes 2308
  203.4 22.0 %all-to-all-start.1 = ((bf16[32,32,512]{2,1,0:T(8,128)(2,1)}), bf16[32,32,512]{2,1,0:T(8,128)(2,1)}, u32[]{:S(2)}, u32[]{:S(2)}) async-start(bf16[32,32,512]{2,1,0:T(8,128)(2,1)} %broadcast_in_dim.13), calls=%async_computation.1 | async-start | bytes 2097152 | tf_op jit(solution)/shard_map/all_to_all | solution.py:16
  213.8 115.4 %copy-start.4 = (bf16[192,512]{1,0:T(8,128)(2,1)}, bf16[192,512]{1,0:T(8,128)(2,1)S(1)}, u32[]{:S(2)}) copy-start(bf16[192,512]{1,0:T(8,128)(2,1)S(1)} %get-tuple-element.6) | copy-start | bytes 589828
  285.7 0.9 copy-start.1
  287.2 0.9 copy-start.3
  290.6 36.1 %all-to-all-start.4 = ((bf16[32,32,512]{2,1,0:T(8,128)(2,1)}), bf16[32,32,512]{2,1,0:T(8,128)(2,1)}, u32[]{:S(2)}, u32[]{:S(2)}) async-start(bf16[32,32,512]{2,1,0:T(8,128)(2,1)} %bitcast.58), calls=%async_computation.4 | async-start | bytes 2097152 | tf_op jit(solution)/shard_map/all_to_all | solution.py:20
  301.6 31.9 %copy-start.2 = (bf16[192,512]{1,0:T(8,128)(2,1)}, bf16[192,512]{1,0:T(8,128)(2,1)S(1)}, u32[]{:S(2)}) copy-start(bf16[192,512]{1,0:T(8,128)(2,1)S(1)} %fusion.3) | copy-start | bytes 589828
  329.1 0.6 copy-start.5
  329.1 0.6 copy-start.7
  331.7 112.2 %copy-start.6 = (bf16[32,512]{1,0:T(8,128)(2,1)S(1)}, bf16[32,512]{1,0:T(8,128)(2,1)}, u32[]{:S(2)}) copy-start(bf16[32,512]{1,0:T(8,128)(2,1)} %copy-done.5) | copy-start | bytes 98308
  331.7 113.3 %copy-start.8 = (bf16[32,512]{1,0:T(8,128)(2,1)S(1)}, bf16[32,512]{1,0:T(8,128)(2,1)}, u32[]{:S(2)}) copy-start(bf16[32,512]{1,0:T(8,128)(2,1)} %copy-done.7) | copy-start | bytes 98308
Sparse Core Ops, SparseCore 0:
  10.1 186.4 all-gather.1

commit v2 on v1

--- a/solution.py
+++ b/solution.py
@@ -3,12 +3,17 @@
 import jax
 import jax.numpy as jnp
 from jax import lax
+from jax.sharding import Mesh
 from jax.sharding import PartitionSpec as P
 
 WIN = 8
 
 
 STEP_GAIN = 0.4
+
+LINE, RING = 4, 8
+TOK = ("line", "ring")
+THIN = 128
 
 
 def gather_blocks(own, axis):
@@ -37,14 +42,78 @@
     partial = jnp.dot(left_a, stack_g, preferred_element_type=jnp.float32) - jnp.dot(
         left_g, stack_a, preferred_element_type=jnp.float32
     )
-    parts = lax.axis_size("tok")
-    return sum_blocks(partial.reshape(parts, -1, partial.shape[1]), "tok")
+    parts = lax.axis_size(TOK)
+    return sum_blocks(partial.reshape(parts, -1, partial.shape[1]), TOK)
+
+
+def roll_blocks(blocks, start, dim):
+    twice = jnp.concatenate([blocks, blocks], dim)
+    return lax.dynamic_slice_in_dim(twice, start, blocks.shape[dim], dim)
+
+
+def ring_pass(own, up_steps, down_steps):
+    up = [(k, (k + 1) % RING) for k in range(RING)]
+    down = [(k, (k - 1) % RING) for k in range(RING)]
+    found = {0: own}
+    for step in range(1, max(up_steps, down_steps) + 1):
+        if step <= up_steps:
+            found[RING - step] = lax.ppermute(found[(RING - step + 1) % RING], "ring", up)
+        if step <= down_steps:
+            found[step] = lax.ppermute(found[step - 1], "ring", down)
+    return [found[k] for k in range(RING)]
+
+
+def times_rotation(lhs_blocks, rot_b, line_pos, ring_pos):
+    rows, narrow = rot_b.shape
+    half = rows // 2
+    wide = narrow - THIN
+    count = lhs_blocks.shape[1]
+
+    line_wide = gather_blocks(rot_b[:, THIN:], "line")
+    near_lo = ring_pass(rot_b[:half], RING // 2, RING // 2 - 1)
+    near_hi = ring_pass(rot_b[half:], RING // 2 - 1, RING // 2)
+    others = roll_blocks(line_wide, line_pos + 1, 0)[: LINE - 1]
+    far_lo = ring_pass(others[:, :half], RING // 2, RING // 2 - 1)
+    far_hi = ring_pass(others[:, half:], RING // 2 - 1, RING // 2)
+    ring_thin = jnp.stack(
+        [jnp.concatenate([lo[:, :THIN], hi[:, :THIN]], 0) for lo, hi in zip(near_lo, near_hi)]
+    )
+    thin = gather_blocks(ring_thin, "line")
+
+    grid = lhs_blocks.reshape(LINE, RING, count, rows)
+    by_ring = roll_blocks(grid, ring_pos, 1)
+    by_both = roll_blocks(by_ring, line_pos, 0)
+    lhs_thin = by_ring.transpose(2, 0, 1, 3).reshape(count, LINE * RING * rows)
+    lhs_far = by_both[1:].reshape(LINE - 1, RING, count, 2, half)
+    lhs_far = lhs_far.transpose(1, 3, 2, 0, 4).reshape(RING, 2, count, (LINE - 1) * half)
+    lhs_near = by_both[0].transpose(1, 0, 2).reshape(count, RING * rows)
+
+    near = [piece[:, THIN:] for pair in zip(near_lo, near_hi) for piece in pair]
+    total = jnp.dot(lhs_near, jnp.concatenate(near, 0), preferred_element_type=jnp.float32)
+    for place in [0, 1, 7, 2, 6, 3, 5, 4]:
+        for part, far in enumerate((far_lo, far_hi)):
+            piece = far[place].reshape((LINE - 1) * half, wide)
+            total = total + jnp.dot(
+                lhs_far[place, part], piece, preferred_element_type=jnp.float32
+            )
+    total_thin = jnp.dot(
+        lhs_thin, thin.reshape(LINE * RING * rows, THIN), preferred_element_type=jnp.float32
+    )
+
+    first_near = jnp.stack([piece[:WIN, THIN:] for piece in near_lo])
+    first_far = jnp.stack([piece[:, :WIN] for piece in far_lo], 1)
+    first = roll_blocks(
+        jnp.concatenate([first_near[None], first_far], 0), (LINE - line_pos) % LINE, 0
+    )
+    first = jnp.concatenate([thin[:, :, :WIN], first], 3)
+    first = roll_blocks(first, (RING - ring_pos) % RING, 1).reshape(LINE * RING * WIN, narrow)
+    return jnp.concatenate([total_thin, total], 1), first
 
 
 def local(activations, rotation, value_weight, token_code, channel_code):
-    n_tok = lax.axis_size("tok")
+    n_tok = lax.axis_size(TOK)
     n_mdl = lax.axis_size("mdl")
-    tok_pos = lax.axis_index("tok")
+    tok_pos = lax.axis_index(TOK)
     mdl_pos = lax.axis_index("mdl")
     block_rows = rotation.shape[0]
     narrow = rotation.shape[1]
@@ -54,25 +123,30 @@
     tok_rows = activations.shape[0]
     width_root = math.sqrt(model_width)
     rot_b = rotation.astype(jnp.bfloat16)
-    rot_panel = lax.all_gather(rot_b, "tok", axis=0, tiled=True)
     own_cols = lax.dynamic_slice_in_dim(value_weight, tok_pos * chan_share, chan_share, 1)
-    weight_rows = gather_blocks(own_cols.T, "mdl").transpose(1, 0, 2).reshape(chan_share, model_width)
+    weight_rows = gather_blocks(own_cols.T, "mdl").reshape(n_mdl, chan_share, -1, block_rows)
+    weight_rows = weight_rows.transpose(0, 2, 1, 3).reshape(n_tok, chan_share, block_rows)
+    act_blocks = activations.reshape(tok_rows, n_tok, block_rows).transpose(1, 0, 2)
+    products, window = times_rotation(
+        jnp.concatenate([act_blocks, weight_rows], 1),
+        rot_b,
+        lax.axis_index("line"),
+        lax.axis_index("ring"),
+    )
+    products = products / width_root
+    rotated, turned = products[:tok_rows], products[tok_rows:]
     own_feats = lax.dynamic_slice_in_dim(activations, mdl_pos * narrow, narrow, 1)
     plain = jnp.dot(own_feats, value_weight, preferred_element_type=jnp.float32)
 
-    turned = jnp.dot(weight_rows, rot_panel, preferred_element_type=jnp.float32) / width_root
     own_codes = lax.dynamic_slice_in_dim(channel_code, tok_pos * chan_share, chan_share, 0)
     weight_clip = own_codes.astype(jnp.float32)[:, None] / (4.0 * width_root)
     weight_tanh = jnp.tanh(turned / weight_clip)
     quant_weight = (weight_clip * weight_tanh).astype(jnp.bfloat16)
-    weight_full = gather_blocks(quant_weight, "tok").reshape(channels, narrow)
+    weight_full = gather_blocks(quant_weight, TOK).reshape(channels, narrow)
 
-    rotated = jnp.dot(activations, rot_panel, preferred_element_type=jnp.float32) / width_root
     act_clip = token_code.astype(jnp.float32)[:, None] * 0.5
     act_tanh = jnp.tanh(rotated / act_clip)
     quant_act = (act_clip * act_tanh).astype(jnp.bfloat16)
-    window = rot_panel.reshape(n_tok, block_rows, narrow)[:, :WIN].reshape(n_tok * WIN, narrow)
-
     partial_err = (
         jnp.einsum("td,cd->tc", quant_act, weight_full, preferred_element_type=jnp.float32) - plain
     )
@@ -86,25 +160,26 @@
         jnp.einsum("tc,td->cd", error_bf, quant_act, preferred_element_type=jnp.float32)
         .astype(jnp.bfloat16)
         .reshape(n_tok, chan_share, narrow),
-        "tok",
+        TOK,
     )
     grad_act = (
         jnp.dot(error_bf, weight_full, preferred_element_type=jnp.float32)
         * (1.0 - act_tanh * act_tanh)
     ).astype(jnp.bfloat16)
     grad_turned = (grad_quant * (1.0 - weight_tanh * weight_tanh)).astype(jnp.bfloat16)
-    stack_a = jnp.concatenate([rotated.astype(jnp.bfloat16), turned.astype(jnp.bfloat16)], 0)
+    stack_a = products.astype(jnp.bfloat16)
     stack_g = jnp.concatenate([grad_act, grad_turned], 0)
     step_size = STEP_GAIN / math.sqrt(tok_rows * n_tok * channels)
     own_rows = rotation[:WIN]
     moved = own_rows - step_size * cayley_own(window, stack_a, stack_g)
-    second_in = gather_blocks((own_rows + moved).astype(jnp.bfloat16), "tok")
+    second_in = gather_blocks((own_rows + moved).astype(jnp.bfloat16), TOK)
     second_in = second_in.reshape(n_tok * WIN, narrow)
     new_rows = own_rows - 0.5 * step_size * cayley_own(second_in, stack_a, stack_g)
     return (new_rows, recon_error)
 
 
 def solution(mesh):
-    in_specs = (P("tok", None), P("tok", "mdl"), P("mdl", None), P("tok"), P())
-    out_specs = (P("tok", "mdl"), P("tok", None))
+    mesh = Mesh(mesh.devices.reshape(LINE, RING, -1), TOK + ("mdl",))
+    in_specs = (P(TOK, None), P(TOK, "mdl"), P("mdl", None), P(TOK), P())
+    out_specs = (P(TOK, "mdl"), P(TOK, None))
     return jax.shard_map(local, mesh=mesh, in_specs=in_specs, out_specs=out_specs, check_vma=False)

time: 483 us -> 477 us (0.988)
  starting transfers between devices: 22.1 us -> 154 us
  waiting for transfers between devices: 210 us -> 88.8 us
  blocking collectives: 185 us -> 128 us
  local copies, waits for them, and re-layouts: 11.1 us -> 62 us
  between operations: 14.3 us -> 1.91 us
  other arithmetic: 11.8 us -> 20.4 us
  matrix products: 27.4 us -> 19.7 us
    all_gather x1 -> x0, waiting for transfers between devices: 157 us -> none  [local(): rot_panel = lax.all_gather(rot_b, 'tok', axis=0, tiled=True)]
    ppermute x0 -> x28, starting transfers between devices: none -> 95.8 us  [the longest x14 61.2 us: ring_pass(): found[step] = lax.ppermute(found[step - 1], 'ring', down)]
    all_to_all x4 -> x3, blocking collectives: 74.6 us -> 46 us  [gather_blocks(): lax.all_to_all(jnp.broadcast_to(own[None], (parts,) + own.shape), axis, 0...]
    all_to_all x5 -> x4, blocking collectives: 110 us -> 81.6 us  [sum_blocks(): return jnp.sum(lax.all_to_all(blocks, axis, 0, 0).astype(jnp.float32), 0)]
    unnamed x22 -> x94, local copies, waits for them, and re-layouts: 2.68 us -> 29 us
    all_to_all x2 -> x5, starting transfers between devices: 14.2 us -> 33.6 us  [gather_blocks(): lax.all_to_all(jnp.broadcast_to(own[None], (parts,) + own.shape), axis, 0...]
    ppermute x0 -> x28, waiting for transfers between devices: none -> 18.2 us  [the longest x14 10.9 us: ring_pass(): found[step] = lax.ppermute(found[step - 1], 'ring', down)]
    reshape x1 -> x4, local copies, waits for them, and re-layouts: 1.88 us -> 19.8 us  [the longest x2 14.9 us: times_rotation(): lhs_far = by_both[1:].reshape(LINE - 1, RING, count, 2, half)]
  transfers between devices with their start and end apart: 4 -> 35, of which waited for: 4 -> 9; matrix products, arithmetic and copies ran while one was open for 3% -> 15% of each run, Pallas kernels for 0% -> 0%
where the time goes in v2:
time: 477 us; the launch traced here: 474 us
  starting transfers between devices  154 us (32%)
  blocking collectives  128 us (27%)
  waiting for transfers between devices  88.8 us (19%)
  local copies, waits for them, and re-layouts  62 us (13%)
  other arithmetic  20.4 us (4%)
  matrix products  19.7 us (4%)
    all_to_all x4, blocking collectives, sum_blocks(): return jnp.sum(lax.all_to_all(blocks, axis, 0, 0).astype(jnp.float32), 0)  81.6 us
    ppermute x14, starting transfers between devices, ring_pass(): found[step] = lax.ppermute(found[step - 1], 'ring', down)  61.2 us
    all_to_all x3, blocking collectives, gather_blocks(): lax.all_to_all(jnp.broadcast_to(own[None], (parts,) + own.shape), axis, 0...  46 us
    all_to_all x2, waiting for transfers between devices, sum_blocks(): return jnp.sum(lax.all_to_all(blocks, axis, 0, 0).astype(jnp.float32), 0)  38.9 us
    ppermute x14, starting transfers between devices, ring_pass(): lax.ppermute(found[(RING - step + 1) % RING], 'ring', up)  34.7 us
    all_to_all x5, starting transfers between devices, gather_blocks(): lax.all_to_all(jnp.broadcast_to(own[None], (parts,) + own.shape), axis, 0...  33.6 us
    all_to_all x5, waiting for transfers between devices, gather_blocks(): lax.all_to_all(jnp.broadcast_to(own[None], (parts,) + own.shape), axis, 0...  31.7 us
    unnamed x94, local copies, waits for them, and re-layouts  29 us
  transfers between devices with their start and end apart: 35, of which 9 were waited for; matrix products, arithmetic and copies ran while one was open for 15% of the time, Pallas kernels for 0%

profile of v2, /device:TPU:64, one launch (start us, length us, event | category | flops | bytes accessed | tf_op | source)
XLA Modules:
  0.0 474.0 jit_solution(1811407787776051529)
XLA Ops:
  1.8 4.3 collective-permute-start.11
  6.1 4.6 collective-permute-start.1
  12.6 5.6 %collective-permute-start = (bf16[128,512]{1,0:T(8,128)(2,1)S(1)}, bf16[128,512]{1,0:T(8,128)(2,1)S(1)}, u32[]{:S(2)}, u32[]{:S(2)}) collective-permute-start(bf16[128,512]{1,0:T(8,128)(2,1)S(1)} %get-tuple-element.9), channel_id=1, source_target_pairs={{0,112},{16,0},{32,16},{48,32},{64,48},{80,64},{96,80},{112,96},{1... | collective-permute-start | bytes 393224 | tf_op jit(solution)/shard_map/ppermute | solution.py:62
  19.3 9.7 %all-to-all-start.2 = ((bf16[16,32,512]{2,1,0:T(8,128)(2,1)}), bf16[16,32,512]{2,1,0:T(8,128)(2,1)S(1)}, u32[]{:S(2)}, u32[]{:S(2)}) async-start(bf16[16,32,512]{2,1,0:T(8,128)(2,1)} %broadcast_in_dim.21), calls=%async_computation.2 | async-start | bytes 1048576 | tf_op jit(solution)/shard_map/all_to_all | solution.py:21
  29.7 3.9 copy.54
  36.3 5.1 %collective-permute-start.3 = (bf16[128,512]{1,0:T(8,128)(2,1)S(1)}, bf16[128,512]{1,0:T(8,128)(2,1)S(1)}, u32[]{:S(2)}, u32[]{:S(2)}) collective-permute-start(bf16[128,512]{1,0:T(8,128)(2,1)S(1)} %collective-permute-done.1), channel_id=1, source_target_pairs={{0,112},{16,0},{32,16},{48,32},{64,48},{80,64},{96,80},{112,96},{1... | collective-permute-start | bytes 393224 | tf_op jit(solution)/shard_map/ppermute | solution.py:62
  43.4 5.1 %collective-permute-start.2 = (bf16[128,512]{1,0:T(8,128)(2,1)S(1)}, bf16[128,512]{1,0:T(8,128)(2,1)S(1)}, u32[]{:S(2)}, u32[]{:S(2)}) collective-permute-start(bf16[128,512]{1,0:T(8,128)(2,1)S(1)} %collective-permute-done), channel_id=1, source_target_pairs={{0,112},{16,0},{32,16},{48,32},{64,48},{80,64},{96,80},{112,96},{1... | collective-permute-start | bytes 393224 | tf_op jit(solution)/shard_map/ppermute | solution.py:62
  51.9 5.1 %collective-permute-start.5 = (bf16[128,512]{1,0:T(8,128)(2,1)S(1)}, bf16[128,512]{1,0:T(8,128)(2,1)S(1)}, u32[]{:S(2)}, u32[]{:S(2)}) collective-permute-start(bf16[128,512]{1,0:T(8,128)(2,1)S(1)} %collective-permute-done.3), channel_id=1, source_target_pairs={{0,112},{16,0},{32,16},{48,32},{64,48},{80,64},{96,80},{112,96},{1... | collective-permute-start | bytes 393224 | tf_op jit(solution)/shard_map/ppermute | solution.py:62
  57.0 2.1 collective-permute-start.8
  59.1 5.1 %collective-permute-start.4 = (bf16[128,512]{1,0:T(8,128)(2,1)S(1)}, bf16[128,512]{1,0:T(8,128)(2,1)S(1)}, u32[]{:S(2)}, u32[]{:S(2)}) collective-permute-start(bf16[128,512]{1,0:T(8,128)(2,1)S(1)} %collective-permute-done.2), channel_id=1, source_target_pairs={{0,112},{16,0},{32,16},{48,32},{64,48},{80,64},{96,80},{112,96},{1... | collective-permute-start | bytes 393224 | tf_op jit(solution)/shard_map/ppermute | solution.py:62
  65.6 5.1 %collective-permute-start.10 = (bf16[128,512]{1,0:T(8,128)(2,1)S(1)}, bf16[128,512]{1,0:T(8,128)(2,1)S(1)}, u32[]{:S(2)}, u32[]{:S(2)}) collective-permute-start(bf16[128,512]{1,0:T(8,128)(2,1)S(1)} %collective-permute-done.5), channel_id=1, source_target_pairs={{0,112},{16,0},{32,16},{48,32},{64,48},{80,64},{96,80},{112,96},{1... | collective-permute-start | bytes 393224 | tf_op jit(solution)/shard_map/ppermute | solution.py:62
  74.2 3.5 collective-permute-done.9
  84.0 3.5 all-to-all-start.1
  87.6 6.5 %fusion.2 = bf16[4,8,224,256]{3,2,1,0:T(8,128)(2,1)S(1)} fusion(s32[]{:T(128)S(6)} %select_n.39, bf16[4,8,192,256]{3,2,1,0:T(8,128)(2,1)} %bitcast.264, bf16[4,8,32,256]{3,2,1,0:T(8,128)(2,1)S(1)} %bitcast.286), kind=kLoop, calls=%fused_computation.8 | loop fusion | flops 14680064 | bytes 7340036 | tf_op jit(solution)/shard_map/concatenate | solution.py:50
  99.6 6.3 %reshape.130 = bf16[3,8,224,2,128]{4,3,2,1,0:T(2,128)(2,1)} reshape(bf16[3,8,224,256]{3,2,1,0:T(8,128)(2,1)} %slice.375) | data formatting | bytes 5505024 | tf_op jit(solution)/shard_map/reshape | solution.py:87
  108.1 8.6 %copy.36 = bf16[3,8,224,2,128]{2,4,0,3,1:T(8,128)(2,1)} copy(bf16[3,8,224,2,128]{4,3,2,1,0:T(2,128)(2,1)} %reshape.130) | data formatting | bytes 5505024 | tf_op jit(solution)/shard_map/reshape | solution.py:87
  118.7 5.1 %all-to-all-start = ((bf16[4,8,256,128]{3,2,1,0:T(8,128)(2,1)}), bf16[4,8,256,128]{3,2,1,0:T(8,128)(2,1)S(1)}, u32[]{:S(2)}, u32[]{:S(2)}) async-start(bf16[4,8,256,128]{3,2,1,0:T(8,128)(2,1)} %broadcast_in_dim.18), calls=%async_computation | async-start | bytes 4194304 | tf_op jit(solution)/shard_map/all_to_all | solution.py:21
  127.3 3.9 collective-permute-start.14
  133.2 4.4 collective-permute-start.21
  139.2 2.1 fusion.9
  144.1 4.7 collective-permute-start.18
  149.2 2.3 collective-permute-start.15
  151.5 5.3 %collective-permute-start.23 = (bf16[3,128,384]{2,1,0:T(8,128)(2,1)S(1)}, bf16[3,128,384]{2,1,0:T(8,128)(2,1)S(1)}, u32[]{:S(2)}, u32[]{:S(2)}) collective-permute-start(bf16[3,128,384]{2,1,0:T(8,128)(2,1)S(1)} %collective-permute-done.21), channel_id=1, source_target_pairs={{0,112},{16,0},{32,16},{48,32},{64,48},{80,64},{96,80},{112,96},{1... | collective-permute-start | bytes 884744 | tf_op jit(solution)/shard_map/ppermute | solution.py:62
  159.4 3.2 collective-permute-done.23
  162.9 3.7 collective-permute-start.19
  166.9 2.2 collective-permute-start.16
  169.1 4.0 collective-permute-start.25
  173.8 5.6 %collective-permute-done.25 = bf16[3,128,384]{2,1,0:T(8,128)(2,1)S(1)} collective-permute-done((bf16[3,128,384]{2,1,0:T(8,128)(2,1)S(1)}, bf16[3,128,384]{2,1,0:T(8,128)(2,1)S(1)}, u32[]{:S(2)}, u32[]{:S(2)}) %collective-permute-start.25) | collective-permute-done | bytes 294944 | tf_op jit(solution)/shard_map/ppermute | solution.py:62
  179.5 3.2 collective-permute-start.27
  182.9 2.7 collective-permute-start.20
  186.0 2.1 collective-permute-done.27
  188.4 3.8 collective-permute-done.20
  193.9 3.2 fusion.21
  199.9 11.1 %all-to-all-start.3 = ((bf16[32,32,512]{2,1,0:T(8,128)(2,1)}), bf16[32,32,512]{2,1,0:T(8,128)(2,1)}, u32[]{:S(2)}, u32[]{:S(2)}) async-start(bf16[32,32,512]{2,1,0:T(8,128)(2,1)} %broadcast_in_dim.22), calls=%async_computation.3 | async-start | bytes 2097152 | tf_op jit(solution)/shard_map/all_to_all | solution.py:21
  211.0 21.7 %all-to-all-done.3 = bf16[32,32,512]{2,1,0:T(8,128)(2,1)} async-done(((bf16[32,32,512]{2,1,0:T(8,128)(2,1)}), bf16[32,32,512]{2,1,0:T(8,128)(2,1)}, u32[]{:S(2)}, u32[]{:S(2)}) %all-to-all-start.3) | async-done | bytes 1048608 | tf_op jit(solution)/shard_map/all_to_all | solution.py:21
  237.1 9.7 %all-to-all-start.4 = ((f32[16,96,128]{2,1,0:T(8,128)}), f32[16,96,128]{2,1,0:T(8,128)}, u32[]{:S(2)}, u32[]{:S(2)}) async-start(f32[16,96,128]{2,1,0:T(8,128)} %bitcast.283), calls=%async_computation.4 | async-start | bytes 1572864 | tf_op jit(solution)/shard_map/all_to_all | solution.py:25
  248.7 20.0 %all-to-all-done.4 = f32[16,96,128]{2,1,0:T(8,128)} async-done(((f32[16,96,128]{2,1,0:T(8,128)}), f32[16,96,128]{2,1,0:T(8,128)}, u32[]{:S(2)}, u32[]{:S(2)}) %all-to-all-start.4) | async-done | bytes 786464 | tf_op jit(solution)/shard_map/all_to_all | solution.py:25
  270.8 4.3 all-to-all-start.5
  282.9 10.0 %all-to-all-done.5 = f32[16,96,128]{2,1,0:T(8,128)} async-done(((f32[16,96,128]{2,1,0:T(8,128)}), f32[16,96,128]{2,1,0:T(8,128)}, u32[]{:S(2)}, u32[]{:S(2)}) %all-to-all-start.5) | async-done | bytes 786464 | tf_op jit(solution)/shard_map/all_to_all | solution.py:21
  297.1 14.6 %all-to-all-start.6 = ((bf16[32,32,512]{2,1,0:T(8,128)(2,1)}), bf16[32,32,512]{2,1,0:T(8,128)(2,1)}, u32[]{:S(2)}, u32[]{:S(2)}) async-start(bf16[32,32,512]{2,1,0:T(8,128)(2,1)} %bitcast.289), calls=%async_computation.6 | async-start | bytes 2097152 | tf_op jit(solution)/shard_map/all_to_all | solution.py:25
  321.0 18.9 %all-to-all-done.6 = bf16[32,32,512]{2,1,0:T(8,128)(2,1)} async-done(((bf16[32,32,512]{2,1,0:T(8,128)(2,1)}), bf16[32,32,512]{2,1,0:T(8,128)(2,1)}, u32[]{:S(2)}, u32[]{:S(2)}) %all-to-all-start.6) | async-done | bytes 1048608 | tf_op jit(solution)/shard_map/all_to_all | solution.py:25
  342.7 15.0 %all_to_all.70 = bf16[16,16,448]{2,1,0:T(8,128)(2,1)S(1)} all-to-all(bf16[16,16,448]{2,1,0:T(8,128)(2,1)S(1)} %bitcast.290), channel_id=1, replica_groups=mesh['line'=4,'ring'=8,'mdl'=16] {'mdl'}, dimensions={0} | all-to-all | bytes 458752 | tf_op jit(solution)/shard_map/all_to_all | solution.py:25
  357.8 14.7 %all_to_all.71 = bf16[16,16,448]{2,1,0:T(8,128)(2,1)S(1)} all-to-all(bf16[16,16,448]{2,1,0:T(8,128)(2,1)S(1)} %broadcast_in_dim.24), channel_id=1, replica_groups=mesh['line'=4,'ring'=8,'mdl'=16] {'mdl'}, dimensions={0} | all-to-all | bytes 458752 | tf_op jit(solution)/shard_map/all_to_all | solution.py:21
  373.0 26.3 %all_to_all.72 = f32[32,8,512]{2,1,0:T(8,128)S(1)} all-to-all(f32[32,8,512]{2,1,0:T(8,128)S(1)} %fusion.8), channel_id=1, replica_groups=mesh['line'=4,'ring'=8,'mdl'=16] {'line','ring'}, dimensions={0} | all-to-all | bytes 1048576 | tf_op jit(solution)/shard_map/all_to_all | solution.py:25
  400.1 16.6 %all_to_all.73 = bf16[32,8,512]{2,1,0:T(8,128)(2,1)S(1)} all-to-all(bf16[32,8,512]{2,1,0:T(8,128)(2,1)S(1)} %broadcast_in_dim.25), channel_id=1, replica_groups=mesh['line'=4,'ring'=8,'mdl'=16] {'line','ring'}, dimensions={0} | all-to-all | bytes 524288 | tf_op jit(solution)/shard_map/all_to_all | solution.py:21
  417.1 14.8 %all_to_all.74 = bf16[16,16,448]{2,1,0:T(8,128)(2,1)S(1)} all-to-all(bf16[16,16,448]{2,1,0:T(8,128)(2,1)S(1)} %bitcast.291), channel_id=1, replica_groups=mesh['line'=4,'ring'=8,'mdl'=16] {'mdl'}, dimensions={0} | all-to-all | bytes 458752 | tf_op jit(solution)/shard_map/all_to_all | solution.py:25
  432.0 14.7 %all_to_all.75 = bf16[16,16,448]{2,1,0:T(8,128)(2,1)S(1)} all-to-all(bf16[16,16,448]{2,1,0:T(8,128)(2,1)S(1)} %broadcast_in_dim.26), channel_id=1, replica_groups=mesh['line'=4,'ring'=8,'mdl'=16] {'mdl'}, dimensions={0} | all-to-all | bytes 458752 | tf_op jit(solution)/shard_map/all_to_all | solution.py:21
  447.1 25.5 %all_to_all.76 = f32[32,8,512]{2,1,0:T(8,128)S(1)} all-to-all(f32[32,8,512]{2,1,0:T(8,128)S(1)} %fusion.7), channel_id=1, replica_groups=mesh['line'=4,'ring'=8,'mdl'=16] {'line','ring'}, dimensions={0} | all-to-all | bytes 1048576 | tf_op jit(solution)/shard_map/all_to_all | solution.py:25
  (220 shorter events, 88.9 us)
Async XLA Ops:
  0.6 17.6 %copy-start = (bf16[512,1024]{1,0:T(8,128)(2,1)S(1)}, bf16[512,1024]{1,0:T(8,128)(2,1)}, u32[]{:S(2)}) copy-start(bf16[512,1024]{1,0:T(8,128)(2,1)} %param.7) | copy-start | bytes 3145732
  1.8 32.5 %collective-permute-start.11 = (bf16[128,512]{1,0:T(8,128)(2,1)S(1)}, bf16[128,512]{1,0:T(8,128)(2,1)S(1)}, u32[]{:S(2)}, u32[]{:S(2)}) collective-permute-start(bf16[128,512]{1,0:T(8,128)(2,1)S(1)} %get-tuple-element.8), channel_id=1, source_target_pairs={{0,16},{16,32},{32,48},{48,64},{64,80},{80,96},{96,112},{112,0},{1... | collective-permute-start | bytes 393224 | tf_op jit(solution)/shard_map/ppermute | solution.py:60
  6.1 30.2 %collective-permute-start.1 = (bf16[128,512]{1,0:T(8,128)(2,1)S(1)}, bf16[128,512]{1,0:T(8,128)(2,1)S(1)}, u32[]{:S(2)}, u32[]{:S(2)}) collective-permute-start(bf16[128,512]{1,0:T(8,128)(2,1)S(1)} %get-tuple-element.8), channel_id=1, source_target_pairs={{0,112},{16,0},{32,16},{48,32},{64,48},{80,64},{96,80},{112,96},{1... | collective-permute-start | bytes 393224 | tf_op jit(solution)/shard_map/ppermute | solution.py:62
  10.7 30.7 %collective-permute-start.6 = (bf16[128,512]{1,0:T(8,128)(2,1)S(1)}, bf16[128,512]{1,0:T(8,128)(2,1)S(1)}, u32[]{:S(2)}, u32[]{:S(2)}) collective-permute-start(bf16[128,512]{1,0:T(8,128)(2,1)S(1)} %get-tuple-element.9), channel_id=1, source_target_pairs={{0,16},{16,32},{32,48},{48,64},{64,80},{80,96},{96,112},{112,0},{1... | collective-permute-start | bytes 393224 | tf_op jit(solution)/shard_map/ppermute | solution.py:60
  12.6 30.7 %collective-permute-start = (bf16[128,512]{1,0:T(8,128)(2,1)S(1)}, bf16[128,512]{1,0:T(8,128)(2,1)S(1)}, u32[]{:S(2)}, u32[]{:S(2)}) collective-permute-start(bf16[128,512]{1,0:T(8,128)(2,1)S(1)} %get-tuple-element.9), channel_id=1, source_target_pairs={{0,112},{16,0},{32,16},{48,32},{64,48},{80,64},{96,80},{112,96},{1... | collective-permute-start | bytes 393224 | tf_op jit(solution)/shard_map/ppermute | solution.py:62
  19.3 63.7 %all-to-all-start.2 = ((bf16[16,32,512]{2,1,0:T(8,128)(2,1)}), bf16[16,32,512]{2,1,0:T(8,128)(2,1)S(1)}, u32[]{:S(2)}, u32[]{:S(2)}) async-start(bf16[16,32,512]{2,1,0:T(8,128)(2,1)} %broadcast_in_dim.21), calls=%async_computation.2 | async-start | bytes 1048576 | tf_op jit(solution)/shard_map/all_to_all | solution.py:21
  34.4 22.6 %copy-start.28 = (bf16[128,512]{1,0:T(8,128)(2,1)}, bf16[128,512]{1,0:T(8,128)(2,1)S(1)}, u32[]{:S(2)}) copy-start(bf16[128,512]{1,0:T(8,128)(2,1)S(1)} %collective-permute-done.11) | copy-start | bytes 393220
  34.4 15.5 %collective-permute-start.12 = (bf16[128,512]{1,0:T(8,128)(2,1)S(1)}, bf16[128,512]{1,0:T(8,128)(2,1)S(1)}, u32[]{:S(2)}, u32[]{:S(2)}) collective-permute-start(bf16[128,512]{1,0:T(8,128)(2,1)S(1)} %collective-permute-done.11), channel_id=1, source_target_pairs={{0,16},{16,32},{32,48},{48,64},{64,80},{80,96},{96,112},{112,0},{1... | collective-permute-start | bytes 393224 | tf_op jit(solution)/shard_map/ppermute | solution.py:60
  36.3 15.6 %collective-permute-start.3 = (bf16[128,512]{1,0:T(8,128)(2,1)S(1)}, bf16[128,512]{1,0:T(8,128)(2,1)S(1)}, u32[]{:S(2)}, u32[]{:S(2)}) collective-permute-start(bf16[128,512]{1,0:T(8,128)(2,1)S(1)} %collective-permute-done.1), channel_id=1, source_target_pairs={{0,112},{16,0},{32,16},{48,32},{64,48},{80,64},{96,80},{112,96},{1... | collective-permute-start | bytes 393224 | tf_op jit(solution)/shard_map/ppermute | solution.py:62
  41.4 15.6 %collective-permute-start.7 = (bf16[128,512]{1,0:T(8,128)(2,1)S(1)}, bf16[128,512]{1,0:T(8,128)(2,1)S(1)}, u32[]{:S(2)}, u32[]{:S(2)}) collective-permute-start(bf16[128,512]{1,0:T(8,128)(2,1)S(1)} %collective-permute-done.6), channel_id=1, source_target_pairs={{0,16},{16,32},{32,48},{48,64},{64,80},{80,96},{96,112},{112,0},{1... | collective-permute-start | bytes 393224 | tf_op jit(solution)/shard_map/ppermute | solution.py:60
  43.4 40.6 %copy-start.22 = (bf16[128,512]{1,0:T(8,128)(2,1)}, bf16[128,512]{1,0:T(8,128)(2,1)S(1)}, u32[]{:S(2)}) copy-start(bf16[128,512]{1,0:T(8,128)(2,1)S(1)} %collective-permute-done) | copy-start | bytes 393220
  43.4 15.7 %collective-permute-start.2 = (bf16[128,512]{1,0:T(8,128)(2,1)S(1)}, bf16[128,512]{1,0:T(8,128)(2,1)S(1)}, u32[]{:S(2)}, u32[]{:S(2)}) collective-permute-start(bf16[128,512]{1,0:T(8,128)(2,1)S(1)} %collective-permute-done), channel_id=1, source_target_pairs={{0,112},{16,0},{32,16},{48,32},{64,48},{80,64},{96,80},{112,96},{1... | collective-permute-start | bytes 393224 | tf_op jit(solution)/shard_map/ppermute | solution.py:62
  49.9 24.2 %collective-permute-start.13 = (bf16[128,512]{1,0:T(8,128)(2,1)S(1)}, bf16[128,512]{1,0:T(8,128)(2,1)S(1)}, u32[]{:S(2)}, u32[]{:S(2)}) collective-permute-start(bf16[128,512]{1,0:T(8,128)(2,1)S(1)} %collective-permute-done.12), channel_id=1, source_target_pairs={{0,16},{16,32},{32,48},{48,64},{64,80},{80,96},{96,112},{112,0},{1... | collective-permute-start | bytes 393224 | tf_op jit(solution)/shard_map/ppermute | solution.py:60
  51.9 13.8 %collective-permute-start.5 = (bf16[128,512]{1,0:T(8,128)(2,1)S(1)}, bf16[128,512]{1,0:T(8,128)(2,1)S(1)}, u32[]{:S(2)}, u32[]{:S(2)}) collective-permute-start(bf16[128,512]{1,0:T(8,128)(2,1)S(1)} %collective-permute-done.3), channel_id=1, source_target_pairs={{0,112},{16,0},{32,16},{48,32},{64,48},{80,64},{96,80},{112,96},{1... | collective-permute-start | bytes 393224 | tf_op jit(solution)/shard_map/ppermute | solution.py:62
  57.0 27.0 %copy-start.23 = (bf16[128,512]{1,0:T(8,128)(2,1)}, bf16[128,512]{1,0:T(8,128)(2,1)S(1)}, u32[]{:S(2)}) copy-start(bf16[128,512]{1,0:T(8,128)(2,1)S(1)} %collective-permute-done.7) | copy-start | bytes 393220
  57.0 25.3 %copy-start.29 = (bf16[128,512]{1,0:T(8,128)(2,1)S(1)}, bf16[128,512]{1,0:T(8,128)(2,1)}, u32[]{:S(2)}) copy-start(bf16[128,512]{1,0:T(8,128)(2,1)} %copy-done.28) | copy-start | bytes 393220
  57.0 13.7 %collective-permute-start.8 = (bf16[128,512]{1,0:T(8,128)(2,1)S(1)}, bf16[128,512]{1,0:T(8,128)(2,1)S(1)}, u32[]{:S(2)}, u32[]{:S(2)}) collective-permute-start(bf16[128,512]{1,0:T(8,128)(2,1)S(1)} %collective-permute-done.7), channel_id=1, source_target_pairs={{0,16},{16,32},{32,48},{48,64},{64,80},{80,96},{96,112},{112,0},{1... | collective-permute-start | bytes 393224 | tf_op jit(solution)/shard_map/ppermute | solution.py:60
  59.1 24.9 %copy-start.24 = (bf16[128,512]{1,0:T(8,128)(2,1)}, bf16[128,512]{1,0:T(8,128)(2,1)S(1)}, u32[]{:S(2)}) copy-start(bf16[128,512]{1,0:T(8,128)(2,1)S(1)} %collective-permute-done.2) | copy-start | bytes 393220
  59.1 13.6 %collective-permute-start.4 = (bf16[128,512]{1,0:T(8,128)(2,1)S(1)}, bf16[128,512]{1,0:T(8,128)(2,1)S(1)}, u32[]{:S(2)}, u32[]{:S(2)}) collective-permute-start(bf16[128,512]{1,0:T(8,128)(2,1)S(1)} %collective-permute-done.2), channel_id=1, source_target_pairs={{0,112},{16,0},{32,16},{48,32},{64,48},{80,64},{96,80},{112,96},{1... | collective-permute-start | bytes 393224 | tf_op jit(solution)/shard_map/ppermute | solution.py:62
  65.6 8.5 %collective-permute-start.10 = (bf16[128,512]{1,0:T(8,128)(2,1)S(1)}, bf16[128,512]{1,0:T(8,128)(2,1)S(1)}, u32[]{:S(2)}, u32[]{:S(2)}) collective-permute-start(bf16[128,512]{1,0:T(8,128)(2,1)S(1)} %collective-permute-done.5), channel_id=1, source_target_pairs={{0,112},{16,0},{32,16},{48,32},{64,48},{80,64},{96,80},{112,96},{1... | collective-permute-start | bytes 393224 | tf_op jit(solution)/shard_map/ppermute | solution.py:62
  70.8 6.9 %collective-permute-start.9 = (bf16[128,512]{1,0:T(8,128)(2,1)S(1)}, bf16[128,512]{1,0:T(8,128)(2,1)S(1)}, u32[]{:S(2)}, u32[]{:S(2)}) collective-permute-start(bf16[128,512]{1,0:T(8,128)(2,1)S(1)} %collective-permute-done.8), channel_id=1, source_target_pairs={{0,16},{16,32},{32,48},{48,64},{64,80},{80,96},{96,112},{112,0},{1... | collective-permute-start | bytes 393224 | tf_op jit(solution)/shard_map/ppermute | solution.py:60
  84.0 32.7 %all-to-all-start.1 = ((bf16[4,256,384]{2,1,0:T(8,128)(2,1)}), bf16[4,256,384]{2,1,0:T(8,128)(2,1)S(1)}, u32[]{:S(2)}, u32[]{:S(2)}) async-start(bf16[4,256,384]{2,1,0:T(8,128)(2,1)} %broadcast_in_dim.20), calls=%async_computation.1 | async-start | bytes 1572864 | tf_op jit(solution)/shard_map/all_to_all | solution.py:21
  118.7 75.2 %all-to-all-start = ((bf16[4,8,256,128]{3,2,1,0:T(8,128)(2,1)}), bf16[4,8,256,128]{3,2,1,0:T(8,128)(2,1)S(1)}, u32[]{:S(2)}, u32[]{:S(2)}) async-start(bf16[4,8,256,128]{3,2,1,0:T(8,128)(2,1)} %broadcast_in_dim.18), calls=%async_computation | async-start | bytes 4194304 | tf_op jit(solution)/shard_map/all_to_all | solution.py:21
  125.3 15.9 %copy-start.6 = (bf16[4,256,384]{2,1,0:T(8,128)(2,1)}, bf16[4,256,384]{2,1,0:T(8,128)(2,1)S(1)}, u32[]{:S(2)}) copy-start(bf16[4,256,384]{2,1,0:T(8,128)(2,1)S(1)} %fusion.24) | copy-start | bytes 2359300
  125.4 16.1 %collective-permute-start.17 = (bf16[3,128,384]{2,1,0:T(8,128)(2,1)S(1)}, bf16[3,128,384]{2,1,0:T(8,128)(2,1)S(1)}, u32[]{:S(2)}, u32[]{:S(2)}) collective-permute-start(bf16[3,128,384]{2,1,0:T(8,128)(2,1)S(1)} %get-tuple-element.2), channel_id=1, source_target_pairs={{0,16},{16,32},{32,48},{48,64},{64,80},{80,96},{96,112},{112,0},{1... | collective-permute-start | bytes 884744 | tf_op jit(solution)/shard_map/ppermute | solution.py:60
  127.3 21.5 %collective-permute-start.14 = (bf16[3,128,384]{2,1,0:T(8,128)(2,1)S(1)}, bf16[3,128,384]{2,1,0:T(8,128)(2,1)S(1)}, u32[]{:S(2)}, u32[]{:S(2)}) collective-permute-start(bf16[3,128,384]{2,1,0:T(8,128)(2,1)S(1)} %get-tuple-element.2), channel_id=1, source_target_pairs={{0,112},{16,0},{32,16},{48,32},{64,48},{80,64},{96,80},{112,96},{1... | collective-permute-start | bytes 884744 | tf_op jit(solution)/shard_map/ppermute | solution.py:62
  131.3 10.0 %collective-permute-start.22 = (bf16[3,128,384]{2,1,0:T(8,128)(2,1)S(1)}, bf16[3,128,384]{2,1,0:T(8,128)(2,1)S(1)}, u32[]{:S(2)}, u32[]{:S(2)}) collective-permute-start(bf16[3,128,384]{2,1,0:T(8,128)(2,1)S(1)} %get-tuple-element.3), channel_id=1, source_target_pairs={{0,16},{16,32},{32,48},{48,64},{64,80},{80,96},{96,112},{112,0},{1... | collective-permute-start | bytes 884744 | tf_op jit(solution)/shard_map/ppermute | solution.py:60
  133.2 10.6 %collective-permute-start.21 = (bf16[3,128,384]{2,1,0:T(8,128)(2,1)S(1)}, bf16[3,128,384]{2,1,0:T(8,128)(2,1)S(1)}, u32[]{:S(2)}, u32[]{:S(2)}) collective-permute-start(bf16[3,128,384]{2,1,0:T(8,128)(2,1)S(1)} %get-tuple-element.3), channel_id=1, source_target_pairs={{0,112},{16,0},{32,16},{48,32},{64,48},{80,64},{96,80},{112,96},{1... | collective-permute-start | bytes 884744 | tf_op jit(solution)/shard_map/ppermute | solution.py:62
  141.5 21.4 %copy-start.18 = (bf16[3,128,384]{2,1,0:T(8,128)(2,1)}, bf16[3,128,384]{2,1,0:T(8,128)(2,1)S(1)}, u32[]{:S(2)}) copy-start(bf16[3,128,384]{2,1,0:T(8,128)(2,1)S(1)} %collective-permute-done.17) | copy-start | bytes 884740
  141.9 15.0 %collective-permute-start.24 = (bf16[3,128,384]{2,1,0:T(8,128)(2,1)S(1)}, bf16[3,128,384]{2,1,0:T(8,128)(2,1)S(1)}, u32[]{:S(2)}, u32[]{:S(2)}) collective-permute-start(bf16[3,128,384]{2,1,0:T(8,128)(2,1)S(1)} %collective-permute-done.22), channel_id=1, source_target_pairs={{0,16},{16,32},{32,48},{48,64},{64,80},{80,96},{96,112},{112,0},{1... | collective-permute-start | bytes 884744 | tf_op jit(solution)/shard_map/ppermute | solution.py:60
  144.1 13.1 %collective-permute-start.18 = (bf16[3,128,384]{2,1,0:T(8,128)(2,1)S(1)}, bf16[3,128,384]{2,1,0:T(8,128)(2,1)S(1)}, u32[]{:S(2)}, u32[]{:S(2)}) collective-permute-start(bf16[3,128,384]{2,1,0:T(8,128)(2,1)S(1)} %collective-permute-done.17), channel_id=1, source_target_pairs={{0,16},{16,32},{32,48},{48,64},{64,80},{80,96},{96,112},{112,0},{1... | collective-permute-start | bytes 884744 | tf_op jit(solution)/shard_map/ppermute | solution.py:60
  148.8 18.1 %copy-start.15 = (bf16[3,128,384]{2,1,0:T(8,128)(2,1)}, bf16[3,128,384]{2,1,0:T(8,128)(2,1)S(1)}, u32[]{:S(2)}) copy-start(bf16[3,128,384]{2,1,0:T(8,128)(2,1)S(1)} %collective-permute-done.14) | copy-start | bytes 884740
  149.2 17.4 %collective-permute-start.15 = (bf16[3,128,384]{2,1,0:T(8,128)(2,1)S(1)}, bf16[3,128,384]{2,1,0:T(8,128)(2,1)S(1)}, u32[]{:S(2)}, u32[]{:S(2)}) collective-permute-start(bf16[3,128,384]{2,1,0:T(8,128)(2,1)S(1)} %collective-permute-done.14), channel_id=1, source_target_pairs={{0,112},{16,0},{32,16},{48,32},{64,48},{80,64},{96,80},{112,96},{1... | collective-permute-start | bytes 884744 | tf_op jit(solution)/shard_map/ppermute | solution.py:62
  151.5 11.1 %collective-permute-start.23 = (bf16[3,128,384]{2,1,0:T(8,128)(2,1)S(1)}, bf16[3,128,384]{2,1,0:T(8,128)(2,1)S(1)}, u32[]{:S(2)}, u32[]{:S(2)}) collective-permute-start(bf16[3,128,384]{2,1,0:T(8,128)(2,1)S(1)} %collective-permute-done.21), channel_id=1, source_target_pairs={{0,112},{16,0},{32,16},{48,32},{64,48},{80,64},{96,80},{112,96},{1... | collective-permute-start | bytes 884744 | tf_op jit(solution)/shard_map/ppermute | solution.py:62
  157.2 25.7 %copy-start.19 = (bf16[3,128,384]{2,1,0:T(8,128)(2,1)}, bf16[3,128,384]{2,1,0:T(8,128)(2,1)S(1)}, u32[]{:S(2)}) copy-start(bf16[3,128,384]{2,1,0:T(8,128)(2,1)S(1)} %collective-permute-done.18) | copy-start | bytes 884740
  157.5 15.7 %collective-permute-start.26 = (bf16[3,128,384]{2,1,0:T(8,128)(2,1)S(1)}, bf16[3,128,384]{2,1,0:T(8,128)(2,1)S(1)}, u32[]{:S(2)}, u32[]{:S(2)}) collective-permute-start(bf16[3,128,384]{2,1,0:T(8,128)(2,1)S(1)} %collective-permute-done.24), channel_id=1, source_target_pairs={{0,16},{16,32},{32,48},{48,64},{64,80},{80,96},{96,112},{112,0},{1... | collective-permute-start | bytes 884744 | tf_op jit(solution)/shard_map/ppermute | solution.py:60
  162.9 10.6 %collective-permute-start.19 = (bf16[3,128,384]{2,1,0:T(8,128)(2,1)S(1)}, bf16[3,128,384]{2,1,0:T(8,128)(2,1)S(1)}, u32[]{:S(2)}, u32[]{:S(2)}) collective-permute-start(bf16[3,128,384]{2,1,0:T(8,128)(2,1)S(1)} %collective-permute-done.18), channel_id=1, source_target_pairs={{0,16},{16,32},{32,48},{48,64},{64,80},{80,96},{96,112},{112,0},{1... | collective-permute-start | bytes 884744 | tf_op jit(solution)/shard_map/ppermute | solution.py:60
  166.6 19.4 %copy-start.16 = (bf16[3,128,384]{2,1,0:T(8,128)(2,1)}, bf16[3,128,384]{2,1,0:T(8,128)(2,1)S(1)}, u32[]{:S(2)}) copy-start(bf16[3,128,384]{2,1,0:T(8,128)(2,1)S(1)} %collective-permute-done.15) | copy-start | bytes 884740
  166.9 18.7 %collective-permute-start.16 = (bf16[3,128,384]{2,1,0:T(8,128)(2,1)S(1)}, bf16[3,128,384]{2,1,0:T(8,128)(2,1)S(1)}, u32[]{:S(2)}, u32[]{:S(2)}) collective-permute-start(bf16[3,128,384]{2,1,0:T(8,128)(2,1)S(1)} %collective-permute-done.15), channel_id=1, source_target_pairs={{0,112},{16,0},{32,16},{48,32},{64,48},{80,64},{96,80},{112,96},{1... | collective-permute-start | bytes 884744 | tf_op jit(solution)/shard_map/ppermute | solution.py:62
  169.1 10.3 %collective-permute-start.25 = (bf16[3,128,384]{2,1,0:T(8,128)(2,1)S(1)}, bf16[3,128,384]{2,1,0:T(8,128)(2,1)S(1)}, u32[]{:S(2)}, u32[]{:S(2)}) collective-permute-start(bf16[3,128,384]{2,1,0:T(8,128)(2,1)S(1)} %collective-permute-done.23), channel_id=1, source_target_pairs={{0,112},{16,0},{32,16},{48,32},{64,48},{80,64},{96,80},{112,96},{1... | collective-permute-start | bytes 884744 | tf_op jit(solution)/shard_map/ppermute | solution.py:62
  173.5 18.6 %copy-start.20 = (bf16[3,128,384]{2,1,0:T(8,128)(2,1)}, bf16[3,128,384]{2,1,0:T(8,128)(2,1)S(1)}, u32[]{:S(2)}) copy-start(bf16[3,128,384]{2,1,0:T(8,128)(2,1)S(1)} %collective-permute-done.19) | copy-start | bytes 884740
  179.5 8.6 %collective-permute-start.27 = (bf16[3,128,384]{2,1,0:T(8,128)(2,1)S(1)}, bf16[3,128,384]{2,1,0:T(8,128)(2,1)S(1)}, u32[]{:S(2)}, u32[]{:S(2)}) collective-permute-start(bf16[3,128,384]{2,1,0:T(8,128)(2,1)S(1)} %collective-permute-done.25), channel_id=1, source_target_pairs={{0,112},{16,0},{32,16},{48,32},{64,48},{80,64},{96,80},{112,96},{1... | collective-permute-start | bytes 884744 | tf_op jit(solution)/shard_map/ppermute | solution.py:62
  182.9 9.2 %collective-permute-start.20 = (bf16[3,128,384]{2,1,0:T(8,128)(2,1)S(1)}, bf16[3,128,384]{2,1,0:T(8,128)(2,1)S(1)}, u32[]{:S(2)}, u32[]{:S(2)}) collective-permute-start(bf16[3,128,384]{2,1,0:T(8,128)(2,1)S(1)} %collective-permute-done.19), channel_id=1, source_target_pairs={{0,16},{16,32},{32,48},{48,64},{64,80},{80,96},{96,112},{112,0},{1... | collective-permute-start | bytes 884744 | tf_op jit(solution)/shard_map/ppermute | solution.py:60
  199.9 32.8 %all-to-all-start.3 = ((bf16[32,32,512]{2,1,0:T(8,128)(2,1)}), bf16[32,32,512]{2,1,0:T(8,128)(2,1)}, u32[]{:S(2)}, u32[]{:S(2)}) async-start(bf16[32,32,512]{2,1,0:T(8,128)(2,1)} %broadcast_in_dim.22), calls=%async_computation.3 | async-start | bytes 2097152 | tf_op jit(solution)/shard_map/all_to_all | solution.py:21
  237.1 31.6 %all-to-all-start.4 = ((f32[16,96,128]{2,1,0:T(8,128)}), f32[16,96,128]{2,1,0:T(8,128)}, u32[]{:S(2)}, u32[]{:S(2)}) async-start(f32[16,96,128]{2,1,0:T(8,128)} %bitcast.283), calls=%async_computation.4 | async-start | bytes 1572864 | tf_op jit(solution)/shard_map/all_to_all | solution.py:25
  270.8 22.0 %all-to-all-start.5 = ((f32[16,96,128]{2,1,0:T(8,128)}), f32[16,96,128]{2,1,0:T(8,128)}, u32[]{:S(2)}, u32[]{:S(2)}) async-start(f32[16,96,128]{2,1,0:T(8,128)} %broadcast_in_dim.23), calls=%async_computation.5 | async-start | bytes 1572864 | tf_op jit(solution)/shard_map/all_to_all | solution.py:21
  297.1 42.8 %all-to-all-start.6 = ((bf16[32,32,512]{2,1,0:T(8,128)(2,1)}), bf16[32,32,512]{2,1,0:T(8,128)(2,1)}, u32[]{:S(2)}, u32[]{:S(2)}) async-start(bf16[32,32,512]{2,1,0:T(8,128)(2,1)} %bitcast.289), calls=%async_computation.6 | async-start | bytes 2097152 | tf_op jit(solution)/shard_map/all_to_all | solution.py:25
  318.0 24.2 %copy-start.7 = (bf16[224,512]{1,0:T(8,128)(2,1)S(1)}, bf16[224,512]{1,0:T(8,128)(2,1)}, u32[]{:S(2)}) copy-start(bf16[224,512]{1,0:T(8,128)(2,1)} %get-tuple-element.6) | copy-start | bytes 688132
  (18 other events, 122.8 us)

commit v3 on v1

--- a/solution.py
+++ b/solution.py
@@ -3,12 +3,17 @@
 import jax
 import jax.numpy as jnp
 from jax import lax
+from jax.sharding import Mesh
 from jax.sharding import PartitionSpec as P
 
 WIN = 8
 
 
 STEP_GAIN = 0.4
+
+LINE, RING = 4, 8
+TOK = ("line", "ring")
+THIN = 128
 
 
 def gather_blocks(own, axis):
@@ -37,16 +42,55 @@
     partial = jnp.dot(left_a, stack_g, preferred_element_type=jnp.float32) - jnp.dot(
         left_g, stack_a, preferred_element_type=jnp.float32
     )
-    parts = lax.axis_size("tok")
-    return sum_blocks(partial.reshape(parts, -1, partial.shape[1]), "tok")
+    partial = partial.astype(jnp.bfloat16)
+    parts = lax.axis_size(TOK)
+    return sum_blocks(partial.reshape(parts, -1, partial.shape[1]), TOK)
+
+
+def roll_blocks(blocks, start, dim):
+    twice = jnp.concatenate([blocks, blocks], dim)
+    return lax.dynamic_slice_in_dim(twice, start, blocks.shape[dim], dim)
+
+
+def times_rotation(lhs, rot_b, line_wide, line_pos):
+    rows, narrow = rot_b.shape
+    wide = narrow - THIN
+    count = lhs.shape[0]
+    span = RING * rows
+
+    near = lax.all_gather(rot_b, "ring", axis=0, tiled=True)
+    others = roll_blocks(line_wide, line_pos + 1, 0)[: LINE - 1]
+    far = lax.all_gather(others.reshape((LINE - 1) * rows, wide), "ring", axis=0, tiled=True)
+    thin = gather_blocks(near[:, :THIN], "line")
+
+    spans = jnp.stack([lhs[:, k * span : (k + 1) * span] for k in range(LINE)])
+    spans = roll_blocks(spans, line_pos, 0)
+    lhs_far = jnp.concatenate(
+        [
+            spans[1 + k, :, ring * rows : (ring + 1) * rows]
+            for ring in range(RING)
+            for k in range(LINE - 1)
+        ],
+        1,
+    )
+    total_thin = jnp.dot(lhs, thin.reshape(LINE * span, THIN), preferred_element_type=jnp.float32)
+    total = jnp.dot(spans[0], near[:, THIN:], preferred_element_type=jnp.float32)
+    total = total + jnp.dot(lhs_far, far, preferred_element_type=jnp.float32)
+
+    first_near = near.reshape(RING, rows, narrow)[None, :, :WIN, THIN:]
+    first_far = far.reshape(RING, LINE - 1, rows, wide)[:, :, :WIN].transpose(1, 0, 2, 3)
+    first = jnp.concatenate([first_near, first_far], 0)
+    first = roll_blocks(first, (LINE - line_pos) % LINE, 0)
+    first_thin = thin.reshape(LINE, RING, rows, THIN)[:, :, :WIN]
+    first = jnp.concatenate([first_thin, first], 3).reshape(LINE * RING * WIN, narrow)
+    return jnp.concatenate([total_thin, total], 1), first
 
 
 def local(activations, rotation, value_weight, token_code, channel_code):
-    n_tok = lax.axis_size("tok")
+    n_tok = lax.axis_size(TOK)
     n_mdl = lax.axis_size("mdl")
-    tok_pos = lax.axis_index("tok")
+    tok_pos = lax.axis_index(TOK)
     mdl_pos = lax.axis_index("mdl")
-    block_rows = rotation.shape[0]
     narrow = rotation.shape[1]
     model_width = activations.shape[1]
     channels = value_weight.shape[1]
@@ -54,25 +98,26 @@
     tok_rows = activations.shape[0]
     width_root = math.sqrt(model_width)
     rot_b = rotation.astype(jnp.bfloat16)
-    rot_panel = lax.all_gather(rot_b, "tok", axis=0, tiled=True)
-    own_cols = lax.dynamic_slice_in_dim(value_weight, tok_pos * chan_share, chan_share, 1)
+    line_wide = gather_blocks(rot_b[:, THIN:], "line")
+    value_late, line_wide = lax.optimization_barrier((value_weight, line_wide))
+    own_cols = lax.dynamic_slice_in_dim(value_late, tok_pos * chan_share, chan_share, 1)
     weight_rows = gather_blocks(own_cols.T, "mdl").transpose(1, 0, 2).reshape(chan_share, model_width)
+    lhs = jnp.concatenate([activations, weight_rows], 0)
+    products, window = times_rotation(lhs, rot_b, line_wide, lax.axis_index("line"))
+    products = products / width_root
+    rotated, turned = products[:tok_rows], products[tok_rows:]
     own_feats = lax.dynamic_slice_in_dim(activations, mdl_pos * narrow, narrow, 1)
     plain = jnp.dot(own_feats, value_weight, preferred_element_type=jnp.float32)
 
-    turned = jnp.dot(weight_rows, rot_panel, preferred_element_type=jnp.float32) / width_root
     own_codes = lax.dynamic_slice_in_dim(channel_code, tok_pos * chan_share, chan_share, 0)
     weight_clip = own_codes.astype(jnp.float32)[:, None] / (4.0 * width_root)
     weight_tanh = jnp.tanh(turned / weight_clip)
     quant_weight = (weight_clip * weight_tanh).astype(jnp.bfloat16)
-    weight_full = gather_blocks(quant_weight, "tok").reshape(channels, narrow)
+    weight_full = gather_blocks(quant_weight, TOK).reshape(channels, narrow)
 
-    rotated = jnp.dot(activations, rot_panel, preferred_element_type=jnp.float32) / width_root
     act_clip = token_code.astype(jnp.float32)[:, None] * 0.5
     act_tanh = jnp.tanh(rotated / act_clip)
     quant_act = (act_clip * act_tanh).astype(jnp.bfloat16)
-    window = rot_panel.reshape(n_tok, block_rows, narrow)[:, :WIN].reshape(n_tok * WIN, narrow)
-
     partial_err = (
         jnp.einsum("td,cd->tc", quant_act, weight_full, preferred_element_type=jnp.float32) - plain
     )
@@ -86,25 +131,26 @@
         jnp.einsum("tc,td->cd", error_bf, quant_act, preferred_element_type=jnp.float32)
         .astype(jnp.bfloat16)
         .reshape(n_tok, chan_share, narrow),
-        "tok",
+        TOK,
     )
     grad_act = (
         jnp.dot(error_bf, weight_full, preferred_element_type=jnp.float32)
         * (1.0 - act_tanh * act_tanh)
     ).astype(jnp.bfloat16)
     grad_turned = (grad_quant * (1.0 - weight_tanh * weight_tanh)).astype(jnp.bfloat16)
-    stack_a = jnp.concatenate([rotated.astype(jnp.bfloat16), turned.astype(jnp.bfloat16)], 0)
+    stack_a = products.astype(jnp.bfloat16)
     stack_g = jnp.concatenate([grad_act, grad_turned], 0)
     step_size = STEP_GAIN / math.sqrt(tok_rows * n_tok * channels)
     own_rows = rotation[:WIN]
     moved = own_rows - step_size * cayley_own(window, stack_a, stack_g)
-    second_in = gather_blocks((own_rows + moved).astype(jnp.bfloat16), "tok")
+    second_in = gather_blocks((own_rows + moved).astype(jnp.bfloat16), TOK)
     second_in = second_in.reshape(n_tok * WIN, narrow)
     new_rows = own_rows - 0.5 * step_size * cayley_own(second_in, stack_a, stack_g)
     return (new_rows, recon_error)
 
 
 def solution(mesh):
-    in_specs = (P("tok", None), P("tok", "mdl"), P("mdl", None), P("tok"), P())
-    out_specs = (P("tok", "mdl"), P("tok", None))
+    mesh = Mesh(mesh.devices.reshape(LINE, RING, -1), TOK + ("mdl",))
+    in_specs = (P(TOK, None), P(TOK, "mdl"), P("mdl", None), P(TOK), P())
+    out_specs = (P(TOK, "mdl"), P(TOK, None))
     return jax.shard_map(local, mesh=mesh, in_specs=in_specs, out_specs=out_specs, check_vma=False)

time: 483 us -> 414 us (0.86)
  the two profiles are of different devices: /device:TPU:64 before, /device:TPU:8 now
where the time goes in v3:
time: 414 us; the launch traced here: 412 us
  blocking collectives  177 us (43%)
  waiting for transfers between devices  76 us (18%)
  local copies, waits for them, and re-layouts  68.4 us (17%)
  starting transfers between devices  46.9 us (11%)
  matrix products  17.8 us (4%)
  between operations  14.4 us (3%)
  other arithmetic  11 us (3%)
    all_to_all x5, blocking collectives, sum_blocks(): return jnp.sum(lax.all_to_all(blocks, axis, 0, 0).astype(jnp.float32), 0)  99.9 us
    all_to_all x4, blocking collectives, gather_blocks(): lax.all_to_all(jnp.broadcast_to(own[None], (parts,) + own.shape), axis, 0...  77.2 us
    all_to_all x4, waiting for transfers between devices, gather_blocks(): lax.all_to_all(jnp.broadcast_to(own[None], (parts,) + own.shape), axis, 0...  54.4 us
    unnamed x51, local copies, waits for them, and re-layouts  54 us
    all_to_all x4, starting transfers between devices, gather_blocks(): lax.all_to_all(jnp.broadcast_to(own[None], (parts,) + own.shape), axis, 0...  40 us
    all_to_all x1, waiting for transfers between devices, sum_blocks(): return jnp.sum(lax.all_to_all(blocks, axis, 0, 0).astype(jnp.float32), 0)  21.6 us
  transfers between devices with their start and end apart: 7, of which 5 were waited for; matrix products, arithmetic and copies ran while one was open for 17% of the time, Pallas kernels for 0%

profile of v3, /device:TPU:8, one launch (start us, length us, event | category | flops | bytes accessed | tf_op | source)
XLA Modules:
  0.0 411.6 jit_solution(10793703024073815941)
XLA Ops:
  7.2 1.8 convert_element_type.63
  11.0 9.3 %all-to-all-start.1 = ((bf16[4,256,384]{2,1,0:T(8,128)(2,1)}), bf16[4,256,384]{2,1,0:T(8,128)(2,1)S(1)}, u32[]{:S(2)}, u32[]{:S(2)}) async-start(bf16[4,256,384]{2,1,0:T(8,128)(2,1)} %broadcast_in_dim.20), calls=%async_computation.1 | async-start | bytes 1572864 | tf_op jit(solution)/shard_map/all_to_all | solution.py:21
  20.3 12.9 %all-to-all-done.1 = bf16[4,256,384]{2,1,0:T(8,128)(2,1)S(1)} async-done(((bf16[4,256,384]{2,1,0:T(8,128)(2,1)}), bf16[4,256,384]{2,1,0:T(8,128)(2,1)S(1)}, u32[]{:S(2)}, u32[]{:S(2)}) %all-to-all-start.1) | async-done | bytes 786464 | tf_op jit(solution)/shard_map/all_to_all | solution.py:21
  34.2 8.5 %all-to-all-start.2 = ((bf16[16,32,512]{2,1,0:T(8,128)(2,1)}), bf16[16,32,512]{2,1,0:T(8,128)(2,1)S(1)}, u32[]{:S(2)}, u32[]{:S(2)}) async-start(bf16[16,32,512]{2,1,0:T(8,128)(2,1)} %broadcast_in_dim.21), calls=%async_computation.2 | async-start | bytes 1048576 | tf_op jit(solution)/shard_map/all_to_all | solution.py:21
  43.9 3.9 constant_dynamic-update-slice_fusion.1
  48.6 11.3 %all-to-all-done.2 = bf16[16,32,512]{2,1,0:T(8,128)(2,1)S(1)} async-done(((bf16[16,32,512]{2,1,0:T(8,128)(2,1)}), bf16[16,32,512]{2,1,0:T(8,128)(2,1)S(1)}, u32[]{:S(2)}, u32[]{:S(2)}) %all-to-all-start.2) | async-done | bytes 524320 | tf_op jit(solution)/shard_map/all_to_all | solution.py:21
  60.8 2.4 fusion.11
  63.2 2.2 fusion.13
  65.4 2.2 fusion.15
  72.8 1.6 broadcast_in_dim.18
  74.4 7.5 %all-to-all-start = ((bf16[4,2048,128]{2,1,0:T(8,128)(2,1)}), bf16[4,2048,128]{2,1,0:T(8,128)(2,1)S(1)}, u32[]{:S(2)}, u32[]{:S(2)}) async-start(bf16[4,2048,128]{2,1,0:T(8,128)(2,1)} %broadcast_in_dim.18), calls=%async_computation | async-start | bytes 4194304 | tf_op jit(solution)/shard_map/all_to_all | solution.py:21
  81.8 2.2 fusion.18
  85.6 1.6 fusion.57
  87.2 1.6 fusion.56
  88.8 1.6 fusion.55
  90.4 1.6 fusion.54
  92.0 1.6 fusion.53
  93.5 1.6 fusion.52
  95.1 1.6 fusion.51
  96.7 1.6 fusion.50
  106.1 1.6 fusion.44
  107.7 1.6 fusion.43
  109.3 1.6 fusion.42
  112.5 1.6 fusion.40
  114.1 1.6 fusion.39
  115.6 1.6 fusion.38
  117.3 1.6 fusion.37
  118.8 1.6 fusion.36
  120.4 1.6 fusion.35
  122.0 4.6 %all-to-all-done = bf16[4,2048,128]{2,1,0:T(8,128)(2,1)S(1)} async-done(((bf16[4,2048,128]{2,1,0:T(8,128)(2,1)}), bf16[4,2048,128]{2,1,0:T(8,128)(2,1)S(1)}, u32[]{:S(2)}, u32[]{:S(2)}) %all-to-all-start) | async-done | bytes 2097184 | tf_op jit(solution)/shard_map/all_to_all | solution.py:21
  126.6 3.1 fusion.69
  129.8 4.9 %fusion.70 = f32[224,384]{1,0:T(8,128)S(1)} fusion(bf16[224,6144]{1,0:T(8,128)(2,1)} %fusion.35, bf16[6144,384]{1,0:T(8,128)(2,1)} %all-gather.5.cloned.1.call-done), kind=kOutput, calls=%fused_computation.132 | convolution fusion | flops 1056964608 | bytes 7815168 | tf_op jit(solution)/shard_map/dot_general | solution.py:78
  134.7 1.8 fusion.5
  138.6 14.7 %all-to-all-start.3 = ((bf16[32,32,512]{2,1,0:T(8,128)(2,1)}), bf16[32,32,512]{2,1,0:T(8,128)(2,1)}, u32[]{:S(2)}, u32[]{:S(2)}) async-start(bf16[32,32,512]{2,1,0:T(8,128)(2,1)} %broadcast_in_dim.22), calls=%async_computation.3 | async-start | bytes 2097152 | tf_op jit(solution)/shard_map/all_to_all | solution.py:21
  153.3 25.6 %all-to-all-done.3 = bf16[32,32,512]{2,1,0:T(8,128)(2,1)} async-done(((bf16[32,32,512]{2,1,0:T(8,128)(2,1)}), bf16[32,32,512]{2,1,0:T(8,128)(2,1)}, u32[]{:S(2)}, u32[]{:S(2)}) %all-to-all-start.3) | async-done | bytes 1048608 | tf_op jit(solution)/shard_map/all_to_all | solution.py:21
  178.9 1.9 fusion.68
  182.4 32.5 %all_to_all.70 = f32[16,96,128]{2,1,0:T(8,128)} all-to-all(f32[16,96,128]{2,1,0:T(8,128)S(1)} %bitcast.186), channel_id=1, replica_groups=mesh['line'=4,'ring'=8,'mdl'=16] {'mdl'}, dimensions={0} | all-to-all | bytes 1572864 | tf_op jit(solution)/shard_map/all_to_all | solution.py:25
  216.2 27.3 %all_to_all.71 = f32[16,96,128]{2,1,0:T(8,128)S(1)} all-to-all(f32[16,96,128]{2,1,0:T(8,128)S(1)} %broadcast_in_dim.23), channel_id=1, replica_groups=mesh['line'=4,'ring'=8,'mdl'=16] {'mdl'}, dimensions={0} | all-to-all | bytes 1572864 | tf_op jit(solution)/shard_map/all_to_all | solution.py:21
  247.5 6.8 %all-to-all-start.6 = ((bf16[32,32,512]{2,1,0:T(8,128)(2,1)}), bf16[32,32,512]{2,1,0:T(8,128)(2,1)}, u32[]{:S(2)}, u32[]{:S(2)}) async-start(bf16[32,32,512]{2,1,0:T(8,128)(2,1)} %bitcast.195), calls=%async_computation.6 | async-start | bytes 2097152 | tf_op jit(solution)/shard_map/all_to_all | solution.py:25
  257.7 1.6 fusion.8
  259.3 21.6 %all-to-all-done.6 = bf16[32,32,512]{2,1,0:T(8,128)(2,1)} async-done(((bf16[32,32,512]{2,1,0:T(8,128)(2,1)}), bf16[32,32,512]{2,1,0:T(8,128)(2,1)}, u32[]{:S(2)}, u32[]{:S(2)}) %all-to-all-start.6) | async-done | bytes 1048608 | tf_op jit(solution)/shard_map/all_to_all | solution.py:25
  283.7 17.3 %all_to_all.72 = bf16[16,16,448]{2,1,0:T(8,128)(2,1)S(1)} all-to-all(bf16[16,16,448]{2,1,0:T(8,128)(2,1)S(1)} %bitcast.196), channel_id=1, replica_groups=mesh['line'=4,'ring'=8,'mdl'=16] {'mdl'}, dimensions={0} | all-to-all | bytes 458752 | tf_op jit(solution)/shard_map/all_to_all | solution.py:25
  301.1 17.5 %all_to_all.73 = bf16[16,16,448]{2,1,0:T(8,128)(2,1)S(1)} all-to-all(bf16[16,16,448]{2,1,0:T(8,128)(2,1)S(1)} %broadcast_in_dim.24), channel_id=1, replica_groups=mesh['line'=4,'ring'=8,'mdl'=16] {'mdl'}, dimensions={0} | all-to-all | bytes 458752 | tf_op jit(solution)/shard_map/all_to_all | solution.py:21
  319.1 16.5 %all_to_all.74 = bf16[32,8,512]{2,1,0:T(8,128)(2,1)S(1)} all-to-all(bf16[32,8,512]{2,1,0:T(8,128)(2,1)S(1)} %fusion.10), channel_id=1, replica_groups=mesh['line'=4,'ring'=8,'mdl'=16] {'line','ring'}, dimensions={0} | all-to-all | bytes 524288 | tf_op jit(solution)/shard_map/all_to_all | solution.py:25
  336.4 16.5 %all_to_all.75 = bf16[32,8,512]{2,1,0:T(8,128)(2,1)S(1)} all-to-all(bf16[32,8,512]{2,1,0:T(8,128)(2,1)S(1)} %broadcast_in_dim.25), channel_id=1, replica_groups=mesh['line'=4,'ring'=8,'mdl'=16] {'line','ring'}, dimensions={0} | all-to-all | bytes 524288 | tf_op jit(solution)/shard_map/all_to_all | solution.py:21
  353.3 17.4 %all_to_all.76 = bf16[16,16,448]{2,1,0:T(8,128)(2,1)S(1)} all-to-all(bf16[16,16,448]{2,1,0:T(8,128)(2,1)S(1)} %bitcast.197), channel_id=1, replica_groups=mesh['line'=4,'ring'=8,'mdl'=16] {'mdl'}, dimensions={0} | all-to-all | bytes 458752 | tf_op jit(solution)/shard_map/all_to_all | solution.py:25
  370.8 15.8 %all_to_all.77 = bf16[16,16,448]{2,1,0:T(8,128)(2,1)S(1)} all-to-all(bf16[16,16,448]{2,1,0:T(8,128)(2,1)S(1)} %broadcast_in_dim.26), channel_id=1, replica_groups=mesh['line'=4,'ring'=8,'mdl'=16] {'mdl'}, dimensions={0} | all-to-all | bytes 458752 | tf_op jit(solution)/shard_map/all_to_all | solution.py:21
  387.2 16.2 %all_to_all.78 = bf16[32,8,512]{2,1,0:T(8,128)(2,1)S(1)} all-to-all(bf16[32,8,512]{2,1,0:T(8,128)(2,1)S(1)} %fusion.9), channel_id=1, replica_groups=mesh['line'=4,'ring'=8,'mdl'=16] {'line','ring'}, dimensions={0} | all-to-all | bytes 524288 | tf_op jit(solution)/shard_map/all_to_all | solution.py:25
  (83 shorter events, 40.5 us)
Async XLA Ops:
  7.2 26.0 %copy-start = (bf16[512,1024]{1,0:T(8,128)(2,1)S(1)}, bf16[512,1024]{1,0:T(8,128)(2,1)}, u32[]{:S(2)}) copy-start(bf16[512,1024]{1,0:T(8,128)(2,1)} %param.7) | copy-start | bytes 3145732
  7.2 64.5 %all-gather.3.cloned.1.call-start = ((), (), s32[]{:S(2)}) async-start(), calls=%async_computation.14 | async-start | bytes 2359296 | tf_op jit(solution)/shard_map/all_gather | solution.py:61
  11.0 22.2 %all-to-all-start.1 = ((bf16[4,256,384]{2,1,0:T(8,128)(2,1)}), bf16[4,256,384]{2,1,0:T(8,128)(2,1)S(1)}, u32[]{:S(2)}, u32[]{:S(2)}) async-start(bf16[4,256,384]{2,1,0:T(8,128)(2,1)} %broadcast_in_dim.20), calls=%async_computation.1 | async-start | bytes 1572864 | tf_op jit(solution)/shard_map/all_to_all | solution.py:21
  34.2 25.7 %all-to-all-start.2 = ((bf16[16,32,512]{2,1,0:T(8,128)(2,1)}), bf16[16,32,512]{2,1,0:T(8,128)(2,1)S(1)}, u32[]{:S(2)}, u32[]{:S(2)}) async-start(bf16[16,32,512]{2,1,0:T(8,128)(2,1)} %broadcast_in_dim.21), calls=%async_computation.2 | async-start | bytes 1048576 | tf_op jit(solution)/shard_map/all_to_all | solution.py:21
  42.7 87.0 %all-gather.5.cloned.1.call-start = ((), (), s32[]{:S(2)}) async-start(), calls=%async_computation.15 | async-start | bytes 5308416 | tf_op jit(solution)/shard_map/all_gather | solution.py:63
  60.8 6.8 %copy-start.1 = (bf16[224,8192]{1,0:T(8,128)(2,1)S(1)}, bf16[224,8192]{1,0:T(8,128)(2,1)}, u32[]{:S(2)}) copy-start(bf16[224,8192]{1,0:T(8,128)(2,1)} %constant_dynamic-update-slice_fusion) | copy-start | bytes 11010052
  74.4 52.2 %all-to-all-start = ((bf16[4,2048,128]{2,1,0:T(8,128)(2,1)}), bf16[4,2048,128]{2,1,0:T(8,128)(2,1)S(1)}, u32[]{:S(2)}, u32[]{:S(2)}) async-start(bf16[4,2048,128]{2,1,0:T(8,128)(2,1)} %broadcast_in_dim.18), calls=%async_computation | async-start | bytes 4194304 | tf_op jit(solution)/shard_map/all_to_all | solution.py:21
  129.8 4.9 %copy-start.7 = (bf16[2048,512]{1,0:T(8,128)(2,1)S(1)}, bf16[2048,512]{1,0:T(8,128)(2,1)}, u32[]{:S(2)}) copy-start(bf16[2048,512]{1,0:T(8,128)(2,1)} %all-gather.3.cloned.1.call-done) | copy-start | bytes 6291460
  136.5 16.8 %copy-start.8 = (s32[192]{0:T(256)S(1)}, s32[192]{0:T(256)}, u32[]{:S(2)}) copy-start(s32[192]{0:T(256)} %param.8) | copy-start | bytes 2308
  136.6 0.8 copy-start.4
  138.6 40.4 %all-to-all-start.3 = ((bf16[32,32,512]{2,1,0:T(8,128)(2,1)}), bf16[32,32,512]{2,1,0:T(8,128)(2,1)}, u32[]{:S(2)}, u32[]{:S(2)}) async-start(bf16[32,32,512]{2,1,0:T(8,128)(2,1)} %broadcast_in_dim.22), calls=%async_computation.3 | async-start | bytes 2097152 | tf_op jit(solution)/shard_map/all_to_all | solution.py:21
  216.1 29.8 %copy-start.5 = (f32[224,512]{1,0:T(8,128)S(1)}, f32[224,512]{1,0:T(8,128)}, u32[]{:S(2)}) copy-start(f32[224,512]{1,0:T(8,128)} %copy-done.4) | copy-start | bytes 1376260
  243.5 0.9 copy-start.2
  245.0 0.9 copy-start.3
  247.5 33.4 %all-to-all-start.6 = ((bf16[32,32,512]{2,1,0:T(8,128)(2,1)}), bf16[32,32,512]{2,1,0:T(8,128)(2,1)}, u32[]{:S(2)}, u32[]{:S(2)}) async-start(bf16[32,32,512]{2,1,0:T(8,128)(2,1)} %bitcast.195), calls=%async_computation.6 | async-start | bytes 2097152 | tf_op jit(solution)/shard_map/all_to_all | solution.py:25
  254.3 3.4 copy-start.6
Sparse Core Ops, SparseCore 0:
  10.1 49.2 all-gather.2
  62.0 61.2 all-gather.4

commit v4 on v3

--- a/solution.py
+++ b/solution.py
@@ -13,6 +13,7 @@
 
 LINE, RING = 4, 8
 TOK = ("line", "ring")
+MDL = ("chip", "core")
 THIN = 128
 
 
@@ -28,12 +29,12 @@
 def cayley_lefts(mats, stack_a, stack_g):
     rows = mats.shape[0]
     row_total = stack_a.shape[0]
-    parts = lax.axis_size("mdl")
+    parts = lax.axis_size(MDL)
     stacked = jnp.concatenate([stack_a, stack_g], 0)
     products = jnp.einsum("rd,kd->rk", mats, stacked, preferred_element_type=jnp.float32)
     products = products.astype(jnp.bfloat16).reshape(parts, rows // parts, 2 * row_total)
-    own_sum = sum_blocks(products, "mdl").astype(jnp.bfloat16)
-    lefts = gather_blocks(own_sum, "mdl").reshape(rows, 2 * row_total)
+    own_sum = lax.optimization_barrier(sum_blocks(products, MDL)).astype(jnp.bfloat16)
+    lefts = gather_blocks(own_sum, MDL).reshape(rows, 2 * row_total)
     return lefts[:, :row_total], lefts[:, row_total:]
 
 
@@ -47,50 +48,50 @@
     return sum_blocks(partial.reshape(parts, -1, partial.shape[1]), TOK)
 
 
-def roll_blocks(blocks, start, dim):
-    twice = jnp.concatenate([blocks, blocks], dim)
-    return lax.dynamic_slice_in_dim(twice, start, blocks.shape[dim], dim)
-
-
 def times_rotation(lhs, rot_b, line_wide, line_pos):
     rows, narrow = rot_b.shape
     wide = narrow - THIN
-    count = lhs.shape[0]
     span = RING * rows
 
+    def other(k, blocks):
+        return jnp.where(line_pos > k, blocks[k], blocks[k + 1])
+
     near = lax.all_gather(rot_b, "ring", axis=0, tiled=True)
-    others = roll_blocks(line_wide, line_pos + 1, 0)[: LINE - 1]
-    far = lax.all_gather(others.reshape((LINE - 1) * rows, wide), "ring", axis=0, tiled=True)
+    others = jnp.stack([other(k, line_wide) for k in range(LINE - 1)])
+    far = lax.all_gather(others, "ring", axis=1, tiled=True)
     thin = gather_blocks(near[:, :THIN], "line")
 
-    spans = jnp.stack([lhs[:, k * span : (k + 1) * span] for k in range(LINE)])
-    spans = roll_blocks(spans, line_pos, 0)
-    lhs_far = jnp.concatenate(
-        [
-            spans[1 + k, :, ring * rows : (ring + 1) * rows]
-            for ring in range(RING)
-            for k in range(LINE - 1)
-        ],
-        1,
-    )
+    spans = [lhs[:, k * span : (k + 1) * span] for k in range(LINE)]
+    lhs_near = spans[LINE - 1]
+    for k in range(LINE - 1):
+        lhs_near = jnp.where(line_pos == k, spans[k], lhs_near)
     total_thin = jnp.dot(lhs, thin.reshape(LINE * span, THIN), preferred_element_type=jnp.float32)
-    total = jnp.dot(spans[0], near[:, THIN:], preferred_element_type=jnp.float32)
-    total = total + jnp.dot(lhs_far, far, preferred_element_type=jnp.float32)
+    total = jnp.dot(lhs_near, near[:, THIN:], preferred_element_type=jnp.float32)
+    for k in range(LINE - 1):
+        total = total + jnp.dot(other(k, spans), far[k], preferred_element_type=jnp.float32)
 
-    first_near = near.reshape(RING, rows, narrow)[None, :, :WIN, THIN:]
-    first_far = far.reshape(RING, LINE - 1, rows, wide)[:, :, :WIN].transpose(1, 0, 2, 3)
-    first = jnp.concatenate([first_near, first_far], 0)
-    first = roll_blocks(first, (LINE - line_pos) % LINE, 0)
+    first_near = near.reshape(RING, rows, narrow)[:, : 2 * WIN]
+    first_far = far.reshape(LINE - 1, RING, rows, wide)[:, :, : 2 * WIN]
+    first_near, first_far = lax.optimization_barrier((first_near, first_far))
+    first_near, first_far = first_near[:, :WIN, THIN:], first_far[:, :, :WIN]
+    first = [
+        jnp.where(
+            line_pos == k,
+            first_near,
+            jnp.where(line_pos > k, first_far[min(k, LINE - 2)], first_far[max(k - 1, 0)]),
+        )
+        for k in range(LINE)
+    ]
     first_thin = thin.reshape(LINE, RING, rows, THIN)[:, :, :WIN]
-    first = jnp.concatenate([first_thin, first], 3).reshape(LINE * RING * WIN, narrow)
+    first = jnp.concatenate([first_thin, jnp.stack(first)], 3).reshape(LINE * RING * WIN, narrow)
     return jnp.concatenate([total_thin, total], 1), first
 
 
 def local(activations, rotation, value_weight, token_code, channel_code):
     n_tok = lax.axis_size(TOK)
-    n_mdl = lax.axis_size("mdl")
+    n_mdl = lax.axis_size(MDL)
     tok_pos = lax.axis_index(TOK)
-    mdl_pos = lax.axis_index("mdl")
+    mdl_pos = lax.axis_index(MDL)
     narrow = rotation.shape[1]
     model_width = activations.shape[1]
     channels = value_weight.shape[1]
@@ -101,7 +102,7 @@
     line_wide = gather_blocks(rot_b[:, THIN:], "line")
     value_late, line_wide = lax.optimization_barrier((value_weight, line_wide))
     own_cols = lax.dynamic_slice_in_dim(value_late, tok_pos * chan_share, chan_share, 1)
-    weight_rows = gather_blocks(own_cols.T, "mdl").transpose(1, 0, 2).reshape(chan_share, model_width)
+    weight_rows = gather_blocks(own_cols.T, MDL).transpose(1, 0, 2).reshape(chan_share, model_width)
     lhs = jnp.concatenate([activations, weight_rows], 0)
     products, window = times_rotation(lhs, rot_b, line_wide, lax.axis_index("line"))
     products = products / width_root
@@ -121,11 +122,13 @@
     partial_err = (
         jnp.einsum("td,cd->tc", quant_act, weight_full, preferred_element_type=jnp.float32) - plain
     )
-    lanes = channels * 2 // n_mdl
-    halves = partial_err.reshape(2, tok_rows // 2, n_mdl // 2, lanes).transpose(0, 2, 1, 3)
-    own_err = sum_blocks(halves.reshape(n_mdl, tok_rows // 2, lanes), "mdl")
-    recon_error = gather_blocks(own_err, "mdl").reshape(2, n_mdl // 2, tok_rows // 2, lanes)
-    recon_error = recon_error.transpose(0, 2, 1, 3).reshape(tok_rows, channels)
+    half = tok_rows // 2
+    chips = lax.axis_size("chip")
+    core_err = sum_blocks(partial_err.reshape(2, half, channels), "core")
+    core_err = core_err.reshape(half, chips, channels // chips).transpose(1, 0, 2)
+    own_err = sum_blocks(core_err, "chip")
+    core_err = gather_blocks(own_err, "chip").transpose(1, 0, 2).reshape(half, channels)
+    recon_error = gather_blocks(core_err, "core").reshape(tok_rows, channels)
     error_bf = recon_error.astype(jnp.bfloat16)
     grad_quant = sum_blocks(
         jnp.einsum("tc,td->cd", error_bf, quant_act, preferred_element_type=jnp.float32)
@@ -150,7 +153,7 @@
 
 
 def solution(mesh):
-    mesh = Mesh(mesh.devices.reshape(LINE, RING, -1), TOK + ("mdl",))
-    in_specs = (P(TOK, None), P(TOK, "mdl"), P("mdl", None), P(TOK), P())
-    out_specs = (P(TOK, "mdl"), P(TOK, None))
+    mesh = Mesh(mesh.devices.reshape(LINE, RING, -1, 2), TOK + MDL)
+    in_specs = (P(TOK, None), P(TOK, MDL), P(MDL, None), P(TOK), P())
+    out_specs = (P(TOK, MDL), P(TOK, None))
     return jax.shard_map(local, mesh=mesh, in_specs=in_specs, out_specs=out_specs, check_vma=False)

time: 414 us -> 397 us (0.959)
  local copies, waits for them, and re-layouts: 68.4 us -> 17.6 us
  waiting for transfers between devices: 76 us -> 121 us
  blocking collectives: 177 us -> 166 us
  starting transfers between devices: 46.9 us -> 41.8 us
    unnamed x51 -> x25, local copies, waits for them, and re-layouts: 54 us -> 7.51 us
    all_to_all x4, waiting for transfers between devices: 54.4 us -> 78.2 us  [gather_blocks(): lax.all_to_all(jnp.broadcast_to(own[None], (parts,) + own.shape), axis, 0...]
    all_gather x1, waiting for transfers between devices: 0.01 us -> 15.6 us  [times_rotation(): near = lax.all_gather(rot_b, 'ring', axis=0, tiled=True)]
    all_to_all x4 -> x5, blocking collectives: 77.2 us -> 68.8 us  [gather_blocks(): lax.all_to_all(jnp.broadcast_to(own[None], (parts,) + own.shape), axis, 0...]
    all_to_all x4, starting transfers between devices: 40 us -> 34.6 us  [gather_blocks(): lax.all_to_all(jnp.broadcast_to(own[None], (parts,) + own.shape), axis, 0...]
    all_gather x1, waiting for transfers between devices: 0.02 us -> 5.35 us  [times_rotation(): far = lax.all_gather(others, 'ring', axis=1, tiled=True)]
    dot_general x2 -> x4, matrix products: 6.73 us -> 9.92 us  [the longest x3 7 us: times_rotation(): jnp.dot(other(k, spans), far[k], preferred_element_type=jnp.float32)]
    all_to_all x5 -> x6, blocking collectives: 99.9 us -> 97.5 us  [sum_blocks(): return jnp.sum(lax.all_to_all(blocks, axis, 0, 0).astype(jnp.float32), 0)]
  transfers between devices with their start and end apart: 7 -> 7, of which waited for: 5 -> 7; matrix products, arithmetic and copies ran while one was open for 17% -> 5% of each run, Pallas kernels for 0% -> 0%
where the time goes in v4:
time: 397 us; the launch traced here: 395 us
  blocking collectives  166 us (42%)
  waiting for transfers between devices  121 us (30%)
  starting transfers between devices  41.8 us (11%)
  matrix products  21.1 us (5%)
  local copies, waits for them, and re-layouts  17.6 us (4%)
  between operations  14.4 us (4%)
  other arithmetic  12.6 us (3%)
    all_to_all x6, blocking collectives, sum_blocks(): return jnp.sum(lax.all_to_all(blocks, axis, 0, 0).astype(jnp.float32), 0)  97.5 us
    all_to_all x4, waiting for transfers between devices, gather_blocks(): lax.all_to_all(jnp.broadcast_to(own[None], (parts,) + own.shape), axis, 0...  78.2 us
    all_to_all x5, blocking collectives, gather_blocks(): lax.all_to_all(jnp.broadcast_to(own[None], (parts,) + own.shape), axis, 0...  68.8 us
    all_to_all x4, starting transfers between devices, gather_blocks(): lax.all_to_all(jnp.broadcast_to(own[None], (parts,) + own.shape), axis, 0...  34.6 us
    all_to_all x1, waiting for transfers between devices, sum_blocks(): return jnp.sum(lax.all_to_all(blocks, axis, 0, 0).astype(jnp.float32), 0)  21.9 us
    all_gather x1, waiting for transfers between devices, times_rotation(): near = lax.all_gather(rot_b, 'ring', axis=0, tiled=True)  15.6 us
  transfers between devices with their start and end apart: 7, of which 7 were waited for; matrix products, arithmetic and copies ran while one was open for 5% of the time, Pallas kernels for 0%

profile of v4, /device:TPU:8, one launch (start us, length us, event | category | flops | bytes accessed | tf_op | source)
XLA Modules:
  0.0 395.0 jit_solution(15116798779284340952)
XLA Ops:
  7.2 1.9 convert_element_type.71
  9.1 0.9 slice.126
  10.1 0.9 broadcast_in_dim.21
  11.0 9.3 %all-to-all-start.1 = ((bf16[4,256,384]{2,1,0:T(8,128)(2,1)}), bf16[4,256,384]{2,1,0:T(8,128)(2,1)S(1)}, u32[]{:S(2)}, u32[]{:S(2)}) async-start(bf16[4,256,384]{2,1,0:T(8,128)(2,1)} %broadcast_in_dim.21), calls=%async_computation.1 | async-start | bytes 1572864 | tf_op jit(solution)/shard_map/all_to_all | solution.py:22
  20.3 12.9 %all-to-all-done.1 = bf16[4,256,384]{2,1,0:T(8,128)(2,1)S(1)} async-done(((bf16[4,256,384]{2,1,0:T(8,128)(2,1)}), bf16[4,256,384]{2,1,0:T(8,128)(2,1)S(1)}, u32[]{:S(2)}, u32[]{:S(2)}) %all-to-all-start.1) | async-done | bytes 786464 | tf_op jit(solution)/shard_map/all_to_all | solution.py:22
  33.2 0.9 pad_maximum_fusion
  35.2 8.5 %all-to-all-start.2 = ((bf16[16,32,512]{2,1,0:T(8,128)(2,1)}), bf16[16,32,512]{2,1,0:T(8,128)(2,1)S(1)}, u32[]{:S(2)}, u32[]{:S(2)}) async-start(bf16[16,32,512]{2,1,0:T(8,128)(2,1)} %broadcast_in_dim.22), calls=%async_computation.2 | async-start | bytes 1048576 | tf_op jit(solution)/shard_map/all_to_all | solution.py:22
  43.8 15.6 %all-gather.3.cloned.1.call-done = bf16[2048,512]{1,0:T(8,128)(2,1)} async-done(((bf16[256,512]{1,0:T(8,128)(2,1)}), bf16[2048,512]{1,0:T(8,128)(2,1)}) %all-gather.3.cloned.1.call-update) | async-done | bytes 2097168 | tf_op jit(solution)/shard_map/all_gather | solution.py:59
  59.3 1.1 slice.123
  60.9 1.6 broadcast_in_dim.20
  62.5 7.4 %all-to-all-start = ((bf16[4,2048,128]{2,1,0:T(8,128)(2,1)}), bf16[4,2048,128]{2,1,0:T(8,128)(2,1)S(1)}, u32[]{:S(2)}, u32[]{:S(2)}) async-start(bf16[4,2048,128]{2,1,0:T(8,128)(2,1)} %broadcast_in_dim.20), calls=%async_computation | async-start | bytes 4194304 | tf_op jit(solution)/shard_map/all_to_all | solution.py:22
  70.8 3.8 constant_dynamic-update-slice_fusion.1
  75.5 39.2 %all-to-all-done = bf16[4,2048,128]{2,1,0:T(8,128)(2,1)S(1)} async-done(((bf16[4,2048,128]{2,1,0:T(8,128)(2,1)}), bf16[4,2048,128]{2,1,0:T(8,128)(2,1)S(1)}, u32[]{:S(2)}, u32[]{:S(2)}) %all-to-all-start) | async-done | bytes 2097184 | tf_op jit(solution)/shard_map/all_to_all | solution.py:22
  114.8 3.2 fusion.62
  117.9 5.3 %all-gather.5.cloned.1.call-done = bf16[3,2048,384]{2,1,0:T(8,128)(2,1)} async-done(((bf16[3,256,384]{2,1,0:T(8,128)(2,1)}), bf16[3,2048,384]{2,1,0:T(8,128)(2,1)}) %all-gather.5.cloned.1.call-update) | async-done | bytes 4718608 | tf_op jit(solution)/shard_map/all_gather | solution.py:61
  123.3 2.8 fusion.2
  126.1 2.9 fusion.7
  129.0 2.1 fusion.10
  131.2 2.1 fusion.11
  134.3 1.1 broadcast_in_dim.23
  135.4 9.4 %all-to-all-start.3 = ((bf16[32,32,512]{2,1,0:T(8,128)(2,1)}), bf16[32,32,512]{2,1,0:T(8,128)(2,1)}, u32[]{:S(2)}, u32[]{:S(2)}) async-start(bf16[32,32,512]{2,1,0:T(8,128)(2,1)} %broadcast_in_dim.23), calls=%async_computation.3 | async-start | bytes 2097152 | tf_op jit(solution)/shard_map/all_to_all | solution.py:22
  144.8 25.6 %all-to-all-done.3 = bf16[32,32,512]{2,1,0:T(8,128)(2,1)} async-done(((bf16[32,32,512]{2,1,0:T(8,128)(2,1)}), bf16[32,32,512]{2,1,0:T(8,128)(2,1)}, u32[]{:S(2)}, u32[]{:S(2)}) %all-to-all-start.3) | async-done | bytes 1048608 | tf_op jit(solution)/shard_map/all_to_all | solution.py:22
  170.4 1.9 fusion.61
  172.3 1.3 convolution_subtract_fusion
  173.6 5.1 %all_to_all.80 = f32[2,96,1024]{2,1,0:T(8,128)} all-to-all(f32[2,96,1024]{2,1,0:T(8,128)S(1)} %bitcast.91), channel_id=1, replica_groups=mesh['line'=4,'ring'=8,'chip'=8,'core'=2] {'core'}, dimensions={0} | all-to-all | bytes 1572864 | tf_op jit(solution)/shard_map/all_to_all | solution.py:26
  178.7 2.0 reduce_sum.63
  180.7 1.1 copy.22
  181.8 23.6 %all_to_all.81 = f32[8,96,128]{2,1,0:T(8,128)} all-to-all(f32[8,96,128]{2,1,0:T(8,128)S(1)} %copy.16), channel_id=1, replica_groups=mesh['line'=4,'ring'=8,'chip'=8,'core'=2] {'chip'}, dimensions={0} | all-to-all | bytes 786432 | tf_op jit(solution)/shard_map/all_to_all | solution.py:26
  205.4 1.0 reduce_sum.64
  206.5 16.0 %all_to_all.82 = f32[8,96,128]{2,1,0:T(8,128)S(1)} all-to-all(f32[8,96,128]{2,1,0:T(8,128)S(1)} %broadcast_in_dim.24), channel_id=1, replica_groups=mesh['line'=4,'ring'=8,'chip'=8,'core'=2] {'chip'}, dimensions={0} | all-to-all | bytes 786432 | tf_op jit(solution)/shard_map/all_to_all | solution.py:22
  222.6 4.4 %all_to_all.83 = f32[2,96,1024]{2,1,0:T(8,128)S(1)} all-to-all(f32[2,96,1024]{2,1,0:T(8,128)S(1)} %broadcast_in_dim.26), channel_id=1, replica_groups=mesh['line'=4,'ring'=8,'chip'=8,'core'=2] {'core'}, dimensions={0} | all-to-all | bytes 1572864 | tf_op jit(solution)/shard_map/all_to_all | solution.py:22
  227.8 1.5 convolution_convert_fusion
  229.4 7.1 %all-to-all-start.8 = ((bf16[32,32,512]{2,1,0:T(8,128)(2,1)}), bf16[32,32,512]{2,1,0:T(8,128)(2,1)}, u32[]{:S(2)}, u32[]{:S(2)}) async-start(bf16[32,32,512]{2,1,0:T(8,128)(2,1)} %bitcast.100), calls=%async_computation.8 | async-start | bytes 2097152 | tf_op jit(solution)/shard_map/all_to_all | solution.py:26
  236.5 0.9 slice.125
  237.5 1.0 slice.127
  238.6 1.2 convert_element_type.77
  239.7 1.7 fusion.12
  241.4 21.9 %all-to-all-done.8 = bf16[32,32,512]{2,1,0:T(8,128)(2,1)} async-done(((bf16[32,32,512]{2,1,0:T(8,128)(2,1)}), bf16[32,32,512]{2,1,0:T(8,128)(2,1)}, u32[]{:S(2)}, u32[]{:S(2)}) %all-to-all-start.8) | async-done | bytes 1048608 | tf_op jit(solution)/shard_map/all_to_all | solution.py:26
  263.4 1.4 convert_reduce_fusion
  264.8 0.9 multiply_convert_fusion.1
  266.2 17.4 %all_to_all.84 = bf16[16,16,448]{2,1,0:T(8,128)(2,1)S(1)} all-to-all(bf16[16,16,448]{2,1,0:T(8,128)(2,1)S(1)} %bitcast.101), channel_id=1, replica_groups=mesh['line'=4,'ring'=8,'chip'=8,'core'=2] {'chip','core'}, dimensions={0} | all-to-all | bytes 458752 | tf_op jit(solution)/shard_map/all_to_all | solution.py:26
  283.6 16.0 %all_to_all.85 = bf16[16,16,448]{2,1,0:T(8,128)(2,1)S(1)} all-to-all(bf16[16,16,448]{2,1,0:T(8,128)(2,1)S(1)} %broadcast_in_dim.27), channel_id=1, replica_groups=mesh['line'=4,'ring'=8,'chip'=8,'core'=2] {'chip','core'}, dimensions={0} | all-to-all | bytes 458752 | tf_op jit(solution)/shard_map/all_to_all | solution.py:22
  300.1 17.9 %all_to_all.86 = bf16[32,8,512]{2,1,0:T(8,128)(2,1)S(1)} all-to-all(bf16[32,8,512]{2,1,0:T(8,128)(2,1)S(1)} %fusion.14), channel_id=1, replica_groups=mesh['line'=4,'ring'=8,'chip'=8,'core'=2] {'line','ring'}, dimensions={0} | all-to-all | bytes 524288 | tf_op jit(solution)/shard_map/all_to_all | solution.py:26
  318.8 16.6 %all_to_all.87 = bf16[32,8,512]{2,1,0:T(8,128)(2,1)S(1)} all-to-all(bf16[32,8,512]{2,1,0:T(8,128)(2,1)S(1)} %broadcast_in_dim.28), channel_id=1, replica_groups=mesh['line'=4,'ring'=8,'chip'=8,'core'=2] {'line','ring'}, dimensions={0} | all-to-all | bytes 524288 | tf_op jit(solution)/shard_map/all_to_all | solution.py:22
  335.8 17.5 %all_to_all.88 = bf16[16,16,448]{2,1,0:T(8,128)(2,1)S(1)} all-to-all(bf16[16,16,448]{2,1,0:T(8,128)(2,1)S(1)} %bitcast.102), channel_id=1, replica_groups=mesh['line'=4,'ring'=8,'chip'=8,'core'=2] {'chip','core'}, dimensions={0} | all-to-all | bytes 458752 | tf_op jit(solution)/shard_map/all_to_all | solution.py:26
  353.4 15.9 %all_to_all.89 = bf16[16,16,448]{2,1,0:T(8,128)(2,1)S(1)} all-to-all(bf16[16,16,448]{2,1,0:T(8,128)(2,1)S(1)} %broadcast_in_dim.29), channel_id=1, replica_groups=mesh['line'=4,'ring'=8,'chip'=8,'core'=2] {'chip','core'}, dimensions={0} | all-to-all | bytes 458752 | tf_op jit(solution)/shard_map/all_to_all | solution.py:22
  369.8 16.1 %all_to_all.90 = bf16[32,8,512]{2,1,0:T(8,128)(2,1)S(1)} all-to-all(bf16[32,8,512]{2,1,0:T(8,128)(2,1)S(1)} %fusion.13), channel_id=1, replica_groups=mesh['line'=4,'ring'=8,'chip'=8,'core'=2] {'line','ring'}, dimensions={0} | all-to-all | bytes 524288 | tf_op jit(solution)/shard_map/all_to_all | solution.py:26
  385.9 1.3 multiply_subtract_fusion
  (62 shorter events, 9.3 us)
Async XLA Ops:
  7.2 27.0 %copy-start = (bf16[512,1024]{1,0:T(8,128)(2,1)S(1)}, bf16[512,1024]{1,0:T(8,128)(2,1)}, u32[]{:S(2)}) copy-start(bf16[512,1024]{1,0:T(8,128)(2,1)} %param.7) | copy-start | bytes 3145732
  7.2 52.2 %all-gather.3.cloned.1.call-start = ((), (), s32[]{:S(2)}) async-start(), calls=%async_computation.16 | async-start | bytes 2359296 | tf_op jit(solution)/shard_map/all_gather | solution.py:59
  11.0 22.2 %all-to-all-start.1 = ((bf16[4,256,384]{2,1,0:T(8,128)(2,1)}), bf16[4,256,384]{2,1,0:T(8,128)(2,1)S(1)}, u32[]{:S(2)}, u32[]{:S(2)}) async-start(bf16[4,256,384]{2,1,0:T(8,128)(2,1)} %broadcast_in_dim.21), calls=%async_computation.1 | async-start | bytes 1572864 | tf_op jit(solution)/shard_map/all_to_all | solution.py:22
  20.3 103.0 %all-gather.5.cloned.1.call-start = ((), (), s32[]{:S(2)}) async-start(), calls=%async_computation.17 | async-start | bytes 5308416 | tf_op jit(solution)/shard_map/all_gather | solution.py:61
  35.2 25.7 %all-to-all-start.2 = ((bf16[16,32,512]{2,1,0:T(8,128)(2,1)}), bf16[16,32,512]{2,1,0:T(8,128)(2,1)S(1)}, u32[]{:S(2)}, u32[]{:S(2)}) async-start(bf16[16,32,512]{2,1,0:T(8,128)(2,1)} %broadcast_in_dim.22), calls=%async_computation.2 | async-start | bytes 1048576 | tf_op jit(solution)/shard_map/all_to_all | solution.py:22
  60.9 1.6 copy-start.3
  62.5 52.2 %all-to-all-start = ((bf16[4,2048,128]{2,1,0:T(8,128)(2,1)}), bf16[4,2048,128]{2,1,0:T(8,128)(2,1)S(1)}, u32[]{:S(2)}, u32[]{:S(2)}) async-start(bf16[4,2048,128]{2,1,0:T(8,128)(2,1)} %broadcast_in_dim.20), calls=%async_computation | async-start | bytes 4194304 | tf_op jit(solution)/shard_map/all_to_all | solution.py:22
  69.9 4.7 %copy-start.4 = (bf16[16,32,512]{2,1,0:T(8,128)(2,1)S(1)}, bf16[16,32,512]{2,1,0:T(8,128)(2,1)}, u32[]{:S(2)}) copy-start(bf16[16,32,512]{2,1,0:T(8,128)(2,1)} %copy-done.3) | copy-start | bytes 1572868
  123.3 2.8 copy-start.7
  123.3 5.7 %slice-start = ((s8[4718592]{0:T(1024)(128)(4,1)}), s8[4194304]{0:T(1024)(128)(4,1)S(1)}, s32[]{:S(2)}) async-start(s8[4718592]{0:T(1024)(128)(4,1)} %bitcast.107), calls=%async_computation.18 | async-start | bytes 8388608
  126.1 3.0 slice-start.1
  131.2 13.6 %copy-start.8 = (s32[192]{0:T(256)S(1)}, s32[192]{0:T(256)}, u32[]{:S(2)}) copy-start(s32[192]{0:T(256)} %param.8) | copy-start | bytes 2308
  133.4 0.8 copy-start.5
  135.4 35.0 %all-to-all-start.3 = ((bf16[32,32,512]{2,1,0:T(8,128)(2,1)}), bf16[32,32,512]{2,1,0:T(8,128)(2,1)}, u32[]{:S(2)}, u32[]{:S(2)}) async-start(bf16[32,32,512]{2,1,0:T(8,128)(2,1)} %broadcast_in_dim.23), calls=%async_computation.3 | async-start | bytes 2097152 | tf_op jit(solution)/shard_map/all_to_all | solution.py:22
  206.4 21.4 %copy-start.6 = (f32[224,512]{1,0:T(8,128)S(1)}, f32[224,512]{1,0:T(8,128)}, u32[]{:S(2)}) copy-start(f32[224,512]{1,0:T(8,128)} %copy-done.5) | copy-start | bytes 1376260
  227.0 0.9 copy-start.1
  229.4 34.0 %all-to-all-start.8 = ((bf16[32,32,512]{2,1,0:T(8,128)(2,1)}), bf16[32,32,512]{2,1,0:T(8,128)(2,1)}, u32[]{:S(2)}, u32[]{:S(2)}) async-start(bf16[32,32,512]{2,1,0:T(8,128)(2,1)} %bitcast.100), calls=%async_computation.8 | async-start | bytes 2097152 | tf_op jit(solution)/shard_map/all_to_all | solution.py:26
  318.7 68.5 %copy-start.2 = (f32[2,96,1024]{2,1,0:T(8,128)S(1)}, f32[2,96,1024]{2,1,0:T(8,128)}, u32[]{:S(2)}) copy-start(f32[2,96,1024]{2,1,0:T(8,128)} %copy-done.1) | copy-start | bytes 2359300
Sparse Core Ops, SparseCore 0:
  10.1 49.2 all-gather.2
  62.0 61.2 all-gather.4

commit v5 on v4

--- a/solution.py
+++ b/solution.py
@@ -48,30 +48,37 @@
     return sum_blocks(partial.reshape(parts, -1, partial.shape[1]), TOK)
 
 
-def times_rotation(lhs, rot_b, line_wide, line_pos):
-    rows, narrow = rot_b.shape
-    wide = narrow - THIN
-    span = RING * rows
+def gather_rotation(rot_b, line_wide, line_pos):
+    near = lax.all_gather(rot_b, "ring", axis=0, tiled=True)
+    others = jnp.stack([pick_other(k, line_wide, line_pos) for k in range(LINE - 1)])
+    far = lax.all_gather(others, "ring", axis=1, tiled=True)
+    thin = gather_blocks(near[:, :THIN], "line").reshape(LINE * near.shape[0], THIN)
+    return thin, near, far
 
-    def other(k, blocks):
-        return jnp.where(line_pos > k, blocks[k], blocks[k + 1])
 
-    near = lax.all_gather(rot_b, "ring", axis=0, tiled=True)
-    others = jnp.stack([other(k, line_wide) for k in range(LINE - 1)])
-    far = lax.all_gather(others, "ring", axis=1, tiled=True)
-    thin = gather_blocks(near[:, :THIN], "line")
+def pick_other(k, blocks, line_pos):
+    return jnp.where(line_pos > k, blocks[k], blocks[k + 1])
 
+
+def times_rotation(lhs, thin, near, far, line_pos):
+    span = near.shape[0]
     spans = [lhs[:, k * span : (k + 1) * span] for k in range(LINE)]
     lhs_near = spans[LINE - 1]
     for k in range(LINE - 1):
         lhs_near = jnp.where(line_pos == k, spans[k], lhs_near)
-    total_thin = jnp.dot(lhs, thin.reshape(LINE * span, THIN), preferred_element_type=jnp.float32)
+    total_thin = jnp.dot(lhs, thin, preferred_element_type=jnp.float32)
     total = jnp.dot(lhs_near, near[:, THIN:], preferred_element_type=jnp.float32)
     for k in range(LINE - 1):
-        total = total + jnp.dot(other(k, spans), far[k], preferred_element_type=jnp.float32)
+        total = total + jnp.dot(
+            pick_other(k, spans, line_pos), far[k], preferred_element_type=jnp.float32
+        )
+    return jnp.concatenate([total_thin, total], 1)
 
+
+def first_rows(thin, near, far, rows, line_pos):
+    narrow = near.shape[1]
     first_near = near.reshape(RING, rows, narrow)[:, : 2 * WIN]
-    first_far = far.reshape(LINE - 1, RING, rows, wide)[:, :, : 2 * WIN]
+    first_far = far.reshape(LINE - 1, RING, rows, narrow - THIN)[:, :, : 2 * WIN]
     first_near, first_far = lax.optimization_barrier((first_near, first_far))
     first_near, first_far = first_near[:, :WIN, THIN:], first_far[:, :, :WIN]
     first = [
@@ -83,8 +90,7 @@
         for k in range(LINE)
     ]
     first_thin = thin.reshape(LINE, RING, rows, THIN)[:, :, :WIN]
-    first = jnp.concatenate([first_thin, jnp.stack(first)], 3).reshape(LINE * RING * WIN, narrow)
-    return jnp.concatenate([total_thin, total], 1), first
+    return jnp.concatenate([first_thin, jnp.stack(first)], 3).reshape(LINE * RING * WIN, narrow)
 
 
 def local(activations, rotation, value_weight, token_code, channel_code):
@@ -103,45 +109,51 @@
     value_late, line_wide = lax.optimization_barrier((value_weight, line_wide))
     own_cols = lax.dynamic_slice_in_dim(value_late, tok_pos * chan_share, chan_share, 1)
     weight_rows = gather_blocks(own_cols.T, MDL).transpose(1, 0, 2).reshape(chan_share, model_width)
-    lhs = jnp.concatenate([activations, weight_rows], 0)
-    products, window = times_rotation(lhs, rot_b, line_wide, lax.axis_index("line"))
-    products = products / width_root
-    rotated, turned = products[:tok_rows], products[tok_rows:]
+    line_pos = lax.axis_index("line")
+    panel = gather_rotation(rot_b, line_wide, line_pos)
     own_feats = lax.dynamic_slice_in_dim(activations, mdl_pos * narrow, narrow, 1)
     plain = jnp.dot(own_feats, value_weight, preferred_element_type=jnp.float32)
 
+    turned = times_rotation(weight_rows, *panel, line_pos) / width_root
     own_codes = lax.dynamic_slice_in_dim(channel_code, tok_pos * chan_share, chan_share, 0)
     weight_clip = own_codes.astype(jnp.float32)[:, None] / (4.0 * width_root)
     weight_tanh = jnp.tanh(turned / weight_clip)
     quant_weight = (weight_clip * weight_tanh).astype(jnp.bfloat16)
-    weight_full = gather_blocks(quant_weight, TOK).reshape(channels, narrow)
-
+    late_panel, quant_late = lax.optimization_barrier((panel, quant_weight))
+    weight_full = gather_blocks(quant_late, TOK).reshape(channels, narrow)
+    rotated = times_rotation(activations, *late_panel, line_pos) / width_root
+    window = first_rows(*late_panel, rotation.shape[0], line_pos)
     act_clip = token_code.astype(jnp.float32)[:, None] * 0.5
     act_tanh = jnp.tanh(rotated / act_clip)
     quant_act = (act_clip * act_tanh).astype(jnp.bfloat16)
-    partial_err = (
-        jnp.einsum("td,cd->tc", quant_act, weight_full, preferred_element_type=jnp.float32) - plain
+    half = channels // 2
+    weight_halves = [weight_full[:half], weight_full[half:]]
+    partial_err = jnp.stack(
+        [
+            jnp.einsum("td,cd->tc", quant_act, weight_half, preferred_element_type=jnp.float32)
+            - plain_half
+            for weight_half, plain_half in zip(weight_halves, (plain[:, :half], plain[:, half:]))
+        ]
     )
-    half = tok_rows // 2
     chips = lax.axis_size("chip")
-    core_err = sum_blocks(partial_err.reshape(2, half, channels), "core")
-    core_err = core_err.reshape(half, chips, channels // chips).transpose(1, 0, 2)
-    own_err = sum_blocks(core_err, "chip")
-    core_err = gather_blocks(own_err, "chip").transpose(1, 0, 2).reshape(half, channels)
-    recon_error = gather_blocks(core_err, "core").reshape(tok_rows, channels)
-    error_bf = recon_error.astype(jnp.bfloat16)
+    core_err = sum_blocks(partial_err, "core").reshape(chips, tok_rows // chips, half)
+    core_err = gather_blocks(sum_blocks(core_err, "chip"), "chip").reshape(tok_rows, half)
+    err_halves = gather_blocks(core_err, "core")
+    recon_error = err_halves.transpose(1, 0, 2).reshape(tok_rows, channels)
+    err_bf = err_halves.astype(jnp.bfloat16)
     grad_quant = sum_blocks(
-        jnp.einsum("tc,td->cd", error_bf, quant_act, preferred_element_type=jnp.float32)
+        jnp.einsum("htc,td->hcd", err_bf, quant_act, preferred_element_type=jnp.float32)
         .astype(jnp.bfloat16)
         .reshape(n_tok, chan_share, narrow),
         TOK,
     )
-    grad_act = (
-        jnp.dot(error_bf, weight_full, preferred_element_type=jnp.float32)
-        * (1.0 - act_tanh * act_tanh)
-    ).astype(jnp.bfloat16)
+    grad_act = sum(
+        jnp.dot(err_half, weight_half, preferred_element_type=jnp.float32)
+        for err_half, weight_half in zip(err_bf, weight_halves)
+    )
+    grad_act = (grad_act * (1.0 - act_tanh * act_tanh)).astype(jnp.bfloat16)
     grad_turned = (grad_quant * (1.0 - weight_tanh * weight_tanh)).astype(jnp.bfloat16)
-    stack_a = products.astype(jnp.bfloat16)
+    stack_a = jnp.concatenate([rotated.astype(jnp.bfloat16), turned.astype(jnp.bfloat16)], 0)
     stack_g = jnp.concatenate([grad_act, grad_turned], 0)
     step_size = STEP_GAIN / math.sqrt(tok_rows * n_tok * channels)
     own_rows = rotation[:WIN]

time: 397 us -> 390 us (0.982)
  blocking collectives: 166 us -> 151 us
  waiting for transfers between devices: 121 us -> 127 us
    all_to_all x6 -> x5, blocking collectives: 97.5 us -> 81.9 us  [sum_blocks(): return jnp.sum(lax.all_to_all(blocks, axis, 0, 0).astype(jnp.float32), 0)]
    all_to_all x1 -> x2, waiting for transfers between devices: 21.9 us -> 33.6 us  [sum_blocks(): return jnp.sum(lax.all_to_all(blocks, axis, 0, 0).astype(jnp.float32), 0)]
    all_to_all x4, waiting for transfers between devices: 78.2 us -> 70.7 us  [gather_blocks(): lax.all_to_all(jnp.broadcast_to(own[None], (parts,) + own.shape), axis, 0...]
    unnamed x25 -> x54, local copies, waits for them, and re-layouts: 7.51 us -> 2.05 us
    all_to_all x1 -> x2, starting transfers between devices: 7.13 us -> 11.8 us  [sum_blocks(): return jnp.sum(lax.all_to_all(blocks, axis, 0, 0).astype(jnp.float32), 0)]
    dot_general x7 -> x13, matrix products: 15.3 us -> 17.8 us  [the longest x6 12.4 us: times_rotation(): jnp.dot(pick_other(k, spans, line_pos), far[k], preferred_element_type=jn...]
  transfers between devices with their start and end apart: 7 -> 8, of which waited for: 7 -> 8; matrix products, arithmetic and copies ran while one was open for 5% -> 7% of each run, Pallas kernels for 0% -> 0%
where the time goes in v5:
time: 390 us; the launch traced here: 388 us
  blocking collectives  151 us (39%)
  waiting for transfers between devices  127 us (33%)
  starting transfers between devices  44.8 us (11%)
  matrix products  23.3 us (6%)
  local copies, waits for them, and re-layouts  16.4 us (4%)
  between operations  14.6 us (4%)
  other arithmetic  11.8 us (3%)
    all_to_all x5, blocking collectives, sum_blocks(): return jnp.sum(lax.all_to_all(blocks, axis, 0, 0).astype(jnp.float32), 0)  81.9 us
    all_to_all x4, waiting for transfers between devices, gather_blocks(): lax.all_to_all(jnp.broadcast_to(own[None], (parts,) + own.shape), axis, 0...  70.7 us
    all_to_all x5, blocking collectives, gather_blocks(): lax.all_to_all(jnp.broadcast_to(own[None], (parts,) + own.shape), axis, 0...  68.6 us
    all_to_all x2, waiting for transfers between devices, sum_blocks(): return jnp.sum(lax.all_to_all(blocks, axis, 0, 0).astype(jnp.float32), 0)  33.6 us
    all_to_all x4, starting transfers between devices, gather_blocks(): lax.all_to_all(jnp.broadcast_to(own[None], (parts,) + own.shape), axis, 0...  33 us
    all_gather x1, waiting for transfers between devices, gather_rotation(): near = lax.all_gather(rot_b, 'ring', axis=0, tiled=True)  15.6 us
    dot_general x6, matrix products, times_rotation(): jnp.dot(pick_other(k, spans, line_pos), far[k], preferred_element_type=jn...  12.4 us
    all_to_all x2, starting transfers between devices, sum_blocks(): return jnp.sum(lax.all_to_all(blocks, axis, 0, 0).astype(jnp.float32), 0)  11.8 us
  transfers between devices with their start and end apart: 8, of which 8 were waited for; matrix products, arithmetic and copies ran while one was open for 7% of the time, Pallas kernels for 0%

profile of v5, /device:TPU:8, one launch (start us, length us, event | category | flops | bytes accessed | tf_op | source)
XLA Modules:
  0.0 388.2 jit_solution(12912183938492603984)
XLA Ops:
  7.2 1.9 convert_element_type.69
  9.1 0.9 slice.172
  10.1 0.9 broadcast_in_dim.21
  11.0 9.3 %all-to-all-start.1 = ((bf16[4,256,384]{2,1,0:T(8,128)(2,1)}), bf16[4,256,384]{2,1,0:T(8,128)(2,1)S(1)}, u32[]{:S(2)}, u32[]{:S(2)}) async-start(bf16[4,256,384]{2,1,0:T(8,128)(2,1)} %broadcast_in_dim.21), calls=%async_computation.1 | async-start | bytes 1572864 | tf_op jit(solution)/shard_map/all_to_all | solution.py:22
  20.3 12.9 %all-to-all-done.1 = bf16[4,256,384]{2,1,0:T(8,128)(2,1)S(1)} async-done(((bf16[4,256,384]{2,1,0:T(8,128)(2,1)}), bf16[4,256,384]{2,1,0:T(8,128)(2,1)S(1)}, u32[]{:S(2)}, u32[]{:S(2)}) %all-to-all-start.1) | async-done | bytes 786464 | tf_op jit(solution)/shard_map/all_to_all | solution.py:22
  35.2 8.5 %all-to-all-start.2 = ((bf16[16,32,512]{2,1,0:T(8,128)(2,1)}), bf16[16,32,512]{2,1,0:T(8,128)(2,1)S(1)}, u32[]{:S(2)}, u32[]{:S(2)}) async-start(bf16[16,32,512]{2,1,0:T(8,128)(2,1)} %broadcast_in_dim.22), calls=%async_computation.2 | async-start | bytes 1048576 | tf_op jit(solution)/shard_map/all_to_all | solution.py:22
  43.8 15.6 %all-gather.3.cloned.1.call-done = bf16[2048,512]{1,0:T(8,128)(2,1)} async-done(((bf16[256,512]{1,0:T(8,128)(2,1)}), bf16[2048,512]{1,0:T(8,128)(2,1)}) %all-gather.3.cloned.1.call-update) | async-done | bytes 2097168 | tf_op jit(solution)/shard_map/all_gather | solution.py:52
  59.3 1.1 slice.171
  60.9 1.6 broadcast_in_dim.20
  62.6 7.4 %all-to-all-start = ((bf16[4,2048,128]{2,1,0:T(8,128)(2,1)}), bf16[4,2048,128]{2,1,0:T(8,128)(2,1)S(1)}, u32[]{:S(2)}, u32[]{:S(2)}) async-start(bf16[4,2048,128]{2,1,0:T(8,128)(2,1)} %broadcast_in_dim.20), calls=%async_computation | async-start | bytes 4194304 | tf_op jit(solution)/shard_map/all_to_all | solution.py:22
  70.8 1.9 copy.22
  72.6 42.2 %all-to-all-done = bf16[4,2048,128]{2,1,0:T(8,128)(2,1)S(1)} async-done(((bf16[4,2048,128]{2,1,0:T(8,128)(2,1)}), bf16[4,2048,128]{2,1,0:T(8,128)(2,1)S(1)}, u32[]{:S(2)}, u32[]{:S(2)}) %all-to-all-start) | async-done | bytes 2097184 | tf_op jit(solution)/shard_map/all_to_all | solution.py:22
  114.8 1.5 fusion.114
  116.3 7.0 %all-gather.5.cloned.1.call-done = bf16[3,2048,384]{2,1,0:T(8,128)(2,1)} async-done(((bf16[3,256,384]{2,1,0:T(8,128)(2,1)}), bf16[3,2048,384]{2,1,0:T(8,128)(2,1)}) %all-gather.5.cloned.1.call-update) | async-done | bytes 4718608 | tf_op jit(solution)/shard_map/all_gather | solution.py:54
  123.3 1.9 fusion.1
  125.2 2.0 fusion
  127.2 1.7 fusion.2
  130.1 1.2 broadcast_in_dim.23
  131.2 7.8 %all-to-all-start.3 = ((bf16[32,32,512]{2,1,0:T(8,128)(2,1)}), bf16[32,32,512]{2,1,0:T(8,128)(2,1)}, u32[]{:S(2)}, u32[]{:S(2)}) async-start(bf16[32,32,512]{2,1,0:T(8,128)(2,1)} %broadcast_in_dim.23), calls=%async_computation.3 | async-start | bytes 2097152 | tf_op jit(solution)/shard_map/all_to_all | solution.py:22
  139.6 2.2 fusion.68
  141.8 2.6 fusion.7
  144.6 2.1 fusion.9
  147.5 2.0 fusion.28
  149.5 1.0 convolution_bitcast_fusion
  150.5 15.2 %all-to-all-done.3 = bf16[32,32,512]{2,1,0:T(8,128)(2,1)} async-done(((bf16[32,32,512]{2,1,0:T(8,128)(2,1)}), bf16[32,32,512]{2,1,0:T(8,128)(2,1)}, u32[]{:S(2)}, u32[]{:S(2)}) %all-to-all-start.3) | async-done | bytes 1048608 | tf_op jit(solution)/shard_map/all_to_all | solution.py:22
  165.7 1.3 fusion.113
  168.1 5.2 %all_to_all.80 = f32[2,192,512]{2,1,0:T(8,128)} all-to-all(f32[2,192,512]{2,1,0:T(8,128)S(1)} %pad_maximum_fusion), channel_id=1, replica_groups=mesh['line'=4,'ring'=8,'chip'=8,'core'=2] {'core'}, dimensions={0} | all-to-all | bytes 1572864 | tf_op jit(solution)/shard_map/all_to_all | solution.py:26
  173.3 2.0 reduce_sum.63
  175.2 23.6 %all_to_all.81 = f32[8,24,512]{2,1,0:T(8,128)S(1)} all-to-all(f32[8,24,512]{2,1,0:T(8,128)} %bitcast.116), channel_id=1, replica_groups=mesh['line'=4,'ring'=8,'chip'=8,'core'=2] {'chip'}, dimensions={0} | all-to-all | bytes 786432 | tf_op jit(solution)/shard_map/all_to_all | solution.py:26
  200.4 15.9 %all_to_all.82 = f32[8,24,512]{2,1,0:T(8,128)S(1)} all-to-all(f32[8,24,512]{2,1,0:T(8,128)S(1)} %broadcast_in_dim.24), channel_id=1, replica_groups=mesh['line'=4,'ring'=8,'chip'=8,'core'=2] {'chip'}, dimensions={0} | all-to-all | bytes 786432 | tf_op jit(solution)/shard_map/all_to_all | solution.py:22
  216.4 4.5 %all_to_all.83 = f32[2,192,512]{2,1,0:T(8,128)S(1)} all-to-all(f32[2,192,512]{2,1,0:T(8,128)S(1)} %broadcast_in_dim.26), channel_id=1, replica_groups=mesh['line'=4,'ring'=8,'chip'=8,'core'=2] {'core'}, dimensions={0} | all-to-all | bytes 1572864 | tf_op jit(solution)/shard_map/all_to_all | solution.py:22
  221.8 1.6 convolution_convert_fusion
  223.4 7.0 %all-to-all-start.8 = ((bf16[32,32,512]{2,1,0:T(8,128)(2,1)}), bf16[32,32,512]{2,1,0:T(8,128)(2,1)}, u32[]{:S(2)}, u32[]{:S(2)}) async-start(bf16[32,32,512]{2,1,0:T(8,128)(2,1)} %bitcast.122), calls=%async_computation.8 | async-start | bytes 2097152 | tf_op jit(solution)/shard_map/all_to_all | solution.py:26
  230.5 1.1 slice.183
  232.5 1.0 fusion.64
  234.3 23.0 %all-to-all-done.8 = bf16[32,32,512]{2,1,0:T(8,128)(2,1)} async-done(((bf16[32,32,512]{2,1,0:T(8,128)(2,1)}), bf16[32,32,512]{2,1,0:T(8,128)(2,1)}, u32[]{:S(2)}, u32[]{:S(2)}) %all-to-all-start.8) | async-done | bytes 1048608 | tf_op jit(solution)/shard_map/all_to_all | solution.py:26
  257.3 1.4 convert_reduce_fusion
  259.2 17.4 %all_to_all.84 = bf16[16,16,448]{2,1,0:T(8,128)(2,1)S(1)} all-to-all(bf16[16,16,448]{2,1,0:T(8,128)(2,1)S(1)} %bitcast.123), channel_id=1, replica_groups=mesh['line'=4,'ring'=8,'chip'=8,'core'=2] {'chip','core'}, dimensions={0} | all-to-all | bytes 458752 | tf_op jit(solution)/shard_map/all_to_all | solution.py:26
  276.7 16.0 %all_to_all.85 = bf16[16,16,448]{2,1,0:T(8,128)(2,1)S(1)} all-to-all(bf16[16,16,448]{2,1,0:T(8,128)(2,1)S(1)} %broadcast_in_dim.27), channel_id=1, replica_groups=mesh['line'=4,'ring'=8,'chip'=8,'core'=2] {'chip','core'}, dimensions={0} | all-to-all | bytes 458752 | tf_op jit(solution)/shard_map/all_to_all | solution.py:22
  293.2 17.9 %all_to_all.86 = bf16[32,8,512]{2,1,0:T(8,128)(2,1)S(1)} all-to-all(bf16[32,8,512]{2,1,0:T(8,128)(2,1)S(1)} %fusion.32), channel_id=1, replica_groups=mesh['line'=4,'ring'=8,'chip'=8,'core'=2] {'line','ring'}, dimensions={0} | all-to-all | bytes 524288 | tf_op jit(solution)/shard_map/all_to_all | solution.py:26
  311.8 16.3 %all_to_all.87 = bf16[32,8,512]{2,1,0:T(8,128)(2,1)S(1)} all-to-all(bf16[32,8,512]{2,1,0:T(8,128)(2,1)S(1)} %broadcast_in_dim.28), channel_id=1, replica_groups=mesh['line'=4,'ring'=8,'chip'=8,'core'=2] {'line','ring'}, dimensions={0} | all-to-all | bytes 524288 | tf_op jit(solution)/shard_map/all_to_all | solution.py:22
  328.6 17.9 %all_to_all.88 = bf16[16,16,448]{2,1,0:T(8,128)(2,1)S(1)} all-to-all(bf16[16,16,448]{2,1,0:T(8,128)(2,1)S(1)} %bitcast.124), channel_id=1, replica_groups=mesh['line'=4,'ring'=8,'chip'=8,'core'=2] {'chip','core'}, dimensions={0} | all-to-all | bytes 458752 | tf_op jit(solution)/shard_map/all_to_all | solution.py:26
  346.6 15.9 %all_to_all.89 = bf16[16,16,448]{2,1,0:T(8,128)(2,1)S(1)} all-to-all(bf16[16,16,448]{2,1,0:T(8,128)(2,1)S(1)} %broadcast_in_dim.29), channel_id=1, replica_groups=mesh['line'=4,'ring'=8,'chip'=8,'core'=2] {'chip','core'}, dimensions={0} | all-to-all | bytes 458752 | tf_op jit(solution)/shard_map/all_to_all | solution.py:22
  362.7 1.0 fusion.31
  363.7 4.8 %all-to-all-start.15 = ((bf16[32,8,512]{2,1,0:T(8,128)(2,1)}), bf16[32,8,512]{2,1,0:T(8,128)(2,1)S(1)}, u32[]{:S(2)}, u32[]{:S(2)}) async-start(bf16[32,8,512]{2,1,0:T(8,128)(2,1)} %fusion.31), calls=%async_computation.15 | async-start | bytes 524288 | tf_op jit(solution)/shard_map/all_to_all | solution.py:26
  368.5 0.9 copy.23
  369.5 10.5 %all-to-all-done.15 = bf16[32,8,512]{2,1,0:T(8,128)(2,1)S(1)} async-done(((bf16[32,8,512]{2,1,0:T(8,128)(2,1)}), bf16[32,8,512]{2,1,0:T(8,128)(2,1)S(1)}, u32[]{:S(2)}, u32[]{:S(2)}) %all-to-all-start.15) | async-done | bytes 262176 | tf_op jit(solution)/shard_map/all_to_all | solution.py:26
  380.1 1.3 multiply_subtract_fusion
  (98 shorter events, 13.7 us)
Async XLA Ops:
  7.2 27.0 %copy-start = (bf16[512,1024]{1,0:T(8,128)(2,1)S(1)}, bf16[512,1024]{1,0:T(8,128)(2,1)}, u32[]{:S(2)}) copy-start(bf16[512,1024]{1,0:T(8,128)(2,1)} %param.7) | copy-start | bytes 3145732
  7.2 52.2 %all-gather.3.cloned.1.call-start = ((), (), s32[]{:S(2)}) async-start(), calls=%async_computation.16 | async-start | bytes 2359296 | tf_op jit(solution)/shard_map/all_gather | solution.py:52
  11.0 22.2 %all-to-all-start.1 = ((bf16[4,256,384]{2,1,0:T(8,128)(2,1)}), bf16[4,256,384]{2,1,0:T(8,128)(2,1)S(1)}, u32[]{:S(2)}, u32[]{:S(2)}) async-start(bf16[4,256,384]{2,1,0:T(8,128)(2,1)} %broadcast_in_dim.21), calls=%async_computation.1 | async-start | bytes 1572864 | tf_op jit(solution)/shard_map/all_to_all | solution.py:22
  20.3 103.0 %all-gather.5.cloned.1.call-start = ((), (), s32[]{:S(2)}) async-start(), calls=%async_computation.17 | async-start | bytes 5308416 | tf_op jit(solution)/shard_map/all_gather | solution.py:54
  35.2 25.7 %all-to-all-start.2 = ((bf16[16,32,512]{2,1,0:T(8,128)(2,1)}), bf16[16,32,512]{2,1,0:T(8,128)(2,1)S(1)}, u32[]{:S(2)}, u32[]{:S(2)}) async-start(bf16[16,32,512]{2,1,0:T(8,128)(2,1)} %broadcast_in_dim.22), calls=%async_computation.2 | async-start | bytes 1048576 | tf_op jit(solution)/shard_map/all_to_all | solution.py:22
  60.9 1.6 copy-start.5
  62.6 52.2 %all-to-all-start = ((bf16[4,2048,128]{2,1,0:T(8,128)(2,1)}), bf16[4,2048,128]{2,1,0:T(8,128)(2,1)S(1)}, u32[]{:S(2)}, u32[]{:S(2)}) async-start(bf16[4,2048,128]{2,1,0:T(8,128)(2,1)} %broadcast_in_dim.20), calls=%async_computation | async-start | bytes 4194304 | tf_op jit(solution)/shard_map/all_to_all | solution.py:22
  70.7 58.6 %copy-start.21 = (f32[32]{0:T(128)}, f32[32]{0:T(128)S(1)}, u32[]{:S(2)}) copy-start(f32[32]{0:T(128)S(1)} %convert_multiply_fusion.1) | copy-start | bytes 388
  123.3 4.0 %copy-start.4 = (bf16[16,4,8,512]{3,2,0,1:T(8,128)(2,1)S(1)}, bf16[16,4,8,512]{3,2,0,1:T(8,128)(2,1)}, u32[]{:S(2)}) copy-start(bf16[16,4,8,512]{3,2,0,1:T(8,128)(2,1)} %copy.22) | copy-start | bytes 1572868
  125.2 3.8 copy-start.17
  129.3 0.6 copy-start.19
  130.0 9.0 %copy-start.23 = (s32[192]{0:T(256)S(1)}, s32[192]{0:T(256)}, u32[]{:S(2)}) copy-start(s32[192]{0:T(256)} %param.8) | copy-start | bytes 2308
  131.2 34.5 %all-to-all-start.3 = ((bf16[32,32,512]{2,1,0:T(8,128)(2,1)}), bf16[32,32,512]{2,1,0:T(8,128)(2,1)}, u32[]{:S(2)}, u32[]{:S(2)}) async-start(bf16[32,32,512]{2,1,0:T(8,128)(2,1)} %broadcast_in_dim.23), calls=%async_computation.3 | async-start | bytes 2097152 | tf_op jit(solution)/shard_map/all_to_all | solution.py:22
  141.8 2.8 copy-start.3
  144.6 2.2 copy-start.18
  149.5 18.1 %copy-start.14 = (f32[192,384]{1,0:T(8,128)}, f32[192,384]{1,0:T(8,128)S(1)}, u32[]{:S(2)}) copy-start(f32[192,384]{1,0:T(8,128)S(1)} %fusion.28) | copy-start | bytes 884740
  150.5 17.0 %copy-start.9 = (f32[192,128]{1,0:T(8,128)}, f32[192,128]{1,0:T(8,128)S(1)}, u32[]{:S(2)}) copy-start(f32[192,128]{1,0:T(8,128)S(1)} %convolution_bitcast_fusion) | copy-start | bytes 294916
  165.7 1.4 copy-start.8
  165.7 1.4 copy-start.24
  167.1 0.8 copy-start.6
  167.1 1.0 copy-start.12
  216.3 5.5 %copy-start.10 = (f32[192,128]{1,0:T(8,128)S(1)}, f32[192,128]{1,0:T(8,128)}, u32[]{:S(2)}) copy-start(f32[192,128]{1,0:T(8,128)} %copy-done.9) | copy-start | bytes 294916
  216.3 5.5 %copy-start.15 = (f32[192,384]{1,0:T(8,128)S(1)}, f32[192,384]{1,0:T(8,128)}, u32[]{:S(2)}) copy-start(f32[192,384]{1,0:T(8,128)} %copy-done.14) | copy-start | bytes 884740
  216.3 5.6 %copy-start.25 = (f32[192]{0:T(256)S(1)}, f32[192]{0:T(256)}, u32[]{:S(2)}) copy-start(f32[192]{0:T(256)} %convert_multiply_fusion) | copy-start | bytes 2308
  220.9 0.9 copy-start.1
  223.4 33.8 %all-to-all-start.8 = ((bf16[32,32,512]{2,1,0:T(8,128)(2,1)}), bf16[32,32,512]{2,1,0:T(8,128)(2,1)}, u32[]{:S(2)}, u32[]{:S(2)}) async-start(bf16[32,32,512]{2,1,0:T(8,128)(2,1)} %bitcast.122), calls=%async_computation.8 | async-start | bytes 2097152 | tf_op jit(solution)/shard_map/all_to_all | solution.py:26
  230.4 3.2 copy-start.7
  230.4 3.5 copy-start.11
  230.4 3.5 copy-start.13
  230.4 3.5 copy-start.16
  230.5 3.5 copy-start.26
  233.9 24.7 %copy-start.20 = (f32[32,384]{1,0:T(8,128)S(1)}, f32[32,384]{1,0:T(8,128)}, u32[]{:S(2)}) copy-start(f32[32,384]{1,0:T(8,128)} %copy-done.19) | copy-start | bytes 147460
  234.0 24.7 %copy-start.22 = (f32[32]{0:T(128)S(1)}, f32[32]{0:T(128)}, u32[]{:S(2)}) copy-start(f32[32]{0:T(128)} %copy-done.21) | copy-start | bytes 388
  328.6 39.9 %copy-start.2 = (f32[2,192,512]{2,1,0:T(8,128)S(1)}, f32[2,192,512]{2,1,0:T(8,128)}, u32[]{:S(2)}) copy-start(f32[2,192,512]{2,1,0:T(8,128)} %copy-done.1) | copy-start | bytes 2359300
  363.7 16.3 %all-to-all-start.15 = ((bf16[32,8,512]{2,1,0:T(8,128)(2,1)}), bf16[32,8,512]{2,1,0:T(8,128)(2,1)S(1)}, u32[]{:S(2)}, u32[]{:S(2)}) async-start(bf16[32,8,512]{2,1,0:T(8,128)(2,1)} %fusion.31), calls=%async_computation.15 | async-start | bytes 524288 | tf_op jit(solution)/shard_map/all_to_all | solution.py:26
Sparse Core Ops, SparseCore 0:
  10.1 49.2 all-gather.2
  62.0 61.2 all-gather.4

commit v6 on v5

--- a/solution.py
+++ b/solution.py
@@ -127,20 +127,14 @@
     act_tanh = jnp.tanh(rotated / act_clip)
     quant_act = (act_clip * act_tanh).astype(jnp.bfloat16)
     half = channels // 2
-    weight_halves = [weight_full[:half], weight_full[half:]]
-    partial_err = jnp.stack(
-        [
-            jnp.einsum("td,cd->tc", quant_act, weight_half, preferred_element_type=jnp.float32)
-            - plain_half
-            for weight_half, plain_half in zip(weight_halves, (plain[:, :half], plain[:, half:]))
-        ]
+    weight_halves = weight_full.reshape(2, half, narrow)
+    partial_err = (
+        jnp.einsum("td,hcd->htc", quant_act, weight_halves, preferred_element_type=jnp.float32)
+        - plain.reshape(tok_rows, 2, half).transpose(1, 0, 2)
     )
-    chips = lax.axis_size("chip")
-    core_err = sum_blocks(partial_err, "core").reshape(chips, tok_rows // chips, half)
-    core_err = gather_blocks(sum_blocks(core_err, "chip"), "chip").reshape(tok_rows, half)
-    err_halves = gather_blocks(core_err, "core")
-    recon_error = err_halves.transpose(1, 0, 2).reshape(tok_rows, channels)
-    err_bf = err_halves.astype(jnp.bfloat16)
+    own_err = sum_blocks(partial_err.reshape(n_mdl, -1, half), MDL)
+    err_bf = gather_blocks(own_err.astype(jnp.bfloat16), MDL).reshape(2, tok_rows, half)
+    recon_error = err_bf.transpose(1, 0, 2).reshape(tok_rows, channels).astype(jnp.float32)
     grad_quant = sum_blocks(
         jnp.einsum("htc,td->hcd", err_bf, quant_act, preferred_element_type=jnp.float32)
         .astype(jnp.bfloat16)

time: 390 us -> 389 us (level)
    all_to_all x5 -> x4, blocking collectives: 81.9 us -> 85.4 us  [sum_blocks(): return jnp.sum(lax.all_to_all(blocks, axis, 0, 0).astype(jnp.float32), 0)]
    all_to_all x5 -> x4, blocking collectives: 68.6 us -> 67 us  [gather_blocks(): lax.all_to_all(jnp.broadcast_to(own[None], (parts,) + own.shape), axis, 0...]
where the time goes in v6:
time: 389 us; the launch traced here: 387 us
  blocking collectives  152 us (39%)
  waiting for transfers between devices  125 us (32%)
  starting transfers between devices  44.6 us (11%)
  matrix products  25.5 us (7%)
  between operations  14.5 us (4%)
  local copies, waits for them, and re-layouts  14.2 us (4%)
  other arithmetic  10.3 us (3%)
    all_to_all x4, blocking collectives, sum_blocks(): return jnp.sum(lax.all_to_all(blocks, axis, 0, 0).astype(jnp.float32), 0)  85.4 us
    all_to_all x4, waiting for transfers between devices, gather_blocks(): lax.all_to_all(jnp.broadcast_to(own[None], (parts,) + own.shape), axis, 0...  70.7 us
    all_to_all x4, blocking collectives, gather_blocks(): lax.all_to_all(jnp.broadcast_to(own[None], (parts,) + own.shape), axis, 0...  67 us
    all_to_all x4, starting transfers between devices, gather_blocks(): lax.all_to_all(jnp.broadcast_to(own[None], (parts,) + own.shape), axis, 0...  33 us
    all_to_all x2, waiting for transfers between devices, sum_blocks(): return jnp.sum(lax.all_to_all(blocks, axis, 0, 0).astype(jnp.float32), 0)  32.2 us
    all_gather x1, waiting for transfers between devices, gather_rotation(): near = lax.all_gather(rot_b, 'ring', axis=0, tiled=True)  15.6 us
    dot_general x6, matrix products, times_rotation(): jnp.dot(pick_other(k, spans, line_pos), far[k], preferred_element_type=jn...  12.4 us
    all_to_all x2, starting transfers between devices, sum_blocks(): return jnp.sum(lax.all_to_all(blocks, axis, 0, 0).astype(jnp.float32), 0)  11.6 us
  transfers between devices with their start and end apart: 8, of which 8 were waited for; matrix products, arithmetic and copies ran while one was open for 7% of the time, Pallas kernels for 0%

profile of v6, /device:TPU:8, one launch (start us, length us, event | category | flops | bytes accessed | tf_op | source)
XLA Modules:
  0.0 387.0 jit_solution(12239242263457742970)
XLA Ops:
  7.2 1.8 convert_element_type.82
  9.1 0.9 slice.152
  10.0 0.9 broadcast_in_dim.17
  11.0 9.3 %all-to-all-start.1 = ((bf16[4,256,384]{2,1,0:T(8,128)(2,1)}), bf16[4,256,384]{2,1,0:T(8,128)(2,1)S(1)}, u32[]{:S(2)}, u32[]{:S(2)}) async-start(bf16[4,256,384]{2,1,0:T(8,128)(2,1)} %broadcast_in_dim.17), calls=%async_computation.1 | async-start | bytes 1572864 | tf_op jit(solution)/shard_map/all_to_all | solution.py:22
  20.3 12.9 %all-to-all-done.1 = bf16[4,256,384]{2,1,0:T(8,128)(2,1)S(1)} async-done(((bf16[4,256,384]{2,1,0:T(8,128)(2,1)}), bf16[4,256,384]{2,1,0:T(8,128)(2,1)S(1)}, u32[]{:S(2)}, u32[]{:S(2)}) %all-to-all-start.1) | async-done | bytes 786464 | tf_op jit(solution)/shard_map/all_to_all | solution.py:22
  35.2 8.5 %all-to-all-start.2 = ((bf16[16,32,512]{2,1,0:T(8,128)(2,1)}), bf16[16,32,512]{2,1,0:T(8,128)(2,1)S(1)}, u32[]{:S(2)}, u32[]{:S(2)}) async-start(bf16[16,32,512]{2,1,0:T(8,128)(2,1)} %broadcast_in_dim.18), calls=%async_computation.2 | async-start | bytes 1048576 | tf_op jit(solution)/shard_map/all_to_all | solution.py:22
  43.8 15.6 %all-gather.3.cloned.1.call-done = bf16[2048,512]{1,0:T(8,128)(2,1)} async-done(((bf16[256,512]{1,0:T(8,128)(2,1)}), bf16[2048,512]{1,0:T(8,128)(2,1)}) %all-gather.3.cloned.1.call-update) | async-done | bytes 2097168 | tf_op jit(solution)/shard_map/all_gather | solution.py:52
  59.3 1.1 slice.151
  60.9 1.7 broadcast_in_dim.16
  62.6 7.4 %all-to-all-start = ((bf16[4,2048,128]{2,1,0:T(8,128)(2,1)}), bf16[4,2048,128]{2,1,0:T(8,128)(2,1)S(1)}, u32[]{:S(2)}, u32[]{:S(2)}) async-start(bf16[4,2048,128]{2,1,0:T(8,128)(2,1)} %broadcast_in_dim.16), calls=%async_computation | async-start | bytes 4194304 | tf_op jit(solution)/shard_map/all_to_all | solution.py:22
  70.8 1.9 copy.20
  72.6 42.2 %all-to-all-done = bf16[4,2048,128]{2,1,0:T(8,128)(2,1)S(1)} async-done(((bf16[4,2048,128]{2,1,0:T(8,128)(2,1)}), bf16[4,2048,128]{2,1,0:T(8,128)(2,1)S(1)}, u32[]{:S(2)}, u32[]{:S(2)}) %all-to-all-start) | async-done | bytes 2097184 | tf_op jit(solution)/shard_map/all_to_all | solution.py:22
  114.8 1.5 fusion.115
  116.3 7.0 %all-gather.5.cloned.1.call-done = bf16[3,2048,384]{2,1,0:T(8,128)(2,1)} async-done(((bf16[3,256,384]{2,1,0:T(8,128)(2,1)}), bf16[3,2048,384]{2,1,0:T(8,128)(2,1)}) %all-gather.5.cloned.1.call-update) | async-done | bytes 4718608 | tf_op jit(solution)/shard_map/all_gather | solution.py:54
  123.3 1.9 fusion.1
  125.2 2.0 fusion
  127.2 1.7 fusion.2
  130.1 1.1 broadcast_in_dim.19
  131.2 7.8 %all-to-all-start.3 = ((bf16[32,32,512]{2,1,0:T(8,128)(2,1)}), bf16[32,32,512]{2,1,0:T(8,128)(2,1)}, u32[]{:S(2)}, u32[]{:S(2)}) async-start(bf16[32,32,512]{2,1,0:T(8,128)(2,1)} %broadcast_in_dim.19), calls=%async_computation.3 | async-start | bytes 2097152 | tf_op jit(solution)/shard_map/all_to_all | solution.py:22
  139.6 2.2 fusion.66
  141.7 2.6 fusion.7
  144.6 2.1 fusion.9
  147.5 2.0 fusion.27
  149.5 1.0 convolution_bitcast_fusion.1
  150.5 15.2 %all-to-all-done.3 = bf16[32,32,512]{2,1,0:T(8,128)(2,1)} async-done(((bf16[32,32,512]{2,1,0:T(8,128)(2,1)}), bf16[32,32,512]{2,1,0:T(8,128)(2,1)}, u32[]{:S(2)}, u32[]{:S(2)}) %all-to-all-start.3) | async-done | bytes 1048608 | tf_op jit(solution)/shard_map/all_to_all | solution.py:22
  165.7 2.0 fusion.16
  167.7 32.6 %all_to_all.70 = f32[16,24,512]{2,1,0:T(8,128)} all-to-all(f32[16,24,512]{2,1,0:T(8,128)S(1)} %bitcast.136), channel_id=1, replica_groups=mesh['line'=4,'ring'=8,'chip'=8,'core'=2] {'chip','core'}, dimensions={0} | all-to-all | bytes 1572864 | tf_op jit(solution)/shard_map/all_to_all | solution.py:26
  200.3 1.2 reduce_sum.54
  201.5 18.7 %all_to_all.71 = bf16[16,24,512]{2,1,0:T(8,128)(2,1)S(1)} all-to-all(bf16[16,24,512]{2,1,0:T(8,128)(2,1)S(1)} %broadcast_in_dim.20), channel_id=1, replica_groups=mesh['line'=4,'ring'=8,'chip'=8,'core'=2] {'chip','core'}, dimensions={0} | all-to-all | bytes 786432 | tf_op jit(solution)/shard_map/all_to_all | solution.py:22
  220.2 2.5 convolution_convert_fusion
  222.8 6.8 %all-to-all-start.6 = ((bf16[32,32,512]{2,1,0:T(8,128)(2,1)}), bf16[32,32,512]{2,1,0:T(8,128)(2,1)}, u32[]{:S(2)}, u32[]{:S(2)}) async-start(bf16[32,32,512]{2,1,0:T(8,128)(2,1)} %bitcast.131), calls=%async_computation.6 | async-start | bytes 2097152 | tf_op jit(solution)/shard_map/all_to_all | solution.py:26
  229.5 1.0 slice.163
  230.5 0.9 slice.162
  231.5 1.0 fusion.63
  232.6 1.3 fusion.113
  234.6 21.7 %all-to-all-done.6 = bf16[32,32,512]{2,1,0:T(8,128)(2,1)} async-done(((bf16[32,32,512]{2,1,0:T(8,128)(2,1)}), bf16[32,32,512]{2,1,0:T(8,128)(2,1)}, u32[]{:S(2)}, u32[]{:S(2)}) %all-to-all-start.6) | async-done | bytes 1048608 | tf_op jit(solution)/shard_map/all_to_all | solution.py:26
  256.3 1.4 convert_reduce_fusion
  258.3 17.5 %all_to_all.72 = bf16[16,16,448]{2,1,0:T(8,128)(2,1)S(1)} all-to-all(bf16[16,16,448]{2,1,0:T(8,128)(2,1)S(1)} %bitcast.132), channel_id=1, replica_groups=mesh['line'=4,'ring'=8,'chip'=8,'core'=2] {'chip','core'}, dimensions={0} | all-to-all | bytes 458752 | tf_op jit(solution)/shard_map/all_to_all | solution.py:26
  275.9 15.9 %all_to_all.73 = bf16[16,16,448]{2,1,0:T(8,128)(2,1)S(1)} all-to-all(bf16[16,16,448]{2,1,0:T(8,128)(2,1)S(1)} %broadcast_in_dim.21), channel_id=1, replica_groups=mesh['line'=4,'ring'=8,'chip'=8,'core'=2] {'chip','core'}, dimensions={0} | all-to-all | bytes 458752 | tf_op jit(solution)/shard_map/all_to_all | solution.py:22
  292.3 17.8 %all_to_all.74 = bf16[32,8,512]{2,1,0:T(8,128)(2,1)S(1)} all-to-all(bf16[32,8,512]{2,1,0:T(8,128)(2,1)S(1)} %fusion.31), channel_id=1, replica_groups=mesh['line'=4,'ring'=8,'chip'=8,'core'=2] {'line','ring'}, dimensions={0} | all-to-all | bytes 524288 | tf_op jit(solution)/shard_map/all_to_all | solution.py:26
  310.9 16.5 %all_to_all.75 = bf16[32,8,512]{2,1,0:T(8,128)(2,1)S(1)} all-to-all(bf16[32,8,512]{2,1,0:T(8,128)(2,1)S(1)} %broadcast_in_dim.22), channel_id=1, replica_groups=mesh['line'=4,'ring'=8,'chip'=8,'core'=2] {'line','ring'}, dimensions={0} | all-to-all | bytes 524288 | tf_op jit(solution)/shard_map/all_to_all | solution.py:22
  327.8 17.4 %all_to_all.76 = bf16[16,16,448]{2,1,0:T(8,128)(2,1)S(1)} all-to-all(bf16[16,16,448]{2,1,0:T(8,128)(2,1)S(1)} %bitcast.133), channel_id=1, replica_groups=mesh['line'=4,'ring'=8,'chip'=8,'core'=2] {'chip','core'}, dimensions={0} | all-to-all | bytes 458752 | tf_op jit(solution)/shard_map/all_to_all | solution.py:26
  345.4 15.9 %all_to_all.77 = bf16[16,16,448]{2,1,0:T(8,128)(2,1)S(1)} all-to-all(bf16[16,16,448]{2,1,0:T(8,128)(2,1)S(1)} %broadcast_in_dim.23), channel_id=1, replica_groups=mesh['line'=4,'ring'=8,'chip'=8,'core'=2] {'chip','core'}, dimensions={0} | all-to-all | bytes 458752 | tf_op jit(solution)/shard_map/all_to_all | solution.py:22
  361.5 1.0 fusion.30
  362.4 4.8 %all-to-all-start.13 = ((bf16[32,8,512]{2,1,0:T(8,128)(2,1)}), bf16[32,8,512]{2,1,0:T(8,128)(2,1)S(1)}, u32[]{:S(2)}, u32[]{:S(2)}) async-start(bf16[32,8,512]{2,1,0:T(8,128)(2,1)} %fusion.30), calls=%async_computation.13 | async-start | bytes 524288 | tf_op jit(solution)/shard_map/all_to_all | solution.py:26
  367.4 1.0 copy.21
  368.3 10.5 %all-to-all-done.13 = bf16[32,8,512]{2,1,0:T(8,128)(2,1)S(1)} async-done(((bf16[32,8,512]{2,1,0:T(8,128)(2,1)}), bf16[32,8,512]{2,1,0:T(8,128)(2,1)S(1)}, u32[]{:S(2)}, u32[]{:S(2)}) %all-to-all-start.13) | async-done | bytes 262176 | tf_op jit(solution)/shard_map/all_to_all | solution.py:26
  378.8 1.3 multiply_subtract_fusion
  (71 shorter events, 9.4 us)
Async XLA Ops:
  7.2 27.0 %copy-start = (bf16[512,1024]{1,0:T(8,128)(2,1)S(1)}, bf16[512,1024]{1,0:T(8,128)(2,1)}, u32[]{:S(2)}) copy-start(bf16[512,1024]{1,0:T(8,128)(2,1)} %param.7) | copy-start | bytes 3145732
  7.2 52.2 %all-gather.3.cloned.1.call-start = ((), (), s32[]{:S(2)}) async-start(), calls=%async_computation.14 | async-start | bytes 2359296 | tf_op jit(solution)/shard_map/all_gather | solution.py:52
  11.0 22.2 %all-to-all-start.1 = ((bf16[4,256,384]{2,1,0:T(8,128)(2,1)}), bf16[4,256,384]{2,1,0:T(8,128)(2,1)S(1)}, u32[]{:S(2)}, u32[]{:S(2)}) async-start(bf16[4,256,384]{2,1,0:T(8,128)(2,1)} %broadcast_in_dim.17), calls=%async_computation.1 | async-start | bytes 1572864 | tf_op jit(solution)/shard_map/all_to_all | solution.py:22
  20.3 103.0 %all-gather.5.cloned.1.call-start = ((), (), s32[]{:S(2)}) async-start(), calls=%async_computation.15 | async-start | bytes 5308416 | tf_op jit(solution)/shard_map/all_gather | solution.py:54
  35.2 25.7 %all-to-all-start.2 = ((bf16[16,32,512]{2,1,0:T(8,128)(2,1)}), bf16[16,32,512]{2,1,0:T(8,128)(2,1)S(1)}, u32[]{:S(2)}, u32[]{:S(2)}) async-start(bf16[16,32,512]{2,1,0:T(8,128)(2,1)} %broadcast_in_dim.18), calls=%async_computation.2 | async-start | bytes 1048576 | tf_op jit(solution)/shard_map/all_to_all | solution.py:22
  60.9 1.7 copy-start.3
  62.6 52.2 %all-to-all-start = ((bf16[4,2048,128]{2,1,0:T(8,128)(2,1)}), bf16[4,2048,128]{2,1,0:T(8,128)(2,1)S(1)}, u32[]{:S(2)}, u32[]{:S(2)}) async-start(bf16[4,2048,128]{2,1,0:T(8,128)(2,1)} %broadcast_in_dim.16), calls=%async_computation | async-start | bytes 4194304 | tf_op jit(solution)/shard_map/all_to_all | solution.py:22
  70.8 58.6 %copy-start.12 = (f32[32]{0:T(128)}, f32[32]{0:T(128)S(1)}, u32[]{:S(2)}) copy-start(f32[32]{0:T(128)S(1)} %convert_multiply_fusion.1) | copy-start | bytes 388
  123.3 4.0 %copy-start.2 = (bf16[16,4,8,512]{3,2,0,1:T(8,128)(2,1)S(1)}, bf16[16,4,8,512]{3,2,0,1:T(8,128)(2,1)}, u32[]{:S(2)}) copy-start(bf16[16,4,8,512]{3,2,0,1:T(8,128)(2,1)} %copy.20) | copy-start | bytes 1572868
  125.2 3.8 copy-start.8
  129.3 0.6 copy-start.10
  130.0 9.0 %copy-start.14 = (s32[192]{0:T(256)S(1)}, s32[192]{0:T(256)}, u32[]{:S(2)}) copy-start(s32[192]{0:T(256)} %param.8) | copy-start | bytes 2308
  131.2 34.5 %all-to-all-start.3 = ((bf16[32,32,512]{2,1,0:T(8,128)(2,1)}), bf16[32,32,512]{2,1,0:T(8,128)(2,1)}, u32[]{:S(2)}, u32[]{:S(2)}) async-start(bf16[32,32,512]{2,1,0:T(8,128)(2,1)} %broadcast_in_dim.19), calls=%async_computation.3 | async-start | bytes 2097152 | tf_op jit(solution)/shard_map/all_to_all | solution.py:22
  141.7 2.8 copy-start.1
  144.6 2.2 copy-start.9
  149.5 16.2 %copy-start.6 = (f32[192,384]{1,0:T(8,128)}, f32[192,384]{1,0:T(8,128)S(1)}, u32[]{:S(2)}) copy-start(f32[192,384]{1,0:T(8,128)S(1)} %fusion.27) | copy-start | bytes 884740
  150.5 49.7 %copy-start.4 = (f32[192,128]{1,0:T(8,128)}, f32[192,128]{1,0:T(8,128)S(1)}, u32[]{:S(2)}) copy-start(f32[192,128]{1,0:T(8,128)S(1)} %convolution_bitcast_fusion.1) | copy-start | bytes 294916
  222.8 33.6 %all-to-all-start.6 = ((bf16[32,32,512]{2,1,0:T(8,128)(2,1)}), bf16[32,32,512]{2,1,0:T(8,128)(2,1)}, u32[]{:S(2)}, u32[]{:S(2)}) async-start(bf16[32,32,512]{2,1,0:T(8,128)(2,1)} %bitcast.131), calls=%async_computation.6 | async-start | bytes 2097152 | tf_op jit(solution)/shard_map/all_to_all | solution.py:26
  232.6 1.7 copy-start.5
  232.6 1.7 copy-start.7
  232.6 1.7 copy-start.15
  234.2 23.5 %copy-start.11 = (f32[32,384]{1,0:T(8,128)S(1)}, f32[32,384]{1,0:T(8,128)}, u32[]{:S(2)}) copy-start(f32[32,384]{1,0:T(8,128)} %copy-done.10) | copy-start | bytes 147460
  234.2 23.5 %copy-start.13 = (f32[32]{0:T(128)S(1)}, f32[32]{0:T(128)}, u32[]{:S(2)}) copy-start(f32[32]{0:T(128)} %copy-done.12) | copy-start | bytes 388
  362.4 16.3 %all-to-all-start.13 = ((bf16[32,8,512]{2,1,0:T(8,128)(2,1)}), bf16[32,8,512]{2,1,0:T(8,128)(2,1)S(1)}, u32[]{:S(2)}, u32[]{:S(2)}) async-start(bf16[32,8,512]{2,1,0:T(8,128)(2,1)} %fusion.30), calls=%async_computation.13 | async-start | bytes 524288 | tf_op jit(solution)/shard_map/all_to_all | solution.py:26
Sparse Core Ops, SparseCore 0:
  10.1 49.2 all-gather.2
  62.0 61.2 all-gather.4

commit v7 on v6

--- a/solution.py
+++ b/solution.py
@@ -48,49 +48,44 @@
     return sum_blocks(partial.reshape(parts, -1, partial.shape[1]), TOK)
 
 
-def gather_rotation(rot_b, line_wide, line_pos):
-    near = lax.all_gather(rot_b, "ring", axis=0, tiled=True)
-    others = jnp.stack([pick_other(k, line_wide, line_pos) for k in range(LINE - 1)])
-    far = lax.all_gather(others, "ring", axis=1, tiled=True)
-    thin = gather_blocks(near[:, :THIN], "line").reshape(LINE * near.shape[0], THIN)
-    return thin, near, far
+def gather_by_doubling(own):
+    held = own[None]
+    for axis in ("core", "chip"):
+        size = lax.axis_size(axis)
+        span = 1
+        while span < size:
+            came = lax.ppermute(held, axis, [(k, k ^ span) for k in range(size)])
+            upper = (lax.axis_index(axis) // span) % 2 == 1
+            held = jnp.concatenate(
+                [jnp.where(upper, came, held), jnp.where(upper, held, came)], 0
+            )
+            span *= 2
+    return held
 
 
-def pick_other(k, blocks, line_pos):
-    return jnp.where(line_pos > k, blocks[k], blocks[k + 1])
+def gather_rotation(rot_b):
+    wide = gather_blocks(rot_b[:, THIN:], "line")
+    thin_own, wide = lax.optimization_barrier((rot_b[:, :THIN], wide))
+    thin = gather_blocks(thin_own, "ring").reshape(-1, THIN)
+    wide = lax.all_gather(wide, "ring", axis=1, tiled=True)
+    wide = wide.reshape(-1, wide.shape[2])
+    return gather_blocks(thin, "line").reshape(-1, THIN), wide, thin
 
 
-def times_rotation(lhs, thin, near, far, line_pos):
-    span = near.shape[0]
-    spans = [lhs[:, k * span : (k + 1) * span] for k in range(LINE)]
-    lhs_near = spans[LINE - 1]
-    for k in range(LINE - 1):
-        lhs_near = jnp.where(line_pos == k, spans[k], lhs_near)
-    total_thin = jnp.dot(lhs, thin, preferred_element_type=jnp.float32)
-    total = jnp.dot(lhs_near, near[:, THIN:], preferred_element_type=jnp.float32)
-    for k in range(LINE - 1):
-        total = total + jnp.dot(
-            pick_other(k, spans, line_pos), far[k], preferred_element_type=jnp.float32
-        )
-    return jnp.concatenate([total_thin, total], 1)
+def times_rotation(lhs, thin, wide):
+    return jnp.concatenate(
+        [
+            jnp.dot(lhs, thin, preferred_element_type=jnp.float32),
+            jnp.dot(lhs, wide, preferred_element_type=jnp.float32),
+        ],
+        1,
+    )
 
 
-def first_rows(thin, near, far, rows, line_pos):
-    narrow = near.shape[1]
-    first_near = near.reshape(RING, rows, narrow)[:, : 2 * WIN]
-    first_far = far.reshape(LINE - 1, RING, rows, narrow - THIN)[:, :, : 2 * WIN]
-    first_near, first_far = lax.optimization_barrier((first_near, first_far))
-    first_near, first_far = first_near[:, :WIN, THIN:], first_far[:, :, :WIN]
-    first = [
-        jnp.where(
-            line_pos == k,
-            first_near,
-            jnp.where(line_pos > k, first_far[min(k, LINE - 2)], first_far[max(k - 1, 0)]),
-        )
-        for k in range(LINE)
-    ]
-    first_thin = thin.reshape(LINE, RING, rows, THIN)[:, :, :WIN]
-    return jnp.concatenate([first_thin, jnp.stack(first)], 3).reshape(LINE * RING * WIN, narrow)
+def first_rows(thin, wide, rows):
+    firsts = [part.reshape(-1, rows, part.shape[1])[:, : 2 * WIN] for part in (thin, wide)]
+    firsts = [part[:, :WIN] for part in lax.optimization_barrier(firsts)]
+    return jnp.concatenate(firsts, 2).reshape(-1, thin.shape[1] + wide.shape[1])
 
 
 def local(activations, rotation, value_weight, token_code, channel_code):
@@ -105,24 +100,22 @@
     tok_rows = activations.shape[0]
     width_root = math.sqrt(model_width)
     rot_b = rotation.astype(jnp.bfloat16)
-    line_wide = gather_blocks(rot_b[:, THIN:], "line")
-    value_late, line_wide = lax.optimization_barrier((value_weight, line_wide))
+    thin, wide, ring_thin = gather_rotation(rot_b)
+    value_late, _ = lax.optimization_barrier((value_weight, ring_thin))
     own_cols = lax.dynamic_slice_in_dim(value_late, tok_pos * chan_share, chan_share, 1)
-    weight_rows = gather_blocks(own_cols.T, MDL).transpose(1, 0, 2).reshape(chan_share, model_width)
-    line_pos = lax.axis_index("line")
-    panel = gather_rotation(rot_b, line_wide, line_pos)
+    weight_rows = gather_by_doubling(own_cols.T).transpose(1, 0, 2).reshape(chan_share, model_width)
     own_feats = lax.dynamic_slice_in_dim(activations, mdl_pos * narrow, narrow, 1)
     plain = jnp.dot(own_feats, value_weight, preferred_element_type=jnp.float32)
 
-    turned = times_rotation(weight_rows, *panel, line_pos) / width_root
+    turned = times_rotation(weight_rows, thin, wide) / width_root
     own_codes = lax.dynamic_slice_in_dim(channel_code, tok_pos * chan_share, chan_share, 0)
     weight_clip = own_codes.astype(jnp.float32)[:, None] / (4.0 * width_root)
     weight_tanh = jnp.tanh(turned / weight_clip)
     quant_weight = (weight_clip * weight_tanh).astype(jnp.bfloat16)
-    late_panel, quant_late = lax.optimization_barrier((panel, quant_weight))
+    thin, wide, quant_late = lax.optimization_barrier((thin, wide, quant_weight))
     weight_full = gather_blocks(quant_late, TOK).reshape(channels, narrow)
-    rotated = times_rotation(activations, *late_panel, line_pos) / width_root
-    window = first_rows(*late_panel, rotation.shape[0], line_pos)
+    rotated = times_rotation(activations, thin, wide) / width_root
+    window = first_rows(thin, wide, rotation.shape[0])
     act_clip = token_code.astype(jnp.float32)[:, None] * 0.5
     act_tanh = jnp.tanh(rotated / act_clip)
     quant_act = (act_clip * act_tanh).astype(jnp.bfloat16)
@@ -132,8 +125,9 @@
         jnp.einsum("td,hcd->htc", quant_act, weight_halves, preferred_element_type=jnp.float32)
         - plain.reshape(tok_rows, 2, half).transpose(1, 0, 2)
     )
-    own_err = sum_blocks(partial_err.reshape(n_mdl, -1, half), MDL)
-    err_bf = gather_blocks(own_err.astype(jnp.bfloat16), MDL).reshape(2, tok_rows, half)
+    own_err = sum_blocks(partial_err.reshape(n_mdl, -1, half), ("core", "chip"))
+    err_bf = gather_blocks(own_err.astype(jnp.bfloat16), "chip").reshape(tok_rows, half)
+    err_bf = gather_blocks(err_bf, "core")
     recon_error = err_bf.transpose(1, 0, 2).reshape(tok_rows, channels).astype(jnp.float32)
     grad_quant = sum_blocks(
         jnp.einsum("htc,td->hcd", err_bf, quant_act, preferred_element_type=jnp.float32)

time: 389 us -> 402 us (1.033)
  waiting for transfers between devices: 125 us -> 88.2 us
  blocking collectives: 152 us -> 183 us
  starting transfers between devices: 44.6 us -> 56.7 us
    all_to_all x4 -> x6, blocking collectives: 67 us -> 93.3 us  [gather_blocks(): lax.all_to_all(jnp.broadcast_to(own[None], (parts,) + own.shape), axis, 0...]
    all_to_all x4 -> x3, waiting for transfers between devices: 70.7 us -> 45.1 us  [gather_blocks(): lax.all_to_all(jnp.broadcast_to(own[None], (parts,) + own.shape), axis, 0...]
    all_gather x2 -> x1, waiting for transfers between devices: 22.6 us -> 0.02 us  [gather_rotation(): wide = lax.all_gather(wide, 'ring', axis=1, tiled=True)]
    ppermute x0 -> x4, starting transfers between devices: none -> 17.3 us  [gather_by_doubling(): came = lax.ppermute(held, axis, [(k, k ^ span) for k in range(size)])]
    ppermute x0 -> x4, waiting for transfers between devices: none -> 13.3 us  [gather_by_doubling(): came = lax.ppermute(held, axis, [(k, k ^ span) for k in range(size)])]
    dot_general x10 -> x4, matrix products: 16 us -> 10.8 us  [the longest x2 5.84 us: times_rotation(): jnp.dot(lhs, wide, preferred_element_type=jnp.float32)]
    all_to_all x4 -> x3, starting transfers between devices: 33 us -> 28.4 us  [gather_blocks(): lax.all_to_all(jnp.broadcast_to(own[None], (parts,) + own.shape), axis, 0...]
  transfers between devices with their start and end apart: 8 -> 10, of which waited for: 8 -> 9; matrix products, arithmetic and copies ran while one was open for 7% -> 6% of each run, Pallas kernels for 0% -> 0%
where the time goes in v7:
time: 402 us; the launch traced here: 400 us
  blocking collectives  183 us (46%)
  waiting for transfers between devices  88.2 us (22%)
  starting transfers between devices  56.7 us (14%)
  matrix products  27.6 us (7%)
  local copies, waits for them, and re-layouts  16.9 us (4%)
  between operations  14.5 us (4%)
  other arithmetic  13.8 us (3%)
    all_to_all x6, blocking collectives, gather_blocks(): lax.all_to_all(jnp.broadcast_to(own[None], (parts,) + own.shape), axis, 0...  93.3 us
    all_to_all x4, blocking collectives, sum_blocks(): return jnp.sum(lax.all_to_all(blocks, axis, 0, 0).astype(jnp.float32), 0)  89.4 us
    all_to_all x3, waiting for transfers between devices, gather_blocks(): lax.all_to_all(jnp.broadcast_to(own[None], (parts,) + own.shape), axis, 0...  45.1 us
    all_to_all x2, waiting for transfers between devices, sum_blocks(): return jnp.sum(lax.all_to_all(blocks, axis, 0, 0).astype(jnp.float32), 0)  29.8 us
    all_to_all x3, starting transfers between devices, gather_blocks(): lax.all_to_all(jnp.broadcast_to(own[None], (parts,) + own.shape), axis, 0...  28.4 us
    ppermute x4, starting transfers between devices, gather_by_doubling(): came = lax.ppermute(held, axis, [(k, k ^ span) for k in range(size)])  17.3 us
    ppermute x4, waiting for transfers between devices, gather_by_doubling(): came = lax.ppermute(held, axis, [(k, k ^ span) for k in range(size)])  13.3 us
    all_to_all x2, starting transfers between devices, sum_blocks(): return jnp.sum(lax.all_to_all(blocks, axis, 0, 0).astype(jnp.float32), 0)  11 us
  transfers between devices with their start and end apart: 10, of which 9 were waited for; matrix products, arithmetic and copies ran while one was open for 6% of the time, Pallas kernels for 0%

profile of v7, /device:TPU:8, one launch (start us, length us, event | category | flops | bytes accessed | tf_op | source)
XLA Modules:
  0.0 400.5 jit_solution(14640296938911655068)
XLA Ops:
  7.2 1.2 convert_element_type.82
  9.4 10.0 %all-to-all-start = ((bf16[4,256,384]{2,1,0:T(8,128)(2,1)}), bf16[4,256,384]{2,1,0:T(8,128)(2,1)}, u32[]{:S(2)}, u32[]{:S(2)}) async-start(bf16[4,256,384]{2,1,0:T(8,128)(2,1)} %broadcast_in_dim.24), calls=%async_computation | async-start | bytes 1572864 | tf_op jit(solution)/shard_map/all_to_all | solution.py:22
  19.4 12.2 %all-to-all-done = bf16[4,256,384]{2,1,0:T(8,128)(2,1)} async-done(((bf16[4,256,384]{2,1,0:T(8,128)(2,1)}), bf16[4,256,384]{2,1,0:T(8,128)(2,1)}, u32[]{:S(2)}, u32[]{:S(2)}) %all-to-all-start) | async-done | bytes 786464 | tf_op jit(solution)/shard_map/all_to_all | solution.py:22
  31.6 26.5 %all_to_all.75 = bf16[8,256,128]{2,1,0:T(8,128)(2,1)S(1)} all-to-all(bf16[8,256,128]{2,1,0:T(8,128)(2,1)S(1)} %broadcast_in_dim.25), channel_id=1, replica_groups=mesh['line'=4,'ring'=8,'chip'=8,'core'=2] {'ring'}, dimensions={0} | all-to-all | bytes 1048576 | tf_op jit(solution)/shard_map/all_to_all | solution.py:22
  58.2 1.7 broadcast_in_dim.27
  59.8 9.4 %all-to-all-start.2 = ((bf16[4,2048,128]{2,1,0:T(8,128)(2,1)}), bf16[4,2048,128]{2,1,0:T(8,128)(2,1)}, u32[]{:S(2)}, u32[]{:S(2)}) async-start(bf16[4,2048,128]{2,1,0:T(8,128)(2,1)} %broadcast_in_dim.27), calls=%async_computation.2 | async-start | bytes 4194304 | tf_op jit(solution)/shard_map/all_to_all | solution.py:22
  70.4 1.9 collective-permute-start
  72.3 1.2 collective-permute-done
  73.5 3.3 collective-permute-start.1
  76.9 2.8 collective-permute-done.1
  79.7 4.9 %collective-permute-start.2 = (bf16[4,32,512]{2,1,0:T(8,128)(2,1)S(1)}, bf16[4,32,512]{2,1,0:T(8,128)(2,1)}, u32[]{:S(2)}, u32[]{:S(2)}) collective-permute-start(bf16[4,32,512]{2,1,0:T(8,128)(2,1)S(1)} %pad_maximum_fusion.8), channel_id=1, source_target_pairs={{0,4},{2,6},{4,0},{6,2},{8,12},{10,14},{12,8},{14,10},{1,5},{3,7},... | collective-permute-start | bytes 393224 | tf_op jit(solution)/shard_map/ppermute | solution.py:57
  84.7 3.5 collective-permute-done.2
  89.8 7.1 %collective-permute-start.3 = (bf16[8,32,512]{2,1,0:T(8,128)(2,1)}, bf16[8,32,512]{2,1,0:T(8,128)(2,1)}, u32[]{:S(2)}, u32[]{:S(2)}) collective-permute-start(bf16[8,32,512]{2,1,0:T(8,128)(2,1)} %pad_maximum_fusion.1), channel_id=1, source_target_pairs={{0,8},{2,10},{4,12},{6,14},{8,0},{10,2},{12,4},{14,6},{1,9},{3,11}... | collective-permute-start | bytes 786440 | tf_op jit(solution)/shard_map/ppermute | solution.py:57
  97.8 5.9 %collective-permute-done.3 = bf16[8,32,512]{2,1,0:T(8,128)(2,1)} collective-permute-done((bf16[8,32,512]{2,1,0:T(8,128)(2,1)}, bf16[8,32,512]{2,1,0:T(8,128)(2,1)}, u32[]{:S(2)}, u32[]{:S(2)}) %collective-permute-start.3) | collective-permute-done | bytes 262176 | tf_op jit(solution)/shard_map/ppermute | solution.py:57
  105.5 16.0 %all-to-all-done.2 = bf16[4,2048,128]{2,1,0:T(8,128)(2,1)} async-done(((bf16[4,2048,128]{2,1,0:T(8,128)(2,1)}), bf16[4,2048,128]{2,1,0:T(8,128)(2,1)}, u32[]{:S(2)}, u32[]{:S(2)}) %all-to-all-start.2) | async-done | bytes 2097184 | tf_op jit(solution)/shard_map/all_to_all | solution.py:22
  121.5 2.2 fusion.33
  123.8 3.9 fusion.34
  129.5 9.0 %all-to-all-start.3 = ((bf16[32,32,512]{2,1,0:T(8,128)(2,1)}), bf16[32,32,512]{2,1,0:T(8,128)(2,1)}, u32[]{:S(2)}, u32[]{:S(2)}) async-start(bf16[32,32,512]{2,1,0:T(8,128)(2,1)} %broadcast_in_dim.29), calls=%async_computation.3 | async-start | bytes 2097152 | tf_op jit(solution)/shard_map/all_to_all | solution.py:22
  139.1 2.5 fusion.13
  141.6 2.7 convolution_bitcast_fusion.2
  145.0 1.9 convolution_bitcast_fusion.1
  147.0 17.0 %all-to-all-done.3 = bf16[32,32,512]{2,1,0:T(8,128)(2,1)} async-done(((bf16[32,32,512]{2,1,0:T(8,128)(2,1)}), bf16[32,32,512]{2,1,0:T(8,128)(2,1)}, u32[]{:S(2)}, u32[]{:S(2)}) %all-to-all-start.3) | async-done | bytes 1048608 | tf_op jit(solution)/shard_map/all_to_all | solution.py:22
  163.9 2.0 fusion
  165.9 34.9 %all_to_all.76 = f32[16,24,512]{2,1,0:T(8,128)} all-to-all(f32[16,24,512]{2,1,0:T(8,128)S(1)} %bitcast.94), channel_id=1, replica_groups=mesh['line'=4,'ring'=8,'chip'=8,'core'=2] {'core','chip'}, dimensions={0} | all-to-all | bytes 1572864 | tf_op jit(solution)/shard_map/all_to_all | solution.py:26
  200.8 1.2 reduce_sum.54
  202.0 14.4 %all_to_all.77 = bf16[8,24,512]{2,1,0:T(8,128)(2,1)S(1)} all-to-all(bf16[8,24,512]{2,1,0:T(8,128)(2,1)S(1)} %broadcast_in_dim.30), channel_id=1, replica_groups=mesh['line'=4,'ring'=8,'chip'=8,'core'=2] {'chip'}, dimensions={0} | all-to-all | bytes 393216 | tf_op jit(solution)/shard_map/all_to_all | solution.py:22
  216.4 4.0 %all_to_all.78 = bf16[2,192,512]{2,1,0:T(8,128)(2,1)S(1)} all-to-all(bf16[2,192,512]{2,1,0:T(8,128)(2,1)S(1)} %broadcast_in_dim.32), channel_id=1, replica_groups=mesh['line'=4,'ring'=8,'chip'=8,'core'=2] {'core'}, dimensions={0} | all-to-all | bytes 786432 | tf_op jit(solution)/shard_map/all_to_all | solution.py:22
  220.5 2.5 convolution_convert_fusion
  223.0 6.0 %all-to-all-start.7 = ((bf16[32,32,512]{2,1,0:T(8,128)(2,1)}), bf16[32,32,512]{2,1,0:T(8,128)(2,1)}, u32[]{:S(2)}, u32[]{:S(2)}) async-start(bf16[32,32,512]{2,1,0:T(8,128)(2,1)} %bitcast.89), calls=%async_computation.7 | async-start | bytes 2097152 | tf_op jit(solution)/shard_map/all_to_all | solution.py:26
  232.4 1.7 fusion.7
  234.1 1.3 fusion.32
  236.6 19.2 %all-to-all-done.7 = bf16[32,32,512]{2,1,0:T(8,128)(2,1)} async-done(((bf16[32,32,512]{2,1,0:T(8,128)(2,1)}), bf16[32,32,512]{2,1,0:T(8,128)(2,1)}, u32[]{:S(2)}, u32[]{:S(2)}) %all-to-all-start.7) | async-done | bytes 1048608 | tf_op jit(solution)/shard_map/all_to_all | solution.py:26
  255.9 1.4 convert_reduce_fusion
  258.8 2.1 convolution_convert_fusion.2
  260.9 1.8 copy.19
  262.7 18.4 %all_to_all.79 = bf16[16,16,448]{2,1,0:T(8,128)(2,1)S(1)} all-to-all(bf16[16,16,448]{2,1,0:T(8,128)(2,1)} %bitcast.90), channel_id=1, replica_groups=mesh['line'=4,'ring'=8,'chip'=8,'core'=2] {'chip','core'}, dimensions={0} | all-to-all | bytes 458752 | tf_op jit(solution)/shard_map/all_to_all | solution.py:26
  281.2 16.0 %all_to_all.80 = bf16[16,16,448]{2,1,0:T(8,128)(2,1)S(1)} all-to-all(bf16[16,16,448]{2,1,0:T(8,128)(2,1)S(1)} %broadcast_in_dim.33), channel_id=1, replica_groups=mesh['line'=4,'ring'=8,'chip'=8,'core'=2] {'chip','core'}, dimensions={0} | all-to-all | bytes 458752 | tf_op jit(solution)/shard_map/all_to_all | solution.py:22
  297.2 1.2 fusion.16
  298.4 1.2 fusion.6
  299.6 17.9 %all_to_all.81 = bf16[32,8,512]{2,1,0:T(8,128)(2,1)S(1)} all-to-all(bf16[32,8,512]{2,1,0:T(8,128)(2,1)S(1)} %fusion.6), channel_id=1, replica_groups=mesh['line'=4,'ring'=8,'chip'=8,'core'=2] {'line','ring'}, dimensions={0} | all-to-all | bytes 524288 | tf_op jit(solution)/shard_map/all_to_all | solution.py:26
  318.3 16.5 %all_to_all.82 = bf16[32,8,512]{2,1,0:T(8,128)(2,1)S(1)} all-to-all(bf16[32,8,512]{2,1,0:T(8,128)(2,1)S(1)} %broadcast_in_dim.34), channel_id=1, replica_groups=mesh['line'=4,'ring'=8,'chip'=8,'core'=2] {'line','ring'}, dimensions={0} | all-to-all | bytes 524288 | tf_op jit(solution)/shard_map/all_to_all | solution.py:22
  335.7 1.8 copy.20
  337.5 18.2 %all_to_all.83 = bf16[16,16,448]{2,1,0:T(8,128)(2,1)S(1)} all-to-all(bf16[16,16,448]{2,1,0:T(8,128)(2,1)} %bitcast.91), channel_id=1, replica_groups=mesh['line'=4,'ring'=8,'chip'=8,'core'=2] {'chip','core'}, dimensions={0} | all-to-all | bytes 458752 | tf_op jit(solution)/shard_map/all_to_all | solution.py:26
  355.8 15.9 %all_to_all.84 = bf16[16,16,448]{2,1,0:T(8,128)(2,1)S(1)} all-to-all(bf16[16,16,448]{2,1,0:T(8,128)(2,1)S(1)} %broadcast_in_dim.35), channel_id=1, replica_groups=mesh['line'=4,'ring'=8,'chip'=8,'core'=2] {'chip','core'}, dimensions={0} | all-to-all | bytes 458752 | tf_op jit(solution)/shard_map/all_to_all | solution.py:22
  372.9 1.9 fusion.5
  374.8 4.9 %all-to-all-start.14 = ((bf16[32,8,512]{2,1,0:T(8,128)(2,1)}), bf16[32,8,512]{2,1,0:T(8,128)(2,1)}, u32[]{:S(2)}, u32[]{:S(2)}) async-start(bf16[32,8,512]{2,1,0:T(8,128)(2,1)} %fusion.5), calls=%async_computation.14 | async-start | bytes 524288 | tf_op jit(solution)/shard_map/all_to_all | solution.py:26
  380.8 10.5 %all-to-all-done.14 = bf16[32,8,512]{2,1,0:T(8,128)(2,1)} async-done(((bf16[32,8,512]{2,1,0:T(8,128)(2,1)}), bf16[32,8,512]{2,1,0:T(8,128)(2,1)}, u32[]{:S(2)}, u32[]{:S(2)}) %all-to-all-start.14) | async-done | bytes 262176 | tf_op jit(solution)/shard_map/all_to_all | solution.py:26
  392.3 1.3 multiply_subtract_fusion
  (75 shorter events, 20.9 us)
Async XLA Ops:
  7.2 132.0 %copy-start = (bf16[192,8192]{1,0:T(8,128)(2,1)S(1)}, bf16[192,8192]{1,0:T(8,128)(2,1)}, u32[]{:S(2)}) copy-start(bf16[192,8192]{1,0:T(8,128)(2,1)} %param.5) | copy-start | bytes 9437188
  9.4 22.2 %all-to-all-start = ((bf16[4,256,384]{2,1,0:T(8,128)(2,1)}), bf16[4,256,384]{2,1,0:T(8,128)(2,1)}, u32[]{:S(2)}, u32[]{:S(2)}) async-start(bf16[4,256,384]{2,1,0:T(8,128)(2,1)} %broadcast_in_dim.24), calls=%async_computation | async-start | bytes 1572864 | tf_op jit(solution)/shard_map/all_to_all | solution.py:22
  19.4 104.4 %all-gather.2.cloned.1.call-start = ((), (), s32[]{:S(2)}) async-start(), calls=%async_computation.15 | async-start | bytes 7077888 | tf_op jit(solution)/shard_map/all_gather | solution.py:70
  59.8 61.7 %all-to-all-start.2 = ((bf16[4,2048,128]{2,1,0:T(8,128)(2,1)}), bf16[4,2048,128]{2,1,0:T(8,128)(2,1)}, u32[]{:S(2)}, u32[]{:S(2)}) async-start(bf16[4,2048,128]{2,1,0:T(8,128)(2,1)} %broadcast_in_dim.27), calls=%async_computation.2 | async-start | bytes 4194304 | tf_op jit(solution)/shard_map/all_to_all | solution.py:22
  70.4 3.1 collective-permute-start
  73.5 6.2 %collective-permute-start.1 = (bf16[2,32,512]{2,1,0:T(8,128)(2,1)S(1)}, bf16[2,32,512]{2,1,0:T(8,128)(2,1)S(1)}, u32[]{:S(2)}, u32[]{:S(2)}) collective-permute-start(bf16[2,32,512]{2,1,0:T(8,128)(2,1)S(1)} %pad_maximum_fusion.11), channel_id=1, source_target_pairs={{0,2},{2,0},{4,6},{6,4},{8,10},{10,8},{12,14},{14,12},{1,3},{3,1},... | collective-permute-start | bytes 196616 | tf_op jit(solution)/shard_map/ppermute | solution.py:57
  79.7 8.5 %collective-permute-start.2 = (bf16[4,32,512]{2,1,0:T(8,128)(2,1)S(1)}, bf16[4,32,512]{2,1,0:T(8,128)(2,1)}, u32[]{:S(2)}, u32[]{:S(2)}) collective-permute-start(bf16[4,32,512]{2,1,0:T(8,128)(2,1)S(1)} %pad_maximum_fusion.8), channel_id=1, source_target_pairs={{0,4},{2,6},{4,0},{6,2},{8,12},{10,14},{12,8},{14,10},{1,5},{3,7},... | collective-permute-start | bytes 393224 | tf_op jit(solution)/shard_map/ppermute | solution.py:57
  89.8 13.8 %collective-permute-start.3 = (bf16[8,32,512]{2,1,0:T(8,128)(2,1)}, bf16[8,32,512]{2,1,0:T(8,128)(2,1)}, u32[]{:S(2)}, u32[]{:S(2)}) collective-permute-start(bf16[8,32,512]{2,1,0:T(8,128)(2,1)} %pad_maximum_fusion.1), channel_id=1, source_target_pairs={{0,8},{2,10},{4,12},{6,14},{8,0},{10,2},{12,4},{14,6},{1,9},{3,11}... | collective-permute-start | bytes 786440 | tf_op jit(solution)/shard_map/ppermute | solution.py:57
  97.7 29.9 %copy-start.13 = (f32[32]{0:T(128)}, f32[32]{0:T(128)S(1)}, u32[]{:S(2)}) copy-start(f32[32]{0:T(128)S(1)} %convert_multiply_fusion.1) | copy-start | bytes 388
  127.7 0.6 copy-start.6
  128.3 10.2 %copy-start.14 = (s32[192]{0:T(256)S(1)}, s32[192]{0:T(256)}, u32[]{:S(2)}) copy-start(s32[192]{0:T(256)} %param.8) | copy-start | bytes 2308
  129.5 34.4 %all-to-all-start.3 = ((bf16[32,32,512]{2,1,0:T(8,128)(2,1)}), bf16[32,32,512]{2,1,0:T(8,128)(2,1)}, u32[]{:S(2)}, u32[]{:S(2)}) async-start(bf16[32,32,512]{2,1,0:T(8,128)(2,1)} %broadcast_in_dim.29), calls=%async_computation.3 | async-start | bytes 2097152 | tf_op jit(solution)/shard_map/all_to_all | solution.py:22
  141.6 3.4 copy-start.1
  145.0 18.9 %copy-start.4 = (f32[192,128]{1,0:T(8,128)}, f32[192,128]{1,0:T(8,128)S(1)}, u32[]{:S(2)}) copy-start(f32[192,128]{1,0:T(8,128)S(1)} %convolution_bitcast_fusion.2) | copy-start | bytes 294916
  147.0 69.4 %copy-start.11 = (f32[192,384]{1,0:T(8,128)}, f32[192,384]{1,0:T(8,128)S(1)}, u32[]{:S(2)}) copy-start(f32[192,384]{1,0:T(8,128)S(1)} %convolution_bitcast_fusion.1) | copy-start | bytes 884740
  223.0 32.9 %all-to-all-start.7 = ((bf16[32,32,512]{2,1,0:T(8,128)(2,1)}), bf16[32,32,512]{2,1,0:T(8,128)(2,1)}, u32[]{:S(2)}, u32[]{:S(2)}) async-start(bf16[32,32,512]{2,1,0:T(8,128)(2,1)} %bitcast.89), calls=%async_computation.7 | async-start | bytes 2097152 | tf_op jit(solution)/shard_map/all_to_all | solution.py:26
  229.0 6.6 %copy-start.5 = (f32[192,128]{1,0:T(8,128)S(1)}, f32[192,128]{1,0:T(8,128)}, u32[]{:S(2)}) copy-start(f32[192,128]{1,0:T(8,128)} %copy-done.4) | copy-start | bytes 294916
  229.0 6.6 %copy-start.12 = (f32[192,384]{1,0:T(8,128)S(1)}, f32[192,384]{1,0:T(8,128)}, u32[]{:S(2)}) copy-start(f32[192,384]{1,0:T(8,128)} %copy-done.11) | copy-start | bytes 884740
  229.0 6.6 %copy-start.15 = (f32[192]{0:T(256)S(1)}, f32[192]{0:T(256)}, u32[]{:S(2)}) copy-start(f32[192]{0:T(256)} %convert_multiply_fusion) | copy-start | bytes 2308
  258.2 0.6 copy-start.7
  258.2 0.6 copy-start.9
  262.7 72.0 %copy-start.2 = (bf16[192,512]{1,0:T(8,128)(2,1)S(1)}, bf16[192,512]{1,0:T(8,128)(2,1)}, u32[]{:S(2)}) copy-start(bf16[192,512]{1,0:T(8,128)(2,1)} %fusion.7) | copy-start | bytes 589828
  262.7 72.0 %copy-start.3 = (bf16[192,512]{1,0:T(8,128)(2,1)S(1)}, bf16[192,512]{1,0:T(8,128)(2,1)}, u32[]{:S(2)}) copy-start(bf16[192,512]{1,0:T(8,128)(2,1)} %fusion.4) | copy-start | bytes 589828
  262.7 72.0 %copy-start.8 = (bf16[32,512]{1,0:T(8,128)(2,1)S(1)}, bf16[32,512]{1,0:T(8,128)(2,1)}, u32[]{:S(2)}) copy-start(bf16[32,512]{1,0:T(8,128)(2,1)} %copy-done.7) | copy-start | bytes 98308
  262.7 72.0 %copy-start.10 = (bf16[32,512]{1,0:T(8,128)(2,1)S(1)}, bf16[32,512]{1,0:T(8,128)(2,1)}, u32[]{:S(2)}) copy-start(bf16[32,512]{1,0:T(8,128)(2,1)} %copy-done.9) | copy-start | bytes 98308
  374.8 16.5 %all-to-all-start.14 = ((bf16[32,8,512]{2,1,0:T(8,128)(2,1)}), bf16[32,8,512]{2,1,0:T(8,128)(2,1)}, u32[]{:S(2)}, u32[]{:S(2)}) async-start(bf16[32,8,512]{2,1,0:T(8,128)(2,1)} %fusion.5), calls=%async_computation.14 | async-start | bytes 524288 | tf_op jit(solution)/shard_map/all_to_all | solution.py:26
Sparse Core Ops, SparseCore 0:
  31.7 85.3 all-gather.1

commit v8 on v6

--- a/solution.py
+++ b/solution.py
@@ -15,6 +15,7 @@
 TOK = ("line", "ring")
 MDL = ("chip", "core")
 THIN = 128
+ERR_PARTS = 4
 
 
 def gather_blocks(own, axis):
@@ -126,14 +127,14 @@
     act_clip = token_code.astype(jnp.float32)[:, None] * 0.5
     act_tanh = jnp.tanh(rotated / act_clip)
     quant_act = (act_clip * act_tanh).astype(jnp.bfloat16)
-    half = channels // 2
-    weight_halves = weight_full.reshape(2, half, narrow)
+    part = channels // ERR_PARTS
+    weight_parts = weight_full.reshape(ERR_PARTS, part, narrow)
     partial_err = (
-        jnp.einsum("td,hcd->htc", quant_act, weight_halves, preferred_element_type=jnp.float32)
-        - plain.reshape(tok_rows, 2, half).transpose(1, 0, 2)
+        jnp.einsum("td,hcd->htc", quant_act, weight_parts, preferred_element_type=jnp.float32)
+        - plain.reshape(tok_rows, ERR_PARTS, part).transpose(1, 0, 2)
     )
-    own_err = sum_blocks(partial_err.reshape(n_mdl, -1, half), MDL)
-    err_bf = gather_blocks(own_err.astype(jnp.bfloat16), MDL).reshape(2, tok_rows, half)
+    own_err = sum_blocks(partial_err.reshape(n_mdl, -1, part), MDL)
+    err_bf = gather_blocks(own_err.astype(jnp.bfloat16), MDL).reshape(ERR_PARTS, tok_rows, part)
     recon_error = err_bf.transpose(1, 0, 2).reshape(tok_rows, channels).astype(jnp.float32)
     grad_quant = sum_blocks(
         jnp.einsum("htc,td->hcd", err_bf, quant_act, preferred_element_type=jnp.float32)
@@ -142,8 +143,8 @@
         TOK,
     )
     grad_act = sum(
-        jnp.dot(err_half, weight_half, preferred_element_type=jnp.float32)
-        for err_half, weight_half in zip(err_bf, weight_halves)
+        jnp.dot(err_part, weight_part, preferred_element_type=jnp.float32)
+        for err_part, weight_part in zip(err_bf, weight_parts)
     )
     grad_act = (grad_act * (1.0 - act_tanh * act_tanh)).astype(jnp.bfloat16)
     grad_turned = (grad_quant * (1.0 - weight_tanh * weight_tanh)).astype(jnp.bfloat16)

time: 389 us -> 389 us (level)
  no operation moved by 1% of the time
where the time goes in v8:
time: 389 us; the launch traced here: 387 us
  blocking collectives  152 us (39%)
  waiting for transfers between devices  125 us (32%)
  starting transfers between devices  44.6 us (11%)
  matrix products  25.8 us (7%)
  local copies, waits for them, and re-layouts  14.5 us (4%)
  between operations  14.5 us (4%)
  other arithmetic  10.3 us (3%)
    all_to_all x4, blocking collectives, sum_blocks(): return jnp.sum(lax.all_to_all(blocks, axis, 0, 0).astype(jnp.float32), 0)  85.5 us
    all_to_all x4, waiting for transfers between devices, gather_blocks(): lax.all_to_all(jnp.broadcast_to(own[None], (parts,) + own.shape), axis, 0...  70.7 us
    all_to_all x4, blocking collectives, gather_blocks(): lax.all_to_all(jnp.broadcast_to(own[None], (parts,) + own.shape), axis, 0...  66.8 us
    all_to_all x4, starting transfers between devices, gather_blocks(): lax.all_to_all(jnp.broadcast_to(own[None], (parts,) + own.shape), axis, 0...  33 us
    all_to_all x2, waiting for transfers between devices, sum_blocks(): return jnp.sum(lax.all_to_all(blocks, axis, 0, 0).astype(jnp.float32), 0)  31.7 us
    all_gather x1, waiting for transfers between devices, gather_rotation(): near = lax.all_gather(rot_b, 'ring', axis=0, tiled=True)  15.6 us
    dot_general x6, matrix products, times_rotation(): jnp.dot(pick_other(k, spans, line_pos), far[k], preferred_element_type=jn...  12.4 us
    all_to_all x2, starting transfers between devices, sum_blocks(): return jnp.sum(lax.all_to_all(blocks, axis, 0, 0).astype(jnp.float32), 0)  11.6 us
  transfers between devices with their start and end apart: 8, of which 8 were waited for; matrix products, arithmetic and copies ran while one was open for 7% of the time, Pallas kernels for 0%

profile of v8, /device:TPU:8, one launch (start us, length us, event | category | flops | bytes accessed | tf_op | source)
XLA Modules:
  0.0 386.9 jit_solution(3428467526587186487)
XLA Ops:
  7.2 1.8 convert_element_type.82
  9.1 0.9 slice.156
  10.0 0.9 broadcast_in_dim.17
  11.0 9.3 %all-to-all-start.1 = ((bf16[4,256,384]{2,1,0:T(8,128)(2,1)}), bf16[4,256,384]{2,1,0:T(8,128)(2,1)S(1)}, u32[]{:S(2)}, u32[]{:S(2)}) async-start(bf16[4,256,384]{2,1,0:T(8,128)(2,1)} %broadcast_in_dim.17), calls=%async_computation.1 | async-start | bytes 1572864 | tf_op jit(solution)/shard_map/all_to_all | solution.py:23
  20.3 12.9 %all-to-all-done.1 = bf16[4,256,384]{2,1,0:T(8,128)(2,1)S(1)} async-done(((bf16[4,256,384]{2,1,0:T(8,128)(2,1)}), bf16[4,256,384]{2,1,0:T(8,128)(2,1)S(1)}, u32[]{:S(2)}, u32[]{:S(2)}) %all-to-all-start.1) | async-done | bytes 786464 | tf_op jit(solution)/shard_map/all_to_all | solution.py:23
  35.2 8.5 %all-to-all-start.2 = ((bf16[16,32,512]{2,1,0:T(8,128)(2,1)}), bf16[16,32,512]{2,1,0:T(8,128)(2,1)S(1)}, u32[]{:S(2)}, u32[]{:S(2)}) async-start(bf16[16,32,512]{2,1,0:T(8,128)(2,1)} %broadcast_in_dim.18), calls=%async_computation.2 | async-start | bytes 1048576 | tf_op jit(solution)/shard_map/all_to_all | solution.py:23
  43.8 15.6 %all-gather.3.cloned.1.call-done = bf16[2048,512]{1,0:T(8,128)(2,1)} async-done(((bf16[256,512]{1,0:T(8,128)(2,1)}), bf16[2048,512]{1,0:T(8,128)(2,1)}) %all-gather.3.cloned.1.call-update) | async-done | bytes 2097168 | tf_op jit(solution)/shard_map/all_gather | solution.py:53
  59.3 1.1 slice.155
  60.9 1.7 broadcast_in_dim.16
  62.6 7.4 %all-to-all-start = ((bf16[4,2048,128]{2,1,0:T(8,128)(2,1)}), bf16[4,2048,128]{2,1,0:T(8,128)(2,1)S(1)}, u32[]{:S(2)}, u32[]{:S(2)}) async-start(bf16[4,2048,128]{2,1,0:T(8,128)(2,1)} %broadcast_in_dim.16), calls=%async_computation | async-start | bytes 4194304 | tf_op jit(solution)/shard_map/all_to_all | solution.py:23
  70.8 1.9 copy.20
  72.6 42.2 %all-to-all-done = bf16[4,2048,128]{2,1,0:T(8,128)(2,1)S(1)} async-done(((bf16[4,2048,128]{2,1,0:T(8,128)(2,1)}), bf16[4,2048,128]{2,1,0:T(8,128)(2,1)S(1)}, u32[]{:S(2)}, u32[]{:S(2)}) %all-to-all-start) | async-done | bytes 2097184 | tf_op jit(solution)/shard_map/all_to_all | solution.py:23
  114.8 1.5 fusion.115
  116.3 7.0 %all-gather.5.cloned.1.call-done = bf16[3,2048,384]{2,1,0:T(8,128)(2,1)} async-done(((bf16[3,256,384]{2,1,0:T(8,128)(2,1)}), bf16[3,2048,384]{2,1,0:T(8,128)(2,1)}) %all-gather.5.cloned.1.call-update) | async-done | bytes 4718608 | tf_op jit(solution)/shard_map/all_gather | solution.py:55
  123.3 1.9 fusion.1
  125.2 2.0 fusion
  127.2 1.7 fusion.2
  130.1 1.1 broadcast_in_dim.19
  131.2 7.8 %all-to-all-start.3 = ((bf16[32,32,512]{2,1,0:T(8,128)(2,1)}), bf16[32,32,512]{2,1,0:T(8,128)(2,1)}, u32[]{:S(2)}, u32[]{:S(2)}) async-start(bf16[32,32,512]{2,1,0:T(8,128)(2,1)} %broadcast_in_dim.19), calls=%async_computation.3 | async-start | bytes 2097152 | tf_op jit(solution)/shard_map/all_to_all | solution.py:23
  139.6 2.2 fusion.66
  141.7 2.6 fusion.7
  144.6 2.1 fusion.9
  147.5 2.0 fusion.26
  149.5 1.0 convolution_bitcast_fusion.1
  150.5 15.2 %all-to-all-done.3 = bf16[32,32,512]{2,1,0:T(8,128)(2,1)} async-done(((bf16[32,32,512]{2,1,0:T(8,128)(2,1)}), bf16[32,32,512]{2,1,0:T(8,128)(2,1)}, u32[]{:S(2)}, u32[]{:S(2)}) %all-to-all-start.3) | async-done | bytes 1048608 | tf_op jit(solution)/shard_map/all_to_all | solution.py:23
  165.7 2.0 fusion.16
  167.7 32.6 %all_to_all.70 = f32[16,48,256]{2,1,0:T(8,128)} all-to-all(f32[16,48,256]{2,1,0:T(8,128)S(1)} %bitcast.146), channel_id=1, replica_groups=mesh['line'=4,'ring'=8,'chip'=8,'core'=2] {'chip','core'}, dimensions={0} | all-to-all | bytes 1572864 | tf_op jit(solution)/shard_map/all_to_all | solution.py:27
  200.3 1.2 reduce_sum.54
  201.5 18.7 %all_to_all.71 = bf16[16,48,256]{2,1,0:T(8,128)(2,1)S(1)} all-to-all(bf16[16,48,256]{2,1,0:T(8,128)(2,1)S(1)} %broadcast_in_dim.20), channel_id=1, replica_groups=mesh['line'=4,'ring'=8,'chip'=8,'core'=2] {'chip','core'}, dimensions={0} | all-to-all | bytes 786432 | tf_op jit(solution)/shard_map/all_to_all | solution.py:23
  220.2 2.5 convolution_convert_fusion
  222.7 6.8 %all-to-all-start.6 = ((bf16[32,32,512]{2,1,0:T(8,128)(2,1)}), bf16[32,32,512]{2,1,0:T(8,128)(2,1)}, u32[]{:S(2)}, u32[]{:S(2)}) async-start(bf16[32,32,512]{2,1,0:T(8,128)(2,1)} %bitcast.138), calls=%async_computation.6 | async-start | bytes 2097152 | tf_op jit(solution)/shard_map/all_to_all | solution.py:27
  229.5 1.0 slice.167
  230.5 0.9 slice.166
  231.5 1.0 fusion.63
  232.6 1.3 fusion.113
  235.1 21.2 %all-to-all-done.6 = bf16[32,32,512]{2,1,0:T(8,128)(2,1)} async-done(((bf16[32,32,512]{2,1,0:T(8,128)(2,1)}), bf16[32,32,512]{2,1,0:T(8,128)(2,1)}, u32[]{:S(2)}, u32[]{:S(2)}) %all-to-all-start.6) | async-done | bytes 1048608 | tf_op jit(solution)/shard_map/all_to_all | solution.py:27
  256.3 1.4 convert_reduce_fusion
  258.3 17.5 %all_to_all.72 = bf16[16,16,448]{2,1,0:T(8,128)(2,1)S(1)} all-to-all(bf16[16,16,448]{2,1,0:T(8,128)(2,1)S(1)} %bitcast.139), channel_id=1, replica_groups=mesh['line'=4,'ring'=8,'chip'=8,'core'=2] {'chip','core'}, dimensions={0} | all-to-all | bytes 458752 | tf_op jit(solution)/shard_map/all_to_all | solution.py:27
  275.9 15.9 %all_to_all.73 = bf16[16,16,448]{2,1,0:T(8,128)(2,1)S(1)} all-to-all(bf16[16,16,448]{2,1,0:T(8,128)(2,1)S(1)} %broadcast_in_dim.21), channel_id=1, replica_groups=mesh['line'=4,'ring'=8,'chip'=8,'core'=2] {'chip','core'}, dimensions={0} | all-to-all | bytes 458752 | tf_op jit(solution)/shard_map/all_to_all | solution.py:23
  292.3 17.6 %all_to_all.74 = bf16[32,8,512]{2,1,0:T(8,128)(2,1)S(1)} all-to-all(bf16[32,8,512]{2,1,0:T(8,128)(2,1)S(1)} %fusion.31), channel_id=1, replica_groups=mesh['line'=4,'ring'=8,'chip'=8,'core'=2] {'line','ring'}, dimensions={0} | all-to-all | bytes 524288 | tf_op jit(solution)/shard_map/all_to_all | solution.py:27
  310.7 16.3 %all_to_all.75 = bf16[32,8,512]{2,1,0:T(8,128)(2,1)S(1)} all-to-all(bf16[32,8,512]{2,1,0:T(8,128)(2,1)S(1)} %broadcast_in_dim.22), channel_id=1, replica_groups=mesh['line'=4,'ring'=8,'chip'=8,'core'=2] {'line','ring'}, dimensions={0} | all-to-all | bytes 524288 | tf_op jit(solution)/shard_map/all_to_all | solution.py:23
  327.4 17.8 %all_to_all.76 = bf16[16,16,448]{2,1,0:T(8,128)(2,1)S(1)} all-to-all(bf16[16,16,448]{2,1,0:T(8,128)(2,1)S(1)} %bitcast.140), channel_id=1, replica_groups=mesh['line'=4,'ring'=8,'chip'=8,'core'=2] {'chip','core'}, dimensions={0} | all-to-all | bytes 458752 | tf_op jit(solution)/shard_map/all_to_all | solution.py:27
  345.3 15.9 %all_to_all.77 = bf16[16,16,448]{2,1,0:T(8,128)(2,1)S(1)} all-to-all(bf16[16,16,448]{2,1,0:T(8,128)(2,1)S(1)} %broadcast_in_dim.23), channel_id=1, replica_groups=mesh['line'=4,'ring'=8,'chip'=8,'core'=2] {'chip','core'}, dimensions={0} | all-to-all | bytes 458752 | tf_op jit(solution)/shard_map/all_to_all | solution.py:23
  361.4 1.0 fusion.30
  362.4 4.8 %all-to-all-start.13 = ((bf16[32,8,512]{2,1,0:T(8,128)(2,1)}), bf16[32,8,512]{2,1,0:T(8,128)(2,1)S(1)}, u32[]{:S(2)}, u32[]{:S(2)}) async-start(bf16[32,8,512]{2,1,0:T(8,128)(2,1)} %fusion.30), calls=%async_computation.13 | async-start | bytes 524288 | tf_op jit(solution)/shard_map/all_to_all | solution.py:27
  367.3 1.0 copy.21
  368.2 10.5 %all-to-all-done.13 = bf16[32,8,512]{2,1,0:T(8,128)(2,1)S(1)} async-done(((bf16[32,8,512]{2,1,0:T(8,128)(2,1)}), bf16[32,8,512]{2,1,0:T(8,128)(2,1)S(1)}, u32[]{:S(2)}, u32[]{:S(2)}) %all-to-all-start.13) | async-done | bytes 262176 | tf_op jit(solution)/shard_map/all_to_all | solution.py:27
  378.7 1.3 multiply_subtract_fusion
  (73 shorter events, 9.9 us)
Async XLA Ops:
  7.2 27.0 %copy-start = (bf16[512,1024]{1,0:T(8,128)(2,1)S(1)}, bf16[512,1024]{1,0:T(8,128)(2,1)}, u32[]{:S(2)}) copy-start(bf16[512,1024]{1,0:T(8,128)(2,1)} %param.7) | copy-start | bytes 3145732
  7.2 52.2 %all-gather.3.cloned.1.call-start = ((), (), s32[]{:S(2)}) async-start(), calls=%async_computation.14 | async-start | bytes 2359296 | tf_op jit(solution)/shard_map/all_gather | solution.py:53
  11.0 22.2 %all-to-all-start.1 = ((bf16[4,256,384]{2,1,0:T(8,128)(2,1)}), bf16[4,256,384]{2,1,0:T(8,128)(2,1)S(1)}, u32[]{:S(2)}, u32[]{:S(2)}) async-start(bf16[4,256,384]{2,1,0:T(8,128)(2,1)} %broadcast_in_dim.17), calls=%async_computation.1 | async-start | bytes 1572864 | tf_op jit(solution)/shard_map/all_to_all | solution.py:23
  20.3 103.0 %all-gather.5.cloned.1.call-start = ((), (), s32[]{:S(2)}) async-start(), calls=%async_computation.15 | async-start | bytes 5308416 | tf_op jit(solution)/shard_map/all_gather | solution.py:55
  35.2 25.7 %all-to-all-start.2 = ((bf16[16,32,512]{2,1,0:T(8,128)(2,1)}), bf16[16,32,512]{2,1,0:T(8,128)(2,1)S(1)}, u32[]{:S(2)}, u32[]{:S(2)}) async-start(bf16[16,32,512]{2,1,0:T(8,128)(2,1)} %broadcast_in_dim.18), calls=%async_computation.2 | async-start | bytes 1048576 | tf_op jit(solution)/shard_map/all_to_all | solution.py:23
  60.9 1.7 copy-start.3
  62.6 52.2 %all-to-all-start = ((bf16[4,2048,128]{2,1,0:T(8,128)(2,1)}), bf16[4,2048,128]{2,1,0:T(8,128)(2,1)S(1)}, u32[]{:S(2)}, u32[]{:S(2)}) async-start(bf16[4,2048,128]{2,1,0:T(8,128)(2,1)} %broadcast_in_dim.16), calls=%async_computation | async-start | bytes 4194304 | tf_op jit(solution)/shard_map/all_to_all | solution.py:23
  70.8 58.6 %copy-start.12 = (f32[32]{0:T(128)}, f32[32]{0:T(128)S(1)}, u32[]{:S(2)}) copy-start(f32[32]{0:T(128)S(1)} %convert_multiply_fusion.1) | copy-start | bytes 388
  123.3 4.0 %copy-start.2 = (bf16[16,4,8,512]{3,2,0,1:T(8,128)(2,1)S(1)}, bf16[16,4,8,512]{3,2,0,1:T(8,128)(2,1)}, u32[]{:S(2)}) copy-start(bf16[16,4,8,512]{3,2,0,1:T(8,128)(2,1)} %copy.20) | copy-start | bytes 1572868
  125.2 3.8 copy-start.8
  129.3 0.6 copy-start.10
  130.0 9.0 %copy-start.14 = (s32[192]{0:T(256)S(1)}, s32[192]{0:T(256)}, u32[]{:S(2)}) copy-start(s32[192]{0:T(256)} %param.8) | copy-start | bytes 2308
  131.2 34.5 %all-to-all-start.3 = ((bf16[32,32,512]{2,1,0:T(8,128)(2,1)}), bf16[32,32,512]{2,1,0:T(8,128)(2,1)}, u32[]{:S(2)}, u32[]{:S(2)}) async-start(bf16[32,32,512]{2,1,0:T(8,128)(2,1)} %broadcast_in_dim.19), calls=%async_computation.3 | async-start | bytes 2097152 | tf_op jit(solution)/shard_map/all_to_all | solution.py:23
  141.7 2.8 copy-start.1
  144.6 2.2 copy-start.9
  149.5 16.2 %copy-start.6 = (f32[192,384]{1,0:T(8,128)}, f32[192,384]{1,0:T(8,128)S(1)}, u32[]{:S(2)}) copy-start(f32[192,384]{1,0:T(8,128)S(1)} %fusion.26) | copy-start | bytes 884740
  150.5 49.7 %copy-start.4 = (f32[192,128]{1,0:T(8,128)}, f32[192,128]{1,0:T(8,128)S(1)}, u32[]{:S(2)}) copy-start(f32[192,128]{1,0:T(8,128)S(1)} %convolution_bitcast_fusion.1) | copy-start | bytes 294916
  222.7 33.6 %all-to-all-start.6 = ((bf16[32,32,512]{2,1,0:T(8,128)(2,1)}), bf16[32,32,512]{2,1,0:T(8,128)(2,1)}, u32[]{:S(2)}, u32[]{:S(2)}) async-start(bf16[32,32,512]{2,1,0:T(8,128)(2,1)} %bitcast.138), calls=%async_computation.6 | async-start | bytes 2097152 | tf_op jit(solution)/shard_map/all_to_all | solution.py:27
  233.9 0.9 copy-start.5
  233.9 1.0 copy-start.7
  233.9 1.0 copy-start.15
  234.4 23.3 %copy-start.11 = (f32[32,384]{1,0:T(8,128)S(1)}, f32[32,384]{1,0:T(8,128)}, u32[]{:S(2)}) copy-start(f32[32,384]{1,0:T(8,128)} %copy-done.10) | copy-start | bytes 147460
  234.4 23.3 %copy-start.13 = (f32[32]{0:T(128)S(1)}, f32[32]{0:T(128)}, u32[]{:S(2)}) copy-start(f32[32]{0:T(128)} %copy-done.12) | copy-start | bytes 388
  362.4 16.3 %all-to-all-start.13 = ((bf16[32,8,512]{2,1,0:T(8,128)(2,1)}), bf16[32,8,512]{2,1,0:T(8,128)(2,1)S(1)}, u32[]{:S(2)}, u32[]{:S(2)}) async-start(bf16[32,8,512]{2,1,0:T(8,128)(2,1)} %fusion.30), calls=%async_computation.13 | async-start | bytes 524288 | tf_op jit(solution)/shard_map/all_to_all | solution.py:27
Sparse Core Ops, SparseCore 0:
  10.1 49.2 all-gather.2
  62.0 61.2 all-gather.4

commit v9 on v7

--- a/solution.py
+++ b/solution.py
@@ -50,17 +50,21 @@
 
 def gather_by_doubling(own):
     held = own[None]
-    for axis in ("core", "chip"):
+    bits = 0
+    for axis in MDL:
         size = lax.axis_size(axis)
-        span = 1
-        while span < size:
+        span = size // 2
+        while span > 0:
             came = lax.ppermute(held, axis, [(k, k ^ span) for k in range(size)])
             upper = (lax.axis_index(axis) // span) % 2 == 1
             held = jnp.concatenate(
                 [jnp.where(upper, came, held), jnp.where(upper, held, came)], 0
             )
-            span *= 2
-    return held
+            span //= 2
+            bits += 1
+    held = held.reshape((2,) * bits + own.shape)
+    order = (bits,) + tuple(range(bits - 1, -1, -1)) + (bits + 1,)
+    return held.transpose(order).reshape(own.shape[0], -1)
 
 
 def gather_rotation(rot_b):
@@ -103,7 +107,7 @@
     thin, wide, ring_thin = gather_rotation(rot_b)
     value_late, _ = lax.optimization_barrier((value_weight, ring_thin))
     own_cols = lax.dynamic_slice_in_dim(value_late, tok_pos * chan_share, chan_share, 1)
-    weight_rows = gather_by_doubling(own_cols.T).transpose(1, 0, 2).reshape(chan_share, model_width)
+    weight_rows = gather_by_doubling(own_cols.T)
     own_feats = lax.dynamic_slice_in_dim(activations, mdl_pos * narrow, narrow, 1)
     plain = jnp.dot(own_feats, value_weight, preferred_element_type=jnp.float32)
 
@@ -115,7 +119,7 @@
     thin, wide, quant_late = lax.optimization_barrier((thin, wide, quant_weight))
     weight_full = gather_blocks(quant_late, TOK).reshape(channels, narrow)
     rotated = times_rotation(activations, thin, wide) / width_root
-    window = first_rows(thin, wide, rotation.shape[0])
+    window = lax.optimization_barrier(first_rows(thin, wide, rotation.shape[0]))
     act_clip = token_code.astype(jnp.float32)[:, None] * 0.5
     act_tanh = jnp.tanh(rotated / act_clip)
     quant_act = (act_clip * act_tanh).astype(jnp.bfloat16)
@@ -125,9 +129,9 @@
         jnp.einsum("td,hcd->htc", quant_act, weight_halves, preferred_element_type=jnp.float32)
         - plain.reshape(tok_rows, 2, half).transpose(1, 0, 2)
     )
-    own_err = sum_blocks(partial_err.reshape(n_mdl, -1, half), ("core", "chip"))
-    err_bf = gather_blocks(own_err.astype(jnp.bfloat16), "chip").reshape(tok_rows, half)
-    err_bf = gather_blocks(err_bf, "core")
+    core_err = sum_blocks(partial_err, "core")
+    own_err = sum_blocks(core_err.reshape(lax.axis_size("chip"), -1, half), "chip")
+    err_bf = gather_blocks(own_err.astype(jnp.bfloat16), ("core", "chip")).reshape(2, tok_rows, half)
     recon_error = err_bf.transpose(1, 0, 2).reshape(tok_rows, channels).astype(jnp.float32)
     grad_quant = sum_blocks(
         jnp.einsum("htc,td->hcd", err_bf, quant_act, preferred_element_type=jnp.float32)

time: 402 us -> 407 us (1.012)
  starting transfers between devices: 56.7 us -> 68 us
  blocking collectives: 183 us -> 175 us
    all_to_all x3, waiting for transfers between devices: 45.1 us -> 30.6 us  [gather_blocks(): lax.all_to_all(jnp.broadcast_to(own[None], (parts,) + own.shape), axis, 0...]
    ppermute x4, waiting for transfers between devices: 13.3 us -> 24.3 us  [gather_by_doubling(): came = lax.ppermute(held, axis, [(k, k ^ span) for k in range(size)])]
    all_to_all x3, starting transfers between devices: 28.4 us -> 39.3 us  [gather_blocks(): lax.all_to_all(jnp.broadcast_to(own[None], (parts,) + own.shape), axis, 0...]
    all_to_all x4 -> x5, blocking collectives: 89.4 us -> 81.4 us  [sum_blocks(): return jnp.sum(lax.all_to_all(blocks, axis, 0, 0).astype(jnp.float32), 0)]
    all_to_all x6 -> x5, blocking collectives: 93.3 us -> 93.7 us  [gather_blocks(): lax.all_to_all(jnp.broadcast_to(own[None], (parts,) + own.shape), axis, 0...]
  transfers between devices with their start and end apart: 10 -> 10, of which waited for: 9 -> 8; matrix products, arithmetic and copies ran while one was open for 6% -> 7% of each run, Pallas kernels for 0% -> 0%
where the time goes in v9:
time: 407 us; the launch traced here: 405 us
  blocking collectives  175 us (43%)
  waiting for transfers between devices  85.2 us (21%)
  starting transfers between devices  68 us (17%)
  matrix products  27.5 us (7%)
  local copies, waits for them, and re-layouts  19.1 us (5%)
  other arithmetic  16 us (4%)
  between operations  14.5 us (4%)
    all_to_all x5, blocking collectives, gather_blocks(): lax.all_to_all(jnp.broadcast_to(own[None], (parts,) + own.shape), axis, 0...  93.7 us
    all_to_all x5, blocking collectives, sum_blocks(): return jnp.sum(lax.all_to_all(blocks, axis, 0, 0).astype(jnp.float32), 0)  81.4 us
    all_to_all x3, starting transfers between devices, gather_blocks(): lax.all_to_all(jnp.broadcast_to(own[None], (parts,) + own.shape), axis, 0...  39.3 us
    all_to_all x3, waiting for transfers between devices, gather_blocks(): lax.all_to_all(jnp.broadcast_to(own[None], (parts,) + own.shape), axis, 0...  30.6 us
    all_to_all x2, waiting for transfers between devices, sum_blocks(): return jnp.sum(lax.all_to_all(blocks, axis, 0, 0).astype(jnp.float32), 0)  30.3 us
    ppermute x4, waiting for transfers between devices, gather_by_doubling(): came = lax.ppermute(held, axis, [(k, k ^ span) for k in range(size)])  24.3 us
    ppermute x4, starting transfers between devices, gather_by_doubling(): came = lax.ppermute(held, axis, [(k, k ^ span) for k in range(size)])  17.4 us
    all_to_all x2, starting transfers between devices, sum_blocks(): return jnp.sum(lax.all_to_all(blocks, axis, 0, 0).astype(jnp.float32), 0)  11.3 us
  transfers between devices with their start and end apart: 10, of which 8 were waited for; matrix products, arithmetic and copies ran while one was open for 7% of the time, Pallas kernels for 0%

profile of v9, /device:TPU:8, one launch (start us, length us, event | category | flops | bytes accessed | tf_op | source)
XLA Modules:
  0.0 405.4 jit_solution(8560960300403649271)
XLA Ops:
  7.2 1.2 convert_element_type.82
  9.4 10.0 %all-to-all-start = ((bf16[4,256,384]{2,1,0:T(8,128)(2,1)}), bf16[4,256,384]{2,1,0:T(8,128)(2,1)}, u32[]{:S(2)}, u32[]{:S(2)}) async-start(bf16[4,256,384]{2,1,0:T(8,128)(2,1)} %broadcast_in_dim.20), calls=%async_computation | async-start | bytes 1572864 | tf_op jit(solution)/shard_map/all_to_all | solution.py:22
  19.4 12.2 %all-to-all-done = bf16[4,256,384]{2,1,0:T(8,128)(2,1)} async-done(((bf16[4,256,384]{2,1,0:T(8,128)(2,1)}), bf16[4,256,384]{2,1,0:T(8,128)(2,1)}, u32[]{:S(2)}, u32[]{:S(2)}) %all-to-all-start) | async-done | bytes 786464 | tf_op jit(solution)/shard_map/all_to_all | solution.py:22
  31.6 26.5 %all_to_all.75 = bf16[8,256,128]{2,1,0:T(8,128)(2,1)S(1)} all-to-all(bf16[8,256,128]{2,1,0:T(8,128)(2,1)S(1)} %broadcast_in_dim.21), channel_id=1, replica_groups=mesh['line'=4,'ring'=8,'chip'=8,'core'=2] {'ring'}, dimensions={0} | all-to-all | bytes 1048576 | tf_op jit(solution)/shard_map/all_to_all | solution.py:22
  58.2 1.7 broadcast_in_dim.23
  59.8 9.4 %all-to-all-start.2 = ((bf16[4,2048,128]{2,1,0:T(8,128)(2,1)}), bf16[4,2048,128]{2,1,0:T(8,128)(2,1)}, u32[]{:S(2)}, u32[]{:S(2)}) async-start(bf16[4,2048,128]{2,1,0:T(8,128)(2,1)} %broadcast_in_dim.23), calls=%async_computation.2 | async-start | bytes 4194304 | tf_op jit(solution)/shard_map/all_to_all | solution.py:22
  70.4 7.1 %collective-permute-start = (bf16[1,32,512]{2,1,0:T(8,128)(2,1)S(1)}, bf16[1,32,512]{2,1,0:T(8,128)(2,1)S(1)}, u32[]{:S(2)}, u32[]{:S(2)}) collective-permute-start(bf16[1,32,512]{2,1,0:T(8,128)(2,1)S(1)} %bitcast.100), channel_id=1, source_target_pairs={{0,8},{2,10},{4,12},{6,14},{8,0},{10,2},{12,4},{14,6},{1,9},{3,11}... | collective-permute-start | bytes 98312 | tf_op jit(solution)/shard_map/ppermute | solution.py:58
  77.5 17.0 %collective-permute-done = bf16[1,32,512]{2,1,0:T(8,128)(2,1)S(1)} collective-permute-done((bf16[1,32,512]{2,1,0:T(8,128)(2,1)S(1)}, bf16[1,32,512]{2,1,0:T(8,128)(2,1)S(1)}, u32[]{:S(2)}, u32[]{:S(2)}) %collective-permute-start) | collective-permute-done | bytes 32800 | tf_op jit(solution)/shard_map/ppermute | solution.py:58
  94.5 4.9 %collective-permute-start.1 = (bf16[2,32,512]{2,1,0:T(8,128)(2,1)S(1)}, bf16[2,32,512]{2,1,0:T(8,128)(2,1)S(1)}, u32[]{:S(2)}, u32[]{:S(2)}) collective-permute-start(bf16[2,32,512]{2,1,0:T(8,128)(2,1)S(1)} %pad_maximum_fusion.12), channel_id=1, source_target_pairs={{0,4},{2,6},{4,0},{6,2},{8,12},{10,14},{12,8},{14,10},{1,5},{3,7},... | collective-permute-start | bytes 196616 | tf_op jit(solution)/shard_map/ppermute | solution.py:58
  99.5 2.7 collective-permute-done.1
  102.2 3.4 collective-permute-start.2
  105.6 3.5 collective-permute-done.2
  110.9 1.9 collective-permute-start.3
  115.7 1.3 copy.29
  117.0 2.2 reshape.87
  119.2 2.2 fusion.31
  121.4 3.9 fusion.32
  127.2 19.9 %all-to-all-start.3 = ((bf16[32,32,512]{2,1,0:T(8,128)(2,1)}), bf16[32,32,512]{2,1,0:T(8,128)(2,1)}, u32[]{:S(2)}, u32[]{:S(2)}) async-start(bf16[32,32,512]{2,1,0:T(8,128)(2,1)} %broadcast_in_dim.25), calls=%async_computation.3 | async-start | bytes 2097152 | tf_op jit(solution)/shard_map/all_to_all | solution.py:22
  147.7 2.5 fusion.10
  150.2 2.7 convolution_bitcast_fusion.2
  153.6 1.9 convolution_bitcast_fusion.1
  155.5 18.4 %all-to-all-done.3 = bf16[32,32,512]{2,1,0:T(8,128)(2,1)} async-done(((bf16[32,32,512]{2,1,0:T(8,128)(2,1)}), bf16[32,32,512]{2,1,0:T(8,128)(2,1)}, u32[]{:S(2)}, u32[]{:S(2)}) %all-to-all-start.3) | async-done | bytes 1048608 | tf_op jit(solution)/shard_map/all_to_all | solution.py:22
  173.9 2.0 fusion
  175.9 5.1 %all_to_all.76 = f32[2,192,512]{2,1,0:T(8,128)} all-to-all(f32[2,192,512]{2,1,0:T(8,128)S(1)} %fusion), channel_id=1, replica_groups=mesh['line'=4,'ring'=8,'chip'=8,'core'=2] {'core'}, dimensions={0} | all-to-all | bytes 1572864 | tf_op jit(solution)/shard_map/all_to_all | solution.py:26
  181.1 2.0 reduce_sum.63
  183.1 21.7 %all_to_all.77 = f32[8,24,512]{2,1,0:T(8,128)S(1)} all-to-all(f32[8,24,512]{2,1,0:T(8,128)} %bitcast.87), channel_id=1, replica_groups=mesh['line'=4,'ring'=8,'chip'=8,'core'=2] {'chip'}, dimensions={0} | all-to-all | bytes 786432 | tf_op jit(solution)/shard_map/all_to_all | solution.py:26
  206.2 18.8 %all_to_all.78 = bf16[16,24,512]{2,1,0:T(8,128)(2,1)S(1)} all-to-all(bf16[16,24,512]{2,1,0:T(8,128)(2,1)S(1)} %broadcast_in_dim.26), channel_id=1, replica_groups=mesh['line'=4,'ring'=8,'chip'=8,'core'=2] {'core','chip'}, dimensions={0} | all-to-all | bytes 786432 | tf_op jit(solution)/shard_map/all_to_all | solution.py:22
  225.0 2.5 convolution_convert_fusion
  227.5 6.4 %all-to-all-start.7 = ((bf16[32,32,512]{2,1,0:T(8,128)(2,1)}), bf16[32,32,512]{2,1,0:T(8,128)(2,1)}, u32[]{:S(2)}, u32[]{:S(2)}) async-start(bf16[32,32,512]{2,1,0:T(8,128)(2,1)} %bitcast.92), calls=%async_computation.7 | async-start | bytes 2097152 | tf_op jit(solution)/shard_map/all_to_all | solution.py:26
  236.8 1.7 fusion.7
  238.4 1.3 fusion.29
  241.0 19.7 %all-to-all-done.7 = bf16[32,32,512]{2,1,0:T(8,128)(2,1)} async-done(((bf16[32,32,512]{2,1,0:T(8,128)(2,1)}), bf16[32,32,512]{2,1,0:T(8,128)(2,1)}, u32[]{:S(2)}, u32[]{:S(2)}) %all-to-all-start.7) | async-done | bytes 1048608 | tf_op jit(solution)/shard_map/all_to_all | solution.py:26
  260.8 1.4 convert_reduce_fusion
  263.7 2.1 convolution_convert_fusion.2
  265.8 1.8 copy.21
  267.6 18.4 %all_to_all.79 = bf16[16,16,448]{2,1,0:T(8,128)(2,1)S(1)} all-to-all(bf16[16,16,448]{2,1,0:T(8,128)(2,1)} %bitcast.93), channel_id=1, replica_groups=mesh['line'=4,'ring'=8,'chip'=8,'core'=2] {'chip','core'}, dimensions={0} | all-to-all | bytes 458752 | tf_op jit(solution)/shard_map/all_to_all | solution.py:26
  286.0 16.0 %all_to_all.80 = bf16[16,16,448]{2,1,0:T(8,128)(2,1)S(1)} all-to-all(bf16[16,16,448]{2,1,0:T(8,128)(2,1)S(1)} %broadcast_in_dim.27), channel_id=1, replica_groups=mesh['line'=4,'ring'=8,'chip'=8,'core'=2] {'chip','core'}, dimensions={0} | all-to-all | bytes 458752 | tf_op jit(solution)/shard_map/all_to_all | solution.py:22
  303.2 1.2 fusion.6
  304.4 17.9 %all_to_all.81 = bf16[32,8,512]{2,1,0:T(8,128)(2,1)S(1)} all-to-all(bf16[32,8,512]{2,1,0:T(8,128)(2,1)S(1)} %fusion.6), channel_id=1, replica_groups=mesh['line'=4,'ring'=8,'chip'=8,'core'=2] {'line','ring'}, dimensions={0} | all-to-all | bytes 524288 | tf_op jit(solution)/shard_map/all_to_all | solution.py:26
  323.1 16.5 %all_to_all.82 = bf16[32,8,512]{2,1,0:T(8,128)(2,1)S(1)} all-to-all(bf16[32,8,512]{2,1,0:T(8,128)(2,1)S(1)} %broadcast_in_dim.28), channel_id=1, replica_groups=mesh['line'=4,'ring'=8,'chip'=8,'core'=2] {'line','ring'}, dimensions={0} | all-to-all | bytes 524288 | tf_op jit(solution)/shard_map/all_to_all | solution.py:22
  340.6 1.8 copy.22
  342.4 18.2 %all_to_all.83 = bf16[16,16,448]{2,1,0:T(8,128)(2,1)S(1)} all-to-all(bf16[16,16,448]{2,1,0:T(8,128)(2,1)} %bitcast.94), channel_id=1, replica_groups=mesh['line'=4,'ring'=8,'chip'=8,'core'=2] {'chip','core'}, dimensions={0} | all-to-all | bytes 458752 | tf_op jit(solution)/shard_map/all_to_all | solution.py:26
  360.7 15.9 %all_to_all.84 = bf16[16,16,448]{2,1,0:T(8,128)(2,1)S(1)} all-to-all(bf16[16,16,448]{2,1,0:T(8,128)(2,1)S(1)} %broadcast_in_dim.29), channel_id=1, replica_groups=mesh['line'=4,'ring'=8,'chip'=8,'core'=2] {'chip','core'}, dimensions={0} | all-to-all | bytes 458752 | tf_op jit(solution)/shard_map/all_to_all | solution.py:22
  376.6 1.2 fusion.12
  377.8 1.9 fusion.5
  379.7 4.9 %all-to-all-start.14 = ((bf16[32,8,512]{2,1,0:T(8,128)(2,1)}), bf16[32,8,512]{2,1,0:T(8,128)(2,1)}, u32[]{:S(2)}, u32[]{:S(2)}) async-start(bf16[32,8,512]{2,1,0:T(8,128)(2,1)} %fusion.5), calls=%async_computation.14 | async-start | bytes 524288 | tf_op jit(solution)/shard_map/all_to_all | solution.py:26
  385.7 10.5 %all-to-all-done.14 = bf16[32,8,512]{2,1,0:T(8,128)(2,1)} async-done(((bf16[32,8,512]{2,1,0:T(8,128)(2,1)}), bf16[32,8,512]{2,1,0:T(8,128)(2,1)}, u32[]{:S(2)}, u32[]{:S(2)}) %all-to-all-start.14) | async-done | bytes 262176 | tf_op jit(solution)/shard_map/all_to_all | solution.py:26
  397.2 1.3 multiply_subtract_fusion
  (78 shorter events, 21.9 us)
Async XLA Ops:
  7.2 140.5 %copy-start = (bf16[192,8192]{1,0:T(8,128)(2,1)S(1)}, bf16[192,8192]{1,0:T(8,128)(2,1)}, u32[]{:S(2)}) copy-start(bf16[192,8192]{1,0:T(8,128)(2,1)} %param.5) | copy-start | bytes 9437188
  9.4 22.2 %all-to-all-start = ((bf16[4,256,384]{2,1,0:T(8,128)(2,1)}), bf16[4,256,384]{2,1,0:T(8,128)(2,1)}, u32[]{:S(2)}, u32[]{:S(2)}) async-start(bf16[4,256,384]{2,1,0:T(8,128)(2,1)} %broadcast_in_dim.20), calls=%async_computation | async-start | bytes 1572864 | tf_op jit(solution)/shard_map/all_to_all | solution.py:22
  19.4 102.1 %all-gather.2.cloned.1.call-start = ((), (), s32[]{:S(2)}) async-start(), calls=%async_computation.15 | async-start | bytes 7077888 | tf_op jit(solution)/shard_map/all_gather | solution.py:74
  59.8 59.4 %all-to-all-start.2 = ((bf16[4,2048,128]{2,1,0:T(8,128)(2,1)}), bf16[4,2048,128]{2,1,0:T(8,128)(2,1)}, u32[]{:S(2)}, u32[]{:S(2)}) async-start(bf16[4,2048,128]{2,1,0:T(8,128)(2,1)} %broadcast_in_dim.23), calls=%async_computation.2 | async-start | bytes 4194304 | tf_op jit(solution)/shard_map/all_to_all | solution.py:22
  70.4 24.1 %collective-permute-start = (bf16[1,32,512]{2,1,0:T(8,128)(2,1)S(1)}, bf16[1,32,512]{2,1,0:T(8,128)(2,1)S(1)}, u32[]{:S(2)}, u32[]{:S(2)}) collective-permute-start(bf16[1,32,512]{2,1,0:T(8,128)(2,1)S(1)} %bitcast.100), channel_id=1, source_target_pairs={{0,8},{2,10},{4,12},{6,14},{8,0},{10,2},{12,4},{14,6},{1,9},{3,11}... | collective-permute-start | bytes 98312 | tf_op jit(solution)/shard_map/ppermute | solution.py:58
  94.5 7.7 %collective-permute-start.1 = (bf16[2,32,512]{2,1,0:T(8,128)(2,1)S(1)}, bf16[2,32,512]{2,1,0:T(8,128)(2,1)S(1)}, u32[]{:S(2)}, u32[]{:S(2)}) collective-permute-start(bf16[2,32,512]{2,1,0:T(8,128)(2,1)S(1)} %pad_maximum_fusion.12), channel_id=1, source_target_pairs={{0,4},{2,6},{4,0},{6,2},{8,12},{10,14},{12,8},{14,10},{1,5},{3,7},... | collective-permute-start | bytes 196616 | tf_op jit(solution)/shard_map/ppermute | solution.py:58
  102.2 7.0 %collective-permute-start.2 = (bf16[4,32,512]{2,1,0:T(8,128)(2,1)S(1)}, bf16[4,32,512]{2,1,0:T(8,128)(2,1)}, u32[]{:S(2)}, u32[]{:S(2)}) collective-permute-start(bf16[4,32,512]{2,1,0:T(8,128)(2,1)S(1)} %pad_maximum_fusion.9), channel_id=1, source_target_pairs={{0,2},{2,0},{4,6},{6,4},{8,10},{10,8},{12,14},{14,12},{1,3},{3,1},... | collective-permute-start | bytes 393224 | tf_op jit(solution)/shard_map/ppermute | solution.py:58
  110.9 3.8 collective-permute-start.3
  113.6 11.8 %copy-start.13 = (f32[32]{0:T(128)}, f32[32]{0:T(128)S(1)}, u32[]{:S(2)}) copy-start(f32[32]{0:T(128)S(1)} %convert_multiply_fusion.1) | copy-start | bytes 388
  125.4 0.6 copy-start.6
  126.0 21.1 %copy-start.14 = (s32[192]{0:T(256)S(1)}, s32[192]{0:T(256)}, u32[]{:S(2)}) copy-start(s32[192]{0:T(256)} %param.8) | copy-start | bytes 2308
  127.2 46.7 %all-to-all-start.3 = ((bf16[32,32,512]{2,1,0:T(8,128)(2,1)}), bf16[32,32,512]{2,1,0:T(8,128)(2,1)}, u32[]{:S(2)}, u32[]{:S(2)}) async-start(bf16[32,32,512]{2,1,0:T(8,128)(2,1)} %broadcast_in_dim.25), calls=%async_computation.3 | async-start | bytes 2097152 | tf_op jit(solution)/shard_map/all_to_all | solution.py:22
  150.2 3.4 copy-start.1
  153.6 20.4 %copy-start.4 = (f32[192,128]{1,0:T(8,128)}, f32[192,128]{1,0:T(8,128)S(1)}, u32[]{:S(2)}) copy-start(f32[192,128]{1,0:T(8,128)S(1)} %convolution_bitcast_fusion.2) | copy-start | bytes 294916
  155.5 27.6 %copy-start.11 = (f32[192,384]{1,0:T(8,128)}, f32[192,384]{1,0:T(8,128)S(1)}, u32[]{:S(2)}) copy-start(f32[192,384]{1,0:T(8,128)S(1)} %convolution_bitcast_fusion.1) | copy-start | bytes 884740
  227.5 33.3 %all-to-all-start.7 = ((bf16[32,32,512]{2,1,0:T(8,128)(2,1)}), bf16[32,32,512]{2,1,0:T(8,128)(2,1)}, u32[]{:S(2)}, u32[]{:S(2)}) async-start(bf16[32,32,512]{2,1,0:T(8,128)(2,1)} %bitcast.92), calls=%async_computation.7 | async-start | bytes 2097152 | tf_op jit(solution)/shard_map/all_to_all | solution.py:26
  235.0 5.1 %copy-start.5 = (f32[192,128]{1,0:T(8,128)S(1)}, f32[192,128]{1,0:T(8,128)}, u32[]{:S(2)}) copy-start(f32[192,128]{1,0:T(8,128)} %copy-done.4) | copy-start | bytes 294916
  235.0 5.1 %copy-start.12 = (f32[192,384]{1,0:T(8,128)S(1)}, f32[192,384]{1,0:T(8,128)}, u32[]{:S(2)}) copy-start(f32[192,384]{1,0:T(8,128)} %copy-done.11) | copy-start | bytes 884740
  235.0 5.1 %copy-start.15 = (f32[192]{0:T(256)S(1)}, f32[192]{0:T(256)}, u32[]{:S(2)}) copy-start(f32[192]{0:T(256)} %convert_multiply_fusion) | copy-start | bytes 2308
  263.0 0.6 copy-start.7
  263.1 0.6 copy-start.9
  267.5 72.0 %copy-start.2 = (bf16[192,512]{1,0:T(8,128)(2,1)S(1)}, bf16[192,512]{1,0:T(8,128)(2,1)}, u32[]{:S(2)}) copy-start(bf16[192,512]{1,0:T(8,128)(2,1)} %fusion.7) | copy-start | bytes 589828
  267.5 72.0 %copy-start.3 = (bf16[192,512]{1,0:T(8,128)(2,1)S(1)}, bf16[192,512]{1,0:T(8,128)(2,1)}, u32[]{:S(2)}) copy-start(bf16[192,512]{1,0:T(8,128)(2,1)} %fusion.4) | copy-start | bytes 589828
  267.5 72.0 %copy-start.8 = (bf16[32,512]{1,0:T(8,128)(2,1)S(1)}, bf16[32,512]{1,0:T(8,128)(2,1)}, u32[]{:S(2)}) copy-start(bf16[32,512]{1,0:T(8,128)(2,1)} %copy-done.7) | copy-start | bytes 98308
  267.5 72.0 %copy-start.10 = (bf16[32,512]{1,0:T(8,128)(2,1)S(1)}, bf16[32,512]{1,0:T(8,128)(2,1)}, u32[]{:S(2)}) copy-start(bf16[32,512]{1,0:T(8,128)(2,1)} %copy-done.9) | copy-start | bytes 98308
  379.7 16.5 %all-to-all-start.14 = ((bf16[32,8,512]{2,1,0:T(8,128)(2,1)}), bf16[32,8,512]{2,1,0:T(8,128)(2,1)}, u32[]{:S(2)}, u32[]{:S(2)}) async-start(bf16[32,8,512]{2,1,0:T(8,128)(2,1)} %fusion.5), calls=%async_computation.14 | async-start | bytes 524288 | tf_op jit(solution)/shard_map/all_to_all | solution.py:26
Sparse Core Ops, SparseCore 0:
  31.7 85.3 all-gather.1

commit v10 on v6

--- a/solution.py
+++ b/solution.py
@@ -132,8 +132,9 @@
         jnp.einsum("td,hcd->htc", quant_act, weight_halves, preferred_element_type=jnp.float32)
         - plain.reshape(tok_rows, 2, half).transpose(1, 0, 2)
     )
-    own_err = sum_blocks(partial_err.reshape(n_mdl, -1, half), MDL)
-    err_bf = gather_blocks(own_err.astype(jnp.bfloat16), MDL).reshape(2, tok_rows, half)
+    core_err = sum_blocks(partial_err, "core")
+    own_err = sum_blocks(core_err.reshape(lax.axis_size("chip"), -1, half), "chip")
+    err_bf = gather_blocks(own_err.astype(jnp.bfloat16), ("core", "chip")).reshape(2, tok_rows, half)
     recon_error = err_bf.transpose(1, 0, 2).reshape(tok_rows, channels).astype(jnp.float32)
     grad_quant = sum_blocks(
         jnp.einsum("htc,td->hcd", err_bf, quant_act, preferred_element_type=jnp.float32)

time: 389 us -> 387 us (level)
    all_to_all x4 -> x5, blocking collectives: 85.4 us -> 81.5 us  [sum_blocks(): return jnp.sum(lax.all_to_all(blocks, axis, 0, 0).astype(jnp.float32), 0)]
where the time goes in v10:
time: 387 us; the launch traced here: 385 us
  blocking collectives  149 us (39%)
  waiting for transfers between devices  126 us (33%)
  starting transfers between devices  43.8 us (11%)
  matrix products  25.5 us (7%)
  local copies, waits for them, and re-layouts  15 us (4%)
  between operations  14.5 us (4%)
  other arithmetic  11.7 us (3%)
    all_to_all x5, blocking collectives, sum_blocks(): return jnp.sum(lax.all_to_all(blocks, axis, 0, 0).astype(jnp.float32), 0)  81.5 us
    all_to_all x4, waiting for transfers between devices, gather_blocks(): lax.all_to_all(jnp.broadcast_to(own[None], (parts,) + own.shape), axis, 0...  70.7 us
    all_to_all x4, blocking collectives, gather_blocks(): lax.all_to_all(jnp.broadcast_to(own[None], (parts,) + own.shape), axis, 0...  67.4 us
    all_to_all x4, starting transfers between devices, gather_blocks(): lax.all_to_all(jnp.broadcast_to(own[None], (parts,) + own.shape), axis, 0...  33 us
    all_to_all x2, waiting for transfers between devices, sum_blocks(): return jnp.sum(lax.all_to_all(blocks, axis, 0, 0).astype(jnp.float32), 0)  32.2 us
    all_gather x1, waiting for transfers between devices, gather_rotation(): near = lax.all_gather(rot_b, 'ring', axis=0, tiled=True)  15.6 us
    dot_general x6, matrix products, times_rotation(): jnp.dot(pick_other(k, spans, line_pos), far[k], preferred_element_type=jn...  12.4 us
    all_to_all x2, starting transfers between devices, sum_blocks(): return jnp.sum(lax.all_to_all(blocks, axis, 0, 0).astype(jnp.float32), 0)  10.8 us
  transfers between devices with their start and end apart: 8, of which 8 were waited for; matrix products, arithmetic and copies ran while one was open for 7% of the time, Pallas kernels for 0%

profile of v10, /device:TPU:8, one launch (start us, length us, event | category | flops | bytes accessed | tf_op | source)
XLA Modules:
  0.0 385.0 jit_solution(15465728195827704539)
XLA Ops:
  7.2 1.8 convert_element_type.82
  9.1 0.9 slice.152
  10.0 0.9 broadcast_in_dim.17
  11.0 9.3 %all-to-all-start.1 = ((bf16[4,256,384]{2,1,0:T(8,128)(2,1)}), bf16[4,256,384]{2,1,0:T(8,128)(2,1)S(1)}, u32[]{:S(2)}, u32[]{:S(2)}) async-start(bf16[4,256,384]{2,1,0:T(8,128)(2,1)} %broadcast_in_dim.17), calls=%async_computation.1 | async-start | bytes 1572864 | tf_op jit(solution)/shard_map/all_to_all | solution.py:22
  20.3 12.9 %all-to-all-done.1 = bf16[4,256,384]{2,1,0:T(8,128)(2,1)S(1)} async-done(((bf16[4,256,384]{2,1,0:T(8,128)(2,1)}), bf16[4,256,384]{2,1,0:T(8,128)(2,1)S(1)}, u32[]{:S(2)}, u32[]{:S(2)}) %all-to-all-start.1) | async-done | bytes 786464 | tf_op jit(solution)/shard_map/all_to_all | solution.py:22
  35.2 8.5 %all-to-all-start.2 = ((bf16[16,32,512]{2,1,0:T(8,128)(2,1)}), bf16[16,32,512]{2,1,0:T(8,128)(2,1)S(1)}, u32[]{:S(2)}, u32[]{:S(2)}) async-start(bf16[16,32,512]{2,1,0:T(8,128)(2,1)} %broadcast_in_dim.18), calls=%async_computation.2 | async-start | bytes 1048576 | tf_op jit(solution)/shard_map/all_to_all | solution.py:22
  43.8 15.6 %all-gather.3.cloned.1.call-done = bf16[2048,512]{1,0:T(8,128)(2,1)} async-done(((bf16[256,512]{1,0:T(8,128)(2,1)}), bf16[2048,512]{1,0:T(8,128)(2,1)}) %all-gather.3.cloned.1.call-update) | async-done | bytes 2097168 | tf_op jit(solution)/shard_map/all_gather | solution.py:52
  59.3 1.1 slice.151
  60.9 1.7 broadcast_in_dim.16
  62.6 7.4 %all-to-all-start = ((bf16[4,2048,128]{2,1,0:T(8,128)(2,1)}), bf16[4,2048,128]{2,1,0:T(8,128)(2,1)S(1)}, u32[]{:S(2)}, u32[]{:S(2)}) async-start(bf16[4,2048,128]{2,1,0:T(8,128)(2,1)} %broadcast_in_dim.16), calls=%async_computation | async-start | bytes 4194304 | tf_op jit(solution)/shard_map/all_to_all | solution.py:22
  70.8 1.9 copy.26
  72.6 42.2 %all-to-all-done = bf16[4,2048,128]{2,1,0:T(8,128)(2,1)S(1)} async-done(((bf16[4,2048,128]{2,1,0:T(8,128)(2,1)}), bf16[4,2048,128]{2,1,0:T(8,128)(2,1)S(1)}, u32[]{:S(2)}, u32[]{:S(2)}) %all-to-all-start) | async-done | bytes 2097184 | tf_op jit(solution)/shard_map/all_to_all | solution.py:22
  114.8 1.5 fusion.115
  116.3 7.0 %all-gather.5.cloned.1.call-done = bf16[3,2048,384]{2,1,0:T(8,128)(2,1)} async-done(((bf16[3,256,384]{2,1,0:T(8,128)(2,1)}), bf16[3,2048,384]{2,1,0:T(8,128)(2,1)}) %all-gather.5.cloned.1.call-update) | async-done | bytes 4718608 | tf_op jit(solution)/shard_map/all_gather | solution.py:54
  123.3 1.9 fusion.1
  125.2 2.0 fusion
  127.2 1.7 fusion.2
  130.1 1.2 broadcast_in_dim.19
  131.2 7.8 %all-to-all-start.3 = ((bf16[32,32,512]{2,1,0:T(8,128)(2,1)}), bf16[32,32,512]{2,1,0:T(8,128)(2,1)}, u32[]{:S(2)}, u32[]{:S(2)}) async-start(bf16[32,32,512]{2,1,0:T(8,128)(2,1)} %broadcast_in_dim.19), calls=%async_computation.3 | async-start | bytes 2097152 | tf_op jit(solution)/shard_map/all_to_all | solution.py:22
  139.5 2.2 fusion.66
  141.7 2.6 fusion.7
  144.6 2.1 fusion.9
  147.5 2.0 fusion.27
  149.5 1.0 convolution_bitcast_fusion.1
  150.5 15.2 %all-to-all-done.3 = bf16[32,32,512]{2,1,0:T(8,128)(2,1)} async-done(((bf16[32,32,512]{2,1,0:T(8,128)(2,1)}), bf16[32,32,512]{2,1,0:T(8,128)(2,1)}, u32[]{:S(2)}, u32[]{:S(2)}) %all-to-all-start.3) | async-done | bytes 1048608 | tf_op jit(solution)/shard_map/all_to_all | solution.py:22
  165.7 2.0 fusion.16
  167.7 5.2 %all_to_all.75 = f32[2,192,512]{2,1,0:T(8,128)} all-to-all(f32[2,192,512]{2,1,0:T(8,128)S(1)} %fusion.16), channel_id=1, replica_groups=mesh['line'=4,'ring'=8,'chip'=8,'core'=2] {'core'}, dimensions={0} | all-to-all | bytes 1572864 | tf_op jit(solution)/shard_map/all_to_all | solution.py:26
  172.9 2.0 reduce_sum.63
  174.9 23.6 %all_to_all.76 = f32[8,24,512]{2,1,0:T(8,128)S(1)} all-to-all(f32[8,24,512]{2,1,0:T(8,128)} %bitcast.127), channel_id=1, replica_groups=mesh['line'=4,'ring'=8,'chip'=8,'core'=2] {'chip'}, dimensions={0} | all-to-all | bytes 786432 | tf_op jit(solution)/shard_map/all_to_all | solution.py:26
  199.9 19.1 %all_to_all.77 = bf16[16,24,512]{2,1,0:T(8,128)(2,1)S(1)} all-to-all(bf16[16,24,512]{2,1,0:T(8,128)(2,1)S(1)} %broadcast_in_dim.20), channel_id=1, replica_groups=mesh['line'=4,'ring'=8,'chip'=8,'core'=2] {'core','chip'}, dimensions={0} | all-to-all | bytes 786432 | tf_op jit(solution)/shard_map/all_to_all | solution.py:22
  219.0 2.5 convolution_convert_fusion
  221.5 6.0 %all-to-all-start.7 = ((bf16[32,32,512]{2,1,0:T(8,128)(2,1)}), bf16[32,32,512]{2,1,0:T(8,128)(2,1)}, u32[]{:S(2)}, u32[]{:S(2)}) async-start(bf16[32,32,512]{2,1,0:T(8,128)(2,1)} %bitcast.132), calls=%async_computation.7 | async-start | bytes 2097152 | tf_op jit(solution)/shard_map/all_to_all | solution.py:26
  227.5 1.0 slice.163
  229.4 1.0 fusion.63
  230.6 1.3 fusion.113
  232.5 21.8 %all-to-all-done.7 = bf16[32,32,512]{2,1,0:T(8,128)(2,1)} async-done(((bf16[32,32,512]{2,1,0:T(8,128)(2,1)}), bf16[32,32,512]{2,1,0:T(8,128)(2,1)}, u32[]{:S(2)}, u32[]{:S(2)}) %all-to-all-start.7) | async-done | bytes 1048608 | tf_op jit(solution)/shard_map/all_to_all | solution.py:26
  254.3 1.4 convert_reduce_fusion
  256.3 17.4 %all_to_all.78 = bf16[16,16,448]{2,1,0:T(8,128)(2,1)S(1)} all-to-all(bf16[16,16,448]{2,1,0:T(8,128)(2,1)S(1)} %bitcast.133), channel_id=1, replica_groups=mesh['line'=4,'ring'=8,'chip'=8,'core'=2] {'chip','core'}, dimensions={0} | all-to-all | bytes 458752 | tf_op jit(solution)/shard_map/all_to_all | solution.py:26
  273.7 16.0 %all_to_all.79 = bf16[16,16,448]{2,1,0:T(8,128)(2,1)S(1)} all-to-all(bf16[16,16,448]{2,1,0:T(8,128)(2,1)S(1)} %broadcast_in_dim.21), channel_id=1, replica_groups=mesh['line'=4,'ring'=8,'chip'=8,'core'=2] {'chip','core'}, dimensions={0} | all-to-all | bytes 458752 | tf_op jit(solution)/shard_map/all_to_all | solution.py:22
  290.2 17.9 %all_to_all.80 = bf16[32,8,512]{2,1,0:T(8,128)(2,1)S(1)} all-to-all(bf16[32,8,512]{2,1,0:T(8,128)(2,1)S(1)} %fusion.31), channel_id=1, replica_groups=mesh['line'=4,'ring'=8,'chip'=8,'core'=2] {'line','ring'}, dimensions={0} | all-to-all | bytes 524288 | tf_op jit(solution)/shard_map/all_to_all | solution.py:26
  308.9 16.5 %all_to_all.81 = bf16[32,8,512]{2,1,0:T(8,128)(2,1)S(1)} all-to-all(bf16[32,8,512]{2,1,0:T(8,128)(2,1)S(1)} %broadcast_in_dim.22), channel_id=1, replica_groups=mesh['line'=4,'ring'=8,'chip'=8,'core'=2] {'line','ring'}, dimensions={0} | all-to-all | bytes 524288 | tf_op jit(solution)/shard_map/all_to_all | solution.py:22
  325.8 17.5 %all_to_all.82 = bf16[16,16,448]{2,1,0:T(8,128)(2,1)S(1)} all-to-all(bf16[16,16,448]{2,1,0:T(8,128)(2,1)S(1)} %bitcast.134), channel_id=1, replica_groups=mesh['line'=4,'ring'=8,'chip'=8,'core'=2] {'chip','core'}, dimensions={0} | all-to-all | bytes 458752 | tf_op jit(solution)/shard_map/all_to_all | solution.py:26
  343.4 15.8 %all_to_all.83 = bf16[16,16,448]{2,1,0:T(8,128)(2,1)S(1)} all-to-all(bf16[16,16,448]{2,1,0:T(8,128)(2,1)S(1)} %broadcast_in_dim.23), channel_id=1, replica_groups=mesh['line'=4,'ring'=8,'chip'=8,'core'=2] {'chip','core'}, dimensions={0} | all-to-all | bytes 458752 | tf_op jit(solution)/shard_map/all_to_all | solution.py:22
  359.4 1.0 fusion.30
  360.4 4.9 %all-to-all-start.14 = ((bf16[32,8,512]{2,1,0:T(8,128)(2,1)}), bf16[32,8,512]{2,1,0:T(8,128)(2,1)S(1)}, u32[]{:S(2)}, u32[]{:S(2)}) async-start(bf16[32,8,512]{2,1,0:T(8,128)(2,1)} %fusion.30), calls=%async_computation.14 | async-start | bytes 524288 | tf_op jit(solution)/shard_map/all_to_all | solution.py:26
  365.4 1.0 copy.27
  366.3 10.5 %all-to-all-done.14 = bf16[32,8,512]{2,1,0:T(8,128)(2,1)S(1)} async-done(((bf16[32,8,512]{2,1,0:T(8,128)(2,1)}), bf16[32,8,512]{2,1,0:T(8,128)(2,1)S(1)}, u32[]{:S(2)}, u32[]{:S(2)}) %all-to-all-start.14) | async-done | bytes 262176 | tf_op jit(solution)/shard_map/all_to_all | solution.py:26
  376.8 1.3 multiply_subtract_fusion
  (73 shorter events, 11.6 us)
Async XLA Ops:
  7.2 27.0 %copy-start = (bf16[512,1024]{1,0:T(8,128)(2,1)S(1)}, bf16[512,1024]{1,0:T(8,128)(2,1)}, u32[]{:S(2)}) copy-start(bf16[512,1024]{1,0:T(8,128)(2,1)} %param.7) | copy-start | bytes 3145732
  7.2 52.2 %all-gather.3.cloned.1.call-start = ((), (), s32[]{:S(2)}) async-start(), calls=%async_computation.15 | async-start | bytes 2359296 | tf_op jit(solution)/shard_map/all_gather | solution.py:52
  11.0 22.2 %all-to-all-start.1 = ((bf16[4,256,384]{2,1,0:T(8,128)(2,1)}), bf16[4,256,384]{2,1,0:T(8,128)(2,1)S(1)}, u32[]{:S(2)}, u32[]{:S(2)}) async-start(bf16[4,256,384]{2,1,0:T(8,128)(2,1)} %broadcast_in_dim.17), calls=%async_computation.1 | async-start | bytes 1572864 | tf_op jit(solution)/shard_map/all_to_all | solution.py:22
  20.3 103.0 %all-gather.5.cloned.1.call-start = ((), (), s32[]{:S(2)}) async-start(), calls=%async_computation.16 | async-start | bytes 5308416 | tf_op jit(solution)/shard_map/all_gather | solution.py:54
  35.2 25.7 %all-to-all-start.2 = ((bf16[16,32,512]{2,1,0:T(8,128)(2,1)}), bf16[16,32,512]{2,1,0:T(8,128)(2,1)S(1)}, u32[]{:S(2)}, u32[]{:S(2)}) async-start(bf16[16,32,512]{2,1,0:T(8,128)(2,1)} %broadcast_in_dim.18), calls=%async_computation.2 | async-start | bytes 1048576 | tf_op jit(solution)/shard_map/all_to_all | solution.py:22
  60.9 1.7 copy-start.3
  62.6 52.2 %all-to-all-start = ((bf16[4,2048,128]{2,1,0:T(8,128)(2,1)}), bf16[4,2048,128]{2,1,0:T(8,128)(2,1)S(1)}, u32[]{:S(2)}, u32[]{:S(2)}) async-start(bf16[4,2048,128]{2,1,0:T(8,128)(2,1)} %broadcast_in_dim.16), calls=%async_computation | async-start | bytes 4194304 | tf_op jit(solution)/shard_map/all_to_all | solution.py:22
  70.7 58.6 %copy-start.12 = (f32[32]{0:T(128)}, f32[32]{0:T(128)S(1)}, u32[]{:S(2)}) copy-start(f32[32]{0:T(128)S(1)} %convert_multiply_fusion.1) | copy-start | bytes 388
  123.3 4.0 %copy-start.2 = (bf16[16,4,8,512]{3,2,0,1:T(8,128)(2,1)S(1)}, bf16[16,4,8,512]{3,2,0,1:T(8,128)(2,1)}, u32[]{:S(2)}) copy-start(bf16[16,4,8,512]{3,2,0,1:T(8,128)(2,1)} %copy.26) | copy-start | bytes 1572868
  125.2 3.8 copy-start.8
  129.3 0.6 copy-start.10
  130.0 9.0 %copy-start.14 = (s32[192]{0:T(256)S(1)}, s32[192]{0:T(256)}, u32[]{:S(2)}) copy-start(s32[192]{0:T(256)} %param.8) | copy-start | bytes 2308
  131.2 34.5 %all-to-all-start.3 = ((bf16[32,32,512]{2,1,0:T(8,128)(2,1)}), bf16[32,32,512]{2,1,0:T(8,128)(2,1)}, u32[]{:S(2)}, u32[]{:S(2)}) async-start(bf16[32,32,512]{2,1,0:T(8,128)(2,1)} %broadcast_in_dim.19), calls=%async_computation.3 | async-start | bytes 2097152 | tf_op jit(solution)/shard_map/all_to_all | solution.py:22
  141.7 2.8 copy-start.1
  144.6 2.2 copy-start.9
  149.5 16.3 %copy-start.6 = (f32[192,384]{1,0:T(8,128)}, f32[192,384]{1,0:T(8,128)S(1)}, u32[]{:S(2)}) copy-start(f32[192,384]{1,0:T(8,128)S(1)} %fusion.27) | copy-start | bytes 884740
  150.5 22.4 %copy-start.4 = (f32[192,128]{1,0:T(8,128)}, f32[192,128]{1,0:T(8,128)S(1)}, u32[]{:S(2)}) copy-start(f32[192,128]{1,0:T(8,128)S(1)} %convolution_bitcast_fusion.1) | copy-start | bytes 294916
  221.5 32.8 %all-to-all-start.7 = ((bf16[32,32,512]{2,1,0:T(8,128)(2,1)}), bf16[32,32,512]{2,1,0:T(8,128)(2,1)}, u32[]{:S(2)}, u32[]{:S(2)}) async-start(bf16[32,32,512]{2,1,0:T(8,128)(2,1)} %bitcast.132), calls=%async_computation.7 | async-start | bytes 2097152 | tf_op jit(solution)/shard_map/all_to_all | solution.py:26
  230.5 1.7 copy-start.5
  230.5 1.7 copy-start.7
  230.5 1.7 copy-start.15
  232.2 23.5 %copy-start.11 = (f32[32,384]{1,0:T(8,128)S(1)}, f32[32,384]{1,0:T(8,128)}, u32[]{:S(2)}) copy-start(f32[32,384]{1,0:T(8,128)} %copy-done.10) | copy-start | bytes 147460
  232.2 23.5 %copy-start.13 = (f32[32]{0:T(128)S(1)}, f32[32]{0:T(128)}, u32[]{:S(2)}) copy-start(f32[32]{0:T(128)} %copy-done.12) | copy-start | bytes 388
  360.4 16.4 %all-to-all-start.14 = ((bf16[32,8,512]{2,1,0:T(8,128)(2,1)}), bf16[32,8,512]{2,1,0:T(8,128)(2,1)S(1)}, u32[]{:S(2)}, u32[]{:S(2)}) async-start(bf16[32,8,512]{2,1,0:T(8,128)(2,1)} %fusion.30), calls=%async_computation.14 | async-start | bytes 524288 | tf_op jit(solution)/shard_map/all_to_all | solution.py:26
Sparse Core Ops, SparseCore 0:
  10.1 49.2 all-gather.2
  62.0 61.2 all-gather.4

commit v11 on v10

--- a/solution.py
+++ b/solution.py
@@ -66,12 +66,13 @@
     lhs_near = spans[LINE - 1]
     for k in range(LINE - 1):
         lhs_near = jnp.where(line_pos == k, spans[k], lhs_near)
+    lhs_far = jnp.concatenate([pick_other(k, spans, line_pos) for k in range(LINE - 1)], 1)
     total_thin = jnp.dot(lhs, thin, preferred_element_type=jnp.float32)
-    total = jnp.dot(lhs_near, near[:, THIN:], preferred_element_type=jnp.float32)
-    for k in range(LINE - 1):
-        total = total + jnp.dot(
-            pick_other(k, spans, line_pos), far[k], preferred_element_type=jnp.float32
-        )
+    total_near = jnp.dot(lhs_near, near[:, THIN:], preferred_element_type=jnp.float32)
+    lhs_far, total_near = lax.optimization_barrier((lhs_far, total_near))
+    total = total_near + jnp.dot(
+        lhs_far, far.reshape(lhs_far.shape[1], -1), preferred_element_type=jnp.float32
+    )
     return jnp.concatenate([total_thin, total], 1)
 
 
@@ -113,6 +114,7 @@
     panel = gather_rotation(rot_b, line_wide, line_pos)
     own_feats = lax.dynamic_slice_in_dim(activations, mdl_pos * narrow, narrow, 1)
     plain = jnp.dot(own_feats, value_weight, preferred_element_type=jnp.float32)
+    plain = plain.reshape(tok_rows, 2, channels // 2).transpose(1, 0, 2)
 
     turned = times_rotation(weight_rows, *panel, line_pos) / width_root
     own_codes = lax.dynamic_slice_in_dim(channel_code, tok_pos * chan_share, chan_share, 0)
@@ -127,12 +129,18 @@
     act_tanh = jnp.tanh(rotated / act_clip)
     quant_act = (act_clip * act_tanh).astype(jnp.bfloat16)
     half = channels // 2
-    weight_halves = weight_full.reshape(2, half, narrow)
-    partial_err = (
-        jnp.einsum("td,hcd->htc", quant_act, weight_halves, preferred_element_type=jnp.float32)
-        - plain.reshape(tok_rows, 2, half).transpose(1, 0, 2)
-    )
-    core_err = sum_blocks(partial_err, "core")
+    core_pos = lax.axis_index("core")
+    weight_parts = weight_full.reshape(2, half, narrow)
+    terms = []
+    for part in (1 - core_pos, core_pos):
+        product = jnp.einsum(
+            "td,cd->tc",
+            quant_act,
+            lax.dynamic_index_in_dim(weight_parts, part, 0, keepdims=False),
+            preferred_element_type=jnp.float32,
+        )
+        terms.append(product - lax.dynamic_index_in_dim(plain, part, 0, keepdims=False))
+    core_err = terms[1] + lax.ppermute(terms[0], "core", [(0, 1), (1, 0)])
     own_err = sum_blocks(core_err.reshape(lax.axis_size("chip"), -1, half), "chip")
     err_bf = gather_blocks(own_err.astype(jnp.bfloat16), ("core", "chip")).reshape(2, tok_rows, half)
     recon_error = err_bf.transpose(1, 0, 2).reshape(tok_rows, channels).astype(jnp.float32)
@@ -144,7 +152,7 @@
     )
     grad_act = sum(
         jnp.dot(err_half, weight_half, preferred_element_type=jnp.float32)
-        for err_half, weight_half in zip(err_bf, weight_halves)
+        for err_half, weight_half in zip(err_bf, weight_parts)
     )
     grad_act = (grad_act * (1.0 - act_tanh * act_tanh)).astype(jnp.bfloat16)
     grad_turned = (grad_quant * (1.0 - weight_tanh * weight_tanh)).astype(jnp.bfloat16)

time: 387 us -> 381 us (0.984)
  waiting for transfers between devices: 126 us -> 117 us
  local copies, waits for them, and re-layouts: 15 us -> 21.6 us
  matrix products: 25.5 us -> 20.1 us
  blocking collectives: 149 us -> 144 us
  other arithmetic: 11.7 us -> 16.4 us
    all_to_all x4, waiting for transfers between devices: 70.7 us -> 61.9 us  [gather_blocks(): lax.all_to_all(jnp.broadcast_to(own[None], (parts,) + own.shape), axis, 0...]
    dot_general x7 -> x4, matrix products: 14.4 us -> 7.44 us  [the longest x2 4.48 us: times_rotation(): jnp.dot(lhs_far, far.reshape(lhs_far.shape[1], -1), preferred_element_typ...]
    all_to_all x5 -> x4, blocking collectives: 81.5 us -> 76.1 us  [sum_blocks(): return jnp.sum(lax.all_to_all(blocks, axis, 0, 0).astype(jnp.float32), 0)]
  transfers between devices with their start and end apart: 8 -> 9, of which waited for: 8 -> 9; matrix products, arithmetic and copies ran while one was open for 7% -> 9% of each run, Pallas kernels for 0% -> 0%
where the time goes in v11:
time: 381 us; the launch traced here: 380 us
  blocking collectives  144 us (38%)
  waiting for transfers between devices  117 us (31%)
  starting transfers between devices  46.3 us (12%)
  local copies, waits for them, and re-layouts  21.6 us (6%)
  matrix products  20.1 us (5%)
  other arithmetic  16.4 us (4%)
  between operations  14.5 us (4%)
    all_to_all x4, blocking collectives, sum_blocks(): return jnp.sum(lax.all_to_all(blocks, axis, 0, 0).astype(jnp.float32), 0)  76.1 us
    all_to_all x4, blocking collectives, gather_blocks(): lax.all_to_all(jnp.broadcast_to(own[None], (parts,) + own.shape), axis, 0...  67.5 us
    all_to_all x4, waiting for transfers between devices, gather_blocks(): lax.all_to_all(jnp.broadcast_to(own[None], (parts,) + own.shape), axis, 0...  61.9 us
    all_to_all x4, starting transfers between devices, gather_blocks(): lax.all_to_all(jnp.broadcast_to(own[None], (parts,) + own.shape), axis, 0...  33.6 us
    all_to_all x2, waiting for transfers between devices, sum_blocks(): return jnp.sum(lax.all_to_all(blocks, axis, 0, 0).astype(jnp.float32), 0)  31.6 us
    all_gather x1, waiting for transfers between devices, gather_rotation(): near = lax.all_gather(rot_b, 'ring', axis=0, tiled=True)  15.6 us
    all_to_all x2, starting transfers between devices, sum_blocks(): return jnp.sum(lax.all_to_all(blocks, axis, 0, 0).astype(jnp.float32), 0)  10.8 us
  transfers between devices with their start and end apart: 9, of which 9 were waited for; matrix products, arithmetic and copies ran while one was open for 9% of the time, Pallas kernels for 0%

profile of v11, /device:TPU:8, one launch (start us, length us, event | category | flops | bytes accessed | tf_op | source)
XLA Modules:
  0.0 379.7 jit_solution(5701583950873096982)
XLA Ops:
  7.2 1.9 convert_element_type.82
  11.0 9.3 %all-to-all-start.1 = ((bf16[4,256,384]{2,1,0:T(8,128)(2,1)}), bf16[4,256,384]{2,1,0:T(8,128)(2,1)S(1)}, u32[]{:S(2)}, u32[]{:S(2)}) async-start(bf16[4,256,384]{2,1,0:T(8,128)(2,1)} %broadcast_in_dim.17), calls=%async_computation.1 | async-start | bytes 1572864 | tf_op jit(solution)/shard_map/all_to_all | solution.py:22
  20.3 12.9 %all-to-all-done.1 = bf16[4,256,384]{2,1,0:T(8,128)(2,1)S(1)} async-done(((bf16[4,256,384]{2,1,0:T(8,128)(2,1)}), bf16[4,256,384]{2,1,0:T(8,128)(2,1)S(1)}, u32[]{:S(2)}, u32[]{:S(2)}) %all-to-all-start.1) | async-done | bytes 786464 | tf_op jit(solution)/shard_map/all_to_all | solution.py:22
  35.2 8.5 %all-to-all-start.2 = ((bf16[16,32,512]{2,1,0:T(8,128)(2,1)}), bf16[16,32,512]{2,1,0:T(8,128)(2,1)S(1)}, u32[]{:S(2)}, u32[]{:S(2)}) async-start(bf16[16,32,512]{2,1,0:T(8,128)(2,1)} %broadcast_in_dim.18), calls=%async_computation.2 | async-start | bytes 1048576 | tf_op jit(solution)/shard_map/all_to_all | solution.py:22
  43.8 15.6 %all-gather.3.cloned.1.call-done = bf16[2048,512]{1,0:T(8,128)(2,1)} async-done(((bf16[256,512]{1,0:T(8,128)(2,1)}), bf16[2048,512]{1,0:T(8,128)(2,1)}) %all-gather.3.cloned.1.call-update) | async-done | bytes 2097168 | tf_op jit(solution)/shard_map/all_gather | solution.py:52
  59.3 1.1 slice.127
  60.9 1.7 broadcast_in_dim.16
  62.6 7.4 %all-to-all-start = ((bf16[4,2048,128]{2,1,0:T(8,128)(2,1)}), bf16[4,2048,128]{2,1,0:T(8,128)(2,1)S(1)}, u32[]{:S(2)}, u32[]{:S(2)}) async-start(bf16[4,2048,128]{2,1,0:T(8,128)(2,1)} %broadcast_in_dim.16), calls=%async_computation | async-start | bytes 4194304 | tf_op jit(solution)/shard_map/all_to_all | solution.py:22
  70.0 2.2 fusion.28
  72.2 2.7 reshape.98
  74.9 1.3 convert_multiply_fusion.1
  76.8 3.4 broadcast_select_fusion.2
  82.0 1.0 fusion
  82.9 31.8 %all-to-all-done = bf16[4,2048,128]{2,1,0:T(8,128)(2,1)S(1)} async-done(((bf16[4,2048,128]{2,1,0:T(8,128)(2,1)}), bf16[4,2048,128]{2,1,0:T(8,128)(2,1)S(1)}, u32[]{:S(2)}, u32[]{:S(2)}) %all-to-all-start) | async-done | bytes 2097184 | tf_op jit(solution)/shard_map/all_to_all | solution.py:22
  114.8 1.5 fusion.65
  116.3 6.4 %all-gather.5.cloned.1.call-done = bf16[3,2048,384]{2,1,0:T(8,128)(2,1)} async-done(((bf16[3,256,384]{2,1,0:T(8,128)(2,1)}), bf16[3,2048,384]{2,1,0:T(8,128)(2,1)}) %all-gather.5.cloned.1.call-update) | async-done | bytes 4718608 | tf_op jit(solution)/shard_map/all_gather | solution.py:54
  122.7 3.1 convolution_add_fusion.2
  126.5 1.2 broadcast_in_dim.19
  127.7 8.3 %all-to-all-start.3 = ((bf16[32,32,512]{2,1,0:T(8,128)(2,1)}), bf16[32,32,512]{2,1,0:T(8,128)(2,1)}, u32[]{:S(2)}, u32[]{:S(2)}) async-start(bf16[32,32,512]{2,1,0:T(8,128)(2,1)} %broadcast_in_dim.19), calls=%async_computation.3 | async-start | bytes 2097152 | tf_op jit(solution)/shard_map/all_to_all | solution.py:22
  136.0 3.2 constant_dynamic-slice_fusion.1
  139.3 2.0 pad_maximum_fusion
  142.6 1.0 convolution_bitcast_fusion
  144.1 1.4 convolution_add_fusion.1
  145.5 16.7 %all-to-all-done.3 = bf16[32,32,512]{2,1,0:T(8,128)(2,1)} async-done(((bf16[32,32,512]{2,1,0:T(8,128)(2,1)}), bf16[32,32,512]{2,1,0:T(8,128)(2,1)}, u32[]{:S(2)}, u32[]{:S(2)}) %all-to-all-start.3) | async-done | bytes 1048608 | tf_op jit(solution)/shard_map/all_to_all | solution.py:22
  162.2 1.6 convolution_subtract_fusion.2
  163.7 1.9 collective-permute-start
  165.7 1.7 collective-permute-done
  167.4 1.4 fusion.6
  168.8 23.4 %all_to_all.70 = f32[8,24,512]{2,1,0:T(8,128)S(1)} all-to-all(f32[8,24,512]{2,1,0:T(8,128)S(1)} %bitcast.125), channel_id=1, replica_groups=mesh['line'=4,'ring'=8,'chip'=8,'core'=2] {'chip'}, dimensions={0} | all-to-all | bytes 786432 | tf_op jit(solution)/shard_map/all_to_all | solution.py:26
  193.6 19.1 %all_to_all.71 = bf16[16,24,512]{2,1,0:T(8,128)(2,1)S(1)} all-to-all(bf16[16,24,512]{2,1,0:T(8,128)(2,1)S(1)} %broadcast_in_dim.20), channel_id=1, replica_groups=mesh['line'=4,'ring'=8,'chip'=8,'core'=2] {'core','chip'}, dimensions={0} | all-to-all | bytes 786432 | tf_op jit(solution)/shard_map/all_to_all | solution.py:22
  212.8 2.5 convolution_convert_fusion
  215.3 5.9 %all-to-all-start.6 = ((bf16[32,32,512]{2,1,0:T(8,128)(2,1)}), bf16[32,32,512]{2,1,0:T(8,128)(2,1)}, u32[]{:S(2)}, u32[]{:S(2)}) async-start(bf16[32,32,512]{2,1,0:T(8,128)(2,1)} %bitcast.119), calls=%async_computation.6 | async-start | bytes 2097152 | tf_op jit(solution)/shard_map/all_to_all | solution.py:26
  222.2 1.0 slice.136
  223.2 1.0 fusion.25
  225.0 1.3 fusion.63
  227.0 21.1 %all-to-all-done.6 = bf16[32,32,512]{2,1,0:T(8,128)(2,1)} async-done(((bf16[32,32,512]{2,1,0:T(8,128)(2,1)}), bf16[32,32,512]{2,1,0:T(8,128)(2,1)}, u32[]{:S(2)}, u32[]{:S(2)}) %all-to-all-start.6) | async-done | bytes 1048608 | tf_op jit(solution)/shard_map/all_to_all | solution.py:26
  248.1 1.4 convert_reduce_fusion
  249.6 1.3 convolution_convert_fusion.2
  251.0 17.4 %all_to_all.72 = bf16[16,16,448]{2,1,0:T(8,128)(2,1)S(1)} all-to-all(bf16[16,16,448]{2,1,0:T(8,128)(2,1)S(1)} %bitcast.120), channel_id=1, replica_groups=mesh['line'=4,'ring'=8,'chip'=8,'core'=2] {'chip','core'}, dimensions={0} | all-to-all | bytes 458752 | tf_op jit(solution)/shard_map/all_to_all | solution.py:26
  268.4 16.0 %all_to_all.73 = bf16[16,16,448]{2,1,0:T(8,128)(2,1)S(1)} all-to-all(bf16[16,16,448]{2,1,0:T(8,128)(2,1)S(1)} %broadcast_in_dim.21), channel_id=1, replica_groups=mesh['line'=4,'ring'=8,'chip'=8,'core'=2] {'chip','core'}, dimensions={0} | all-to-all | bytes 458752 | tf_op jit(solution)/shard_map/all_to_all | solution.py:22
  285.0 17.8 %all_to_all.74 = bf16[32,8,512]{2,1,0:T(8,128)(2,1)S(1)} all-to-all(bf16[32,8,512]{2,1,0:T(8,128)(2,1)S(1)} %fusion.10), channel_id=1, replica_groups=mesh['line'=4,'ring'=8,'chip'=8,'core'=2] {'line','ring'}, dimensions={0} | all-to-all | bytes 524288 | tf_op jit(solution)/shard_map/all_to_all | solution.py:26
  303.6 16.5 %all_to_all.75 = bf16[32,8,512]{2,1,0:T(8,128)(2,1)S(1)} all-to-all(bf16[32,8,512]{2,1,0:T(8,128)(2,1)S(1)} %broadcast_in_dim.22), channel_id=1, replica_groups=mesh['line'=4,'ring'=8,'chip'=8,'core'=2] {'line','ring'}, dimensions={0} | all-to-all | bytes 524288 | tf_op jit(solution)/shard_map/all_to_all | solution.py:22
  320.5 17.4 %all_to_all.76 = bf16[16,16,448]{2,1,0:T(8,128)(2,1)S(1)} all-to-all(bf16[16,16,448]{2,1,0:T(8,128)(2,1)S(1)} %bitcast.121), channel_id=1, replica_groups=mesh['line'=4,'ring'=8,'chip'=8,'core'=2] {'chip','core'}, dimensions={0} | all-to-all | bytes 458752 | tf_op jit(solution)/shard_map/all_to_all | solution.py:26
  338.0 15.8 %all_to_all.77 = bf16[16,16,448]{2,1,0:T(8,128)(2,1)S(1)} all-to-all(bf16[16,16,448]{2,1,0:T(8,128)(2,1)S(1)} %broadcast_in_dim.23), channel_id=1, replica_groups=mesh['line'=4,'ring'=8,'chip'=8,'core'=2] {'chip','core'}, dimensions={0} | all-to-all | bytes 458752 | tf_op jit(solution)/shard_map/all_to_all | solution.py:22
  354.1 1.0 fusion.9
  355.1 4.9 %all-to-all-start.13 = ((bf16[32,8,512]{2,1,0:T(8,128)(2,1)}), bf16[32,8,512]{2,1,0:T(8,128)(2,1)S(1)}, u32[]{:S(2)}, u32[]{:S(2)}) async-start(bf16[32,8,512]{2,1,0:T(8,128)(2,1)} %fusion.9), calls=%async_computation.13 | async-start | bytes 524288 | tf_op jit(solution)/shard_map/all_to_all | solution.py:26
  361.0 10.5 %all-to-all-done.13 = bf16[32,8,512]{2,1,0:T(8,128)(2,1)S(1)} async-done(((bf16[32,8,512]{2,1,0:T(8,128)(2,1)}), bf16[32,8,512]{2,1,0:T(8,128)(2,1)S(1)}, u32[]{:S(2)}, u32[]{:S(2)}) %all-to-all-start.13) | async-done | bytes 262176 | tf_op jit(solution)/shard_map/all_to_all | solution.py:26
  371.5 1.3 multiply_subtract_fusion
  (87 shorter events, 16.5 us)
Async XLA Ops:
  7.2 27.0 %copy-start = (bf16[512,1024]{1,0:T(8,128)(2,1)S(1)}, bf16[512,1024]{1,0:T(8,128)(2,1)}, u32[]{:S(2)}) copy-start(bf16[512,1024]{1,0:T(8,128)(2,1)} %param.7) | copy-start | bytes 3145732
  7.2 52.2 %all-gather.3.cloned.1.call-start = ((), (), s32[]{:S(2)}) async-start(), calls=%async_computation.14 | async-start | bytes 2359296 | tf_op jit(solution)/shard_map/all_gather | solution.py:52
  11.0 22.2 %all-to-all-start.1 = ((bf16[4,256,384]{2,1,0:T(8,128)(2,1)}), bf16[4,256,384]{2,1,0:T(8,128)(2,1)S(1)}, u32[]{:S(2)}, u32[]{:S(2)}) async-start(bf16[4,256,384]{2,1,0:T(8,128)(2,1)} %broadcast_in_dim.17), calls=%async_computation.1 | async-start | bytes 1572864 | tf_op jit(solution)/shard_map/all_to_all | solution.py:22
  20.3 102.4 %all-gather.5.cloned.1.call-start = ((), (), s32[]{:S(2)}) async-start(), calls=%async_computation.15 | async-start | bytes 5308416 | tf_op jit(solution)/shard_map/all_gather | solution.py:54
  35.2 25.7 %all-to-all-start.2 = ((bf16[16,32,512]{2,1,0:T(8,128)(2,1)}), bf16[16,32,512]{2,1,0:T(8,128)(2,1)S(1)}, u32[]{:S(2)}, u32[]{:S(2)}) async-start(bf16[16,32,512]{2,1,0:T(8,128)(2,1)} %broadcast_in_dim.18), calls=%async_computation.2 | async-start | bytes 1048576 | tf_op jit(solution)/shard_map/all_to_all | solution.py:22
  60.9 1.7 copy-start.3
  62.6 52.2 %all-to-all-start = ((bf16[4,2048,128]{2,1,0:T(8,128)(2,1)}), bf16[4,2048,128]{2,1,0:T(8,128)(2,1)S(1)}, u32[]{:S(2)}, u32[]{:S(2)}) async-start(bf16[4,2048,128]{2,1,0:T(8,128)(2,1)} %broadcast_in_dim.16), calls=%async_computation | async-start | bytes 4194304 | tf_op jit(solution)/shard_map/all_to_all | solution.py:22
  70.0 6.2 %copy-start.16 = (s32[192]{0:T(256)S(1)}, s32[192]{0:T(256)}, u32[]{:S(2)}) copy-start(s32[192]{0:T(256)} %param.8) | copy-start | bytes 2308
  76.8 3.4 copy-start.4
  80.2 1.8 copy-start.12
  80.2 0.8 copy-start.2
  122.7 3.7 copy-start.14
  125.8 0.6 copy-start.9
  127.7 34.5 %all-to-all-start.3 = ((bf16[32,32,512]{2,1,0:T(8,128)(2,1)}), bf16[32,32,512]{2,1,0:T(8,128)(2,1)}, u32[]{:S(2)}, u32[]{:S(2)}) async-start(bf16[32,32,512]{2,1,0:T(8,128)(2,1)} %broadcast_in_dim.19), calls=%async_computation.3 | async-start | bytes 2097152 | tf_op jit(solution)/shard_map/all_to_all | solution.py:22
  136.0 5.2 %copy-start.13 = (bf16[2048,512]{1,0:T(8,128)(2,1)S(1)}, bf16[2048,512]{1,0:T(8,128)(2,1)}, u32[]{:S(2)}) copy-start(bf16[2048,512]{1,0:T(8,128)(2,1)} %all-gather.3.cloned.1.call-done) | copy-start | bytes 6291460
  139.3 2.6 copy-start.1
  139.3 4.3 %slice-start = ((s8[4718592]{0:T(1024)(128)(4,1)}), s8[524288]{0:T(1024)(128)(4,1)S(1)}, s32[]{:S(2)}) async-start(s8[4718592]{0:T(1024)(128)(4,1)} %bitcast.102), calls=%async_computation.16 | async-start | bytes 1048576
  141.9 2.2 slice-start.1
  143.6 23.8 %copy-start.7 = (f32[192,128]{1,0:T(8,128)}, f32[192,128]{1,0:T(8,128)S(1)}, u32[]{:S(2)}) copy-start(f32[192,128]{1,0:T(8,128)S(1)} %convolution_bitcast_fusion) | copy-start | bytes 294916
  145.5 23.3 %copy-start.5 = (f32[192,384]{1,0:T(8,128)}, f32[192,384]{1,0:T(8,128)S(1)}, u32[]{:S(2)}) copy-start(f32[192,384]{1,0:T(8,128)S(1)} %convolution_add_fusion.1) | copy-start | bytes 884740
  162.2 5.2 %copy-start.11 = (f32[192,1,512]{2,1,0:T(1,128)S(1)}, f32[192,1,512]{2,1,0:T(1,128)}, u32[]{:S(2)}) copy-start(f32[192,1,512]{2,1,0:T(1,128)} %get-tuple-element.31) | copy-start | bytes 1179652
  162.2 5.2 %copy-start.17 = (f32[192]{0:T(256)S(1)}, f32[192]{0:T(256)}, u32[]{:S(2)}) copy-start(f32[192]{0:T(256)} %convert_multiply_fusion) | copy-start | bytes 2308
  163.7 3.6 collective-permute-start
  215.3 32.8 %all-to-all-start.6 = ((bf16[32,32,512]{2,1,0:T(8,128)(2,1)}), bf16[32,32,512]{2,1,0:T(8,128)(2,1)}, u32[]{:S(2)}, u32[]{:S(2)}) async-start(bf16[32,32,512]{2,1,0:T(8,128)(2,1)} %bitcast.119), calls=%async_computation.6 | async-start | bytes 2097152 | tf_op jit(solution)/shard_map/all_to_all | solution.py:26
  224.3 2.4 copy-start.6
  224.3 2.4 copy-start.8
  224.3 2.4 copy-start.18
  226.4 23.1 %copy-start.10 = (f32[32,384]{1,0:T(8,128)S(1)}, f32[32,384]{1,0:T(8,128)}, u32[]{:S(2)}) copy-start(f32[32,384]{1,0:T(8,128)} %copy-done.9) | copy-start | bytes 147460
  226.4 23.1 %copy-start.15 = (f32[32]{0:T(128)S(1)}, f32[32]{0:T(128)}, u32[]{:S(2)}) copy-start(f32[32]{0:T(128)} %convert_multiply_fusion.1) | copy-start | bytes 388
  355.1 16.4 %all-to-all-start.13 = ((bf16[32,8,512]{2,1,0:T(8,128)(2,1)}), bf16[32,8,512]{2,1,0:T(8,128)(2,1)S(1)}, u32[]{:S(2)}, u32[]{:S(2)}) async-start(bf16[32,8,512]{2,1,0:T(8,128)(2,1)} %fusion.9), calls=%async_computation.13 | async-start | bytes 524288 | tf_op jit(solution)/shard_map/all_to_all | solution.py:26
Sparse Core Ops, SparseCore 0:
  10.1 49.2 all-gather.2
  61.4 61.2 all-gather.4

commit v12 on v11

--- a/solution.py
+++ b/solution.py
@@ -109,7 +109,17 @@
     line_wide = gather_blocks(rot_b[:, THIN:], "line")
     value_late, line_wide = lax.optimization_barrier((value_weight, line_wide))
     own_cols = lax.dynamic_slice_in_dim(value_late, tok_pos * chan_share, chan_share, 1)
-    weight_rows = gather_blocks(own_cols.T, MDL).transpose(1, 0, 2).reshape(chan_share, model_width)
+    core_pos = lax.axis_index("core")
+    chip_rows = gather_blocks(own_cols.T, "chip")
+    pair_rows = lax.ppermute(chip_rows, "core", [(0, 1), (1, 0)])
+    weight_rows = jnp.stack(
+        [
+            jnp.where(core_pos == 0, chip_rows, pair_rows),
+            jnp.where(core_pos == 0, pair_rows, chip_rows),
+        ],
+        1,
+    )
+    weight_rows = weight_rows.transpose(2, 0, 1, 3).reshape(chan_share, model_width)
     line_pos = lax.axis_index("line")
     panel = gather_rotation(rot_b, line_wide, line_pos)
     own_feats = lax.dynamic_slice_in_dim(activations, mdl_pos * narrow, narrow, 1)
@@ -129,7 +139,6 @@
     act_tanh = jnp.tanh(rotated / act_clip)
     quant_act = (act_clip * act_tanh).astype(jnp.bfloat16)
     half = channels // 2
-    core_pos = lax.axis_index("core")
     weight_parts = weight_full.reshape(2, half, narrow)
     terms = []
     for part in (1 - core_pos, core_pos):

time: 381 us -> 382 us (level)
  waiting for transfers between devices: 117 us -> 113 us
    all_to_all x4, waiting for transfers between devices: 61.9 us -> 50.5 us  [gather_blocks(): lax.all_to_all(jnp.broadcast_to(own[None], (parts,) + own.shape), axis, 0...]
    all_gather x1, waiting for transfers between devices: 6.41 us -> 13.1 us  [gather_rotation(): far = lax.all_gather(others, 'ring', axis=1, tiled=True)]
  transfers between devices with their start and end apart: 9 -> 10, of which waited for: 9 -> 8; matrix products, arithmetic and copies ran while one was open for 9% -> 11% of each run, Pallas kernels for 0% -> 0%
where the time goes in v12:
time: 382 us; the launch traced here: 380 us
  blocking collectives  144 us (38%)
  waiting for transfers between devices  113 us (30%)
  starting transfers between devices  45.2 us (12%)
  local copies, waits for them, and re-layouts  23.4 us (6%)
  matrix products  21.8 us (6%)
  other arithmetic  18.6 us (5%)
  between operations  14.5 us (4%)
    all_to_all x4, blocking collectives, sum_blocks(): return jnp.sum(lax.all_to_all(blocks, axis, 0, 0).astype(jnp.float32), 0)  76.2 us
    all_to_all x4, blocking collectives, gather_blocks(): lax.all_to_all(jnp.broadcast_to(own[None], (parts,) + own.shape), axis, 0...  67.5 us
    all_to_all x4, waiting for transfers between devices, gather_blocks(): lax.all_to_all(jnp.broadcast_to(own[None], (parts,) + own.shape), axis, 0...  50.5 us
    all_to_all x2, waiting for transfers between devices, sum_blocks(): return jnp.sum(lax.all_to_all(blocks, axis, 0, 0).astype(jnp.float32), 0)  31.6 us
    all_to_all x4, starting transfers between devices, gather_blocks(): lax.all_to_all(jnp.broadcast_to(own[None], (parts,) + own.shape), axis, 0...  30.5 us
    all_gather x1, waiting for transfers between devices, gather_rotation(): near = lax.all_gather(rot_b, 'ring', axis=0, tiled=True)  15.8 us
    all_gather x1, waiting for transfers between devices, gather_rotation(): far = lax.all_gather(others, 'ring', axis=1, tiled=True)  13.1 us
    all_to_all x2, starting transfers between devices, sum_blocks(): return jnp.sum(lax.all_to_all(blocks, axis, 0, 0).astype(jnp.float32), 0)  10.8 us
  transfers between devices with their start and end apart: 10, of which 8 were waited for; matrix products, arithmetic and copies ran while one was open for 11% of the time, Pallas kernels for 0%

profile of v12, /device:TPU:8, one launch (start us, length us, event | category | flops | bytes accessed | tf_op | source)
XLA Modules:
  0.0 379.8 jit_solution(5022206575549722148)
XLA Ops:
  7.2 1.9 convert_element_type.82
  11.0 9.3 %all-to-all-start.1 = ((bf16[4,256,384]{2,1,0:T(8,128)(2,1)}), bf16[4,256,384]{2,1,0:T(8,128)(2,1)S(1)}, u32[]{:S(2)}, u32[]{:S(2)}) async-start(bf16[4,256,384]{2,1,0:T(8,128)(2,1)} %broadcast_in_dim.17), calls=%async_computation.1 | async-start | bytes 1572864 | tf_op jit(solution)/shard_map/all_to_all | solution.py:22
  20.3 12.9 %all-to-all-done.1 = bf16[4,256,384]{2,1,0:T(8,128)(2,1)S(1)} async-done(((bf16[4,256,384]{2,1,0:T(8,128)(2,1)}), bf16[4,256,384]{2,1,0:T(8,128)(2,1)S(1)}, u32[]{:S(2)}, u32[]{:S(2)}) %all-to-all-start.1) | async-done | bytes 786464 | tf_op jit(solution)/shard_map/all_to_all | solution.py:22
  35.1 8.4 %all-to-all-start.2 = ((bf16[8,32,512]{2,1,0:T(8,128)(2,1)}), bf16[8,32,512]{2,1,0:T(8,128)(2,1)S(1)}, u32[]{:S(2)}, u32[]{:S(2)}) async-start(bf16[8,32,512]{2,1,0:T(8,128)(2,1)} %broadcast_in_dim.18), calls=%async_computation.2 | async-start | bytes 524288 | tf_op jit(solution)/shard_map/all_to_all | solution.py:22
  43.6 15.8 %all-gather.3.cloned.1.call-done = bf16[2048,512]{1,0:T(8,128)(2,1)} async-done(((bf16[256,512]{1,0:T(8,128)(2,1)}), bf16[2048,512]{1,0:T(8,128)(2,1)}) %all-gather.3.cloned.1.call-update) | async-done | bytes 2097168 | tf_op jit(solution)/shard_map/all_gather | solution.py:52
  59.3 1.1 slice.127
  60.4 1.7 broadcast_in_dim.16
  62.1 5.1 %all-to-all-start = ((bf16[4,2048,128]{2,1,0:T(8,128)(2,1)}), bf16[4,2048,128]{2,1,0:T(8,128)(2,1)S(1)}, u32[]{:S(2)}, u32[]{:S(2)}) async-start(bf16[4,2048,128]{2,1,0:T(8,128)(2,1)} %broadcast_in_dim.16), calls=%async_computation | async-start | bytes 4194304 | tf_op jit(solution)/shard_map/all_to_all | solution.py:22
  67.2 2.2 fusion.28
  69.4 3.4 broadcast_select_fusion.2
  72.8 1.9 collective-permute-start
  74.7 1.3 convert_multiply_fusion.1
  76.0 2.7 reshape.98
  80.3 1.3 copy.18
  81.6 2.3 reshape.91
  83.9 1.1 broadcast_select_fusion.6
  85.1 2.7 fusion
  87.8 20.3 %all-to-all-done = bf16[4,2048,128]{2,1,0:T(8,128)(2,1)S(1)} async-done(((bf16[4,2048,128]{2,1,0:T(8,128)(2,1)}), bf16[4,2048,128]{2,1,0:T(8,128)(2,1)S(1)}, u32[]{:S(2)}, u32[]{:S(2)}) %all-to-all-start) | async-done | bytes 2097184 | tf_op jit(solution)/shard_map/all_to_all | solution.py:22
  108.1 1.5 fusion.65
  109.6 13.1 %all-gather.5.cloned.1.call-done = bf16[3,2048,384]{2,1,0:T(8,128)(2,1)} async-done(((bf16[3,256,384]{2,1,0:T(8,128)(2,1)}), bf16[3,2048,384]{2,1,0:T(8,128)(2,1)}) %all-gather.5.cloned.1.call-update) | async-done | bytes 4718608 | tf_op jit(solution)/shard_map/all_gather | solution.py:54
  122.7 3.1 convolution_add_fusion.2
  126.5 1.2 broadcast_in_dim.19
  127.7 7.7 %all-to-all-start.3 = ((bf16[32,32,512]{2,1,0:T(8,128)(2,1)}), bf16[32,32,512]{2,1,0:T(8,128)(2,1)}, u32[]{:S(2)}, u32[]{:S(2)}) async-start(bf16[32,32,512]{2,1,0:T(8,128)(2,1)} %broadcast_in_dim.19), calls=%async_computation.3 | async-start | bytes 2097152 | tf_op jit(solution)/shard_map/all_to_all | solution.py:22
  135.4 3.2 constant_dynamic-slice_fusion.1
  138.6 2.0 pad_maximum_fusion
  143.4 1.4 convolution_add_fusion.1
  144.9 17.3 %all-to-all-done.3 = bf16[32,32,512]{2,1,0:T(8,128)(2,1)} async-done(((bf16[32,32,512]{2,1,0:T(8,128)(2,1)}), bf16[32,32,512]{2,1,0:T(8,128)(2,1)}, u32[]{:S(2)}, u32[]{:S(2)}) %all-to-all-start.3) | async-done | bytes 1048608 | tf_op jit(solution)/shard_map/all_to_all | solution.py:22
  162.2 1.6 convolution_subtract_fusion.2
  163.7 1.9 collective-permute-start.1
  165.7 1.7 collective-permute-done.1
  167.4 1.4 fusion.6
  168.8 23.5 %all_to_all.70 = f32[8,24,512]{2,1,0:T(8,128)S(1)} all-to-all(f32[8,24,512]{2,1,0:T(8,128)S(1)} %bitcast.124), channel_id=1, replica_groups=mesh['line'=4,'ring'=8,'chip'=8,'core'=2] {'chip'}, dimensions={0} | all-to-all | bytes 786432 | tf_op jit(solution)/shard_map/all_to_all | solution.py:26
  193.6 19.1 %all_to_all.71 = bf16[16,24,512]{2,1,0:T(8,128)(2,1)S(1)} all-to-all(bf16[16,24,512]{2,1,0:T(8,128)(2,1)S(1)} %broadcast_in_dim.20), channel_id=1, replica_groups=mesh['line'=4,'ring'=8,'chip'=8,'core'=2] {'core','chip'}, dimensions={0} | all-to-all | bytes 786432 | tf_op jit(solution)/shard_map/all_to_all | solution.py:22
  212.8 2.6 convolution_convert_fusion
  215.3 5.9 %all-to-all-start.6 = ((bf16[32,32,512]{2,1,0:T(8,128)(2,1)}), bf16[32,32,512]{2,1,0:T(8,128)(2,1)}, u32[]{:S(2)}, u32[]{:S(2)}) async-start(bf16[32,32,512]{2,1,0:T(8,128)(2,1)} %bitcast.118), calls=%async_computation.6 | async-start | bytes 2097152 | tf_op jit(solution)/shard_map/all_to_all | solution.py:26
  225.1 1.3 fusion.63
  227.0 21.1 %all-to-all-done.6 = bf16[32,32,512]{2,1,0:T(8,128)(2,1)} async-done(((bf16[32,32,512]{2,1,0:T(8,128)(2,1)}), bf16[32,32,512]{2,1,0:T(8,128)(2,1)}, u32[]{:S(2)}, u32[]{:S(2)}) %all-to-all-start.6) | async-done | bytes 1048608 | tf_op jit(solution)/shard_map/all_to_all | solution.py:26
  248.1 1.4 convert_reduce_fusion
  249.6 1.3 convolution_convert_fusion.2
  251.0 17.4 %all_to_all.72 = bf16[16,16,448]{2,1,0:T(8,128)(2,1)S(1)} all-to-all(bf16[16,16,448]{2,1,0:T(8,128)(2,1)S(1)} %bitcast.119), channel_id=1, replica_groups=mesh['line'=4,'ring'=8,'chip'=8,'core'=2] {'chip','core'}, dimensions={0} | all-to-all | bytes 458752 | tf_op jit(solution)/shard_map/all_to_all | solution.py:26
  268.5 16.0 %all_to_all.73 = bf16[16,16,448]{2,1,0:T(8,128)(2,1)S(1)} all-to-all(bf16[16,16,448]{2,1,0:T(8,128)(2,1)S(1)} %broadcast_in_dim.21), channel_id=1, replica_groups=mesh['line'=4,'ring'=8,'chip'=8,'core'=2] {'chip','core'}, dimensions={0} | all-to-all | bytes 458752 | tf_op jit(solution)/shard_map/all_to_all | solution.py:22
  285.0 17.9 %all_to_all.74 = bf16[32,8,512]{2,1,0:T(8,128)(2,1)S(1)} all-to-all(bf16[32,8,512]{2,1,0:T(8,128)(2,1)S(1)} %fusion.10), channel_id=1, replica_groups=mesh['line'=4,'ring'=8,'chip'=8,'core'=2] {'line','ring'}, dimensions={0} | all-to-all | bytes 524288 | tf_op jit(solution)/shard_map/all_to_all | solution.py:26
  303.7 16.5 %all_to_all.75 = bf16[32,8,512]{2,1,0:T(8,128)(2,1)S(1)} all-to-all(bf16[32,8,512]{2,1,0:T(8,128)(2,1)S(1)} %broadcast_in_dim.22), channel_id=1, replica_groups=mesh['line'=4,'ring'=8,'chip'=8,'core'=2] {'line','ring'}, dimensions={0} | all-to-all | bytes 524288 | tf_op jit(solution)/shard_map/all_to_all | solution.py:22
  320.6 17.5 %all_to_all.76 = bf16[16,16,448]{2,1,0:T(8,128)(2,1)S(1)} all-to-all(bf16[16,16,448]{2,1,0:T(8,128)(2,1)S(1)} %bitcast.120), channel_id=1, replica_groups=mesh['line'=4,'ring'=8,'chip'=8,'core'=2] {'chip','core'}, dimensions={0} | all-to-all | bytes 458752 | tf_op jit(solution)/shard_map/all_to_all | solution.py:26
  338.1 15.8 %all_to_all.77 = bf16[16,16,448]{2,1,0:T(8,128)(2,1)S(1)} all-to-all(bf16[16,16,448]{2,1,0:T(8,128)(2,1)S(1)} %broadcast_in_dim.23), channel_id=1, replica_groups=mesh['line'=4,'ring'=8,'chip'=8,'core'=2] {'chip','core'}, dimensions={0} | all-to-all | bytes 458752 | tf_op jit(solution)/shard_map/all_to_all | solution.py:22
  355.2 4.9 %all-to-all-start.13 = ((bf16[32,8,512]{2,1,0:T(8,128)(2,1)}), bf16[32,8,512]{2,1,0:T(8,128)(2,1)S(1)}, u32[]{:S(2)}, u32[]{:S(2)}) async-start(bf16[32,8,512]{2,1,0:T(8,128)(2,1)} %fusion.9), calls=%async_computation.13 | async-start | bytes 524288 | tf_op jit(solution)/shard_map/all_to_all | solution.py:26
  361.1 10.5 %all-to-all-done.13 = bf16[32,8,512]{2,1,0:T(8,128)(2,1)S(1)} async-done(((bf16[32,8,512]{2,1,0:T(8,128)(2,1)}), bf16[32,8,512]{2,1,0:T(8,128)(2,1)S(1)}, u32[]{:S(2)}, u32[]{:S(2)}) %all-to-all-start.13) | async-done | bytes 262176 | tf_op jit(solution)/shard_map/all_to_all | solution.py:26
  371.6 1.3 multiply_subtract_fusion
  (84 shorter events, 19.1 us)
Async XLA Ops:
  7.2 27.0 %copy-start = (bf16[512,1024]{1,0:T(8,128)(2,1)S(1)}, bf16[512,1024]{1,0:T(8,128)(2,1)}, u32[]{:S(2)}) copy-start(bf16[512,1024]{1,0:T(8,128)(2,1)} %param.7) | copy-start | bytes 3145732
  7.2 52.2 %all-gather.3.cloned.1.call-start = ((), (), s32[]{:S(2)}) async-start(), calls=%async_computation.14 | async-start | bytes 2359296 | tf_op jit(solution)/shard_map/all_gather | solution.py:52
  11.0 22.2 %all-to-all-start.1 = ((bf16[4,256,384]{2,1,0:T(8,128)(2,1)}), bf16[4,256,384]{2,1,0:T(8,128)(2,1)S(1)}, u32[]{:S(2)}, u32[]{:S(2)}) async-start(bf16[4,256,384]{2,1,0:T(8,128)(2,1)} %broadcast_in_dim.17), calls=%async_computation.1 | async-start | bytes 1572864 | tf_op jit(solution)/shard_map/all_to_all | solution.py:22
  20.3 102.4 %all-gather.5.cloned.1.call-start = ((), (), s32[]{:S(2)}) async-start(), calls=%async_computation.15 | async-start | bytes 5308416 | tf_op jit(solution)/shard_map/all_gather | solution.py:54
  35.1 25.3 %all-to-all-start.2 = ((bf16[8,32,512]{2,1,0:T(8,128)(2,1)}), bf16[8,32,512]{2,1,0:T(8,128)(2,1)S(1)}, u32[]{:S(2)}, u32[]{:S(2)}) async-start(bf16[8,32,512]{2,1,0:T(8,128)(2,1)} %broadcast_in_dim.18), calls=%async_computation.2 | async-start | bytes 524288 | tf_op jit(solution)/shard_map/all_to_all | solution.py:22
  62.1 46.0 %all-to-all-start = ((bf16[4,2048,128]{2,1,0:T(8,128)(2,1)}), bf16[4,2048,128]{2,1,0:T(8,128)(2,1)S(1)}, u32[]{:S(2)}, u32[]{:S(2)}) async-start(bf16[4,2048,128]{2,1,0:T(8,128)(2,1)} %broadcast_in_dim.16), calls=%async_computation | async-start | bytes 4194304 | tf_op jit(solution)/shard_map/all_to_all | solution.py:22
  69.4 9.3 %copy-start.12 = (s32[192]{0:T(256)S(1)}, s32[192]{0:T(256)}, u32[]{:S(2)}) copy-start(s32[192]{0:T(256)} %param.8) | copy-start | bytes 2308
  72.8 6.5 %collective-permute-start = (bf16[8,32,512]{2,1,0:T(8,128)(2,1)S(1)}, bf16[8,32,512]{2,1,0:T(8,128)(2,1)}, u32[]{:S(2)}, u32[]{:S(2)}) collective-permute-start(bf16[8,32,512]{2,1,0:T(8,128)(2,1)S(1)} %all-to-all-done.2), channel_id=1, source_target_pairs={{0,1},{1,0},{2,3},{3,2},{4,5},{5,4},{6,7},{7,6},{8,9},{9,8},{10,11... | collective-permute-start | bytes 786440 | tf_op jit(solution)/shard_map/ppermute | solution.py:114
  122.7 3.7 copy-start.10
  125.8 0.6 copy-start.6
  127.7 34.4 %all-to-all-start.3 = ((bf16[32,32,512]{2,1,0:T(8,128)(2,1)}), bf16[32,32,512]{2,1,0:T(8,128)(2,1)}, u32[]{:S(2)}, u32[]{:S(2)}) async-start(bf16[32,32,512]{2,1,0:T(8,128)(2,1)} %broadcast_in_dim.19), calls=%async_computation.3 | async-start | bytes 2097152 | tf_op jit(solution)/shard_map/all_to_all | solution.py:22
  135.4 5.2 %copy-start.9 = (bf16[2048,512]{1,0:T(8,128)(2,1)S(1)}, bf16[2048,512]{1,0:T(8,128)(2,1)}, u32[]{:S(2)}) copy-start(bf16[2048,512]{1,0:T(8,128)(2,1)} %all-gather.3.cloned.1.call-done) | copy-start | bytes 6291460
  138.6 2.6 copy-start.1
  138.6 4.3 %slice-start = ((s8[4718592]{0:T(1024)(128)(4,1)}), s8[524288]{0:T(1024)(128)(4,1)S(1)}, s32[]{:S(2)}) async-start(s8[4718592]{0:T(1024)(128)(4,1)} %bitcast.105), calls=%async_computation.16 | async-start | bytes 1048576
  141.2 2.2 slice-start.1
  142.9 24.4 %copy-start.4 = (f32[192,128]{1,0:T(8,128)}, f32[192,128]{1,0:T(8,128)S(1)}, u32[]{:S(2)}) copy-start(f32[192,128]{1,0:T(8,128)S(1)} %convolution_bitcast_fusion) | copy-start | bytes 294916
  144.8 23.9 %copy-start.2 = (f32[192,384]{1,0:T(8,128)}, f32[192,384]{1,0:T(8,128)S(1)}, u32[]{:S(2)}) copy-start(f32[192,384]{1,0:T(8,128)S(1)} %convolution_add_fusion.1) | copy-start | bytes 884740
  162.2 5.2 %copy-start.8 = (f32[192,1,512]{2,1,0:T(1,128)S(1)}, f32[192,1,512]{2,1,0:T(1,128)}, u32[]{:S(2)}) copy-start(f32[192,1,512]{2,1,0:T(1,128)} %get-tuple-element.31) | copy-start | bytes 1179652
  162.2 5.2 %copy-start.13 = (f32[192]{0:T(256)S(1)}, f32[192]{0:T(256)}, u32[]{:S(2)}) copy-start(f32[192]{0:T(256)} %convert_multiply_fusion) | copy-start | bytes 2308
  163.7 3.6 collective-permute-start.1
  215.3 32.8 %all-to-all-start.6 = ((bf16[32,32,512]{2,1,0:T(8,128)(2,1)}), bf16[32,32,512]{2,1,0:T(8,128)(2,1)}, u32[]{:S(2)}, u32[]{:S(2)}) async-start(bf16[32,32,512]{2,1,0:T(8,128)(2,1)} %bitcast.118), calls=%async_computation.6 | async-start | bytes 2097152 | tf_op jit(solution)/shard_map/all_to_all | solution.py:26
  224.3 2.4 copy-start.3
  224.3 2.4 copy-start.5
  224.3 2.4 copy-start.14
  226.4 23.1 %copy-start.7 = (f32[32,384]{1,0:T(8,128)S(1)}, f32[32,384]{1,0:T(8,128)}, u32[]{:S(2)}) copy-start(f32[32,384]{1,0:T(8,128)} %copy-done.6) | copy-start | bytes 147460
  226.4 23.1 %copy-start.11 = (f32[32]{0:T(128)S(1)}, f32[32]{0:T(128)}, u32[]{:S(2)}) copy-start(f32[32]{0:T(128)} %convert_multiply_fusion.1) | copy-start | bytes 388
  355.2 16.4 %all-to-all-start.13 = ((bf16[32,8,512]{2,1,0:T(8,128)(2,1)}), bf16[32,8,512]{2,1,0:T(8,128)(2,1)S(1)}, u32[]{:S(2)}, u32[]{:S(2)}) async-start(bf16[32,8,512]{2,1,0:T(8,128)(2,1)} %fusion.9), calls=%async_computation.13 | async-start | bytes 524288 | tf_op jit(solution)/shard_map/all_to_all | solution.py:26
Sparse Core Ops, SparseCore 0:
  10.1 49.2 all-gather.2
  61.4 61.2 all-gather.4

commit v13 on v12

--- a/solution.py
+++ b/solution.py
@@ -51,16 +51,32 @@
 def gather_rotation(rot_b, line_wide, line_pos):
     near = lax.all_gather(rot_b, "ring", axis=0, tiled=True)
     others = jnp.stack([pick_other(k, line_wide, line_pos) for k in range(LINE - 1)])
-    far = lax.all_gather(others, "ring", axis=1, tiled=True)
+    middle = ring_pass(others[:, :, :THIN])
+    far = lax.all_gather(others[:, :, THIN:], "ring", axis=1, tiled=True)
     thin = gather_blocks(near[:, :THIN], "line").reshape(LINE * near.shape[0], THIN)
-    return thin, near, far
+    return thin, near, middle, far
+
+
+def ring_pass(own):
+    up = [(k, (k + 1) % RING) for k in range(RING)]
+    down = [(k, (k - 1) % RING) for k in range(RING)]
+    found = {0: own}
+    for step in range(1, RING // 2 + 1):
+        found[RING - step] = lax.ppermute(found[(RING - step + 1) % RING], "ring", up)
+        if step < RING // 2:
+            found[step] = lax.ppermute(found[step - 1], "ring", down)
+    near_first = [found[k] for k in range(RING)]
+    twice = jnp.stack(near_first + near_first, 1)
+    start = (RING - lax.axis_index("ring")) % RING
+    ordered = lax.dynamic_slice_in_dim(twice, start, RING, 1)
+    return ordered.reshape(own.shape[0], -1, own.shape[2])
 
 
 def pick_other(k, blocks, line_pos):
     return jnp.where(line_pos > k, blocks[k], blocks[k + 1])
 
 
-def times_rotation(lhs, thin, near, far, line_pos):
+def times_rotation(lhs, thin, near, middle, far, line_pos):
     span = near.shape[0]
     spans = [lhs[:, k * span : (k + 1) * span] for k in range(LINE)]
     lhs_near = spans[LINE - 1]
@@ -69,19 +85,27 @@
     lhs_far = jnp.concatenate([pick_other(k, spans, line_pos) for k in range(LINE - 1)], 1)
     total_thin = jnp.dot(lhs, thin, preferred_element_type=jnp.float32)
     total_near = jnp.dot(lhs_near, near[:, THIN:], preferred_element_type=jnp.float32)
-    lhs_far, total_near = lax.optimization_barrier((lhs_far, total_near))
+    total_mid = total_near[:, :THIN] + jnp.dot(
+        lhs_far, middle.reshape(lhs_far.shape[1], -1), preferred_element_type=jnp.float32
+    )
+    lhs_far, total_near, total_mid = lax.optimization_barrier(
+        (lhs_far, total_near[:, THIN:], total_mid)
+    )
     total = total_near + jnp.dot(
         lhs_far, far.reshape(lhs_far.shape[1], -1), preferred_element_type=jnp.float32
     )
-    return jnp.concatenate([total_thin, total], 1)
-
-
-def first_rows(thin, near, far, rows, line_pos):
+    return jnp.concatenate([total_thin, total_mid, total], 1)
+
+
+def first_rows(thin, near, middle, far, rows, line_pos):
     narrow = near.shape[1]
     first_near = near.reshape(RING, rows, narrow)[:, : 2 * WIN]
-    first_far = far.reshape(LINE - 1, RING, rows, narrow - THIN)[:, :, : 2 * WIN]
+    first_far = [
+        part.reshape(LINE - 1, RING, rows, -1)[:, :, : 2 * WIN] for part in (middle, far)
+    ]
     first_near, first_far = lax.optimization_barrier((first_near, first_far))
-    first_near, first_far = first_near[:, :WIN, THIN:], first_far[:, :, :WIN]
+    first_near = first_near[:, :WIN, THIN:]
+    first_far = jnp.concatenate([part[:, :, :WIN] for part in first_far], 3)
     first = [
         jnp.where(
             line_pos == k,

time: 382 us -> 404 us (1.058)
  starting transfers between devices: 45.2 us -> 80.6 us
  waiting for transfers between devices: 113 us -> 82.3 us
  local copies, waits for them, and re-layouts: 23.4 us -> 38.3 us
    ppermute x0 -> x7, starting transfers between devices: none -> 29.8 us  [the longest x3 21.7 us: ring_pass(): found[step] = lax.ppermute(found[step - 1], 'ring', down)]
    unnamed x34 -> x90, local copies, waits for them, and re-layouts: 1.79 us -> 19.5 us
    all_gather x1, waiting for transfers between devices: 15.8 us -> 0.01 us  [gather_rotation(): near = lax.all_gather(rot_b, 'ring', axis=0, tiled=True)]
    all_to_all x4, waiting for transfers between devices: 50.5 us -> 35.1 us  [gather_blocks(): lax.all_to_all(jnp.broadcast_to(own[None], (parts,) + own.shape), axis, 0...]
    ppermute x0 -> x7, waiting for transfers between devices: none -> 14.5 us  [the longest x4 14 us: ring_pass(): lax.ppermute(found[(RING - step + 1) % RING], 'ring', up)]
    all_gather x1, waiting for transfers between devices: 13.1 us -> 0.02 us  [gather_rotation(): far = lax.all_gather(others[:, :, THIN:], 'ring', axis=1, tiled=True)]
    all_to_all x4, starting transfers between devices: 30.5 us -> 35.6 us  [gather_blocks(): lax.all_to_all(jnp.broadcast_to(own[None], (parts,) + own.shape), axis, 0...]
  transfers between devices with their start and end apart: 10 -> 17, of which waited for: 8 -> 9; matrix products, arithmetic and copies ran while one was open for 11% -> 14% of each run, Pallas kernels for 0% -> 0%
where the time goes in v13:
time: 404 us; the launch traced here: 402 us
  blocking collectives  146 us (36%)
  waiting for transfers between devices  82.3 us (20%)
  starting transfers between devices  80.6 us (20%)
  local copies, waits for them, and re-layouts  38.3 us (9%)
  matrix products  22.2 us (5%)
  other arithmetic  17.4 us (4%)
  between operations  14.9 us (4%)
    all_to_all x4, blocking collectives, sum_blocks(): return jnp.sum(lax.all_to_all(blocks, axis, 0, 0).astype(jnp.float32), 0)  79 us
    all_to_all x4, blocking collectives, gather_blocks(): lax.all_to_all(jnp.broadcast_to(own[None], (parts,) + own.shape), axis, 0...  66.9 us
    all_to_all x4, starting transfers between devices, gather_blocks(): lax.all_to_all(jnp.broadcast_to(own[None], (parts,) + own.shape), axis, 0...  35.6 us
    all_to_all x4, waiting for transfers between devices, gather_blocks(): lax.all_to_all(jnp.broadcast_to(own[None], (parts,) + own.shape), axis, 0...  35.1 us
    all_to_all x2, waiting for transfers between devices, sum_blocks(): return jnp.sum(lax.all_to_all(blocks, axis, 0, 0).astype(jnp.float32), 0)  31.2 us
    ppermute x3, starting transfers between devices, ring_pass(): found[step] = lax.ppermute(found[step - 1], 'ring', down)  21.7 us
    unnamed x90, local copies, waits for them, and re-layouts  19.5 us
    ppermute x4, waiting for transfers between devices, ring_pass(): lax.ppermute(found[(RING - step + 1) % RING], 'ring', up)  14 us
  transfers between devices with their start and end apart: 17, of which 9 were waited for; matrix products, arithmetic and copies ran while one was open for 14% of the time, Pallas kernels for 0%

profile of v13, /device:TPU:8, one launch (start us, length us, event | category | flops | bytes accessed | tf_op | source)
XLA Modules:
  0.0 401.6 jit_solution(15732566024435290343)
XLA Ops:
  7.2 1.9 convert_element_type.82
  11.0 9.4 %all-to-all-start.1 = ((bf16[4,256,384]{2,1,0:T(8,128)(2,1)}), bf16[4,256,384]{2,1,0:T(8,128)(2,1)S(1)}, u32[]{:S(2)}, u32[]{:S(2)}) async-start(bf16[4,256,384]{2,1,0:T(8,128)(2,1)} %broadcast_in_dim.17), calls=%async_computation.1 | async-start | bytes 1572864 | tf_op jit(solution)/shard_map/all_to_all | solution.py:22
  22.4 1.6 constant_dynamic-slice_fusion.1
  24.6 3.4 broadcast_select_fusion.2
  28.0 5.3 %all-to-all-done.1 = bf16[4,256,384]{2,1,0:T(8,128)(2,1)S(1)} async-done(((bf16[4,256,384]{2,1,0:T(8,128)(2,1)}), bf16[4,256,384]{2,1,0:T(8,128)(2,1)S(1)}, u32[]{:S(2)}, u32[]{:S(2)}) %all-to-all-start.1) | async-done | bytes 786464 | tf_op jit(solution)/shard_map/all_to_all | solution.py:22
  34.1 10.9 %collective-permute-start = (bf16[3,256,128]{2,1,0:T(8,128)(2,1)S(1)}, bf16[3,256,128]{2,1,0:T(8,128)(2,1)S(1)}, u32[]{:S(2)}, u32[]{:S(2)}) collective-permute-start(bf16[3,256,128]{2,1,0:T(8,128)(2,1)S(1)} %get-tuple-element.35), channel_id=1, source_target_pairs={{0,112},{16,0},{32,16},{48,32},{64,48},{80,64},{96,80},{112,96},{1... | collective-permute-start | bytes 589832 | tf_op jit(solution)/shard_map/ppermute | solution.py:67
  45.0 1.9 collective-permute-start.3
  47.9 8.4 %all-to-all-start.2 = ((bf16[8,32,512]{2,1,0:T(8,128)(2,1)}), bf16[8,32,512]{2,1,0:T(8,128)(2,1)S(1)}, u32[]{:S(2)}, u32[]{:S(2)}) async-start(bf16[8,32,512]{2,1,0:T(8,128)(2,1)} %broadcast_in_dim.18), calls=%async_computation.2 | async-start | bytes 524288 | tf_op jit(solution)/shard_map/all_to_all | solution.py:22
  58.6 5.1 %collective-permute-start.1 = (bf16[3,256,128]{2,1,0:T(8,128)(2,1)S(1)}, bf16[3,256,128]{2,1,0:T(8,128)(2,1)S(1)}, u32[]{:S(2)}, u32[]{:S(2)}) collective-permute-start(bf16[3,256,128]{2,1,0:T(8,128)(2,1)S(1)} %collective-permute-done), channel_id=1, source_target_pairs={{0,112},{16,0},{32,16},{48,32},{64,48},{80,64},{96,80},{112,96},{1... | collective-permute-start | bytes 589832 | tf_op jit(solution)/shard_map/ppermute | solution.py:67
  63.7 1.9 collective-permute-start.4
  66.9 5.6 %collective-permute-start.2 = (bf16[3,256,128]{2,1,0:T(8,128)(2,1)S(1)}, bf16[3,256,128]{2,1,0:T(8,128)(2,1)S(1)}, u32[]{:S(2)}, u32[]{:S(2)}) collective-permute-start(bf16[3,256,128]{2,1,0:T(8,128)(2,1)S(1)} %collective-permute-done.1), channel_id=1, source_target_pairs={{0,112},{16,0},{32,16},{48,32},{64,48},{80,64},{96,80},{112,96},{1... | collective-permute-start | bytes 589832 | tf_op jit(solution)/shard_map/ppermute | solution.py:67
  72.5 1.9 collective-permute-start.5
  74.4 1.9 collective-permute-start.7
  77.1 5.0 %collective-permute-done.5 = bf16[3,256,128]{2,1,0:T(8,128)(2,1)S(1)} collective-permute-done((bf16[3,256,128]{2,1,0:T(8,128)(2,1)S(1)}, bf16[3,256,128]{2,1,0:T(8,128)(2,1)S(1)}, u32[]{:S(2)}, u32[]{:S(2)}) %collective-permute-start.5) | collective-permute-done | bytes 196640 | tf_op jit(solution)/shard_map/ppermute | solution.py:65
  82.1 2.3 collective-permute-start.6
  86.4 9.0 %collective-permute-done.6 = bf16[3,256,128]{2,1,0:T(8,128)(2,1)S(1)} collective-permute-done((bf16[3,256,128]{2,1,0:T(8,128)(2,1)S(1)}, bf16[3,256,128]{2,1,0:T(8,128)(2,1)S(1)}, u32[]{:S(2)}, u32[]{:S(2)}) %collective-permute-start.6) | collective-permute-done | bytes 196640 | tf_op jit(solution)/shard_map/ppermute | solution.py:65
  97.9 1.6 broadcast_in_dim.16
  99.5 10.2 %all-to-all-start = ((bf16[4,2048,128]{2,1,0:T(8,128)(2,1)}), bf16[4,2048,128]{2,1,0:T(8,128)(2,1)S(1)}, u32[]{:S(2)}, u32[]{:S(2)}) async-start(bf16[4,2048,128]{2,1,0:T(8,128)(2,1)} %broadcast_in_dim.16), calls=%async_computation | async-start | bytes 4194304 | tf_op jit(solution)/shard_map/all_to_all | solution.py:22
  109.7 1.7 bitcast_dynamic-update-slice_fusion
  111.4 1.6 bitcast_dynamic-update-slice_fusion.14
  113.1 1.8 bitcast_dynamic-update-slice_fusion.13
  114.9 1.6 bitcast_dynamic-update-slice_fusion.11
  116.5 1.6 bitcast_dynamic-update-slice_fusion.9
  118.1 1.6 bitcast_dynamic-update-slice_fusion.7
  119.7 1.6 bitcast_dynamic-update-slice_fusion.5
  121.4 1.6 bitcast_dynamic-update-slice_fusion.3
  124.5 1.5 constant_dynamic-slice_fusion.2
  126.0 2.0 fusion
  129.0 3.2 convolution_add_fusion.3
  132.2 14.8 %all-to-all-done = bf16[4,2048,128]{2,1,0:T(8,128)(2,1)S(1)} async-done(((bf16[4,2048,128]{2,1,0:T(8,128)(2,1)}), bf16[4,2048,128]{2,1,0:T(8,128)(2,1)S(1)}, u32[]{:S(2)}, u32[]{:S(2)}) %all-to-all-start) | async-done | bytes 2097184 | tf_op jit(solution)/shard_map/all_to_all | solution.py:22
  150.4 7.6 %all-to-all-start.3 = ((bf16[32,32,512]{2,1,0:T(8,128)(2,1)}), bf16[32,32,512]{2,1,0:T(8,128)(2,1)}, u32[]{:S(2)}, u32[]{:S(2)}) async-start(bf16[32,32,512]{2,1,0:T(8,128)(2,1)} %broadcast_in_dim.19), calls=%async_computation.3 | async-start | bytes 2097152 | tf_op jit(solution)/shard_map/all_to_all | solution.py:22
  158.0 2.0 pad_maximum_fusion
  160.6 2.3 fusion.2
  167.3 15.0 %all-to-all-done.3 = bf16[32,32,512]{2,1,0:T(8,128)(2,1)} async-done(((bf16[32,32,512]{2,1,0:T(8,128)(2,1)}), bf16[32,32,512]{2,1,0:T(8,128)(2,1)}, u32[]{:S(2)}, u32[]{:S(2)}) %all-to-all-start.3) | async-done | bytes 1048608 | tf_op jit(solution)/shard_map/all_to_all | solution.py:22
  183.8 2.1 collective-permute-start.8
  189.0 26.3 %all_to_all.70 = f32[8,24,512]{2,1,0:T(8,128)S(1)} all-to-all(f32[8,24,512]{2,1,0:T(8,128)S(1)} %bitcast.172), channel_id=1, replica_groups=mesh['line'=4,'ring'=8,'chip'=8,'core'=2] {'chip'}, dimensions={0} | all-to-all | bytes 786432 | tf_op jit(solution)/shard_map/all_to_all | solution.py:26
  216.7 18.5 %all_to_all.71 = bf16[16,24,512]{2,1,0:T(8,128)(2,1)S(1)} all-to-all(bf16[16,24,512]{2,1,0:T(8,128)(2,1)S(1)} %broadcast_in_dim.20), channel_id=1, replica_groups=mesh['line'=4,'ring'=8,'chip'=8,'core'=2] {'core','chip'}, dimensions={0} | all-to-all | bytes 786432 | tf_op jit(solution)/shard_map/all_to_all | solution.py:22
  235.2 2.6 convolution_convert_fusion
  237.8 6.3 %all-to-all-start.6 = ((bf16[32,32,512]{2,1,0:T(8,128)(2,1)}), bf16[32,32,512]{2,1,0:T(8,128)(2,1)}, u32[]{:S(2)}, u32[]{:S(2)}) async-start(bf16[32,32,512]{2,1,0:T(8,128)(2,1)} %bitcast.166), calls=%async_computation.6 | async-start | bytes 2097152 | tf_op jit(solution)/shard_map/all_to_all | solution.py:26
  250.2 20.8 %all-to-all-done.6 = bf16[32,32,512]{2,1,0:T(8,128)(2,1)} async-done(((bf16[32,32,512]{2,1,0:T(8,128)(2,1)}), bf16[32,32,512]{2,1,0:T(8,128)(2,1)}, u32[]{:S(2)}, u32[]{:S(2)}) %all-to-all-start.6) | async-done | bytes 1048608 | tf_op jit(solution)/shard_map/all_to_all | solution.py:26
  272.9 17.4 %all_to_all.72 = bf16[16,16,448]{2,1,0:T(8,128)(2,1)S(1)} all-to-all(bf16[16,16,448]{2,1,0:T(8,128)(2,1)S(1)} %bitcast.167), channel_id=1, replica_groups=mesh['line'=4,'ring'=8,'chip'=8,'core'=2] {'chip','core'}, dimensions={0} | all-to-all | bytes 458752 | tf_op jit(solution)/shard_map/all_to_all | solution.py:26
  290.4 16.0 %all_to_all.73 = bf16[16,16,448]{2,1,0:T(8,128)(2,1)S(1)} all-to-all(bf16[16,16,448]{2,1,0:T(8,128)(2,1)S(1)} %broadcast_in_dim.21), channel_id=1, replica_groups=mesh['line'=4,'ring'=8,'chip'=8,'core'=2] {'chip','core'}, dimensions={0} | all-to-all | bytes 458752 | tf_op jit(solution)/shard_map/all_to_all | solution.py:22
  306.9 17.9 %all_to_all.74 = bf16[32,8,512]{2,1,0:T(8,128)(2,1)S(1)} all-to-all(bf16[32,8,512]{2,1,0:T(8,128)(2,1)S(1)} %fusion.10), channel_id=1, replica_groups=mesh['line'=4,'ring'=8,'chip'=8,'core'=2] {'line','ring'}, dimensions={0} | all-to-all | bytes 524288 | tf_op jit(solution)/shard_map/all_to_all | solution.py:26
  325.6 16.5 %all_to_all.75 = bf16[32,8,512]{2,1,0:T(8,128)(2,1)S(1)} all-to-all(bf16[32,8,512]{2,1,0:T(8,128)(2,1)S(1)} %broadcast_in_dim.22), channel_id=1, replica_groups=mesh['line'=4,'ring'=8,'chip'=8,'core'=2] {'line','ring'}, dimensions={0} | all-to-all | bytes 524288 | tf_op jit(solution)/shard_map/all_to_all | solution.py:22
  342.5 17.4 %all_to_all.76 = bf16[16,16,448]{2,1,0:T(8,128)(2,1)S(1)} all-to-all(bf16[16,16,448]{2,1,0:T(8,128)(2,1)S(1)} %bitcast.168), channel_id=1, replica_groups=mesh['line'=4,'ring'=8,'chip'=8,'core'=2] {'chip','core'}, dimensions={0} | all-to-all | bytes 458752 | tf_op jit(solution)/shard_map/all_to_all | solution.py:26
  360.0 15.9 %all_to_all.77 = bf16[16,16,448]{2,1,0:T(8,128)(2,1)S(1)} all-to-all(bf16[16,16,448]{2,1,0:T(8,128)(2,1)S(1)} %broadcast_in_dim.23), channel_id=1, replica_groups=mesh['line'=4,'ring'=8,'chip'=8,'core'=2] {'chip','core'}, dimensions={0} | all-to-all | bytes 458752 | tf_op jit(solution)/shard_map/all_to_all | solution.py:22
  377.1 4.8 %all-to-all-start.13 = ((bf16[32,8,512]{2,1,0:T(8,128)(2,1)}), bf16[32,8,512]{2,1,0:T(8,128)(2,1)S(1)}, u32[]{:S(2)}, u32[]{:S(2)}) async-start(bf16[32,8,512]{2,1,0:T(8,128)(2,1)} %fusion.9), calls=%async_computation.13 | async-start | bytes 524288 | tf_op jit(solution)/shard_map/all_to_all | solution.py:26
  383.0 10.5 %all-to-all-done.13 = bf16[32,8,512]{2,1,0:T(8,128)(2,1)S(1)} async-done(((bf16[32,8,512]{2,1,0:T(8,128)(2,1)}), bf16[32,8,512]{2,1,0:T(8,128)(2,1)S(1)}, u32[]{:S(2)}, u32[]{:S(2)}) %all-to-all-start.13) | async-done | bytes 262176 | tf_op jit(solution)/shard_map/all_to_all | solution.py:26
  (164 shorter events, 44.8 us)
Async XLA Ops:
  7.2 13.3 %copy-start = (bf16[512,1024]{1,0:T(8,128)(2,1)S(1)}, bf16[512,1024]{1,0:T(8,128)(2,1)}, u32[]{:S(2)}) copy-start(bf16[512,1024]{1,0:T(8,128)(2,1)} %param.7) | copy-start | bytes 3145732
  7.2 89.6 %all-gather.3.cloned.1.call-start = ((), (), s32[]{:S(2)}) async-start(), calls=%async_computation.14 | async-start | bytes 2359296 | tf_op jit(solution)/shard_map/all_gather | solution.py:52
  11.0 13.0 %copy-start.36 = (s32[192]{0:T(256)S(1)}, s32[192]{0:T(256)}, u32[]{:S(2)}) copy-start(s32[192]{0:T(256)} %param.8) | copy-start | bytes 2308
  11.0 22.3 %all-to-all-start.1 = ((bf16[4,256,384]{2,1,0:T(8,128)(2,1)}), bf16[4,256,384]{2,1,0:T(8,128)(2,1)S(1)}, u32[]{:S(2)}, u32[]{:S(2)}) async-start(bf16[4,256,384]{2,1,0:T(8,128)(2,1)} %broadcast_in_dim.17), calls=%async_computation.1 | async-start | bytes 1572864 | tf_op jit(solution)/shard_map/all_to_all | solution.py:22
  34.1 38.4 %copy-start.26 = (bf16[3,256,128]{2,1,0:T(8,128)(2,1)}, bf16[3,256,128]{2,1,0:T(8,128)(2,1)S(1)}, u32[]{:S(2)}) copy-start(bf16[3,256,128]{2,1,0:T(8,128)(2,1)S(1)} %get-tuple-element.35) | copy-start | bytes 589828
  34.1 24.4 %collective-permute-start = (bf16[3,256,128]{2,1,0:T(8,128)(2,1)S(1)}, bf16[3,256,128]{2,1,0:T(8,128)(2,1)S(1)}, u32[]{:S(2)}, u32[]{:S(2)}) collective-permute-start(bf16[3,256,128]{2,1,0:T(8,128)(2,1)S(1)} %get-tuple-element.35), channel_id=1, source_target_pairs={{0,112},{16,0},{32,16},{48,32},{64,48},{80,64},{96,80},{112,96},{1... | collective-permute-start | bytes 589832 | tf_op jit(solution)/shard_map/ppermute | solution.py:67
  45.0 18.7 %collective-permute-start.3 = (bf16[3,256,128]{2,1,0:T(8,128)(2,1)S(1)}, bf16[3,256,128]{2,1,0:T(8,128)(2,1)S(1)}, u32[]{:S(2)}, u32[]{:S(2)}) collective-permute-start(bf16[3,256,128]{2,1,0:T(8,128)(2,1)S(1)} %get-tuple-element.35), channel_id=1, source_target_pairs={{0,16},{16,32},{32,48},{48,64},{64,80},{80,96},{96,112},{112,0},{1... | collective-permute-start | bytes 589832 | tf_op jit(solution)/shard_map/ppermute | solution.py:65
  47.9 26.5 %all-to-all-start.2 = ((bf16[8,32,512]{2,1,0:T(8,128)(2,1)}), bf16[8,32,512]{2,1,0:T(8,128)(2,1)S(1)}, u32[]{:S(2)}, u32[]{:S(2)}) async-start(bf16[8,32,512]{2,1,0:T(8,128)(2,1)} %broadcast_in_dim.18), calls=%async_computation.2 | async-start | bytes 524288 | tf_op jit(solution)/shard_map/all_to_all | solution.py:22
  56.3 72.7 %all-gather.5.cloned.1.call-start = ((), (), s32[]{:S(2)}) async-start(), calls=%async_computation.15 | async-start | bytes 3538944 | tf_op jit(solution)/shard_map/all_gather | solution.py:55
  58.5 26.7 %copy-start.19 = (bf16[3,256,128]{2,1,0:T(8,128)(2,1)}, bf16[3,256,128]{2,1,0:T(8,128)(2,1)S(1)}, u32[]{:S(2)}) copy-start(bf16[3,256,128]{2,1,0:T(8,128)(2,1)S(1)} %collective-permute-done) | copy-start | bytes 589828
  58.6 8.3 %collective-permute-start.1 = (bf16[3,256,128]{2,1,0:T(8,128)(2,1)S(1)}, bf16[3,256,128]{2,1,0:T(8,128)(2,1)S(1)}, u32[]{:S(2)}, u32[]{:S(2)}) collective-permute-start(bf16[3,256,128]{2,1,0:T(8,128)(2,1)S(1)} %collective-permute-done), channel_id=1, source_target_pairs={{0,112},{16,0},{32,16},{48,32},{64,48},{80,64},{96,80},{112,96},{1... | collective-permute-start | bytes 589832 | tf_op jit(solution)/shard_map/ppermute | solution.py:67
  63.7 21.6 %copy-start.17 = (bf16[3,256,128]{2,1,0:T(8,128)(2,1)}, bf16[3,256,128]{2,1,0:T(8,128)(2,1)S(1)}, u32[]{:S(2)}) copy-start(bf16[3,256,128]{2,1,0:T(8,128)(2,1)S(1)} %collective-permute-done.3) | copy-start | bytes 589828
  63.7 8.8 %collective-permute-start.4 = (bf16[3,256,128]{2,1,0:T(8,128)(2,1)S(1)}, bf16[3,256,128]{2,1,0:T(8,128)(2,1)S(1)}, u32[]{:S(2)}, u32[]{:S(2)}) collective-permute-start(bf16[3,256,128]{2,1,0:T(8,128)(2,1)S(1)} %collective-permute-done.3), channel_id=1, source_target_pairs={{0,16},{16,32},{32,48},{48,64},{64,80},{80,96},{96,112},{112,0},{1... | collective-permute-start | bytes 589832 | tf_op jit(solution)/shard_map/ppermute | solution.py:65
  66.9 18.4 %copy-start.22 = (bf16[3,256,128]{2,1,0:T(8,128)(2,1)}, bf16[3,256,128]{2,1,0:T(8,128)(2,1)S(1)}, u32[]{:S(2)}) copy-start(bf16[3,256,128]{2,1,0:T(8,128)(2,1)S(1)} %collective-permute-done.1) | copy-start | bytes 589828
  66.9 17.5 %collective-permute-start.2 = (bf16[3,256,128]{2,1,0:T(8,128)(2,1)S(1)}, bf16[3,256,128]{2,1,0:T(8,128)(2,1)S(1)}, u32[]{:S(2)}, u32[]{:S(2)}) collective-permute-start(bf16[3,256,128]{2,1,0:T(8,128)(2,1)S(1)} %collective-permute-done.1), channel_id=1, source_target_pairs={{0,112},{16,0},{32,16},{48,32},{64,48},{80,64},{96,80},{112,96},{1... | collective-permute-start | bytes 589832 | tf_op jit(solution)/shard_map/ppermute | solution.py:67
  72.5 12.8 %copy-start.20 = (bf16[3,256,128]{2,1,0:T(8,128)(2,1)}, bf16[3,256,128]{2,1,0:T(8,128)(2,1)S(1)}, u32[]{:S(2)}) copy-start(bf16[3,256,128]{2,1,0:T(8,128)(2,1)S(1)} %collective-permute-done.4) | copy-start | bytes 589828
  72.5 9.6 %collective-permute-start.5 = (bf16[3,256,128]{2,1,0:T(8,128)(2,1)S(1)}, bf16[3,256,128]{2,1,0:T(8,128)(2,1)S(1)}, u32[]{:S(2)}, u32[]{:S(2)}) collective-permute-start(bf16[3,256,128]{2,1,0:T(8,128)(2,1)S(1)} %collective-permute-done.4), channel_id=1, source_target_pairs={{0,16},{16,32},{32,48},{48,64},{64,80},{80,96},{96,112},{112,0},{1... | collective-permute-start | bytes 589832 | tf_op jit(solution)/shard_map/ppermute | solution.py:65
  74.4 10.7 %collective-permute-start.7 = (bf16[8,32,512]{2,1,0:T(8,128)(2,1)S(1)}, bf16[8,32,512]{2,1,0:T(8,128)(2,1)S(1)}, u32[]{:S(2)}, u32[]{:S(2)}) collective-permute-start(bf16[8,32,512]{2,1,0:T(8,128)(2,1)S(1)} %all-to-all-done.2), channel_id=1, source_target_pairs={{0,1},{1,0},{2,3},{3,2},{4,5},{5,4},{6,7},{7,6},{8,9},{9,8},{10,11... | collective-permute-start | bytes 786440 | tf_op jit(solution)/shard_map/ppermute | solution.py:138
  82.1 14.1 %copy-start.24 = (bf16[3,256,128]{2,1,0:T(8,128)(2,1)}, bf16[3,256,128]{2,1,0:T(8,128)(2,1)S(1)}, u32[]{:S(2)}) copy-start(bf16[3,256,128]{2,1,0:T(8,128)(2,1)S(1)} %collective-permute-done.5) | copy-start | bytes 589828
  82.1 13.3 %collective-permute-start.6 = (bf16[3,256,128]{2,1,0:T(8,128)(2,1)S(1)}, bf16[3,256,128]{2,1,0:T(8,128)(2,1)S(1)}, u32[]{:S(2)}, u32[]{:S(2)}) collective-permute-start(bf16[3,256,128]{2,1,0:T(8,128)(2,1)S(1)} %collective-permute-done.5), channel_id=1, source_target_pairs={{0,16},{16,32},{32,48},{48,64},{64,80},{80,96},{96,112},{112,0},{1... | collective-permute-start | bytes 589832 | tf_op jit(solution)/shard_map/ppermute | solution.py:65
  86.3 13.2 %copy-start.5 = (bf16[32,8192]{1,0:T(8,128)(2,1)}, bf16[32,8192]{1,0:T(8,128)(2,1)S(1)}, u32[]{:S(2)}) copy-start(bf16[32,8192]{1,0:T(8,128)(2,1)S(1)} %reshape.101) | copy-start | bytes 1572868
  86.3 13.2 %copy-start.9 = (bf16[32,2048]{1,0:T(8,128)(2,1)}, bf16[32,2048]{1,0:T(8,128)(2,1)S(1)}, u32[]{:S(2)}) copy-start(bf16[32,2048]{1,0:T(8,128)(2,1)S(1)} %get-tuple-element.46) | copy-start | bytes 393220
  86.3 13.2 %copy-start.11 = (bf16[32,2048]{1,0:T(8,128)(2,1)}, bf16[32,2048]{1,0:T(8,128)(2,1)S(1)}, u32[]{:S(2)}) copy-start(bf16[32,2048]{1,0:T(8,128)(2,1)S(1)} %get-tuple-element.47) | copy-start | bytes 393220
  86.4 13.2 %copy-start.13 = (bf16[32,2048]{1,0:T(8,128)(2,1)}, bf16[32,2048]{1,0:T(8,128)(2,1)S(1)}, u32[]{:S(2)}) copy-start(bf16[32,2048]{1,0:T(8,128)(2,1)S(1)} %get-tuple-element.48) | copy-start | bytes 393220
  95.4 4.1 %copy-start.25 = (bf16[3,256,128]{2,1,0:T(8,128)(2,1)}, bf16[3,256,128]{2,1,0:T(8,128)(2,1)S(1)}, u32[]{:S(2)}) copy-start(bf16[3,256,128]{2,1,0:T(8,128)(2,1)S(1)} %collective-permute-done.6) | copy-start | bytes 589828
  99.5 47.5 %all-to-all-start = ((bf16[4,2048,128]{2,1,0:T(8,128)(2,1)}), bf16[4,2048,128]{2,1,0:T(8,128)(2,1)S(1)}, u32[]{:S(2)}, u32[]{:S(2)}) async-start(bf16[4,2048,128]{2,1,0:T(8,128)(2,1)} %broadcast_in_dim.16), calls=%async_computation | async-start | bytes 4194304 | tf_op jit(solution)/shard_map/all_to_all | solution.py:22
  109.7 13.3 %copy-start.21 = (bf16[3,256,128]{2,1,0:T(8,128)(2,1)S(1)}, bf16[3,256,128]{2,1,0:T(8,128)(2,1)}, u32[]{:S(2)}) copy-start(bf16[3,256,128]{2,1,0:T(8,128)(2,1)} %copy-done.20) | copy-start | bytes 589828
  109.7 14.0 %copy-start.18 = (bf16[3,256,128]{2,1,0:T(8,128)(2,1)S(1)}, bf16[3,256,128]{2,1,0:T(8,128)(2,1)}, u32[]{:S(2)}) copy-start(bf16[3,256,128]{2,1,0:T(8,128)(2,1)} %copy-done.17) | copy-start | bytes 589828
  113.1 12.9 %copy-start.30 = (bf16[2048,512]{1,0:T(8,128)(2,1)S(1)}, bf16[2048,512]{1,0:T(8,128)(2,1)}, u32[]{:S(2)}) copy-start(bf16[2048,512]{1,0:T(8,128)(2,1)} %all-gather.3.cloned.1.call-done) | copy-start | bytes 6291460
  123.0 5.6 %copy-start.10 = (bf16[32,2048]{1,0:T(8,128)(2,1)S(1)}, bf16[32,2048]{1,0:T(8,128)(2,1)}, u32[]{:S(2)}) copy-start(bf16[32,2048]{1,0:T(8,128)(2,1)} %copy-done.9) | copy-start | bytes 393220
  123.0 5.6 %copy-start.12 = (bf16[32,2048]{1,0:T(8,128)(2,1)S(1)}, bf16[32,2048]{1,0:T(8,128)(2,1)}, u32[]{:S(2)}) copy-start(bf16[32,2048]{1,0:T(8,128)(2,1)} %copy-done.11) | copy-start | bytes 393220
  123.0 5.6 %copy-start.14 = (bf16[32,2048]{1,0:T(8,128)(2,1)S(1)}, bf16[32,2048]{1,0:T(8,128)(2,1)}, u32[]{:S(2)}) copy-start(bf16[32,2048]{1,0:T(8,128)(2,1)} %copy-done.13) | copy-start | bytes 393220
  126.0 2.6 copy-start.3
  148.5 11.5 %copy-start.31 = (f32[32,128]{1,0:T(8,128)}, f32[32,128]{1,0:T(8,128)S(1)}, u32[]{:S(2)}) copy-start(f32[32,128]{1,0:T(8,128)S(1)} %fusion.64) | copy-start | bytes 49156
  150.4 31.9 %all-to-all-start.3 = ((bf16[32,32,512]{2,1,0:T(8,128)(2,1)}), bf16[32,32,512]{2,1,0:T(8,128)(2,1)}, u32[]{:S(2)}, u32[]{:S(2)}) async-start(bf16[32,32,512]{2,1,0:T(8,128)(2,1)} %broadcast_in_dim.19), calls=%async_computation.3 | async-start | bytes 2097152 | tf_op jit(solution)/shard_map/all_to_all | solution.py:22
  165.6 21.9 %copy-start.27 = (f32[192,128]{1,0:T(8,128)}, f32[192,128]{1,0:T(8,128)S(1)}, u32[]{:S(2)}) copy-start(f32[192,128]{1,0:T(8,128)S(1)} %convolution_bitcast_fusion) | copy-start | bytes 294916
  165.6 16.7 %copy-start.33 = (f32[192,128]{1,0:T(8,128)S(1)}, f32[192,128]{1,0:T(8,128)}, u32[]{:S(2)}) copy-start(f32[192,128]{1,0:T(8,128)} %convolution_add_fusion.2) | copy-start | bytes 294916
  167.3 21.7 %copy-start.15 = (f32[192,256]{1,0:T(8,128)}, f32[192,256]{1,0:T(8,128)S(1)}, u32[]{:S(2)}) copy-start(f32[192,256]{1,0:T(8,128)S(1)} %convolution_add_fusion.1) | copy-start | bytes 589828
  183.8 3.6 collective-permute-start.8
  237.8 33.2 %all-to-all-start.6 = ((bf16[32,32,512]{2,1,0:T(8,128)(2,1)}), bf16[32,32,512]{2,1,0:T(8,128)(2,1)}, u32[]{:S(2)}, u32[]{:S(2)}) async-start(bf16[32,32,512]{2,1,0:T(8,128)(2,1)} %bitcast.166), calls=%async_computation.6 | async-start | bytes 2097152 | tf_op jit(solution)/shard_map/all_to_all | solution.py:26
  246.0 3.9 copy-start.16
  246.0 3.9 copy-start.28
  246.0 3.9 copy-start.34
  246.0 3.9 copy-start.37
  249.5 22.8 %copy-start.29 = (f32[32,256]{1,0:T(8,128)S(1)}, f32[32,256]{1,0:T(8,128)}, u32[]{:S(2)}) copy-start(f32[32,256]{1,0:T(8,128)} %convolution_add_fusion.3) | copy-start | bytes 98308
  249.5 22.8 %copy-start.32 = (f32[32,128]{1,0:T(8,128)S(1)}, f32[32,128]{1,0:T(8,128)}, u32[]{:S(2)}) copy-start(f32[32,128]{1,0:T(8,128)} %copy-done.31) | copy-start | bytes 49156
  249.6 22.8 %copy-start.35 = (f32[32]{0:T(128)S(1)}, f32[32]{0:T(128)}, u32[]{:S(2)}) copy-start(f32[32]{0:T(128)} %convert_multiply_fusion.1) | copy-start | bytes 388
  377.1 16.3 %all-to-all-start.13 = ((bf16[32,8,512]{2,1,0:T(8,128)(2,1)}), bf16[32,8,512]{2,1,0:T(8,128)(2,1)S(1)}, u32[]{:S(2)}, u32[]{:S(2)}) async-start(bf16[32,8,512]{2,1,0:T(8,128)(2,1)} %fusion.9), calls=%async_computation.13 | async-start | bytes 524288 | tf_op jit(solution)/shard_map/all_to_all | solution.py:26
  (7 other events, 16.0 us)
Sparse Core Ops, SparseCore 0:
  10.1 51.4 all-gather.2
  63.7 51.8 all-gather.4

commit v14 on v13

--- a/solution.py
+++ b/solution.py
@@ -51,10 +51,10 @@
 def gather_rotation(rot_b, line_wide, line_pos):
     near = lax.all_gather(rot_b, "ring", axis=0, tiled=True)
     others = jnp.stack([pick_other(k, line_wide, line_pos) for k in range(LINE - 1)])
-    middle = ring_pass(others[:, :, :THIN])
     far = lax.all_gather(others[:, :, THIN:], "ring", axis=1, tiled=True)
-    thin = gather_blocks(near[:, :THIN], "line").reshape(LINE * near.shape[0], THIN)
-    return thin, near, middle, far
+    thin_own, middle_own = lax.optimization_barrier((near[:, :THIN], others[:, :, :THIN]))
+    thin = gather_blocks(thin_own, "line").reshape(LINE * near.shape[0], THIN)
+    return thin, near, ring_pass(middle_own), far
 
 
 def ring_pass(own):
@@ -65,10 +65,10 @@
         found[RING - step] = lax.ppermute(found[(RING - step + 1) % RING], "ring", up)
         if step < RING // 2:
             found[step] = lax.ppermute(found[step - 1], "ring", down)
-    near_first = [found[k] for k in range(RING)]
-    twice = jnp.stack(near_first + near_first, 1)
-    start = (RING - lax.axis_index("ring")) % RING
-    ordered = lax.dynamic_slice_in_dim(twice, start, RING, 1)
+    ordered = jnp.zeros((own.shape[0], RING) + own.shape[1:], own.dtype)
+    for k in range(RING):
+        place = (lax.axis_index("ring") + k) % RING
+        ordered = lax.dynamic_update_index_in_dim(ordered, found[k], place, 1)
     return ordered.reshape(own.shape[0], -1, own.shape[2])
 
 

time: 404 us -> 390 us (0.965)
  local copies, waits for them, and re-layouts: 38.3 us -> 20.4 us
  waiting for transfers between devices: 82.3 us -> 90.2 us
  starting transfers between devices: 80.6 us -> 75.8 us
    unnamed x90 -> x58, local copies, waits for them, and re-layouts: 19.5 us -> 3.07 us
    ppermute x4, waiting for transfers between devices: 14 us -> 20.7 us  [ring_pass(): lax.ppermute(found[(RING - step + 1) % RING], 'ring', up)]
    all_to_all x4, starting transfers between devices: 35.6 us -> 31.4 us  [gather_blocks(): lax.all_to_all(jnp.broadcast_to(own[None], (parts,) + own.shape), axis, 0...]
  transfers between devices with their start and end apart: 17 -> 17, of which waited for: 9 -> 10; matrix products, arithmetic and copies ran while one was open for 14% -> 11% of each run, Pallas kernels for 0% -> 0%
where the time goes in v14:
time: 390 us; the launch traced here: 388 us
  blocking collectives  145 us (37%)
  waiting for transfers between devices  90.2 us (23%)
  starting transfers between devices  75.8 us (19%)
  matrix products  22.2 us (6%)
  local copies, waits for them, and re-layouts  20.4 us (5%)
  other arithmetic  19.3 us (5%)
  between operations  14.9 us (4%)
    all_to_all x4, blocking collectives, sum_blocks(): return jnp.sum(lax.all_to_all(blocks, axis, 0, 0).astype(jnp.float32), 0)  77.7 us
    all_to_all x4, blocking collectives, gather_blocks(): lax.all_to_all(jnp.broadcast_to(own[None], (parts,) + own.shape), axis, 0...  67.5 us
    all_to_all x4, waiting for transfers between devices, gather_blocks(): lax.all_to_all(jnp.broadcast_to(own[None], (parts,) + own.shape), axis, 0...  36.6 us
    all_to_all x4, starting transfers between devices, gather_blocks(): lax.all_to_all(jnp.broadcast_to(own[None], (parts,) + own.shape), axis, 0...  31.4 us
    all_to_all x2, waiting for transfers between devices, sum_blocks(): return jnp.sum(lax.all_to_all(blocks, axis, 0, 0).astype(jnp.float32), 0)  31.2 us
    ppermute x4, waiting for transfers between devices, ring_pass(): lax.ppermute(found[(RING - step + 1) % RING], 'ring', up)  20.7 us
    ppermute x3, starting transfers between devices, ring_pass(): found[step] = lax.ppermute(found[step - 1], 'ring', down)  19 us
    all_to_all x2, starting transfers between devices, sum_blocks(): return jnp.sum(lax.all_to_all(blocks, axis, 0, 0).astype(jnp.float32), 0)  11.4 us
  transfers between devices with their start and end apart: 17, of which 10 were waited for; matrix products, arithmetic and copies ran while one was open for 11% of the time, Pallas kernels for 0%

profile of v14, /device:TPU:8, one launch (start us, length us, event | category | flops | bytes accessed | tf_op | source)
XLA Modules:
  0.0 387.9 jit_solution(11287637107432186113)
XLA Ops:
  7.2 1.9 convert_element_type.82
  11.0 9.4 %all-to-all-start = ((bf16[4,256,384]{2,1,0:T(8,128)(2,1)}), bf16[4,256,384]{2,1,0:T(8,128)(2,1)S(1)}, u32[]{:S(2)}, u32[]{:S(2)}) async-start(bf16[4,256,384]{2,1,0:T(8,128)(2,1)} %broadcast_in_dim.78), calls=%async_computation | async-start | bytes 1572864 | tf_op jit(solution)/shard_map/all_to_all | solution.py:22
  20.4 12.9 %all-to-all-done = bf16[4,256,384]{2,1,0:T(8,128)(2,1)S(1)} async-done(((bf16[4,256,384]{2,1,0:T(8,128)(2,1)}), bf16[4,256,384]{2,1,0:T(8,128)(2,1)S(1)}, u32[]{:S(2)}, u32[]{:S(2)}) %all-to-all-start) | async-done | bytes 786464 | tf_op jit(solution)/shard_map/all_to_all | solution.py:22
  37.0 8.4 %all-to-all-start.2 = ((bf16[8,32,512]{2,1,0:T(8,128)(2,1)}), bf16[8,32,512]{2,1,0:T(8,128)(2,1)S(1)}, u32[]{:S(2)}, u32[]{:S(2)}) async-start(bf16[8,32,512]{2,1,0:T(8,128)(2,1)} %broadcast_in_dim.89), calls=%async_computation.2 | async-start | bytes 524288 | tf_op jit(solution)/shard_map/all_to_all | solution.py:22
  45.5 3.4 broadcast_select_fusion.2
  48.8 8.9 %all-to-all-done.2 = bf16[8,32,512]{2,1,0:T(8,128)(2,1)S(1)} async-done(((bf16[8,32,512]{2,1,0:T(8,128)(2,1)}), bf16[8,32,512]{2,1,0:T(8,128)(2,1)S(1)}, u32[]{:S(2)}, u32[]{:S(2)}) %all-to-all-start.2) | async-done | bytes 262176 | tf_op jit(solution)/shard_map/all_to_all | solution.py:22
  57.8 1.9 collective-permute-start.7
  59.7 1.3 convert_multiply_fusion.1
  61.7 1.6 constant_dynamic-slice_fusion.1
  67.9 1.6 broadcast_in_dim.79
  69.5 5.8 %all-to-all-start.1 = ((bf16[4,2048,128]{2,1,0:T(8,128)(2,1)}), bf16[4,2048,128]{2,1,0:T(8,128)(2,1)S(1)}, u32[]{:S(2)}, u32[]{:S(2)}) async-start(bf16[4,2048,128]{2,1,0:T(8,128)(2,1)} %broadcast_in_dim.79), calls=%async_computation.1 | async-start | bytes 4194304 | tf_op jit(solution)/shard_map/all_to_all | solution.py:22
  76.4 4.4 %collective-permute-start.3 = (bf16[3,256,128]{2,1,0:T(8,128)(2,1)}, bf16[3,256,128]{2,1,0:T(8,128)(2,1)S(1)}, u32[]{:S(2)}, u32[]{:S(2)}) collective-permute-start(bf16[3,256,128]{2,1,0:T(8,128)(2,1)} %pad_maximum_fusion.7), channel_id=1, source_target_pairs={{0,16},{16,32},{32,48},{48,64},{64,80},{80,96},{96,112},{112,0},{1... | collective-permute-start | bytes 589832 | tf_op jit(solution)/shard_map/ppermute | solution.py:65
  80.8 8.6 %collective-permute-start = (bf16[3,256,128]{2,1,0:T(8,128)(2,1)}, bf16[3,256,128]{2,1,0:T(8,128)(2,1)S(1)}, u32[]{:S(2)}, u32[]{:S(2)}) collective-permute-start(bf16[3,256,128]{2,1,0:T(8,128)(2,1)} %pad_maximum_fusion.7), channel_id=1, source_target_pairs={{0,112},{16,0},{32,16},{48,32},{64,48},{80,64},{96,80},{112,96},{1... | collective-permute-start | bytes 589832 | tf_op jit(solution)/shard_map/ppermute | solution.py:67
  89.4 2.0 fusion
  92.4 4.7 %collective-permute-done.3 = bf16[3,256,128]{2,1,0:T(8,128)(2,1)S(1)} collective-permute-done((bf16[3,256,128]{2,1,0:T(8,128)(2,1)}, bf16[3,256,128]{2,1,0:T(8,128)(2,1)S(1)}, u32[]{:S(2)}, u32[]{:S(2)}) %collective-permute-start.3) | collective-permute-done | bytes 196640 | tf_op jit(solution)/shard_map/ppermute | solution.py:65
  97.1 1.9 collective-permute-start.4
  99.0 5.1 %collective-permute-start.1 = (bf16[3,256,128]{2,1,0:T(8,128)(2,1)S(1)}, bf16[3,256,128]{2,1,0:T(8,128)(2,1)S(1)}, u32[]{:S(2)}, u32[]{:S(2)}) collective-permute-start(bf16[3,256,128]{2,1,0:T(8,128)(2,1)S(1)} %collective-permute-done), channel_id=1, source_target_pairs={{0,112},{16,0},{32,16},{48,32},{64,48},{80,64},{96,80},{112,96},{1... | collective-permute-start | bytes 589832 | tf_op jit(solution)/shard_map/ppermute | solution.py:67
  104.2 7.5 %collective-permute-done.4 = bf16[3,256,128]{2,1,0:T(8,128)(2,1)S(1)} collective-permute-done((bf16[3,256,128]{2,1,0:T(8,128)(2,1)S(1)}, bf16[3,256,128]{2,1,0:T(8,128)(2,1)S(1)}, u32[]{:S(2)}, u32[]{:S(2)}) %collective-permute-start.4) | collective-permute-done | bytes 196640 | tf_op jit(solution)/shard_map/ppermute | solution.py:65
  111.7 1.9 collective-permute-start.5
  113.6 5.2 %collective-permute-start.2 = (bf16[3,256,128]{2,1,0:T(8,128)(2,1)S(1)}, bf16[3,256,128]{2,1,0:T(8,128)(2,1)S(1)}, u32[]{:S(2)}, u32[]{:S(2)}) collective-permute-start(bf16[3,256,128]{2,1,0:T(8,128)(2,1)S(1)} %collective-permute-done.1), channel_id=1, source_target_pairs={{0,112},{16,0},{32,16},{48,32},{64,48},{80,64},{96,80},{112,96},{1... | collective-permute-start | bytes 589832 | tf_op jit(solution)/shard_map/ppermute | solution.py:67
  118.9 1.7 collective-permute-done.5
  120.6 1.9 collective-permute-start.6
  122.6 6.8 %collective-permute-done.6 = bf16[3,256,128]{2,1,0:T(8,128)(2,1)S(1)} collective-permute-done((bf16[3,256,128]{2,1,0:T(8,128)(2,1)S(1)}, bf16[3,256,128]{2,1,0:T(8,128)(2,1)S(1)}, u32[]{:S(2)}, u32[]{:S(2)}) %collective-permute-start.6) | collective-permute-done | bytes 196640 | tf_op jit(solution)/shard_map/ppermute | solution.py:65
  131.4 3.1 convolution_add_fusion.3
  134.5 1.5 fusion.64
  137.2 7.8 %all-to-all-start.3 = ((bf16[32,32,512]{2,1,0:T(8,128)(2,1)}), bf16[32,32,512]{2,1,0:T(8,128)(2,1)}, u32[]{:S(2)}, u32[]{:S(2)}) async-start(bf16[32,32,512]{2,1,0:T(8,128)(2,1)} %broadcast_in_dim.90), calls=%async_computation.3 | async-start | bytes 2097152 | tf_op jit(solution)/shard_map/all_to_all | solution.py:22
  145.1 2.0 pad_maximum_fusion
  147.7 2.3 fusion.2
  150.2 1.4 convolution_add_fusion.2
  154.4 14.7 %all-to-all-done.3 = bf16[32,32,512]{2,1,0:T(8,128)(2,1)} async-done(((bf16[32,32,512]{2,1,0:T(8,128)(2,1)}), bf16[32,32,512]{2,1,0:T(8,128)(2,1)}, u32[]{:S(2)}, u32[]{:S(2)}) %all-to-all-start.3) | async-done | bytes 1048608 | tf_op jit(solution)/shard_map/all_to_all | solution.py:22
  169.1 1.6 convolution_subtract_fusion.2
  170.7 1.9 collective-permute-start.8
  172.6 1.7 collective-permute-done.8
  174.3 1.4 fusion.6
  175.7 25.0 %all_to_all.70 = f32[8,24,512]{2,1,0:T(8,128)S(1)} all-to-all(f32[8,24,512]{2,1,0:T(8,128)S(1)} %bitcast.145), channel_id=1, replica_groups=mesh['line'=4,'ring'=8,'chip'=8,'core'=2] {'chip'}, dimensions={0} | all-to-all | bytes 786432 | tf_op jit(solution)/shard_map/all_to_all | solution.py:26
  202.1 19.2 %all_to_all.71 = bf16[16,24,512]{2,1,0:T(8,128)(2,1)S(1)} all-to-all(bf16[16,24,512]{2,1,0:T(8,128)(2,1)S(1)} %broadcast_in_dim.91), channel_id=1, replica_groups=mesh['line'=4,'ring'=8,'chip'=8,'core'=2] {'core','chip'}, dimensions={0} | all-to-all | bytes 786432 | tf_op jit(solution)/shard_map/all_to_all | solution.py:22
  221.3 2.6 convolution_convert_fusion
  223.9 6.5 %all-to-all-start.6 = ((bf16[32,32,512]{2,1,0:T(8,128)(2,1)}), bf16[32,32,512]{2,1,0:T(8,128)(2,1)}, u32[]{:S(2)}, u32[]{:S(2)}) async-start(bf16[32,32,512]{2,1,0:T(8,128)(2,1)} %bitcast.139), calls=%async_computation.6 | async-start | bytes 2097152 | tf_op jit(solution)/shard_map/all_to_all | solution.py:26
  236.5 20.8 %all-to-all-done.6 = bf16[32,32,512]{2,1,0:T(8,128)(2,1)} async-done(((bf16[32,32,512]{2,1,0:T(8,128)(2,1)}), bf16[32,32,512]{2,1,0:T(8,128)(2,1)}, u32[]{:S(2)}, u32[]{:S(2)}) %all-to-all-start.6) | async-done | bytes 1048608 | tf_op jit(solution)/shard_map/all_to_all | solution.py:26
  257.2 1.4 convert_reduce_fusion
  259.2 17.4 %all_to_all.72 = bf16[16,16,448]{2,1,0:T(8,128)(2,1)S(1)} all-to-all(bf16[16,16,448]{2,1,0:T(8,128)(2,1)S(1)} %bitcast.140), channel_id=1, replica_groups=mesh['line'=4,'ring'=8,'chip'=8,'core'=2] {'chip','core'}, dimensions={0} | all-to-all | bytes 458752 | tf_op jit(solution)/shard_map/all_to_all | solution.py:26
  276.6 16.0 %all_to_all.73 = bf16[16,16,448]{2,1,0:T(8,128)(2,1)S(1)} all-to-all(bf16[16,16,448]{2,1,0:T(8,128)(2,1)S(1)} %broadcast_in_dim.92), channel_id=1, replica_groups=mesh['line'=4,'ring'=8,'chip'=8,'core'=2] {'chip','core'}, dimensions={0} | all-to-all | bytes 458752 | tf_op jit(solution)/shard_map/all_to_all | solution.py:22
  293.1 17.8 %all_to_all.74 = bf16[32,8,512]{2,1,0:T(8,128)(2,1)S(1)} all-to-all(bf16[32,8,512]{2,1,0:T(8,128)(2,1)S(1)} %fusion.10), channel_id=1, replica_groups=mesh['line'=4,'ring'=8,'chip'=8,'core'=2] {'line','ring'}, dimensions={0} | all-to-all | bytes 524288 | tf_op jit(solution)/shard_map/all_to_all | solution.py:26
  311.8 16.5 %all_to_all.75 = bf16[32,8,512]{2,1,0:T(8,128)(2,1)S(1)} all-to-all(bf16[32,8,512]{2,1,0:T(8,128)(2,1)S(1)} %broadcast_in_dim.93), channel_id=1, replica_groups=mesh['line'=4,'ring'=8,'chip'=8,'core'=2] {'line','ring'}, dimensions={0} | all-to-all | bytes 524288 | tf_op jit(solution)/shard_map/all_to_all | solution.py:22
  328.7 17.5 %all_to_all.76 = bf16[16,16,448]{2,1,0:T(8,128)(2,1)S(1)} all-to-all(bf16[16,16,448]{2,1,0:T(8,128)(2,1)S(1)} %bitcast.141), channel_id=1, replica_groups=mesh['line'=4,'ring'=8,'chip'=8,'core'=2] {'chip','core'}, dimensions={0} | all-to-all | bytes 458752 | tf_op jit(solution)/shard_map/all_to_all | solution.py:26
  346.3 15.8 %all_to_all.77 = bf16[16,16,448]{2,1,0:T(8,128)(2,1)S(1)} all-to-all(bf16[16,16,448]{2,1,0:T(8,128)(2,1)S(1)} %broadcast_in_dim.94), channel_id=1, replica_groups=mesh['line'=4,'ring'=8,'chip'=8,'core'=2] {'chip','core'}, dimensions={0} | all-to-all | bytes 458752 | tf_op jit(solution)/shard_map/all_to_all | solution.py:22
  363.3 4.9 %all-to-all-start.13 = ((bf16[32,8,512]{2,1,0:T(8,128)(2,1)}), bf16[32,8,512]{2,1,0:T(8,128)(2,1)S(1)}, u32[]{:S(2)}, u32[]{:S(2)}) async-start(bf16[32,8,512]{2,1,0:T(8,128)(2,1)} %fusion.9), calls=%async_computation.13 | async-start | bytes 524288 | tf_op jit(solution)/shard_map/all_to_all | solution.py:26
  369.2 10.5 %all-to-all-done.13 = bf16[32,8,512]{2,1,0:T(8,128)(2,1)S(1)} async-done(((bf16[32,8,512]{2,1,0:T(8,128)(2,1)}), bf16[32,8,512]{2,1,0:T(8,128)(2,1)S(1)}, u32[]{:S(2)}, u32[]{:S(2)}) %all-to-all-start.13) | async-done | bytes 262176 | tf_op jit(solution)/shard_map/all_to_all | solution.py:26
  (140 shorter events, 33.0 us)
Async XLA Ops:
  7.2 27.6 %copy-start = (bf16[512,1024]{1,0:T(8,128)(2,1)S(1)}, bf16[512,1024]{1,0:T(8,128)(2,1)}, u32[]{:S(2)}) copy-start(bf16[512,1024]{1,0:T(8,128)(2,1)} %param.7) | copy-start | bytes 3145732
  7.2 59.7 %all-gather.3.cloned.1.call-start = ((), (), s32[]{:S(2)}) async-start(), calls=%async_computation.14 | async-start | bytes 2359296 | tf_op jit(solution)/shard_map/all_gather | solution.py:52
  11.0 23.2 %copy-start.26 = (s32[192]{0:T(256)S(1)}, s32[192]{0:T(256)}, u32[]{:S(2)}) copy-start(s32[192]{0:T(256)} %param.8) | copy-start | bytes 2308
  11.0 22.3 %all-to-all-start = ((bf16[4,256,384]{2,1,0:T(8,128)(2,1)}), bf16[4,256,384]{2,1,0:T(8,128)(2,1)S(1)}, u32[]{:S(2)}, u32[]{:S(2)}) async-start(bf16[4,256,384]{2,1,0:T(8,128)(2,1)} %broadcast_in_dim.78), calls=%async_computation | async-start | bytes 1572864 | tf_op jit(solution)/shard_map/all_to_all | solution.py:22
  20.4 110.9 %all-gather.5.cloned.1.call-start = ((), (), s32[]{:S(2)}) async-start(), calls=%async_computation.15 | async-start | bytes 3538944 | tf_op jit(solution)/shard_map/all_gather | solution.py:54
  37.0 20.7 %all-to-all-start.2 = ((bf16[8,32,512]{2,1,0:T(8,128)(2,1)}), bf16[8,32,512]{2,1,0:T(8,128)(2,1)S(1)}, u32[]{:S(2)}, u32[]{:S(2)}) async-start(bf16[8,32,512]{2,1,0:T(8,128)(2,1)} %broadcast_in_dim.89), calls=%async_computation.2 | async-start | bytes 524288 | tf_op jit(solution)/shard_map/all_to_all | solution.py:22
  57.8 6.3 %collective-permute-start.7 = (bf16[8,32,512]{2,1,0:T(8,128)(2,1)S(1)}, bf16[8,32,512]{2,1,0:T(8,128)(2,1)}, u32[]{:S(2)}, u32[]{:S(2)}) collective-permute-start(bf16[8,32,512]{2,1,0:T(8,128)(2,1)S(1)} %all-to-all-done.2), channel_id=1, source_target_pairs={{0,1},{1,0},{2,3},{3,2},{4,5},{5,4},{6,7},{7,6},{8,9},{9,8},{10,11... | collective-permute-start | bytes 786440 | tf_op jit(solution)/shard_map/ppermute | solution.py:138
  66.0 3.5 copy-start.5
  69.5 65.0 %all-to-all-start.1 = ((bf16[4,2048,128]{2,1,0:T(8,128)(2,1)}), bf16[4,2048,128]{2,1,0:T(8,128)(2,1)S(1)}, u32[]{:S(2)}, u32[]{:S(2)}) async-start(bf16[4,2048,128]{2,1,0:T(8,128)(2,1)} %broadcast_in_dim.79), calls=%async_computation.1 | async-start | bytes 4194304 | tf_op jit(solution)/shard_map/all_to_all | solution.py:22
  76.4 16.0 %copy-start.14 = (bf16[3,256,128]{2,1,0:T(8,128)(2,1)S(1)}, bf16[3,256,128]{2,1,0:T(8,128)(2,1)}, u32[]{:S(2)}) copy-start(bf16[3,256,128]{2,1,0:T(8,128)(2,1)} %pad_maximum_fusion.7) | copy-start | bytes 589828
  76.4 20.7 %collective-permute-start.3 = (bf16[3,256,128]{2,1,0:T(8,128)(2,1)}, bf16[3,256,128]{2,1,0:T(8,128)(2,1)S(1)}, u32[]{:S(2)}, u32[]{:S(2)}) collective-permute-start(bf16[3,256,128]{2,1,0:T(8,128)(2,1)} %pad_maximum_fusion.7), channel_id=1, source_target_pairs={{0,16},{16,32},{32,48},{48,64},{64,80},{80,96},{96,112},{112,0},{1... | collective-permute-start | bytes 589832 | tf_op jit(solution)/shard_map/ppermute | solution.py:65
  80.8 18.3 %collective-permute-start = (bf16[3,256,128]{2,1,0:T(8,128)(2,1)}, bf16[3,256,128]{2,1,0:T(8,128)(2,1)S(1)}, u32[]{:S(2)}, u32[]{:S(2)}) collective-permute-start(bf16[3,256,128]{2,1,0:T(8,128)(2,1)} %pad_maximum_fusion.7), channel_id=1, source_target_pairs={{0,112},{16,0},{32,16},{48,32},{64,48},{80,64},{96,80},{112,96},{1... | collective-permute-start | bytes 589832 | tf_op jit(solution)/shard_map/ppermute | solution.py:67
  97.1 14.6 %collective-permute-start.4 = (bf16[3,256,128]{2,1,0:T(8,128)(2,1)S(1)}, bf16[3,256,128]{2,1,0:T(8,128)(2,1)S(1)}, u32[]{:S(2)}, u32[]{:S(2)}) collective-permute-start(bf16[3,256,128]{2,1,0:T(8,128)(2,1)S(1)} %collective-permute-done.3), channel_id=1, source_target_pairs={{0,16},{16,32},{32,48},{48,64},{64,80},{80,96},{96,112},{112,0},{1... | collective-permute-start | bytes 589832 | tf_op jit(solution)/shard_map/ppermute | solution.py:65
  99.0 14.6 %collective-permute-start.1 = (bf16[3,256,128]{2,1,0:T(8,128)(2,1)S(1)}, bf16[3,256,128]{2,1,0:T(8,128)(2,1)S(1)}, u32[]{:S(2)}, u32[]{:S(2)}) collective-permute-start(bf16[3,256,128]{2,1,0:T(8,128)(2,1)S(1)} %collective-permute-done), channel_id=1, source_target_pairs={{0,112},{16,0},{32,16},{48,32},{64,48},{80,64},{96,80},{112,96},{1... | collective-permute-start | bytes 589832 | tf_op jit(solution)/shard_map/ppermute | solution.py:67
  111.7 8.9 %collective-permute-start.5 = (bf16[3,256,128]{2,1,0:T(8,128)(2,1)S(1)}, bf16[3,256,128]{2,1,0:T(8,128)(2,1)S(1)}, u32[]{:S(2)}, u32[]{:S(2)}) collective-permute-start(bf16[3,256,128]{2,1,0:T(8,128)(2,1)S(1)} %collective-permute-done.4), channel_id=1, source_target_pairs={{0,16},{16,32},{32,48},{48,64},{64,80},{80,96},{96,112},{112,0},{1... | collective-permute-start | bytes 589832 | tf_op jit(solution)/shard_map/ppermute | solution.py:65
  113.6 8.9 %collective-permute-start.2 = (bf16[3,256,128]{2,1,0:T(8,128)(2,1)S(1)}, bf16[3,256,128]{2,1,0:T(8,128)(2,1)S(1)}, u32[]{:S(2)}, u32[]{:S(2)}) collective-permute-start(bf16[3,256,128]{2,1,0:T(8,128)(2,1)S(1)} %collective-permute-done.1), channel_id=1, source_target_pairs={{0,112},{16,0},{32,16},{48,32},{64,48},{80,64},{96,80},{112,96},{1... | collective-permute-start | bytes 589832 | tf_op jit(solution)/shard_map/ppermute | solution.py:67
  120.6 8.8 %collective-permute-start.6 = (bf16[3,256,128]{2,1,0:T(8,128)(2,1)S(1)}, bf16[3,256,128]{2,1,0:T(8,128)(2,1)S(1)}, u32[]{:S(2)}, u32[]{:S(2)}) collective-permute-start(bf16[3,256,128]{2,1,0:T(8,128)(2,1)S(1)} %collective-permute-done.5), channel_id=1, source_target_pairs={{0,16},{16,32},{32,48},{48,64},{64,80},{80,96},{96,112},{112,0},{1... | collective-permute-start | bytes 589832 | tf_op jit(solution)/shard_map/ppermute | solution.py:65
  129.4 1.5 copy-start.9
  129.4 1.5 copy-start.10
  129.5 1.5 copy-start.11
  129.7 1.2 copy-start.3
  134.5 1.5 copy-start.18
  134.5 1.5 copy-start.24
  136.1 11.0 %copy-start.20 = (f32[32,128]{1,0:T(8,128)}, f32[32,128]{1,0:T(8,128)S(1)}, u32[]{:S(2)}) copy-start(f32[32,128]{1,0:T(8,128)S(1)} %fusion.64) | copy-start | bytes 49156
  137.2 31.9 %all-to-all-start.3 = ((bf16[32,32,512]{2,1,0:T(8,128)(2,1)}), bf16[32,32,512]{2,1,0:T(8,128)(2,1)}, u32[]{:S(2)}, u32[]{:S(2)}) async-start(bf16[32,32,512]{2,1,0:T(8,128)(2,1)} %broadcast_in_dim.90), calls=%async_computation.3 | async-start | bytes 2097152 | tf_op jit(solution)/shard_map/all_to_all | solution.py:22
  145.1 2.6 copy-start.1
  147.7 2.3 copy-start.4
  147.7 2.3 copy-start.6
  147.7 2.3 copy-start.7
  147.7 2.5 copy-start.8
  151.6 1.9 copy-start.2
  152.6 21.7 %copy-start.15 = (f32[192,128]{1,0:T(8,128)}, f32[192,128]{1,0:T(8,128)S(1)}, u32[]{:S(2)}) copy-start(f32[192,128]{1,0:T(8,128)S(1)} %convolution_bitcast_fusion) | copy-start | bytes 294916
  153.5 15.6 %copy-start.22 = (f32[192,128]{1,0:T(8,128)S(1)}, f32[192,128]{1,0:T(8,128)}, u32[]{:S(2)}) copy-start(f32[192,128]{1,0:T(8,128)} %convolution_add_fusion.2) | copy-start | bytes 294916
  154.4 21.4 %copy-start.12 = (f32[192,256]{1,0:T(8,128)}, f32[192,256]{1,0:T(8,128)S(1)}, u32[]{:S(2)}) copy-start(f32[192,256]{1,0:T(8,128)S(1)} %convolution_add_fusion.1) | copy-start | bytes 589828
  169.1 5.2 %copy-start.17 = (f32[192,1,512]{2,1,0:T(1,128)S(1)}, f32[192,1,512]{2,1,0:T(1,128)}, u32[]{:S(2)}) copy-start(f32[192,1,512]{2,1,0:T(1,128)} %get-tuple-element.43) | copy-start | bytes 1179652
  169.1 5.2 %copy-start.27 = (f32[192]{0:T(256)S(1)}, f32[192]{0:T(256)}, u32[]{:S(2)}) copy-start(f32[192]{0:T(256)} %convert_multiply_fusion) | copy-start | bytes 2308
  170.7 3.6 collective-permute-start.8
  223.9 33.4 %all-to-all-start.6 = ((bf16[32,32,512]{2,1,0:T(8,128)(2,1)}), bf16[32,32,512]{2,1,0:T(8,128)(2,1)}, u32[]{:S(2)}, u32[]{:S(2)}) async-start(bf16[32,32,512]{2,1,0:T(8,128)(2,1)} %bitcast.139), calls=%async_computation.6 | async-start | bytes 2097152 | tf_op jit(solution)/shard_map/all_to_all | solution.py:26
  234.4 1.7 copy-start.13
  234.4 1.7 copy-start.16
  234.4 1.7 copy-start.23
  234.4 1.7 copy-start.28
  236.1 22.5 %copy-start.19 = (f32[32,256]{1,0:T(8,128)S(1)}, f32[32,256]{1,0:T(8,128)}, u32[]{:S(2)}) copy-start(f32[32,256]{1,0:T(8,128)} %convolution_add_fusion.3) | copy-start | bytes 98308
  236.1 22.5 %copy-start.21 = (f32[32,128]{1,0:T(8,128)S(1)}, f32[32,128]{1,0:T(8,128)}, u32[]{:S(2)}) copy-start(f32[32,128]{1,0:T(8,128)} %copy-done.20) | copy-start | bytes 49156
  236.1 22.5 %copy-start.25 = (f32[32]{0:T(128)S(1)}, f32[32]{0:T(128)}, u32[]{:S(2)}) copy-start(f32[32]{0:T(128)} %convert_multiply_fusion.1) | copy-start | bytes 388
  363.3 16.4 %all-to-all-start.13 = ((bf16[32,8,512]{2,1,0:T(8,128)(2,1)}), bf16[32,8,512]{2,1,0:T(8,128)(2,1)S(1)}, u32[]{:S(2)}, u32[]{:S(2)}) async-start(bf16[32,8,512]{2,1,0:T(8,128)(2,1)} %fusion.9), calls=%async_computation.13 | async-start | bytes 524288 | tf_op jit(solution)/shard_map/all_to_all | solution.py:26
Sparse Core Ops, SparseCore 0:
  10.1 49.2 all-gather.2
  61.4 54.9 all-gather.4

commit v15 on v12

--- a/solution.py
+++ b/solution.py
@@ -149,7 +149,8 @@
             preferred_element_type=jnp.float32,
         )
         terms.append(product - lax.dynamic_index_in_dim(plain, part, 0, keepdims=False))
-    core_err = terms[1] + lax.ppermute(terms[0], "core", [(0, 1), (1, 0)])
+    core_err = lax.optimization_barrier(terms[1])
+    core_err = core_err + lax.ppermute(terms[0], "core", [(0, 1), (1, 0)])
     own_err = sum_blocks(core_err.reshape(lax.axis_size("chip"), -1, half), "chip")
     err_bf = gather_blocks(own_err.astype(jnp.bfloat16), ("core", "chip")).reshape(2, tok_rows, half)
     recon_error = err_bf.transpose(1, 0, 2).reshape(tok_rows, channels).astype(jnp.float32)

time: 382 us -> 380 us (level)
  no operation moved by 1% of the time
where the time goes in v15:
time: 380 us; the launch traced here: 379 us
  blocking collectives  144 us (38%)
  waiting for transfers between devices  111 us (29%)
  starting transfers between devices  45.2 us (12%)
  local copies, waits for them, and re-layouts  23.4 us (6%)
  matrix products  21.8 us (6%)
  other arithmetic  18.6 us (5%)
  between operations  14.5 us (4%)
    all_to_all x4, blocking collectives, sum_blocks(): return jnp.sum(lax.all_to_all(blocks, axis, 0, 0).astype(jnp.float32), 0)  76.3 us
    all_to_all x4, blocking collectives, gather_blocks(): lax.all_to_all(jnp.broadcast_to(own[None], (parts,) + own.shape), axis, 0...  67.5 us
    all_to_all x4, waiting for transfers between devices, gather_blocks(): lax.all_to_all(jnp.broadcast_to(own[None], (parts,) + own.shape), axis, 0...  50.5 us
    all_to_all x2, waiting for transfers between devices, sum_blocks(): return jnp.sum(lax.all_to_all(blocks, axis, 0, 0).astype(jnp.float32), 0)  31.6 us
    all_to_all x4, starting transfers between devices, gather_blocks(): lax.all_to_all(jnp.broadcast_to(own[None], (parts,) + own.shape), axis, 0...  30.5 us
    all_gather x1, waiting for transfers between devices, gather_rotation(): near = lax.all_gather(rot_b, 'ring', axis=0, tiled=True)  15.8 us
    all_gather x1, waiting for transfers between devices, gather_rotation(): far = lax.all_gather(others, 'ring', axis=1, tiled=True)  13.1 us
    all_to_all x2, starting transfers between devices, sum_blocks(): return jnp.sum(lax.all_to_all(blocks, axis, 0, 0).astype(jnp.float32), 0)  10.8 us
  transfers between devices with their start and end apart: 10, of which 8 were waited for; matrix products, arithmetic and copies ran while one was open for 11% of the time, Pallas kernels for 0%

profile of v15, /device:TPU:8, one launch (start us, length us, event | category | flops | bytes accessed | tf_op | source)
XLA Modules:
  0.0 378.5 jit_solution(5864834809094999998)
XLA Ops:
  7.2 1.9 convert_element_type.82
  11.0 9.3 %all-to-all-start.1 = ((bf16[4,256,384]{2,1,0:T(8,128)(2,1)}), bf16[4,256,384]{2,1,0:T(8,128)(2,1)S(1)}, u32[]{:S(2)}, u32[]{:S(2)}) async-start(bf16[4,256,384]{2,1,0:T(8,128)(2,1)} %broadcast_in_dim.17), calls=%async_computation.1 | async-start | bytes 1572864 | tf_op jit(solution)/shard_map/all_to_all | solution.py:22
  20.3 12.9 %all-to-all-done.1 = bf16[4,256,384]{2,1,0:T(8,128)(2,1)S(1)} async-done(((bf16[4,256,384]{2,1,0:T(8,128)(2,1)}), bf16[4,256,384]{2,1,0:T(8,128)(2,1)S(1)}, u32[]{:S(2)}, u32[]{:S(2)}) %all-to-all-start.1) | async-done | bytes 786464 | tf_op jit(solution)/shard_map/all_to_all | solution.py:22
  35.1 8.4 %all-to-all-start.2 = ((bf16[8,32,512]{2,1,0:T(8,128)(2,1)}), bf16[8,32,512]{2,1,0:T(8,128)(2,1)S(1)}, u32[]{:S(2)}, u32[]{:S(2)}) async-start(bf16[8,32,512]{2,1,0:T(8,128)(2,1)} %broadcast_in_dim.18), calls=%async_computation.2 | async-start | bytes 524288 | tf_op jit(solution)/shard_map/all_to_all | solution.py:22
  43.6 15.8 %all-gather.3.cloned.1.call-done = bf16[2048,512]{1,0:T(8,128)(2,1)} async-done(((bf16[256,512]{1,0:T(8,128)(2,1)}), bf16[2048,512]{1,0:T(8,128)(2,1)}) %all-gather.3.cloned.1.call-update) | async-done | bytes 2097168 | tf_op jit(solution)/shard_map/all_gather | solution.py:52
  59.3 1.1 slice.127
  60.4 1.7 broadcast_in_dim.16
  62.1 5.1 %all-to-all-start = ((bf16[4,2048,128]{2,1,0:T(8,128)(2,1)}), bf16[4,2048,128]{2,1,0:T(8,128)(2,1)S(1)}, u32[]{:S(2)}, u32[]{:S(2)}) async-start(bf16[4,2048,128]{2,1,0:T(8,128)(2,1)} %broadcast_in_dim.16), calls=%async_computation | async-start | bytes 4194304 | tf_op jit(solution)/shard_map/all_to_all | solution.py:22
  67.2 2.2 fusion.27
  69.4 3.4 broadcast_select_fusion.2
  72.8 1.9 collective-permute-start
  74.7 1.3 convert_multiply_fusion.1
  76.0 2.7 reshape.98
  80.3 1.3 copy.18
  81.6 2.3 reshape.91
  83.9 1.1 broadcast_select_fusion.6
  85.1 2.7 fusion
  87.8 20.3 %all-to-all-done = bf16[4,2048,128]{2,1,0:T(8,128)(2,1)S(1)} async-done(((bf16[4,2048,128]{2,1,0:T(8,128)(2,1)}), bf16[4,2048,128]{2,1,0:T(8,128)(2,1)S(1)}, u32[]{:S(2)}, u32[]{:S(2)}) %all-to-all-start) | async-done | bytes 2097184 | tf_op jit(solution)/shard_map/all_to_all | solution.py:22
  108.1 1.5 fusion.64
  109.6 13.1 %all-gather.5.cloned.1.call-done = bf16[3,2048,384]{2,1,0:T(8,128)(2,1)} async-done(((bf16[3,256,384]{2,1,0:T(8,128)(2,1)}), bf16[3,2048,384]{2,1,0:T(8,128)(2,1)}) %all-gather.5.cloned.1.call-update) | async-done | bytes 4718608 | tf_op jit(solution)/shard_map/all_gather | solution.py:54
  122.7 3.1 convolution_add_fusion.2
  126.5 1.2 broadcast_in_dim.19
  127.7 7.7 %all-to-all-start.3 = ((bf16[32,32,512]{2,1,0:T(8,128)(2,1)}), bf16[32,32,512]{2,1,0:T(8,128)(2,1)}, u32[]{:S(2)}, u32[]{:S(2)}) async-start(bf16[32,32,512]{2,1,0:T(8,128)(2,1)} %broadcast_in_dim.19), calls=%async_computation.3 | async-start | bytes 2097152 | tf_op jit(solution)/shard_map/all_to_all | solution.py:22
  135.4 3.2 constant_dynamic-slice_fusion
  138.6 2.0 pad_maximum_fusion
  143.4 1.4 convolution_add_fusion.1
  144.9 17.3 %all-to-all-done.3 = bf16[32,32,512]{2,1,0:T(8,128)(2,1)} async-done(((bf16[32,32,512]{2,1,0:T(8,128)(2,1)}), bf16[32,32,512]{2,1,0:T(8,128)(2,1)}, u32[]{:S(2)}, u32[]{:S(2)}) %all-to-all-start.3) | async-done | bytes 1048608 | tf_op jit(solution)/shard_map/all_to_all | solution.py:22
  162.2 1.6 convolution_subtract_fusion.2
  163.7 1.9 collective-permute-start.1
  165.7 1.4 convolution_subtract_fusion.3
  167.4 23.6 %all_to_all.70 = f32[8,24,512]{2,1,0:T(8,128)S(1)} all-to-all(f32[8,24,512]{2,1,0:T(8,128)S(1)} %bitcast.114), channel_id=1, replica_groups=mesh['line'=4,'ring'=8,'chip'=8,'core'=2] {'chip'}, dimensions={0} | all-to-all | bytes 786432 | tf_op jit(solution)/shard_map/all_to_all | solution.py:26
  192.4 19.1 %all_to_all.71 = bf16[16,24,512]{2,1,0:T(8,128)(2,1)S(1)} all-to-all(bf16[16,24,512]{2,1,0:T(8,128)(2,1)S(1)} %broadcast_in_dim.20), channel_id=1, replica_groups=mesh['line'=4,'ring'=8,'chip'=8,'core'=2] {'core','chip'}, dimensions={0} | all-to-all | bytes 786432 | tf_op jit(solution)/shard_map/all_to_all | solution.py:22
  211.5 2.6 convolution_convert_fusion
  214.1 6.0 %all-to-all-start.6 = ((bf16[32,32,512]{2,1,0:T(8,128)(2,1)}), bf16[32,32,512]{2,1,0:T(8,128)(2,1)}, u32[]{:S(2)}, u32[]{:S(2)}) async-start(bf16[32,32,512]{2,1,0:T(8,128)(2,1)} %bitcast.119), calls=%async_computation.6 | async-start | bytes 2097152 | tf_op jit(solution)/shard_map/all_to_all | solution.py:26
  222.0 1.0 fusion.24
  223.8 1.3 fusion.62
  225.8 21.1 %all-to-all-done.6 = bf16[32,32,512]{2,1,0:T(8,128)(2,1)} async-done(((bf16[32,32,512]{2,1,0:T(8,128)(2,1)}), bf16[32,32,512]{2,1,0:T(8,128)(2,1)}, u32[]{:S(2)}, u32[]{:S(2)}) %all-to-all-start.6) | async-done | bytes 1048608 | tf_op jit(solution)/shard_map/all_to_all | solution.py:26
  246.9 1.4 convert_reduce_fusion
  248.4 1.3 convolution_convert_fusion.2
  249.8 17.4 %all_to_all.72 = bf16[16,16,448]{2,1,0:T(8,128)(2,1)S(1)} all-to-all(bf16[16,16,448]{2,1,0:T(8,128)(2,1)S(1)} %bitcast.120), channel_id=1, replica_groups=mesh['line'=4,'ring'=8,'chip'=8,'core'=2] {'chip','core'}, dimensions={0} | all-to-all | bytes 458752 | tf_op jit(solution)/shard_map/all_to_all | solution.py:26
  267.2 16.0 %all_to_all.73 = bf16[16,16,448]{2,1,0:T(8,128)(2,1)S(1)} all-to-all(bf16[16,16,448]{2,1,0:T(8,128)(2,1)S(1)} %broadcast_in_dim.21), channel_id=1, replica_groups=mesh['line'=4,'ring'=8,'chip'=8,'core'=2] {'chip','core'}, dimensions={0} | all-to-all | bytes 458752 | tf_op jit(solution)/shard_map/all_to_all | solution.py:22
  283.8 17.9 %all_to_all.74 = bf16[32,8,512]{2,1,0:T(8,128)(2,1)S(1)} all-to-all(bf16[32,8,512]{2,1,0:T(8,128)(2,1)S(1)} %fusion.9), channel_id=1, replica_groups=mesh['line'=4,'ring'=8,'chip'=8,'core'=2] {'line','ring'}, dimensions={0} | all-to-all | bytes 524288 | tf_op jit(solution)/shard_map/all_to_all | solution.py:26
  302.4 16.5 %all_to_all.75 = bf16[32,8,512]{2,1,0:T(8,128)(2,1)S(1)} all-to-all(bf16[32,8,512]{2,1,0:T(8,128)(2,1)S(1)} %broadcast_in_dim.22), channel_id=1, replica_groups=mesh['line'=4,'ring'=8,'chip'=8,'core'=2] {'line','ring'}, dimensions={0} | all-to-all | bytes 524288 | tf_op jit(solution)/shard_map/all_to_all | solution.py:22
  319.3 17.5 %all_to_all.76 = bf16[16,16,448]{2,1,0:T(8,128)(2,1)S(1)} all-to-all(bf16[16,16,448]{2,1,0:T(8,128)(2,1)S(1)} %bitcast.121), channel_id=1, replica_groups=mesh['line'=4,'ring'=8,'chip'=8,'core'=2] {'chip','core'}, dimensions={0} | all-to-all | bytes 458752 | tf_op jit(solution)/shard_map/all_to_all | solution.py:26
  336.9 15.8 %all_to_all.77 = bf16[16,16,448]{2,1,0:T(8,128)(2,1)S(1)} all-to-all(bf16[16,16,448]{2,1,0:T(8,128)(2,1)S(1)} %broadcast_in_dim.23), channel_id=1, replica_groups=mesh['line'=4,'ring'=8,'chip'=8,'core'=2] {'chip','core'}, dimensions={0} | all-to-all | bytes 458752 | tf_op jit(solution)/shard_map/all_to_all | solution.py:22
  354.0 4.9 %all-to-all-start.13 = ((bf16[32,8,512]{2,1,0:T(8,128)(2,1)}), bf16[32,8,512]{2,1,0:T(8,128)(2,1)S(1)}, u32[]{:S(2)}, u32[]{:S(2)}) async-start(bf16[32,8,512]{2,1,0:T(8,128)(2,1)} %fusion.8), calls=%async_computation.13 | async-start | bytes 524288 | tf_op jit(solution)/shard_map/all_to_all | solution.py:26
  359.9 10.5 %all-to-all-done.13 = bf16[32,8,512]{2,1,0:T(8,128)(2,1)S(1)} async-done(((bf16[32,8,512]{2,1,0:T(8,128)(2,1)}), bf16[32,8,512]{2,1,0:T(8,128)(2,1)S(1)}, u32[]{:S(2)}, u32[]{:S(2)}) %all-to-all-start.13) | async-done | bytes 262176 | tf_op jit(solution)/shard_map/all_to_all | solution.py:26
  370.4 1.3 multiply_subtract_fusion
  (85 shorter events, 18.4 us)
Async XLA Ops:
  7.2 27.0 %copy-start = (bf16[512,1024]{1,0:T(8,128)(2,1)S(1)}, bf16[512,1024]{1,0:T(8,128)(2,1)}, u32[]{:S(2)}) copy-start(bf16[512,1024]{1,0:T(8,128)(2,1)} %param.7) | copy-start | bytes 3145732
  7.2 52.2 %all-gather.3.cloned.1.call-start = ((), (), s32[]{:S(2)}) async-start(), calls=%async_computation.14 | async-start | bytes 2359296 | tf_op jit(solution)/shard_map/all_gather | solution.py:52
  11.0 22.2 %all-to-all-start.1 = ((bf16[4,256,384]{2,1,0:T(8,128)(2,1)}), bf16[4,256,384]{2,1,0:T(8,128)(2,1)S(1)}, u32[]{:S(2)}, u32[]{:S(2)}) async-start(bf16[4,256,384]{2,1,0:T(8,128)(2,1)} %broadcast_in_dim.17), calls=%async_computation.1 | async-start | bytes 1572864 | tf_op jit(solution)/shard_map/all_to_all | solution.py:22
  20.3 102.4 %all-gather.5.cloned.1.call-start = ((), (), s32[]{:S(2)}) async-start(), calls=%async_computation.15 | async-start | bytes 5308416 | tf_op jit(solution)/shard_map/all_gather | solution.py:54
  35.1 25.3 %all-to-all-start.2 = ((bf16[8,32,512]{2,1,0:T(8,128)(2,1)}), bf16[8,32,512]{2,1,0:T(8,128)(2,1)S(1)}, u32[]{:S(2)}, u32[]{:S(2)}) async-start(bf16[8,32,512]{2,1,0:T(8,128)(2,1)} %broadcast_in_dim.18), calls=%async_computation.2 | async-start | bytes 524288 | tf_op jit(solution)/shard_map/all_to_all | solution.py:22
  62.1 46.0 %all-to-all-start = ((bf16[4,2048,128]{2,1,0:T(8,128)(2,1)}), bf16[4,2048,128]{2,1,0:T(8,128)(2,1)S(1)}, u32[]{:S(2)}, u32[]{:S(2)}) async-start(bf16[4,2048,128]{2,1,0:T(8,128)(2,1)} %broadcast_in_dim.16), calls=%async_computation | async-start | bytes 4194304 | tf_op jit(solution)/shard_map/all_to_all | solution.py:22
  69.4 9.3 %copy-start.12 = (s32[192]{0:T(256)S(1)}, s32[192]{0:T(256)}, u32[]{:S(2)}) copy-start(s32[192]{0:T(256)} %param.8) | copy-start | bytes 2308
  72.8 6.5 %collective-permute-start = (bf16[8,32,512]{2,1,0:T(8,128)(2,1)S(1)}, bf16[8,32,512]{2,1,0:T(8,128)(2,1)}, u32[]{:S(2)}, u32[]{:S(2)}) collective-permute-start(bf16[8,32,512]{2,1,0:T(8,128)(2,1)S(1)} %all-to-all-done.2), channel_id=1, source_target_pairs={{0,1},{1,0},{2,3},{3,2},{4,5},{5,4},{6,7},{7,6},{8,9},{9,8},{10,11... | collective-permute-start | bytes 786440 | tf_op jit(solution)/shard_map/ppermute | solution.py:114
  122.7 3.7 copy-start.10
  125.8 0.6 copy-start.6
  127.7 34.4 %all-to-all-start.3 = ((bf16[32,32,512]{2,1,0:T(8,128)(2,1)}), bf16[32,32,512]{2,1,0:T(8,128)(2,1)}, u32[]{:S(2)}, u32[]{:S(2)}) async-start(bf16[32,32,512]{2,1,0:T(8,128)(2,1)} %broadcast_in_dim.19), calls=%async_computation.3 | async-start | bytes 2097152 | tf_op jit(solution)/shard_map/all_to_all | solution.py:22
  135.4 5.2 %copy-start.9 = (bf16[2048,512]{1,0:T(8,128)(2,1)S(1)}, bf16[2048,512]{1,0:T(8,128)(2,1)}, u32[]{:S(2)}) copy-start(bf16[2048,512]{1,0:T(8,128)(2,1)} %all-gather.3.cloned.1.call-done) | copy-start | bytes 6291460
  138.6 2.6 copy-start.1
  138.6 4.3 %slice-start = ((s8[4718592]{0:T(1024)(128)(4,1)}), s8[524288]{0:T(1024)(128)(4,1)S(1)}, s32[]{:S(2)}) async-start(s8[4718592]{0:T(1024)(128)(4,1)} %bitcast.105), calls=%async_computation.16 | async-start | bytes 1048576
  141.2 2.2 slice-start.1
  142.9 22.7 %copy-start.4 = (f32[192,128]{1,0:T(8,128)}, f32[192,128]{1,0:T(8,128)S(1)}, u32[]{:S(2)}) copy-start(f32[192,128]{1,0:T(8,128)S(1)} %convolution_bitcast_fusion) | copy-start | bytes 294916
  144.8 22.2 %copy-start.2 = (f32[192,384]{1,0:T(8,128)}, f32[192,384]{1,0:T(8,128)S(1)}, u32[]{:S(2)}) copy-start(f32[192,384]{1,0:T(8,128)S(1)} %convolution_add_fusion.1) | copy-start | bytes 884740
  162.2 3.5 copy-start.8
  162.2 3.5 copy-start.13
  163.7 3.6 collective-permute-start.1
  214.1 32.8 %all-to-all-start.6 = ((bf16[32,32,512]{2,1,0:T(8,128)(2,1)}), bf16[32,32,512]{2,1,0:T(8,128)(2,1)}, u32[]{:S(2)}, u32[]{:S(2)}) async-start(bf16[32,32,512]{2,1,0:T(8,128)(2,1)} %bitcast.119), calls=%async_computation.6 | async-start | bytes 2097152 | tf_op jit(solution)/shard_map/all_to_all | solution.py:26
  223.1 2.4 copy-start.3
  223.1 2.4 copy-start.5
  223.1 2.4 copy-start.14
  225.2 23.1 %copy-start.7 = (f32[32,384]{1,0:T(8,128)S(1)}, f32[32,384]{1,0:T(8,128)}, u32[]{:S(2)}) copy-start(f32[32,384]{1,0:T(8,128)} %copy-done.6) | copy-start | bytes 147460
  225.2 23.1 %copy-start.11 = (f32[32]{0:T(128)S(1)}, f32[32]{0:T(128)}, u32[]{:S(2)}) copy-start(f32[32]{0:T(128)} %convert_multiply_fusion.1) | copy-start | bytes 388
  354.0 16.4 %all-to-all-start.13 = ((bf16[32,8,512]{2,1,0:T(8,128)(2,1)}), bf16[32,8,512]{2,1,0:T(8,128)(2,1)S(1)}, u32[]{:S(2)}, u32[]{:S(2)}) async-start(bf16[32,8,512]{2,1,0:T(8,128)(2,1)} %fusion.8), calls=%async_computation.13 | async-start | bytes 524288 | tf_op jit(solution)/shard_map/all_to_all | solution.py:26
Sparse Core Ops, SparseCore 0:
  10.1 49.2 all-gather.2
  61.4 61.2 all-gather.4
